TPU v7x, 32 devices: a whole 2x2x4 slice. The times are simulated.
32 devices in a mesh: dp: 16 (over z, y, x), tensor: 2 (over core).
Axes of the slice: x: 2, y: 2, z: 4, core: 2. Of those that a mesh axis runs over, the one named last changes fastest.
Arguments:
- states: bfloat16 [128, 128, 768], P('dp'), may hold values from -6 to 6
- cotangent: bfloat16 [128, 128, 768], P('dp'), may hold values from -6 to 6
- word_counts: int32 [128], P('dp'), may hold values from 5 to 60, as said below
- region_counts: int32 [128], P('dp'), may hold values from 36 to 68, as said below
- attend_in: float32 [3, 768, 768], P(None, 'dp', 'tensor')
- attend_out: float32 [768, 768], P('tensor', 'dp')
- expand_up: float32 [768, 3072], P('dp', 'tensor')
- expand_down: float32 [3072, 768], P(('tensor', 'dp'))
- first_in: float32 [3, 768, 768], P(None, 'dp', 'tensor')
- first_out: float32 [768, 768], P('tensor', 'dp')
- first_up: float32 [768, 3072], P('dp', 'tensor')
- first_down: float32 [3072, 768], P(('tensor', 'dp'))
- second_in: float32 [3, 768, 768], P(None, 'dp', 'tensor'), may hold values from 8.192 to 32.768
- second_out: float32 [768, 768], P('tensor', 'dp'), may hold values from 0.32768 to 1.31072
- second_up: float32 [768, 3072], P('dp', 'tensor'), may hold values from 8.192 to 32.768
- second_down: float32 [3072, 768], P(('tensor', 'dp')), may hold values from 8.192 to 32.768
- vectors: float32 [12, 768], replicated, as said below
- vector_first: float32 [12, 768], replicated, may hold values from -64 to 64
- vector_second: float32 [12, 768], replicated, may hold values from 8.192 to 32.768
Outputs:
- layer_output: bfloat16 [128, 128, 768], P('dp')
- states_grad: float32 [128, 128, 768], P('dp')
- updated_in: float32 [3, 768, 768], P(None, 'dp', 'tensor')
- updated_out: float32 [768, 768], P('tensor', 'dp')
- updated_up: float32 [768, 3072], P('dp', 'tensor')
- updated_down: float32 [3072, 768], P(('tensor', 'dp'))
- moment_in: float32 [3, 768, 768], P(None, 'dp', 'tensor')
- moment_out: float32 [768, 768], P('tensor', 'dp')
- moment_up: float32 [768, 3072], P('dp', 'tensor')
- moment_down: float32 [3072, 768], P(('tensor', 'dp'))
- square_in: float32 [3, 768, 768], P(None, 'dp', 'tensor')
- square_out: float32 [768, 768], P('tensor', 'dp')
- square_up: float32 [768, 3072], P('dp', 'tensor')
- square_down: float32 [3072, 768], P(('tensor', 'dp'))
- copy_in: bfloat16 [3, 768, 768], P(None, 'dp', 'tensor')
- copy_out: bfloat16 [768, 768], P('tensor', 'dp')
- copy_up: bfloat16 [768, 3072], P('dp', 'tensor')
- copy_down: bfloat16 [3072, 768], P(('tensor', 'dp'))
- updated_vectors: float32 [12, 768], replicated
- moment_vectors: float32 [12, 768], replicated
- square_vectors: float32 [12, 768], replicated
- norm_pairs: float32 [6, 2], replicated
Inputs may be any that keep to these rules, and one draw needn't show every extreme that they name: `word_counts`: each pair's number of words; in every draw some pair has exactly 60 and some pair exactly 5, most pairs few. `region_counts`: each pair's number of image regions; in every draw some pair has exactly 68 and some pair exactly 36. `vectors`: rows 3 and 6 are positive.
All inputs are finite; a program needn't handle non-finite values.
Results may differ from a plain program's by a relative error of at most 0.014.
Values may be sent and summed in bfloat16 or wider, within the bound.
No kernel may reach another device: no remote copies, remote signals or barrier semaphores. Data moves between devices by JAX's collectives and lax.ppermute only.
A program may use at most 128 MiB of HBM per device.

v0:
```python
import jax
import jax.numpy as jnp
from jax import lax
from jax.sharding import PartitionSpec as P

HEAD_DIM = 64
FF = 3072
STEP = 10


NORM_EPS = 1e-05
BETA_ONE = 0.9
BETA_TWO = 0.999
ADAM_EPS = 1e-06
RATE = 0.3
DECAY = 0.01
MASKED = -1e30


def norm_forward(values, gain, shift):
    center = values - jnp.mean(values, axis=-1, keepdims=True)
    inverse = lax.rsqrt(jnp.mean(center * center, axis=-1, keepdims=True) + NORM_EPS)
    normed = center * inverse
    return (normed * gain + shift, normed, inverse)


def norm_backward(upstream, normed, inverse, gain):
    scaled = upstream * gain
    inner = jnp.mean(scaled * normed, axis=-1, keepdims=True)
    downstream = inverse * (scaled - jnp.mean(scaled, axis=-1, keepdims=True) - normed * inner)
    return (downstream, jnp.sum(upstream * normed, axis=0), jnp.sum(upstream, axis=0))


def attend_scores(query, key_rows, valid, scale):
    scores = (
        jnp.einsum("pqhd,pkhd->phqk", query, key_rows, preferred_element_type=jnp.float32) * scale
    )
    return jnp.where(valid[:, None, None, :], scores, MASKED)


def adam_terms(grad, first, second):
    first_new = BETA_ONE * first + (1.0 - BETA_ONE) * grad
    second_new = BETA_TWO * second + (1.0 - BETA_TWO) * grad * grad
    corrected = first_new / (1.0 - BETA_ONE**STEP)
    spread = jnp.sqrt(second_new / (1.0 - BETA_TWO**STEP))
    return (first_new, second_new, corrected / (spread + ADAM_EPS))


def weight_squares(mats):
    rest = jnp.stack([jnp.sum(item * item) for item in mats[1:]])
    return jnp.concatenate([jnp.sum(mats[0] * mats[0], axis=(1, 2)), rest])


def body(
    states,
    cotangent,
    word_counts,
    region_counts,
    attend_in,
    attend_out,
    expand_up,
    expand_down,
    first_in,
    first_out,
    first_up,
    first_down,
    second_in,
    second_out,
    second_up,
    second_down,
    vectors,
    vector_first,
    vector_second,
):
    pairs, length, width = states.shape
    total_rows = pairs * length
    local_cols = attend_in.shape[2]
    heads_local = local_cols // HEAD_DIM
    ffn_local = expand_up.shape[1]
    tensor_rank = lax.axis_index("tensor")
    scale = HEAD_DIM ** (-0.5)
    masters = (attend_in, attend_out, expand_up, expand_down)
    weight_in, weight_out, weight_up, weight_down = (
        lax.all_gather(attend_in.astype(jnp.bfloat16), "dp", axis=1, tiled=True),
        lax.all_gather(attend_out.astype(jnp.bfloat16), "dp", axis=1, tiled=True),
        lax.all_gather(expand_up.astype(jnp.bfloat16), "dp", axis=0, tiled=True),
        lax.all_gather(expand_down.astype(jnp.bfloat16), "dp", axis=0, tiled=True),
    )
    bias_query = lax.dynamic_slice_in_dim(vectors[0], tensor_rank * local_cols, local_cols)
    bias_value = lax.dynamic_slice_in_dim(vectors[1], tensor_rank * local_cols, local_cols)
    bias_up = lax.dynamic_slice_in_dim(vectors[8:].reshape(-1), tensor_rank * ffn_local, ffn_local)
    lengths = word_counts + region_counts
    valid = jnp.arange(length, dtype=jnp.int32)[None, :] < lengths[:, None]
    flat = states.reshape(total_rows, width)
    head_shape = (pairs, length, heads_local, HEAD_DIM)
    row_valid = valid.reshape(total_rows, 1).astype(jnp.float32)
    cot_flat = cotangent.reshape(total_rows, width)
    projected = jnp.einsum("rd,kdc->krc", flat, weight_in, preferred_element_type=jnp.float32)
    query = (projected[0] + bias_query).astype(jnp.bfloat16).reshape(head_shape)
    key_rows = projected[1].astype(jnp.bfloat16).reshape(head_shape)
    value = (projected[2] + bias_value).astype(jnp.bfloat16).reshape(head_shape)
    scores = attend_scores(query, key_rows, valid, scale)
    top = jnp.max(scores, axis=-1, keepdims=True)
    expo = jnp.exp(scores - top)
    total = jnp.sum(expo, axis=-1, keepdims=True)
    probs = (expo / total).astype(jnp.bfloat16)
    log_total = top + jnp.log(total)
    context = (
        jnp.einsum("phqk,pkhd->pqhd", probs, value, preferred_element_type=jnp.float32)
        .reshape(total_rows, local_cols)
        .astype(jnp.bfloat16)
    )
    attend_part = jnp.dot(context, weight_out, preferred_element_type=jnp.float32)
    attended = lax.psum(attend_part, "tensor")
    hidden, normed_one, inverse_one = norm_forward(
        flat.astype(jnp.float32) + attended + vectors[2], vectors[3], vectors[4]
    )
    hidden_low = hidden.astype(jnp.bfloat16)
    lifted = jnp.dot(hidden_low, weight_up, preferred_element_type=jnp.float32) + bias_up
    activated = jax.nn.gelu(lifted, approximate=False).astype(jnp.bfloat16)
    lowered_part = jnp.dot(activated, weight_down, preferred_element_type=jnp.float32)
    lowered = lax.psum(lowered_part, "tensor")
    output, normed_two, inverse_two = norm_forward(
        hidden + lowered + vectors[5], vectors[6], vectors[7]
    )
    layer_output = output.astype(jnp.bfloat16).reshape(pairs, length, width)
    upstream = cot_flat.astype(jnp.float32) * row_valid
    grad_top, gain_two_grad, shift_two_grad = norm_backward(
        upstream, normed_two, inverse_two, vectors[6]
    )
    grad_lowered = grad_top.astype(jnp.bfloat16)
    grad_down = jnp.einsum("rf,rd->fd", activated, grad_lowered, preferred_element_type=jnp.float32)
    grad_active = jnp.einsum(
        "rd,fd->rf", grad_lowered, weight_down, preferred_element_type=jnp.float32
    )
    unused, gelu_back = jax.vjp(lambda inner: jax.nn.gelu(inner, approximate=False), lifted)
    grad_lifted = gelu_back(grad_active)[0]
    grad_lifted_low = grad_lifted.astype(jnp.bfloat16)
    grad_up = jnp.einsum(
        "rd,rf->df", hidden_low, grad_lifted_low, preferred_element_type=jnp.float32
    )
    hidden_part = jnp.einsum(
        "rf,df->rd", grad_lifted_low, weight_up, preferred_element_type=jnp.float32
    )
    grad_hidden = grad_top + lax.psum(hidden_part, "tensor")
    grad_mid, gain_one_grad, shift_one_grad = norm_backward(
        grad_hidden, normed_one, inverse_one, vectors[3]
    )
    grad_attended = grad_mid.astype(jnp.bfloat16)
    grad_out = jnp.einsum("rc,rd->cd", context, grad_attended, preferred_element_type=jnp.float32)
    grad_context = (
        jnp.einsum("rd,cd->rc", grad_attended, weight_out, preferred_element_type=jnp.float32)
        .astype(jnp.bfloat16)
        .reshape(head_shape)
    )
    probs_again = jnp.exp(attend_scores(query, key_rows, valid, scale) - log_total)
    grad_probs = jnp.einsum(
        "pqhd,pkhd->phqk", grad_context, value, preferred_element_type=jnp.float32
    )
    grad_scores = (
        probs_again * (grad_probs - jnp.sum(probs_again * grad_probs, axis=-1, keepdims=True))
    ).astype(jnp.bfloat16)
    grad_query = (
        jnp.einsum("phqk,pkhd->pqhd", grad_scores, key_rows, preferred_element_type=jnp.float32)
        * scale
    )
    grad_key = (
        jnp.einsum("phqk,pqhd->pkhd", grad_scores, query, preferred_element_type=jnp.float32)
        * scale
    )
    grad_value = jnp.einsum(
        "phqk,pqhd->pkhd", probs, grad_context, preferred_element_type=jnp.float32
    )
    grad_parts = jnp.stack([grad_query, grad_key, grad_value]).reshape(3, total_rows, local_cols)
    grad_parts_low = grad_parts.astype(jnp.bfloat16)
    grad_in = jnp.einsum("rd,krc->kdc", flat, grad_parts_low, preferred_element_type=jnp.float32)
    states_part = jnp.einsum(
        "krc,kdc->rd", grad_parts_low, weight_in, preferred_element_type=jnp.float32
    )
    states_grad = (
        grad_mid + lax.psum(states_part.astype(jnp.bfloat16), "tensor").astype(jnp.float32)
    ).reshape(pairs, length, width)
    keep = (tensor_rank == 0).astype(jnp.float32)
    shard_in, shard_out, shard_up, shard_down = (
        lax.psum_scatter(grad_in, "dp", scatter_dimension=1, tiled=True),
        lax.psum_scatter(grad_out, "dp", scatter_dimension=1, tiled=True),
        lax.psum_scatter(grad_up, "dp", scatter_dimension=0, tiled=True),
        lax.psum_scatter(grad_down, "dp", scatter_dimension=0, tiled=True),
    )
    zeros_width = jnp.zeros((width,), jnp.float32)
    start_cols = tensor_rank * local_cols
    bias_rows = jnp.stack(
        [
            lax.dynamic_update_slice_in_dim(
                zeros_width, jnp.sum(grad_parts[0], axis=0), start_cols, 0
            ),
            lax.dynamic_update_slice_in_dim(
                zeros_width, jnp.sum(grad_parts[2], axis=0), start_cols, 0
            ),
            keep * jnp.sum(grad_mid, axis=0),
            keep * gain_one_grad,
            keep * shift_one_grad,
            keep * jnp.sum(grad_top, axis=0),
            keep * gain_two_grad,
            keep * shift_two_grad,
        ]
    )
    up_rows = lax.dynamic_update_slice_in_dim(
        jnp.zeros((FF,), jnp.float32), jnp.sum(grad_lifted, axis=0), tensor_rank * ffn_local, 0
    ).reshape(-1, width)
    vector_grad = lax.psum(jnp.concatenate([bias_rows, up_rows], axis=0), ("dp", "tensor"))
    grads = (shard_in, shard_out, shard_up, shard_down)
    firsts = (first_in, first_out, first_up, first_down)
    seconds = (second_in, second_out, second_up, second_down)
    terms = [adam_terms(grad, first, second) for grad, first, second in zip(grads, firsts, seconds)]
    directions = [term[2] + DECAY * master for term, master in zip(terms, masters)]
    update_squares = weight_squares(directions)
    norm_total = lax.psum(
        jnp.stack([weight_squares(masters), update_squares], axis=1), ("dp", "tensor")
    )
    norm_pairs = jnp.sqrt(norm_total)
    trust = norm_pairs[:, 0] / norm_pairs[:, 1]
    factors = (trust[0:3].reshape(3, 1, 1), trust[3], trust[4], trust[5])
    updated = [
        master - RATE * factor * direction
        for master, factor, direction in zip(masters, factors, directions)
    ]
    vector_moment, vector_square, vector_direction = adam_terms(
        vector_grad, vector_first, vector_second
    )
    updated_vectors = vectors - RATE * vector_direction
    return (
        layer_output,
        states_grad,
        updated[0],
        updated[1],
        updated[2],
        updated[3],
        terms[0][0],
        terms[1][0],
        terms[2][0],
        terms[3][0],
        terms[0][1],
        terms[1][1],
        terms[2][1],
        terms[3][1],
        updated[0].astype(jnp.bfloat16),
        updated[1].astype(jnp.bfloat16),
        updated[2].astype(jnp.bfloat16),
        updated[3].astype(jnp.bfloat16),
        updated_vectors,
        vector_moment,
        vector_square,
        norm_pairs,
    )


def solution(mesh):
    in_specs = (
        P("dp", None, None),
        P("dp", None, None),
        P("dp"),
        P("dp"),
        P(None, "dp", "tensor"),
        P("tensor", "dp"),
        P("dp", "tensor"),
        P(("tensor", "dp"), None),
        P(None, "dp", "tensor"),
        P("tensor", "dp"),
        P("dp", "tensor"),
        P(("tensor", "dp"), None),
        P(None, "dp", "tensor"),
        P("tensor", "dp"),
        P("dp", "tensor"),
        P(("tensor", "dp"), None),
        P(),
        P(),
        P(),
    )
    out_specs = (
        P("dp", None, None),
        P("dp", None, None),
        P(None, "dp", "tensor"),
        P("tensor", "dp"),
        P("dp", "tensor"),
        P(("tensor", "dp"), None),
        P(None, "dp", "tensor"),
        P("tensor", "dp"),
        P("dp", "tensor"),
        P(("tensor", "dp"), None),
        P(None, "dp", "tensor"),
        P("tensor", "dp"),
        P("dp", "tensor"),
        P(("tensor", "dp"), None),
        P(None, "dp", "tensor"),
        P("tensor", "dp"),
        P("dp", "tensor"),
        P(("tensor", "dp"), None),
        P(),
        P(),
        P(),
        P(),
    )
    return jax.shard_map(body, mesh=mesh, in_specs=in_specs, out_specs=out_specs, check_vma=False)
```

profile of v0, /device:TPU:0, one launch (start us, length us, event | category | flops | bytes accessed | tf_op | source)
XLA Modules:
  0.0 1016.4 jit_solution(17823963112772290869)
XLA Ops:
  7.2 1.6 convert_element_type.111
  8.9 1.7 slice_reduce_fusion.1
  13.0 48.8 %all_gather.13 = bf16[384,768]{0,1:T(8,128)(2,1)} all-gather(bf16[384,48]{0,1:T(8,128)(2,1)S(1)} %convert_element_type.119), channel_id=1, replica_groups=mesh['dp'=16,'tensor'=2] {'dp'}, dimensions={1}, use_global_device_ids=true | all-gather | bytes 626688 | tf_op jit(solution)/shard_map/all_gather | solution.py:85
  61.9 12.4 %all-gather.4.cloned.1.call-done = bf16[3,768,384]{2,1,0:T(8,128)(2,1)} async-done(((bf16[3,48,384]{2,1,0:T(8,128)(2,1)}), bf16[3,768,384]{2,1,0:T(8,128)(2,1)}) %all-gather.4.cloned.1.call-update) | async-done | bytes 1769488 | tf_op jit(solution)/shard_map/all_gather | solution.py:84
  74.2 4.0 convolution_bitcast_fusion
  79.6 1.2 fusion.69
  85.5 2.7 fusion.21
  88.3 1.6 convert_element_type.121
  91.1 19.3 %all-reduce.8.cloned.1.call-done = f32[1024,768]{1,0:T(8,128)} async-done(((f32[1024,768]{1,0:T(8,128)}), f32[1024,768]{1,0:T(8,128)}) %all-reduce.8.cloned.1.call-update) | async-done | bytes 3145744 | tf_op jit(solution)/shard_map/psum | solution.py:114
  110.4 2.8 fusion.67
  113.2 1.6 copy-done
  115.4 62.3 %all-gather.6.cloned.1.call-done = bf16[768,1536]{1,0:T(8,128)(2,1)} async-done(((bf16[48,1536]{1,0:T(8,128)(2,1)}), bf16[768,1536]{1,0:T(8,128)(2,1)}) %all-gather.6.cloned.1.call-update) | async-done | bytes 2359312 | tf_op jit(solution)/shard_map/all_gather | solution.py:86
  177.6 19.8 %multiply_convert_fusion = (bf16[1024,1536]{1,0:T(8,128)(2,1)}, f32[1024,1536]{1,0:T(8,128)}, f32[1024,1536]{1,0:T(8,128)}) fusion(f32[1536]{0:T(1024)S(1)} %dynamic_slice.11, bf16[768,1536]{1,0:T(8,128)(2,1)} %all-gather.6.cloned.1.call-done, f32[1024,768]{1,0:T(8,128)} %copy-done, f32[768]{0:T(1024)S(1)} %get-tuple-element.106, ...), kind=kOutput, calls=%fused_computation.3 | convolution fusion | flops 2523660288 | bytes 21254144 | tf_op jit(solution)/shard_map/dot_general | solution.py:119
  197.4 45.0 %all-gather.8.cloned.1.call-done = bf16[1536,768]{1,0:T(8,128)(2,1)} async-done(((bf16[96,768]{1,0:T(8,128)(2,1)}), bf16[1536,768]{1,0:T(8,128)(2,1)}) %all-gather.8.cloned.1.call-update) | async-done | bytes 2359312 | tf_op jit(solution)/shard_map/all_gather | solution.py:87
  242.4 6.9 fusion.71
  250.0 2.7 fusion.7
  252.7 18.8 %all-reduce.10.cloned.1.call-done = f32[1024,768]{1,0:T(8,128)} async-done(((f32[1024,768]{1,0:T(8,128)}), f32[1024,768]{1,0:T(8,128)}) %all-reduce.10.cloned.1.call-update) | async-done | bytes 3145744 | tf_op jit(solution)/shard_map/psum | solution.py:122
  271.5 4.0 fusion.65
  276.9 2.1 multiply_reduce_fusion
  279.1 3.0 fusion.59
  282.1 8.5 fusion.70
  290.6 1.8 copy-done.45
  292.3 4.3 fusion.14
  296.7 24.5 %all-reduce.12.cloned.1.call-done = f32[1024,768]{1,0:T(8,128)} async-done(((f32[1024,768]{1,0:T(8,128)}), f32[1024,768]{1,0:T(8,128)}) %all-reduce.12.cloned.1.call-update) | async-done | bytes 3145744 | tf_op jit(solution)/shard_map/psum | solution.py:145
  321.2 5.4 multiply_reduce_fusion.1
  326.6 1.7 fusion.60
  328.3 2.0 convolution_convert_fusion
  330.3 2.1 fusion.19
  332.3 2.3 copy.120
  334.7 2.2 copy.147
  337.2 4.0 bitcast_convert_fusion.1
  341.2 1.4 copy.129
  342.6 2.2 stack.53
  344.8 2.3 copy.132
  347.2 3.0 multiply_reduce_fusion.2
  351.5 1.2 fusion.17
  353.3 1.2 stack.52
  354.5 2.3 copy.131
  356.9 1.7 bitcast_convert_fusion.2
  360.6 4.2 convolution_bitcast_fusion.1
  364.8 4.0 copy.134
  369.0 1.8 copy-done.2
  370.8 6.6 fusion.12
  377.7 1.6 copy-done.13
  379.3 6.7 fusion.25
  390.1 5.6 bitcast_convert_fusion
  396.6 2.1 concatenate.13
  398.7 64.0 %reduce-scatter.4.cloned.1.call-done = f32[384,48]{0,1:T(8,128)} async-done(((f32[384,768]{0,1:T(8,128)}), f32[384,48]{0,1:T(8,128)}) %reduce-scatter.4.cloned.1.call-update) | async-done | bytes 73744 | tf_op jit(solution)/shard_map/reduce_scatter | solution.py:186
  462.7 2.3 multiply_reduce_fusion.16
  465.0 183.1 %all-reduce.16.cloned.1.call-done = f32[3,768,384]{2,0,1:T(4,128)} async-done(((f32[3,768,384]{2,0,1:T(4,128)}), f32[3,768,384]{2,0,1:T(4,128)}) %all-reduce.16.cloned.1.call-update) | async-done | bytes 3538960
  649.1 2.1 multiply_reduce_fusion.14
  651.2 138.7 %reduce-scatter.6.cloned.1.call-done = f32[48,1536]{1,0:T(8,128)} async-done(((f32[768,1536]{1,0:T(8,128)}), f32[48,1536]{1,0:T(8,128)}) %reduce-scatter.6.cloned.1.call-update) | async-done | bytes 294928 | tf_op jit(solution)/shard_map/reduce_scatter | solution.py:187
  789.9 2.9 multiply_reduce_fusion.12
  792.8 139.4 %reduce-scatter.8.cloned.1.call-done = f32[96,768]{1,0:T(8,128)} async-done(((f32[1536,768]{1,0:T(8,128)}), f32[96,768]{1,0:T(8,128)}) %reduce-scatter.8.cloned.1.call-update) | async-done | bytes 294928 | tf_op jit(solution)/shard_map/reduce_scatter | solution.py:188
  932.2 2.8 multiply_reduce_fusion.11
  935.0 2.0 maximum_bitcast_fusion.1
  937.0 2.0 maximum_bitcast_fusion
  939.0 15.5 %all-reduce.14.cloned.1.call-done = bf16[1024,768]{1,0:T(8,128)(2,1)} async-done(((bf16[1024,768]{1,0:T(8,128)(2,1)}), bf16[1024,768]{1,0:T(8,128)(2,1)}) %all-reduce.14.cloned.1.call-update) | async-done | bytes 1572880 | tf_op jit(solution)/shard_map/psum | solution.py:181
  954.5 3.4 convert_add_fusion
  957.9 41.0 %all-reduce.1 = (f32[6,2]{0,1:T(2,128)S(1)}, f32[12,768]{1,0:T(8,128)S(1)}) all-reduce(f32[6,2]{0,1:T(2,128)S(1)} %pad_maximum_fusion.3, f32[12,768]{1,0:T(8,128)} %concatenate.13), channel_id=1, replica_groups=mesh['dp'=16,'tensor'=2] {'dp','tensor'}, use_global_device_ids=true, to_apply=%region_27.28 | all-reduce | flops 9228 | bytes 73824 | tf_op jit(solution)/shard_map/psum | solution.py:218
  1001.5 1.6 fusion.57
  1003.2 1.5 multiply_subtract_fusion.4
  1004.7 2.0 fusion.58
  1006.7 2.0 fusion.55
  (182 shorter events, 23.5 us)
Async XLA Ops:
  7.2 67.1 %all-gather.4.cloned.1.call-start = ((), (), s32[]{:S(2)}) async-start(), calls=%async_computation.3 | async-start | bytes 1880064 | tf_op jit(solution)/shard_map/all_gather | solution.py:84
  8.9 101.5 %all-reduce.8.cloned.1.call-start = ((), (), s32[]{:S(2)}) async-start(), calls=%async_computation.4 | async-start | bytes 6291456 | tf_op jit(solution)/shard_map/psum | solution.py:114
  10.6 260.9 %copy-start.29 = (f32[768]{0:T(1024)}, f32[768]{0:T(1024)S(1)}, u32[]{:S(2)}) copy-start(f32[768]{0:T(1024)S(1)} %get-tuple-element.106) | copy-start | bytes 9220
  79.0 3.2 copy-start.9
  79.2 1.5 copy-start.14
  79.6 1.4 copy-start.7
  82.3 1.1 copy-start.6
  82.3 3.3 copy-start.20
  84.6 0.9 copy-start.16
  85.5 4.5 copy-start.22
  88.2 2.8 slice-start
  88.2 89.4 %all-gather.6.cloned.1.call-start = ((), (), s32[]{:S(2)}) async-start(), calls=%async_computation.5 | async-start | bytes 2506752 | tf_op jit(solution)/shard_map/all_gather | solution.py:86
  90.0 152.4 %all-gather.8.cloned.1.call-start = ((), (), s32[]{:S(2)}) async-start(), calls=%async_computation.6 | async-start | bytes 2506752 | tf_op jit(solution)/shard_map/all_gather | solution.py:87
  90.7 180.8 %all-reduce.10.cloned.1.call-start = ((), (), s32[]{:S(2)}) async-start(), calls=%async_computation.7 | async-start | bytes 6291456 | tf_op jit(solution)/shard_map/psum | solution.py:122
  113.2 1.7 copy-start
  249.3 0.7 copy-start.37
  249.3 22.2 %copy-start.32 = (f32[768]{0:T(1024)S(1)}, f32[768]{0:T(1024)}, u32[]{:S(2)}) copy-start(f32[768]{0:T(1024)} %get-tuple-element.105) | copy-start | bytes 9220
  249.3 71.9 %all-reduce.12.cloned.1.call-start = ((), (), s32[]{:S(2)}) async-start(), calls=%async_computation.8 | async-start | bytes 6291456 | tf_op jit(solution)/shard_map/psum | solution.py:145
  271.5 10.6 %slice-start.1 = ((s8[6291456]{0:T(1024)(128)(4,1)}), s8[4194304]{0:T(1024)(128)(4,1)S(1)}, s32[]{:S(2)}) async-start(s8[6291456]{0:T(1024)(128)(4,1)} %bitcast.134), calls=%async_computation.15 | async-start | bytes 8388608
  275.5 1.4 copy-start.5
  276.1 3.0 copy-start.31
  276.9 5.1 slice-start.2
  279.1 3.0 copy-start.43
  282.0 8.5 copy-start.12
  282.1 10.3 %copy-start.42 = (bf16[768,1536]{1,0:T(8,128)(2,1)S(1)}, bf16[768,1536]{1,0:T(8,128)(2,1)}, u32[]{:S(2)}) copy-start(bf16[768,1536]{1,0:T(8,128)(2,1)} %all-gather.6.cloned.1.call-done) | copy-start | bytes 7077892
  290.6 1.8 copy-start.45
  296.6 166.1 %reduce-scatter.4.cloned.1.call-start = ((), (), s32[]{:S(2)}) async-start(), calls=%async_computation.10 | async-start | bytes 1253376 | tf_op jit(solution)/shard_map/reduce_scatter | solution.py:186
  321.2 5.4 copy-start.1
  326.6 1.7 copy-start.21
  328.3 2.0 copy-start.3
  328.3 2.0 copy-start.17
  336.9 311.2 %all-reduce.16.cloned.1.call-start = ((), (), s32[]{:S(2)}) async-start(), calls=%async_computation.13 | async-start | bytes 9437184
  350.1 1.4 copy-start.8
  351.5 1.2 copy-start.10
  352.7 4.1 copy-start.15
  353.3 3.6 copy-start.11
  368.9 1.9 copy-start.2
  368.9 1.9 copy-start.30
  368.9 421.0 %reduce-scatter.6.cloned.1.call-start = ((), (), s32[]{:S(2)}) async-start(), calls=%async_computation.11 | async-start | bytes 5013504 | tf_op jit(solution)/shard_map/reduce_scatter | solution.py:187
  377.4 1.9 copy-start.13
  377.4 554.8 %reduce-scatter.8.cloned.1.call-start = ((), (), s32[]{:S(2)}) async-start(), calls=%async_computation.12 | async-start | bytes 5013504 | tf_op jit(solution)/shard_map/reduce_scatter | solution.py:188
  386.0 0.7 copy-start.34
  386.0 0.7 copy-start.44
  386.0 1.9 copy-start.35
  386.0 2.0 copy-start.40
  386.0 2.3 copy-start.33
  386.0 2.9 copy-start.28
  386.0 2.9 copy-start.36
  386.0 2.9 copy-start.18
  386.1 3.2 copy-start.19
  386.1 568.4 %all-reduce.14.cloned.1.call-start = ((), (), s32[]{:S(2)}) async-start(), calls=%async_computation.9 | async-start | bytes 3145728 | tf_op jit(solution)/shard_map/psum | solution.py:181
  390.1 5.7 copy-start.39
  390.1 6.6 copy-start.38
  390.1 72.7 %copy-start.27 = (f32[384,48]{0,1:T(8,128)S(1)}, f32[384,48]{0,1:T(8,128)}, u32[]{:S(2)}) copy-start(f32[384,48]{0,1:T(8,128)} %param.24) | copy-start | bytes 221188
  395.7 536.5 %copy-start.23 = (f32[96,768]{1,0:T(8,128)S(1)}, f32[96,768]{1,0:T(8,128)}, u32[]{:S(2)}) copy-start(f32[96,768]{1,0:T(8,128)} %param.26) | copy-start | bytes 884740
  395.8 558.8 %copy-start.4 = (f32[1024,768]{1,0:T(8,128)S(1)}, f32[1024,768]{1,0:T(8,128)}, u32[]{:S(2)}) copy-start(f32[1024,768]{1,0:T(8,128)} %copy-done.3) | copy-start | bytes 9437188
  957.9 50.8 %copy-start.24 = (f32[48,1536]{1,0:T(8,128)S(1)}, f32[48,1536]{1,0:T(8,128)}, u32[]{:S(2)}) copy-start(f32[48,1536]{1,0:T(8,128)} %param.25) | copy-start | bytes 884740
  957.9 50.8 %copy-start.25 = (f32[48,1536]{1,0:T(8,128)S(1)}, f32[48,1536]{1,0:T(8,128)}, u32[]{:S(2)}) copy-start(f32[48,1536]{1,0:T(8,128)} %get-tuple-element.131) | copy-start | bytes 884740
  957.9 50.8 %copy-start.26 = (f32[48,1536]{1,0:T(8,128)S(1)}, f32[48,1536]{1,0:T(8,128)}, u32[]{:S(2)}) copy-start(f32[48,1536]{1,0:T(8,128)} %get-tuple-element.132) | copy-start | bytes 884740
  999.0 10.6 %copy-start.41 = (f32[6,2]{0,1:T(2,128)}, f32[6,2]{0,1:T(2,128)S(1)}, u32[]{:S(2)}) copy-start(f32[6,2]{0,1:T(2,128)S(1)} %sqrt.22) | copy-start | bytes 148
Sparse Core Ops, SparseCore 0:
  11.3 62.9 all-gather.3
  88.4 21.9 all-reduce.7
  114.1 63.4 all-gather.5
  181.2 61.0 all-gather.7
  249.4 22.0 all-reduce.9
  296.8 24.3 all-reduce.11
  337.1 125.6 reduce-scatter.3
  469.4 178.6 all-reduce.15
  653.3 136.5 reduce-scatter.5
  795.7 136.4 reduce-scatter.7
  935.1 19.3 all-reduce.13
where the time goes:
time: 1020 us
  waiting for transfers between devices  723 us (71%)
  blocking collectives  89.9 us (9%)
  matrix products  85 us (8%)
  other arithmetic  57 us (6%)
  local copies, waits for them, and re-layouts  42.6 us (4%)
  between operations  17.4 us (2%)
    unnamed x12, waiting for transfers between devices  183 us
    reduce_scatter x1, waiting for transfers between devices, body(): lax.psum_scatter(grad_down, 'dp', scatter_dimension=0, tiled=True)  139 us
    reduce_scatter x1, waiting for transfers between devices, body(): lax.psum_scatter(grad_up, 'dp', scatter_dimension=0, tiled=True)  139 us
    reduce_scatter x1, waiting for transfers between devices, body(): lax.psum_scatter(grad_out, 'dp', scatter_dimension=1, tiled=True)  64 us
    all_gather x1, waiting for transfers between devices, body(): lax.all_gather(expand_up.astype(jnp.bfloat16), 'dp', axis=0, tiled=True)  62.3 us
    all_gather x1, blocking collectives, body(): lax.all_gather(attend_out.astype(jnp.bfloat16), 'dp', axis=1, tiled=True)  48.8 us
    all_gather x1, waiting for transfers between devices, body(): lax.all_gather(expand_down.astype(jnp.bfloat16), 'dp', axis=0, tiled=True)  45 us
    psum x1, blocking collectives, body(): lax.psum(jnp.stack([weight_squares(masters), update_squares], axis=1), ('...  41 us
  transfers between devices with their start and end apart: 11, of which 11 were waited for; matrix products, arithmetic and copies ran while one was open for 10% of the time, Pallas kernels for 0%

commit v1 on v0

v1 whole, which is shorter than its diff:
```python
import math

import jax
import jax.numpy as jnp
import numpy as np
from jax import lax
from jax.experimental import pallas as pl
from jax.experimental.pallas import tpu as pltpu
from jax.sharding import PartitionSpec as P

HEAD_DIM = 64
STEP = 10
NORM_EPS = 1e-05
BETA_ONE = 0.9
BETA_TWO = 0.999
ADAM_EPS = 1e-06
RATE = 0.3
DECAY = 0.01
MASKED = -1e30
AXES = ("dp", "tensor")
F32, BF16 = jnp.float32, jnp.bfloat16
VMEM = pltpu.VMEM
LANES = 128
NT = (((1,), (1,)), ((), ()))
TN = (((0,), (0,)), ((), ()))
MIB = 1 << 20


class Grid:
    def __init__(self, mesh):
        self.dp, self.cores = mesh.shape["dp"], mesh.shape["tensor"]
        chips = mesh.devices.reshape(self.dp, self.cores)[:, 0]
        spots = [tuple(getattr(chip, "coords", ())) for chip in chips]
        if any(len(spot) != 3 for spot in spots) or len(set(spots)) != self.dp:
            side = 1 << ((self.dp.bit_length() - 1) // 3)
            spots = [(i % side, i // side % side, i // (side * side)) for i in range(self.dp)]
        spots = np.array(spots) - np.min(spots, axis=0)
        sizes = spots.max(axis=0) + 1
        order = sorted(range(3), key=lambda k: -sizes[k])
        order = order[:1] + sorted(order[1:])
        self.spots = spots[:, order].tolist()
        self.long, self.side, _ = (int(sizes[k]) for k in order)
        self.at = {tuple(spot): i for i, spot in enumerate(self.spots)}
        unit = [tuple(int(j == k) for j in range(3)) for k in range(3)]
        self.stride = [self.at.get(u, 0) for u in unit]
        self.sizes = [int(sizes[k]) for k in order]

    def send(self, value, hop):
        pairs = []
        for i, spot in enumerate(self.spots):
            for core in range(self.cores):
                offsets, turn = hop(core)
                target = self.at[tuple(u ^ v for u, v in zip(spot, offsets))]
                pairs.append((i * self.cores + core, target * self.cores + (core ^ turn)))
        return lax.ppermute(value, AXES, pairs)

    def place(self):
        index = lax.axis_index("dp")
        spot = [lax.rem(lax.div(index, s), n) if n > 1 else index * 0 for s, n in zip(self.stride, self.sizes)]
        return jnp.stack(spot + [lax.axis_index("tensor")]).astype(jnp.int32)

    def first(self, k):
        return lambda core: ((0, k, 0) if core == 0 else (0, 0, k), 0)

    def second(self, k):
        return lambda core: ((0, 0, k) if core == 0 else (0, k, 0), 0)

    def along(self, k):
        return lambda core: ((k, 0, 0), 0)

    def cross(self, j, k):
        return lambda core: ((0, j, k), 0)

    def core(self, value):
        return self.send(value, lambda core: ((0, 0, 0), 1))

    def slot(self, s, k, m, a):
        zero = s[3] == 0
        b = s[1] ^ jnp.where(zero, k, m)
        c = s[2] ^ jnp.where(zero, m, k)
        return self.stride[0] * a + self.stride[1] * b + self.stride[2] * c


def kernel_call(body, outs, ins, place=None, limit=4, flops=0, moved=0, exps=0, scratch=(), spill=()):
    specs = [pl.BlockSpec(memory_space=VMEM)] * len(ins)
    ins = [pltpu.with_memory_space_constraint(v, VMEM) for v in ins]
    if place is not None:
        specs = [pl.BlockSpec(memory_space=pltpu.SMEM)] + specs
        ins = [place] + ins
    shapes = [
        jax.ShapeDtypeStruct(s, d) if i in spill else VMEM(s, d) for i, (s, d) in enumerate(outs)
    ]
    return pl.pallas_call(
        body,
        out_shape=shapes,
        in_specs=specs,
        out_specs=[pl.BlockSpec(memory_space=VMEM)] * len(outs),
        scratch_shapes=list(scratch),
        cost_estimate=pl.CostEstimate(flops=flops, bytes_accessed=moved, transcendentals=exps),
        compiler_params=pltpu.CompilerParams(vmem_limit_bytes=limit * MIB),
    )(*ins)


def gather(grid, place, shard):
    long, side = grid.long, grid.side
    many, rows, width = shard.shape
    got = [shard] + [grid.send(shard, grid.along(k)) for k in range(1, long)]

    def line(s, *refs):
        for k in range(long):
            refs[-1][s[0] ^ k] = refs[k][...]

    block = kernel_call(line, [((long, many, rows, width), BF16)], got, place)[0]
    pieces = {(0, 0): block}
    for k in range(1, side):
        pieces[k, 0] = grid.send(block, grid.first(k))
    for m in range(1, side):
        for k in range(side):
            pieces[k, m] = grid.send(pieces[k, 0], grid.second(m))
    keys = list(pieces)

    def whole(s, *refs):
        for (k, m), ref in zip(keys, refs[:-1]):
            for a in range(long):
                spot = grid.slot(s, k, m, a)
                for j in range(many):
                    refs[-1][j, spot] = ref[a, j]

    full = kernel_call(
        whole, [((many, grid.dp, rows, width), BF16)], [pieces[key] for key in keys], place
    )[0]
    return full, grid.core(full)


def scatter(grid, place, own, other):
    long, side = grid.long, grid.side
    many, _, rows, width = own.shape
    got = grid.core(other)
    block = (side, long, many, rows, width)

    def pair(s, own_ref, got_ref, keep, *sends):
        for m in range(side):
            out = keep if m == 0 else sends[m - 1]
            for k in range(side):
                for a in range(long):
                    spot = grid.slot(s, k, m, a)
                    for j in range(many):
                        total = own_ref[j, spot] + got_ref[j, spot].astype(F32)
                        out[k, a, j] = total.astype(out.dtype)

    keep, *sends = kernel_call(
        pair, [(block, F32)] + [(block, BF16)] * (side - 1), [own, got], place, limit=6
    )
    came = [grid.send(v, grid.second(m + 1)) for m, v in enumerate(sends)]

    def sides(*refs):
        came_refs, outs = refs[1:side], refs[side:]
        for k in range(side):
            total = refs[0][k]
            for ref in came_refs:
                total = total + ref[k].astype(F32)
            outs[k][...] = total.astype(outs[k].dtype)

    keep, *sends = kernel_call(
        sides, [(block[1:], F32)] + [(block[1:], BF16)] * (side - 1), [keep] + came, limit=6
    )
    came = [grid.send(v, grid.first(k + 1)) for k, v in enumerate(sends)]

    def line(s, *refs):
        outs = refs[side:]
        for k in range(long):
            total = refs[0][s[0] ^ k]
            for ref in refs[1:side]:
                total = total + ref[s[0] ^ k].astype(F32)
            outs[k][...] = total.astype(outs[k].dtype)

    keep, *sends = kernel_call(
        line, [(block[2:], F32)] + [(block[2:], BF16)] * (long - 1), [keep] + came, place
    )
    return [keep] + [grid.send(v, grid.along(k + 1)) for k, v in enumerate(sends)]


def tree(values):
    values = list(values)
    while len(values) > 1:
        values = [a + b for a, b in zip(values[::2], values[1::2])]
    return values[0]


def add_kernel(*refs):
    refs[-1][...] = tree(ref[...] for ref in refs[:-1])


def total_of(grid, value):
    shape = [(value.shape, F32)]
    value = kernel_call(
        add_kernel, shape, [value] + [grid.send(value, grid.along(k)) for k in range(1, grid.long)]
    )[0]
    offsets = [(j, k) for j in range(grid.side) for k in range(grid.side)]
    value = kernel_call(
        add_kernel, shape, [value] + [grid.send(value, grid.cross(j, k)) for j, k in offsets[1:]]
    )[0]
    return value, grid.core(value)


def normed_of(values):
    center = values - jnp.mean(values, axis=-1, keepdims=True)
    inverse = lax.rsqrt(jnp.mean(center * center, axis=-1, keepdims=True) + NORM_EPS)
    return center * inverse, inverse


def norm_back(upstream, normed, inverse, gain):
    scaled = upstream * gain
    inner = jnp.mean(scaled * normed, axis=-1, keepdims=True)
    return inverse * (scaled - jnp.mean(scaled, axis=-1, keepdims=True) - normed * inner)


def sum_rows(values):
    return jnp.sum(values, axis=0, keepdims=True)


def adam(grad, first, second):
    first_new = BETA_ONE * first + (1.0 - BETA_ONE) * grad
    second_new = BETA_TWO * second + (1.0 - BETA_TWO) * grad * grad
    corrected = first_new / (1.0 - BETA_ONE**STEP)
    spread = jnp.sqrt(second_new / (1.0 - BETA_TWO**STEP))
    return first_new, second_new, corrected / (spread + ADAM_EPS)


def squares(values):
    return jnp.sum(sum_rows(values * values), axis=1, keepdims=True)


def norm_tile(entries):
    row = lax.broadcasted_iota(jnp.int32, (8, LANES), 0)
    lane = lax.broadcasted_iota(jnp.int32, (8, LANES), 1)
    tile = jnp.zeros((8, LANES), F32)
    for index, weight, direction in entries:
        tile = jnp.where((row == index) & (lane == 0), squares(weight), tile)
        tile = jnp.where((row == index) & (lane == 1), squares(direction), tile)
    return tile


def make_body(grid):
    def body(
        states, cotangent, word_counts, region_counts,
        attend_in, attend_out, expand_up, expand_down,
        first_in, first_out, first_up, first_down,
        second_in, second_out, second_up, second_down,
        vectors, vector_first, vector_second,
    ):
        cores = grid.cores
        pairs, length, width = states.shape
        mine = pairs // cores
        rows = mine * length
        cols = attend_in.shape[2]
        units = expand_up.shape[1]
        twins = width // LANES
        scale = HEAD_DIM**-0.5
        place = grid.place()
        rank = place[3]
        shard_rows = attend_in.shape[1]

        shard_a = jnp.concatenate([attend_in, attend_out.T[None]]).astype(BF16)
        a_own, a_oth = gather(grid, place, shard_a)
        b_own, b_oth = gather(grid, place, expand_up.astype(BF16)[None])
        c_own, c_oth = gather(grid, place, expand_down.astype(BF16)[None])
        a_own, a_oth = (v.reshape(4, width, cols) for v in (a_own, a_oth))
        b_own, b_oth = (v.reshape(width, units) for v in (b_own, b_oth))
        c_own, c_oth = (v.reshape(units, width) for v in (c_own, c_oth))

        part = lambda v: lax.dynamic_slice_in_dim(v, rank * mine, mine, 0)
        x = part(states).reshape(rows, width)
        cot = part(cotangent).reshape(rows, width)
        lengths = part(word_counts + region_counts)

        def turned(v):
            return jnp.where(rank == 0, v, jnp.roll(v, v.shape[-1] // 2, axis=-1))

        bias_up = turned(vectors[8:].reshape(1, -1))
        bias_in = turned(jnp.stack([vectors[0], jnp.zeros_like(vectors[0]), vectors[1]])).reshape(3, 1, width)

        def project(x_ref, own, oth, bias, out, x_t):
            x_t[...] = x_ref[...].T

            @pl.loop(0, 3)
            def _(j):
                for h, ref in enumerate((own, oth)):
                    at = slice(h * cols, (h + 1) * cols)
                    value = jnp.dot(x_ref[...], ref[j], preferred_element_type=F32)
                    out[j, :, at] = (value + bias[j, :, at]).astype(BF16)

        qkv, x_t = kernel_call(
            project, [((3, rows, width), BF16), ((width, rows), BF16)], [x, a_own, a_oth, bias_in],
            limit=8, flops=6 * rows * width * width, moved=8 * MIB,
        )

        def split(v):
            low = lax.broadcasted_iota(jnp.int32, v.shape, 1) < HEAD_DIM
            zero = jnp.zeros_like(v)
            return jnp.concatenate([jnp.where(low, v, zero), jnp.where(low, zero, v)], axis=0)

        def join(v):
            low = lax.broadcasted_iota(jnp.int32, (length, LANES), 1) < HEAD_DIM
            return jnp.where(low, v[:length], v[length:])

        def attend(count, qkv_ref, probs, context):
            @pl.loop(0, mine)
            def _(p):
                at = pl.ds(pl.multiple_of(p * length, length), length)
                known = lax.broadcasted_iota(jnp.int32, (length, length), 1) < count[p]
                for u in range(twins):
                    lanes = slice(u * LANES, (u + 1) * LANES)
                    both = lax.dot_general(
                        qkv_ref[0, at, lanes], split(qkv_ref[1, at, lanes]), NT, preferred_element_type=F32
                    )
                    soft = []
                    for h in range(2):
                        score = jnp.where(known, both[:, h * length : (h + 1) * length] * scale, MASKED)
                        power = jnp.exp(score - jnp.max(score, axis=-1, keepdims=True))
                        soft.append(power / jnp.sum(power, axis=-1, keepdims=True))
                    prob = jnp.concatenate(soft, axis=1).astype(BF16)
                    probs[at, 2 * u * length : 2 * (u + 1) * length] = prob
                    context[at, lanes] = jnp.dot(
                        prob, split(qkv_ref[2, at, lanes]), preferred_element_type=F32
                    ).astype(BF16)

        probs, context = kernel_call(
            attend, [((rows, 2 * twins * length), BF16), ((rows, width), BF16)], [qkv], lengths,
            limit=4, flops=4 * rows * length * width * 4, moved=5 * MIB, exps=rows * twins * 2 * length,
        )

        block = min(rows, 256)

        def hide(context_ref, x_ref, own, oth, vec, hidden, hidden_t, normed, inverse):
            for r in range(0, rows, block):
                at = slice(r, r + block)
                value = x_ref[at].astype(F32) + vec[2:3]
                for h, ref in enumerate((own, oth)):
                    value += lax.dot_general(
                        context_ref[at, h * cols : (h + 1) * cols], ref[3], NT, preferred_element_type=F32
                    )
                normal, spread = normed_of(value)
                normed[at], inverse[at] = normal, spread
                hidden[at] = (normal * vec[3:4] + vec[4:5]).astype(BF16)
            hidden_t[...] = hidden[...].T

        hidden, hidden_t, normed_one, inverse_one = kernel_call(
            hide,
            [((rows, width), BF16), ((width, rows), BF16), ((rows, width), F32), ((rows, 1), F32)],
            [context, x, a_own, a_oth, vectors],
            limit=8, flops=2 * rows * width * width, moved=6 * MIB,
        )

        tile = 256

        def lift(hidden_ref, up, bias, active, active_t, slope):
            @pl.loop(0, units // tile)
            def _(i):
                at = pl.ds(pl.multiple_of(i * tile, tile), tile)
                value = jnp.dot(hidden_ref[...], up[:, at], preferred_element_type=F32) + bias[:, at]
                half = 0.5 * (1.0 + lax.erf(value * math.sqrt(0.5)))
                result = (value * half).astype(BF16)
                active[:, at] = result
                active_t[at, :] = result.T
                bell = jnp.exp(-0.5 * value * value) * (1.0 / math.sqrt(2.0 * math.pi))
                slope[:, at] = (half + value * bell).astype(BF16)

        lifted = [
            kernel_call(
                lift, [((rows, units), BF16), ((units, rows), BF16), ((rows, units), BF16)],
                [hidden, up, bias_up[:, h * units : (h + 1) * units]],
                limit=8, flops=2 * rows * width * units, moved=8 * MIB, exps=2 * rows * units,
            )
            for h, up in enumerate((b_own, b_oth))
        ]

        def lower(count, active_own, active_oth, own, oth, normed, cot_ref, vec, output, top, top16, sums, work):
            @pl.loop(0, width // tile)
            def _(i):
                at = pl.ds(pl.multiple_of(i * tile, tile), tile)
                work[:, at] = jnp.dot(active_own[...], own[:, at], preferred_element_type=F32) + jnp.dot(
                    active_oth[...], oth[:, at], preferred_element_type=F32
                )

            sums[...] = jnp.zeros_like(sums)

            @pl.loop(0, mine)
            def _(p):
                at = pl.ds(pl.multiple_of(p * length, length), length)
                value = normed[at] * vec[3:4] + vec[4:5] + work[at] + vec[5:6]
                normal, spread = normed_of(value)
                output[at] = (normal * vec[6:7] + vec[7:8]).astype(BF16)
                live = lax.broadcasted_iota(jnp.int32, (length, 1), 0) < count[p]
                upstream = jnp.where(live, cot_ref[at].astype(F32), 0.0)
                grad = norm_back(upstream, normal, spread, vec[6:7])
                top[at] = grad
                top16[at] = grad.astype(BF16)
                sums[0:1] += sum_rows(grad)
                sums[1:2] += sum_rows(upstream * normal)
                sums[2:3] += sum_rows(upstream)

        output, top, top16, sums_two = kernel_call(
            lower,
            [((rows, width), BF16), ((rows, width), F32), ((rows, width), BF16), ((8, width), F32)],
            [lifted[0][0], lifted[1][0], c_own, c_oth, normed_one, cot, vectors],
            lengths, limit=8, flops=4 * rows * width * units, moved=14 * MIB,
            scratch=[VMEM((rows, width), F32)],
        )

        def product(left, right, out):
            step = min(left.shape[0], 256)

            @pl.loop(0, left.shape[0] // step)
            def _(i):
                at = pl.ds(pl.multiple_of(i * step, step), step)
                out[at, :] = jnp.dot(left[at, :], right[...], preferred_element_type=F32).astype(out.dtype)

        def weight_grad(left, right, kind):
            shape = (left.shape[0], right.shape[1])
            return kernel_call(
                product, [(shape, kind)], [left, right],
                limit=6, flops=2 * shape[0] * shape[1] * rows, moved=8 * MIB,
            )[0]

        down_oth = weight_grad(lifted[1][1], top16, BF16)
        down_own = weight_grad(lifted[0][1], top16, F32)
        sharded = lambda v, many: v.reshape(many, grid.dp, -1, v.shape[-1])
        down_parts = scatter(grid, place, sharded(down_own, 1), sharded(down_oth, 1))

        def sink(top16_ref, down, slope, grad, sums):
            @pl.loop(0, units // tile)
            def _(i):
                at = pl.ds(pl.multiple_of(i * tile, tile), tile)
                value = lax.dot_general(top16_ref[...], down[at, :], NT, preferred_element_type=F32)
                value = value * slope[:, at].astype(F32)
                grad[:, at] = value.astype(BF16)
                sums[:, at] = sum_rows(value)

        sunk = [
            kernel_call(
                sink, [((rows, units), BF16), ((1, units), F32)], [top16, down, lifted[h][2]],
                limit=8, flops=2 * rows * width * units, moved=8 * MIB,
            )
            for h, down in enumerate((c_own, c_oth))
        ]
        up_oth = weight_grad(hidden_t, sunk[1][0], BF16)
        up_own = weight_grad(hidden_t, sunk[0][0], F32)
        up_parts = scatter(grid, place, sharded(up_own, 1), sharded(up_oth, 1))

        def surface(grad_own, grad_oth, own, oth, top_ref, normed, inverse, vec, a_own_ref, a_oth_ref,
                    mid, mid_t, back, sums, work, mid16):
            @pl.loop(0, width // tile)
            def _(i):
                at = pl.ds(pl.multiple_of(i * tile, tile), tile)
                work[:, at] = (
                    top_ref[:, at]
                    + lax.dot_general(grad_own[...], own[at, :], NT, preferred_element_type=F32)
                    + lax.dot_general(grad_oth[...], oth[at, :], NT, preferred_element_type=F32)
                )

            sums[...] = jnp.zeros_like(sums)

            @pl.loop(0, mine)
            def _(p):
                at = pl.ds(pl.multiple_of(p * length, length), length)
                upstream, normal = work[at], normed[at]
                grad = norm_back(upstream, normal, inverse[at], vec[3:4])
                mid[at] = grad
                mid16[at] = grad.astype(BF16)
                sums[0:1] += sum_rows(grad)
                sums[1:2] += sum_rows(upstream * normal)
                sums[2:3] += sum_rows(upstream)

            mid_t[...] = mid16[...].T
            for h, ref in enumerate((a_own_ref, a_oth_ref)):
                back[:, h * cols : (h + 1) * cols] = jnp.dot(
                    mid16[...], ref[3], preferred_element_type=F32
                ).astype(BF16)

        mid, mid_t, back, sums_one = kernel_call(
            surface,
            [((rows, width), F32), ((width, rows), BF16), ((rows, width), BF16), ((8, width), F32)],
            [sunk[0][0], sunk[1][0], b_own, b_oth, top, normed_one, inverse_one, vectors, a_own, a_oth],
            limit=14, flops=4 * rows * width * units + 2 * rows * width * width, moved=14 * MIB,
            scratch=[VMEM((rows, width), F32), VMEM((rows, width), BF16)],
        )

        def values_back(probs_ref, back_ref, grad, sums):
            sums[...] = jnp.zeros_like(sums)

            @pl.loop(0, mine)
            def _(p):
                at = pl.ds(pl.multiple_of(p * length, length), length)
                for u in range(twins):
                    lanes = slice(u * LANES, (u + 1) * LANES)
                    value = join(lax.dot_general(
                        probs_ref[at, 2 * u * length : 2 * (u + 1) * length], back_ref[at, lanes], TN,
                        preferred_element_type=F32,
                    ))
                    grad[at, lanes] = value.astype(BF16)
                    sums[:, lanes] += sum_rows(value)

        grad_v, sum_v = kernel_call(
            values_back, [((rows, width), BF16), ((1, width), F32)], [probs, back],
            limit=4, flops=4 * rows * length * width, moved=3 * MIB,
        )

        def halves(left_v, right_v, h, kind, left_w, right_w):
            def both(left_v_ref, right_v_ref, left_w_ref, right_w_ref, out):
                at = slice(h * cols, (h + 1) * cols)
                for j, (left, right) in enumerate(((left_v_ref, right_v_ref), (left_w_ref, right_w_ref))):
                    out[j] = jnp.dot(left[...], right[:, at], preferred_element_type=F32).astype(out.dtype)

            return kernel_call(
                both, [((2, width, cols), kind)], [left_v, right_v, left_w, right_w],
                limit=6, flops=4 * rows * width * cols, moved=5 * MIB,
            )[0]

        vo_oth = halves(x_t, grad_v, 1, BF16, mid_t, context)
        vo_own = halves(x_t, grad_v, 0, F32, mid_t, context)
        vo_parts = scatter(grid, place, sharded(vo_own, 2), sharded(vo_oth, 2))

        def attend_back(probs_ref, back_ref, qkv_ref, grad_q, grad_k, sums):
            sums[...] = jnp.zeros_like(sums)

            @pl.loop(0, mine)
            def _(p):
                at = pl.ds(pl.multiple_of(p * length, length), length)
                for u in range(twins):
                    lanes = slice(u * LANES, (u + 1) * LANES)
                    prob = probs_ref[at, 2 * u * length : 2 * (u + 1) * length].astype(F32)
                    both = lax.dot_general(
                        back_ref[at, lanes], split(qkv_ref[2, at, lanes]), NT, preferred_element_type=F32
                    )
                    parts = []
                    for h in range(2):
                        half = slice(h * length, (h + 1) * length)
                        inner = jnp.sum(prob[:, half] * both[:, half], axis=-1, keepdims=True)
                        parts.append(prob[:, half] * (both[:, half] - inner))
                    grad = jnp.concatenate(parts, axis=1).astype(BF16)
                    value = jnp.dot(grad, split(qkv_ref[1, at, lanes]), preferred_element_type=F32) * scale
                    grad_q[at, lanes] = value.astype(BF16)
                    sums[:, lanes] += sum_rows(value)
                    value = join(lax.dot_general(grad, qkv_ref[0, at, lanes], TN, preferred_element_type=F32))
                    grad_k[at, lanes] = (value * scale).astype(BF16)

        grad_q, grad_k, sum_q = kernel_call(
            attend_back, [((rows, width), BF16), ((rows, width), BF16), ((1, width), F32)], [probs, back, qkv],
            limit=4, flops=16 * rows * length * width, moved=6 * MIB,
        )
        qk_oth = halves(x_t, grad_q, 1, BF16, x_t, grad_k)
        qk_own = halves(x_t, grad_q, 0, F32, x_t, grad_k)
        qk_parts = scatter(grid, place, sharded(qk_own, 2), sharded(qk_oth, 2))

        def states_back(grad_q_ref, grad_k_ref, grad_v_ref, own, oth, mid_ref, out):
            @pl.loop(0, width // tile)
            def _(i):
                at = pl.ds(pl.multiple_of(i * tile, tile), tile)
                value = mid_ref[:, at]
                for j, ref in enumerate((grad_q_ref, grad_k_ref, grad_v_ref)):
                    for h, weight in enumerate((own, oth)):
                        value += lax.dot_general(
                            ref[:, h * cols : (h + 1) * cols], weight[j, at, :], NT, preferred_element_type=F32
                        )
                out[:, at] = value

        states_own = kernel_call(
            states_back, [((rows, width), F32)], [grad_q, grad_k, grad_v, a_own, a_oth, mid],
            limit=8, flops=6 * rows * width * width, moved=8 * MIB,
        )[0]

        def pair_up(s, own, oth, out):
            out[s[3]] = own[...]
            out[1 - s[3]] = oth[...]

        def paired(value):
            shape = ((cores,) + value.shape, value.dtype)
            result = kernel_call(pair_up, [shape], [value, grid.core(value)], place, limit=8, spill=(0,))[0]
            return result.reshape(pairs, length, width)

        layer_output = paired(output)
        states_grad = paired(states_own)

        def collect(s, sum_q_ref, sum_v_ref, one, two, up_own_ref, up_oth_ref, out):
            for t in range(cores):

                @pl.when(s[3] == t)
                def _():
                    for row, ref in enumerate((sum_q_ref, sum_v_ref)):
                        for h in range(2):
                            out[row : row + 1, (h ^ t) * cols : ((h ^ t) + 1) * cols] = ref[
                                :, h * cols : (h + 1) * cols
                            ]
                    for h, ref in enumerate((up_own_ref, up_oth_ref)):
                        for i in range(units // width):
                            row = 8 + (h ^ t) * (units // width) + i
                            out[row : row + 1] = ref[:, i * width : (i + 1) * width]

            out[2:5] = one[0:3]
            out[5:8] = two[0:3]

        vector_part = kernel_call(
            collect, [(vectors.shape, F32)], [sum_q, sum_v, sums_one, sums_two, sunk[0][1], sunk[1][1]], place
        )[0]
        vector_own, vector_oth = total_of(grid, vector_part)

        def vector_step(own, oth, vec, first, second, out, moment, square):
            one, two, direction = adam(own[...] + oth[...], first[...], second[...])
            moment[...], square[...] = one, two
            out[...] = vec[...] - RATE * direction

        updated_vectors, moment_vectors, square_vectors = kernel_call(
            vector_step, [(vectors.shape, F32)] * 3,
            [vector_own, vector_oth, vectors, vector_first, vector_second], spill=(0, 1, 2),
        )

        def matrix_step(index):
            def step(*refs):
                grad = sum((ref[0].astype(F32) for ref in refs[1 : grid.long]), refs[0][0])
                master, first, second, moment, square, direction, tile_ref = refs[grid.long :]
                one, two, way = adam(grad, first[...], second[...])
                way = way + DECAY * master[...]
                moment[...], square[...], direction[...] = one, two, way
                tile_ref[...] = norm_tile([(index, master[...], way)])

            return step

        def stepped(step, parts, masters, shapes):
            outs = [(s, F32) for s in shapes for _ in range(2)] + [(s, F32) for s in shapes] + [((8, LANES), F32)]
            return kernel_call(step, outs, parts + masters, limit=6, spill=tuple(range(2 * len(shapes))))

        moment_down, square_down, way_down, tile_down = stepped(
            matrix_step(5), down_parts, [expand_down, first_down, second_down], [expand_down.shape]
        )
        moment_up, square_up, way_up, tile_up = stepped(
            matrix_step(4), up_parts, [expand_up, first_up, second_up], [expand_up.shape]
        )

        def attend_step(*refs):
            n = grid.long
            vo, qk = refs[:n], refs[n : 2 * n]
            m_in, f_in, s_in, m_out, f_out, s_out = refs[2 * n : 2 * n + 6]
            mo_in, sq_in, mo_out, sq_out, way_in, way_out, tile_ref = refs[2 * n + 6 :]
            whole = lambda parts, j: sum((ref[j].astype(F32) for ref in parts[1:]), parts[0][j])
            entries = []
            for j, grad in enumerate((whole(qk, 0), whole(qk, 1), whole(vo, 0))):
                mo_in[j], sq_in[j], way = adam(grad, f_in[j], s_in[j])
                way_in[j] = way + DECAY * m_in[j]
                entries.append((j, m_in[j], way_in[j]))
            mo_out[...], sq_out[...], way = adam(whole(vo, 1).T, f_out[...], s_out[...])
            way_out[...] = way + DECAY * m_out[...]
            entries.append((3, m_out[...], way_out[...]))
            tile_ref[...] = norm_tile(entries)

        moment_in, square_in, moment_out, square_out, way_in, way_out, tile_attend = stepped(
            attend_step, vo_parts + qk_parts,
            [attend_in, first_in, second_in, attend_out, first_out, second_out],
            [attend_in.shape, attend_out.shape],
        )

        def add_tiles(*refs):
            refs[-1][...] = refs[0][...] + refs[1][...] + refs[2][...]

        tiles = kernel_call(add_tiles, [((8, LANES), F32)], [tile_attend, tile_up, tile_down])[0]
        tile_own, tile_oth = total_of(grid, tiles)

        def update(own, oth, *refs):
            masters, ways, outs = refs[:4], refs[4:8], refs[8:]
            norms = jnp.sqrt(own[...] + oth[...])
            outs[8][...] = norms[0:6, 0:2]
            trust = RATE * (norms[:, 0:1] / norms[:, 1:2])
            for j in range(3):
                value = masters[0][j] - trust[j : j + 1] * ways[0][j]
                outs[0][j], outs[4][j] = value, value.astype(BF16)
            for i in range(1, 4):
                value = masters[i][...] - trust[i + 2 : i + 3] * ways[i][...]
                outs[i][...], outs[4 + i][...] = value, value.astype(BF16)

        masters = [attend_in, attend_out, expand_up, expand_down]
        results = kernel_call(
            update,
            [(m.shape, F32) for m in masters] + [(m.shape, BF16) for m in masters] + [((6, 2), F32)],
            [tile_own, tile_oth] + masters + [way_in, way_out, way_up, way_down],
            limit=6, spill=tuple(range(9)),
        )
        return (
            layer_output, states_grad, *results[:4],
            moment_in, moment_out, moment_up, moment_down,
            square_in, square_out, square_up, square_down,
            *results[4:8], updated_vectors, moment_vectors, square_vectors, results[8],
        )

    return body


def solution(mesh):
    rows = P("dp", None, None)
    matrices = (P(None, "dp", "tensor"), P("tensor", "dp"), P("dp", "tensor"), P(("tensor", "dp"), None))
    in_specs = (rows, rows, P("dp"), P("dp")) + matrices * 3 + (P(), P(), P())
    out_specs = (rows, rows) + matrices * 4 + (P(), P(), P(), P())
    body = make_body(Grid(mesh))
    return jax.shard_map(body, mesh=mesh, in_specs=in_specs, out_specs=out_specs, check_vma=False)
```

time: 1020 us -> 340 us (0.33)
  waiting for transfers between devices: 723 us -> 110 us
  Pallas kernels: 0 us -> 102 us
  blocking collectives: 89.9 us -> 0 us
  matrix products: 85 us -> 0 us
  starting transfers between devices: 1.46 us -> 83.5 us
  other arithmetic: 57 us -> 3.24 us
  between operations: 17.4 us -> 1.5 us
    reduce_scatter x3 -> x0, waiting for transfers between devices: 342 us -> none  [the longest x1 139 us: body(): lax.psum_scatter(grad_down, 'dp', scatter_dimension=0, tiled=True)]
    unnamed x12 -> x0, waiting for transfers between devices: 183 us -> none
    all_gather x3 -> x0, waiting for transfers between devices: 120 us -> none  [the longest x1 62.3 us: body(): lax.all_gather(expand_up.astype(jnp.bfloat16), 'dp', axis=0, tiled=True)]
    ppermute x0 -> x61, waiting for transfers between devices: none -> 110 us  [send(): return lax.ppermute(value, AXES, pairs)]
    pallas_call x0 -> x51, Pallas kernels: none -> 102 us  [kernel_call(): pl.pallas_call(body, out_shape=shapes, in_specs=specs, out_specs=[pl.Bloc...]
    dot_general x18 -> x0, matrix products: 85 us -> none  [the longest x1 19.8 us: body(): jnp.dot(hidden_low, weight_up, preferred_element_type=jnp.float32) + bias_up]
    ppermute x0 -> x61, starting transfers between devices: none -> 83.5 us  [send(): return lax.ppermute(value, AXES, pairs)]
    psum x4 -> x0, waiting for transfers between devices: 78.1 us -> none  [the longest x1 24.5 us: body(): grad_hidden = grad_top + lax.psum(hidden_part, 'tensor')]
  transfers between devices with their start and end apart: 11 -> 61, of which waited for: 11 -> 22; matrix products, arithmetic and copies ran while one was open for 10% -> 3% of each run, Pallas kernels for 0% -> 27%
where the time goes in v1:
time: 340 us; the launch traced here: 338 us
  waiting for transfers between devices  110 us (32%)
  Pallas kernels  102 us (30%)
  starting transfers between devices  83.5 us (25%)
  local copies, waits for them, and re-layouts  38.3 us (11%)
    ppermute x61, waiting for transfers between devices, send(): return lax.ppermute(value, AXES, pairs)  110 us
    pallas_call x51, Pallas kernels, kernel_call(): pl.pallas_call(body, out_shape=shapes, in_specs=specs, out_specs=[pl.Bloc...  102 us
    ppermute x61, starting transfers between devices, send(): return lax.ppermute(value, AXES, pairs)  83.5 us
    unnamed x136, local copies, waits for them, and re-layouts  37.1 us
  transfers between devices with their start and end apart: 61, of which 22 were waited for; matrix products, arithmetic and copies ran while one was open for 3% of the time, Pallas kernels for 27%

profile of v1, /device:TPU:0, one launch (start us, length us, event | category | flops | bytes accessed | tf_op | source)
XLA Modules:
  0.0 338.4 jit_solution(5493268912226409156)
XLA Ops:
  2.7 3.1 collective-permute-start
  5.8 2.6 collective-permute-start.1
  10.3 3.5 %collective-permute-start.8 = (bf16[1,48,1536]{2,1,0:T(8,128)(2,1)S(1)}, bf16[1,48,1536]{2,1,0:T(8,128)(2,1)S(1)}, u32[]{:S(2)}, u32[]{:S(2)}) collective-permute-start(bf16[1,48,1536]{2,1,0:T(8,128)(2,1)S(1)} %convert_bitcast_fusion.1.refs_0_), channel_id=1, source_target_pairs={{0,16},{1,17},{2,18},{3,19},{4,20},{5,21},{6,22},{7,23},{8,24},{9,... | collective-permute-start | bytes 442376 | tf_op jit(solution)/shard_map/ppermute | solution.py:55
  13.9 2.0 collective-permute-start.9
  15.9 3.9 %collective-permute-done.1.refs_2_ = bf16[4,48,384]{2,1,0:T(8,128)(2,1)S(1)} collective-permute-done((bf16[4,48,384]{2,1,0:T(8,128)(2,1)S(1)}, bf16[4,48,384]{2,1,0:T(8,128)(2,1)S(1)}, u32[]{:S(2)}, u32[]{:S(2)}) %collective-permute-start.1) | collective-permute-done | bytes 147488 | tf_op jit(solution)/shard_map/ppermute | solution.py:55
  22.0 10.2 %collective-permute-start.14 = (bf16[1,96,768]{2,1,0:T(8,128)(2,1)S(1)}, bf16[1,96,768]{2,1,0:T(8,128)(2,1)S(1)}, u32[]{:S(2)}, u32[]{:S(2)}) collective-permute-start(bf16[1,96,768]{2,1,0:T(8,128)(2,1)S(1)} %convert_bitcast_fusion.refs_0_), channel_id=1, source_target_pairs={{0,8},{1,9},{2,10},{3,11},{4,12},{5,13},{6,14},{7,15},{8,0},{9,1},... | collective-permute-start | bytes 442376 | tf_op jit(solution)/shard_map/ppermute | solution.py:55
  33.0 3.3 collective-permute-start.16
  38.4 1.6 collective-permute-start.10
  40.0 5.2 %collective-permute-done.15.refs_2_ = bf16[1,96,768]{2,1,0:T(8,128)(2,1)S(1)} collective-permute-done((bf16[1,96,768]{2,1,0:T(8,128)(2,1)S(1)}, bf16[1,96,768]{2,1,0:T(8,128)(2,1)S(1)}, u32[]{:S(2)}, u32[]{:S(2)}) %collective-permute-start.15) | collective-permute-done | bytes 147488 | tf_op jit(solution)/shard_map/ppermute | solution.py:55
  49.5 3.1 collective-permute-done.4.refs_2_
  54.6 8.0 %collective-permute-done.17.refs_1_ = bf16[4,1,96,768]{3,2,1,0:T(8,128)(2,1)} collective-permute-done((bf16[4,1,96,768]{3,2,1,0:T(8,128)(2,1)S(1)}, bf16[4,1,96,768]{3,2,1,0:T(8,128)(2,1)}, u32[]{:S(2)}, u32[]{:S(2)}) %collective-permute-start.17) | collective-permute-done | bytes 589856 | tf_op jit(solution)/shard_map/ppermute | solution.py:55
  63.7 2.2 shard_map.355
  65.8 2.4 collective-permute-done.11.refs_2_
  68.3 12.6 %collective-permute-done.12.refs_3_ = bf16[4,1,48,1536]{3,2,1,0:T(8,128)(2,1)} collective-permute-done((bf16[4,1,48,1536]{3,2,1,0:T(8,128)(2,1)}, bf16[4,1,48,1536]{3,2,1,0:T(8,128)(2,1)}, u32[]{:S(2)}, u32[]{:S(2)}) %collective-permute-start.12) | collective-permute-done | bytes 589856 | tf_op jit(solution)/shard_map/ppermute | solution.py:55
  80.9 3.0 shard_map.360
  84.9 2.4 collective-permute-done.19.refs_3_
  87.2 1.6 shard_map.364
  90.9 5.8 %shard_map.356 = (bf16[3,512,768]{2,1,0:T(8,128)(2,1)S(1)}, bf16[768,512]{1,0:T(8,128)(2,1)S(1)}) custom-call(bf16[512,768]{1,0:T(8,128)(2,1)S(1)} %bitcast.49, bf16[4,768,384]{2,1,0:T(8,128)(2,1)} %bitcast.7.own.a_own_ref, bf16[4,768,384]{2,1,0:T(8,128)(2,1)} %bitcast.8.oth.a_oth_ref, f32[3,1,768]{2,1,0:T(1,128)S(1)} %broadcast_select_fusion.1.bias), custom_call_target="tpu_custom_call" | custom-call | flops 1811939328 | bytes 8388608 | tf_op jit(solution)/shard_map/pallas_call | solution.py:93
  96.6 4.6 %shard_map.357 = (bf16[512,1536]{1,0:T(8,128)(2,1)S(1)}, bf16[512,768]{1,0:T(8,128)(2,1)S(1)}) custom-call(s32[4]{0:T(128)S(1)} %dynamic_slice.9.count, bf16[3,512,768]{2,1,0:T(8,128)(2,1)S(1)} %get-tuple-element.112.qkv_ref), custom_call_target="tpu_custom_call" | custom-call | flops 805306368 | bytes 5242880 | tf_op jit(solution)/shard_map/pallas_call | solution.py:93
  101.3 3.9 %shard_map.358 = (bf16[512,768]{1,0:T(8,128)(2,1)S(1)}, bf16[768,512]{1,0:T(8,128)(2,1)S(1)}, f32[512,768]{1,0:T(8,128)S(1)}, f32[512,1]{1,0:T(8,128)S(1)}) custom-call(bf16[512,768]{1,0:T(8,128)(2,1)S(1)} %get-tuple-element.113.context_ref.right_w_ref, bf16[512,768]{1,0:T(8,128)(2,1)S(1)} %bitcast.50, bf16[4,768,384]{2,1,0:T(8,128)(2,1)} %bitcast.7.own.a_own_ref, ...), custom_call_target="tpu_custom_call" | custom-call | flops 603979776 | bytes 6291456 | tf_op jit(solution)/shard_map/pallas_call | solution.py:93
  105.2 5.0 %shard_map.362 = (bf16[512,1536]{1,0:T(8,128)(2,1)S(1)}, bf16[1536,512]{1,0:T(8,128)(2,1)S(1)}, bf16[512,1536]{1,0:T(8,128)(2,1)S(1)}) custom-call(bf16[512,768]{1,0:T(8,128)(2,1)S(1)} %get-tuple-element.114.hidden_ref, bf16[768,1536]{1,0:T(8,128)(2,1)} %bitcast.14.up.oth, f32[1,1536]{1,0:T(1,128)S(1)} %get-tuple-element.228.bias), custom_call_target="tpu_custom_call" | custom-call | flops 1207959552 | bytes 8388608 | tf_op jit(solution)/shard_map/pallas_call | solution.py:93
  110.2 5.0 %shard_map.361 = (bf16[512,1536]{1,0:T(8,128)(2,1)S(1)}, bf16[1536,512]{1,0:T(8,128)(2,1)S(1)}, bf16[512,1536]{1,0:T(8,128)(2,1)S(1)}) custom-call(bf16[512,768]{1,0:T(8,128)(2,1)S(1)} %get-tuple-element.114.hidden_ref, bf16[768,1536]{1,0:T(8,128)(2,1)} %bitcast.13.up.own, f32[1,1536]{1,0:T(1,128)S(1)} %get-tuple-element.229.bias), custom_call_target="tpu_custom_call" | custom-call | flops 1207959552 | bytes 8388608 | tf_op jit(solution)/shard_map/pallas_call | solution.py:93
  115.2 7.2 %shard_map.365 = (bf16[512,768]{1,0:T(8,128)(2,1)}, f32[512,768]{1,0:T(8,128)S(1)}, bf16[512,768]{1,0:T(8,128)(2,1)S(1)}, f32[8,768]{1,0:T(8,128)S(1)}) custom-call(s32[4]{0:T(128)S(1)} %dynamic_slice.9.count, bf16[512,1536]{1,0:T(8,128)(2,1)S(1)} %get-tuple-element.115.active_own, bf16[512,1536]{1,0:T(8,128)(2,1)S(1)} %get-tuple-element.116.active_oth, ...), custom_call_target="tpu_custom_call" | custom-call | flops 2415919104 | bytes 14680064 | tf_op jit(solution)/shard_map/pallas_call | solution.py:93
  122.4 2.2 shard_map.392
  124.8 4.2 %shard_map.368 = (bf16[512,1536]{1,0:T(8,128)(2,1)S(1)}, f32[1,1536]{1,0:T(1,128)S(1)}) custom-call(bf16[512,768]{1,0:T(8,128)(2,1)S(1)} %get-tuple-element.120.top16_ref.right, bf16[1536,768]{1,0:T(8,128)(2,1)} %bitcast.17.oth.down, bf16[512,1536]{1,0:T(8,128)(2,1)S(1)} %get-tuple-element.123.slope), custom_call_target="tpu_custom_call" | custom-call | flops 1207959552 | bytes 8388608 | tf_op jit(solution)/shard_map/pallas_call | solution.py:93
  128.9 1.7 shard_map.386
  131.2 2.5 shard_map.367
  133.7 8.9 %shard_map.369 = (f32[512,768]{1,0:T(8,128)S(1)}, bf16[768,512]{1,0:T(8,128)(2,1)S(1)}, bf16[512,768]{1,0:T(8,128)(2,1)S(1)}, f32[8,768]{1,0:T(8,128)S(1)}) custom-call(bf16[512,1536]{1,0:T(8,128)(2,1)S(1)} %get-tuple-element.122.grad_own.right, bf16[512,1536]{1,0:T(8,128)(2,1)S(1)} %get-tuple-element.124.grad_oth.right, bf16[768,1536]{1,0:T(8,128)(2,1)} %bitcast.13.up.own, ...), custom_call_target="tpu_custom_call" | custom-call | flops 3019898880 | bytes 14680064 | tf_op jit(solution)/shard_map/pallas_call | solution.py:93
  143.8 6.6 %shard_map.370 = (bf16[512,768]{1,0:T(8,128)(2,1)S(1)}, bf16[512,768]{1,0:T(8,128)(2,1)S(1)}, f32[1,768]{1,0:T(1,128)S(1)}) custom-call(bf16[512,1536]{1,0:T(8,128)(2,1)S(1)} %get-tuple-element.119.probs_ref, bf16[512,768]{1,0:T(8,128)(2,1)S(1)} %get-tuple-element.127.back_ref, bf16[3,512,768]{2,1,0:T(8,128)(2,1)S(1)} %get-tuple-element.112.qkv_ref), custom_call_target="tpu_custom_call" | custom-call | flops 805306368 | bytes 6291456 | tf_op jit(solution)/shard_map/pallas_call | solution.py:93
  153.0 2.2 shard_map.391
  156.4 1.6 collective-permute-start.42
  157.9 1.9 shard_map.385
  162.1 4.8 %collective-permute-start.54 = (f32[12,768]{1,0:T(8,128)S(1)}, f32[12,768]{1,0:T(8,128)S(1)}, u32[]{:S(2)}, u32[]{:S(2)}) collective-permute-start(f32[12,768]{1,0:T(8,128)S(1)} %shard_map.401.refs_0_), channel_id=1, source_target_pairs={{0,8},{1,9},{2,10},{3,11},{4,12},{5,13},{6,14},{7,15},{8,0},{9,1},... | collective-permute-start | bytes 110600 | tf_op jit(solution)/shard_map/ppermute | solution.py:55
  170.6 1.6 collective-permute-start.56
  175.1 5.3 %shard_map.372.own = f32[512,768]{1,0:T(8,128)S(1)} custom-call(bf16[512,768]{1,0:T(8,128)(2,1)S(1)} %get-tuple-element.128.grad_q_ref.right_v_ref, bf16[512,768]{1,0:T(8,128)(2,1)S(1)} %get-tuple-element.129.grad_k_ref.right_w_ref, bf16[512,768]{1,0:T(8,128)(2,1)S(1)} %get-tuple-element.130.grad_v_ref.right_v_ref, ...), custom_call_target="tpu_custom_call" | custom-call | flops 1811939328 | bytes 8388608 | tf_op jit(solution)/shard_map/pallas_call | solution.py:93
  180.5 11.1 %collective-permute-done.30.refs_1_ = bf16[2,4,2,48,384]{4,3,2,1,0:T(8,128)(2,1)S(1)} collective-permute-done((bf16[2,4,2,48,384]{4,3,2,1,0:T(8,128)(2,1)S(1)}, bf16[2,4,2,48,384]{4,3,2,1,0:T(8,128)(2,1)S(1)}, u32[]{:S(2)}, u32[]{:S(2)}) %collective-permute-start.30) | collective-permute-done | bytes 589856 | tf_op jit(solution)/shard_map/ppermute | solution.py:55
  193.2 7.4 %collective-permute-done.57.refs_1_ = f32[12,768]{1,0:T(8,128)S(1)} collective-permute-done((f32[12,768]{1,0:T(8,128)S(1)}, f32[12,768]{1,0:T(8,128)S(1)}, u32[]{:S(2)}, u32[]{:S(2)}) %collective-permute-start.57) | collective-permute-done | bytes 36896 | tf_op jit(solution)/shard_map/ppermute | solution.py:55
  201.1 1.6 collective-permute-start.58
  203.7 4.7 %collective-permute-done.58.refs_2_ = f32[12,768]{1,0:T(8,128)S(1)} collective-permute-done((f32[12,768]{1,0:T(8,128)S(1)}, f32[12,768]{1,0:T(8,128)S(1)}, u32[]{:S(2)}, u32[]{:S(2)}) %collective-permute-start.58) | collective-permute-done | bytes 36896 | tf_op jit(solution)/shard_map/ppermute | solution.py:55
  208.9 2.4 collective-permute-start.59
  211.6 8.1 %collective-permute-done.59.refs_3_ = f32[12,768]{1,0:T(8,128)S(1)} collective-permute-done((f32[12,768]{1,0:T(8,128)S(1)}, f32[12,768]{1,0:T(8,128)S(1)}, u32[]{:S(2)}, u32[]{:S(2)}) %collective-permute-start.59) | collective-permute-done | bytes 36896 | tf_op jit(solution)/shard_map/ppermute | solution.py:55
  220.9 4.5 %collective-permute-start.32 = (bf16[2,48,384]{2,1,0:T(8,128)(2,1)S(1)}, bf16[2,48,384]{2,1,0:T(8,128)(2,1)S(1)}, u32[]{:S(2)}, u32[]{:S(2)}) collective-permute-start(bf16[2,48,384]{2,1,0:T(8,128)(2,1)S(1)} %get-tuple-element.147), channel_id=1, source_target_pairs={{0,8},{1,9},{2,10},{3,11},{4,12},{5,13},{6,14},{7,15},{8,0},{9,1},... | collective-permute-start | bytes 221192 | tf_op jit(solution)/shard_map/ppermute | solution.py:55
  225.4 2.9 collective-permute-done.32.refs_5_
  229.0 2.6 collective-permute-start.33
  231.5 4.2 %collective-permute-done.33.refs_6_ = bf16[2,48,384]{2,1,0:T(8,128)(2,1)S(1)} collective-permute-done((bf16[2,48,384]{2,1,0:T(8,128)(2,1)S(1)}, bf16[2,48,384]{2,1,0:T(8,128)(2,1)S(1)}, u32[]{:S(2)}, u32[]{:S(2)}) %collective-permute-start.33) | collective-permute-done | bytes 73760 | tf_op jit(solution)/shard_map/ppermute | solution.py:55
  236.4 2.3 collective-permute-start.34
  239.3 4.0 %collective-permute-done.34.refs_7_ = bf16[2,48,384]{2,1,0:T(8,128)(2,1)S(1)} collective-permute-done((bf16[2,48,384]{2,1,0:T(8,128)(2,1)S(1)}, bf16[2,48,384]{2,1,0:T(8,128)(2,1)S(1)}, u32[]{:S(2)}, u32[]{:S(2)}) %collective-permute-start.34) | collective-permute-done | bytes 73760 | tf_op jit(solution)/shard_map/ppermute | solution.py:55
  243.2 5.1 %collective-permute-done.26.refs_1_ = bf16[2,48,384]{2,1,0:T(8,128)(2,1)S(1)} collective-permute-done((bf16[2,48,384]{2,1,0:T(8,128)(2,1)S(1)}, bf16[2,48,384]{2,1,0:T(8,128)(2,1)S(1)}, u32[]{:S(2)}, u32[]{:S(2)}) %collective-permute-start.26) | collective-permute-done | bytes 73760 | tf_op jit(solution)/shard_map/ppermute | solution.py:55
  249.3 1.9 collective-permute-start.28
  251.9 7.5 %collective-permute-done.27.refs_2_ = bf16[2,48,384]{2,1,0:T(8,128)(2,1)S(1)} collective-permute-done((bf16[2,48,384]{2,1,0:T(8,128)(2,1)S(1)}, bf16[2,48,384]{2,1,0:T(8,128)(2,1)S(1)}, u32[]{:S(2)}, u32[]{:S(2)}) %collective-permute-start.27) | collective-permute-done | bytes 73760 | tf_op jit(solution)/shard_map/ppermute | solution.py:55
  261.6 3.5 %collective-permute-start.46 = (bf16[1,96,768]{2,1,0:T(8,128)(2,1)S(1)}, bf16[1,96,768]{2,1,0:T(8,128)(2,1)S(1)}, u32[]{:S(2)}, u32[]{:S(2)}) collective-permute-start(bf16[1,96,768]{2,1,0:T(8,128)(2,1)S(1)} %get-tuple-element.170), channel_id=1, source_target_pairs={{0,24},{1,25},{2,26},{3,27},{4,28},{5,29},{6,30},{7,31},{8,16},{9,... | collective-permute-start | bytes 442376 | tf_op jit(solution)/shard_map/ppermute | solution.py:55
  267.2 6.5 %collective-permute-done.45.refs_2_ = bf16[1,96,768]{2,1,0:T(8,128)(2,1)S(1)} collective-permute-done((bf16[1,96,768]{2,1,0:T(8,128)(2,1)S(1)}, bf16[1,96,768]{2,1,0:T(8,128)(2,1)S(1)}, u32[]{:S(2)}, u32[]{:S(2)}) %collective-permute-start.45) | collective-permute-done | bytes 147488 | tf_op jit(solution)/shard_map/ppermute | solution.py:55
  275.0 2.4 collective-permute-start.40
  279.1 1.8 copy.43.refs_12_
  280.9 1.7 copy.44.refs_13_
  298.3 2.3 shard_map.390
  300.6 2.2 collective-permute-start.47
  307.2 2.5 collective-permute-done.49.refs_3_
  311.6 1.7 collective-permute-done.50.refs_1_
  314.7 3.2 collective-permute-done.52.refs_3_
  319.4 2.4 shard_map.366
  321.8 3.4 %shard_map.373 = f32[2,512,768]{2,1,0:T(8,128)} custom-call(s32[4]{0:T(128)S(1)} %pad_add_fusion.s, f32[512,768]{1,0:T(8,128)S(1)} %shard_map.372.own, f32[512,768]{1,0:T(8,128)} %collective-permute-done.22.oth), custom_call_target="tpu_custom_call" | custom-call | tf_op jit(solution)/shard_map/pallas_call | solution.py:93
  325.2 1.7 copy.47
  326.9 1.7 copy.48
  (265 shorter events, 84.3 us)
Async XLA Ops:
  0.7 83.3 %copy-start = (bf16[8,128,768]{2,1,0:T(8,128)(2,1)S(1)}, bf16[8,128,768]{2,1,0:T(8,128)(2,1)}, u32[]{:S(2)}) copy-start(bf16[8,128,768]{2,1,0:T(8,128)(2,1)} %param.19) | copy-start | bytes 4718596
  2.7 11.2 %collective-permute-start = (bf16[4,48,384]{2,1,0:T(8,128)(2,1)S(1)}, bf16[4,48,384]{2,1,0:T(8,128)(2,1)S(1)}, u32[]{:S(2)}, u32[]{:S(2)}) collective-permute-start(bf16[4,48,384]{2,1,0:T(8,128)(2,1)S(1)} %pad_maximum_fusion.refs_0_), channel_id=1, source_target_pairs={{0,8},{1,9},{2,10},{3,11},{4,12},{5,13},{6,14},{7,15},{8,0},{9,1},... | collective-permute-start | bytes 442376 | tf_op jit(solution)/shard_map/ppermute | solution.py:55
  5.8 14.0 %collective-permute-start.1 = (bf16[4,48,384]{2,1,0:T(8,128)(2,1)S(1)}, bf16[4,48,384]{2,1,0:T(8,128)(2,1)S(1)}, u32[]{:S(2)}, u32[]{:S(2)}) collective-permute-start(bf16[4,48,384]{2,1,0:T(8,128)(2,1)S(1)} %pad_maximum_fusion.refs_0_), channel_id=1, source_target_pairs={{0,16},{1,17},{2,18},{3,19},{4,20},{5,21},{6,22},{7,23},{8,24},{9,... | collective-permute-start | bytes 442376 | tf_op jit(solution)/shard_map/ppermute | solution.py:55
  8.4 11.4 %collective-permute-start.2 = (bf16[4,48,384]{2,1,0:T(8,128)(2,1)S(1)}, bf16[4,48,384]{2,1,0:T(8,128)(2,1)S(1)}, u32[]{:S(2)}, u32[]{:S(2)}) collective-permute-start(bf16[4,48,384]{2,1,0:T(8,128)(2,1)S(1)} %pad_maximum_fusion.refs_0_), channel_id=1, source_target_pairs={{0,24},{1,25},{2,26},{3,27},{4,28},{5,29},{6,30},{7,31},{8,16},{9,... | collective-permute-start | bytes 442376 | tf_op jit(solution)/shard_map/ppermute | solution.py:55
  9.4 22.8 %collective-permute-start.7 = (bf16[1,48,1536]{2,1,0:T(8,128)(2,1)S(1)}, bf16[1,48,1536]{2,1,0:T(8,128)(2,1)S(1)}, u32[]{:S(2)}, u32[]{:S(2)}) collective-permute-start(bf16[1,48,1536]{2,1,0:T(8,128)(2,1)S(1)} %convert_bitcast_fusion.1.refs_0_), channel_id=1, source_target_pairs={{0,8},{1,9},{2,10},{3,11},{4,12},{5,13},{6,14},{7,15},{8,0},{9,1},... | collective-permute-start | bytes 442376 | tf_op jit(solution)/shard_map/ppermute | solution.py:55
  10.3 22.7 %collective-permute-start.8 = (bf16[1,48,1536]{2,1,0:T(8,128)(2,1)S(1)}, bf16[1,48,1536]{2,1,0:T(8,128)(2,1)S(1)}, u32[]{:S(2)}, u32[]{:S(2)}) collective-permute-start(bf16[1,48,1536]{2,1,0:T(8,128)(2,1)S(1)} %convert_bitcast_fusion.1.refs_0_), channel_id=1, source_target_pairs={{0,16},{1,17},{2,18},{3,19},{4,20},{5,21},{6,22},{7,23},{8,24},{9,... | collective-permute-start | bytes 442376 | tf_op jit(solution)/shard_map/ppermute | solution.py:55
  13.9 22.4 %collective-permute-start.9 = (bf16[1,48,1536]{2,1,0:T(8,128)(2,1)S(1)}, bf16[1,48,1536]{2,1,0:T(8,128)(2,1)S(1)}, u32[]{:S(2)}, u32[]{:S(2)}) collective-permute-start(bf16[1,48,1536]{2,1,0:T(8,128)(2,1)S(1)} %convert_bitcast_fusion.1.refs_0_), channel_id=1, source_target_pairs={{0,24},{1,25},{2,26},{3,27},{4,28},{5,29},{6,30},{7,31},{8,16},{9,... | collective-permute-start | bytes 442376 | tf_op jit(solution)/shard_map/ppermute | solution.py:55
  20.4 26.9 %collective-permute-start.3 = (bf16[4,4,48,384]{3,2,1,0:T(8,128)(2,1)S(1)}, bf16[4,4,48,384]{3,2,1,0:T(8,128)(2,1)S(1)}, u32[]{:S(2)}, u32[]{:S(2)}) collective-permute-start(bf16[4,4,48,384]{3,2,1,0:T(8,128)(2,1)S(1)} %shard_map.354.refs_0_), channel_id=1, source_target_pairs={{0,2},{1,5},{2,0},{3,7},{4,6},{5,1},{6,4},{7,3},{8,10},{9,13},{10,... | collective-permute-start | bytes 1769480 | tf_op jit(solution)/shard_map/ppermute | solution.py:55
  22.0 16.4 %collective-permute-start.14 = (bf16[1,96,768]{2,1,0:T(8,128)(2,1)S(1)}, bf16[1,96,768]{2,1,0:T(8,128)(2,1)S(1)}, u32[]{:S(2)}, u32[]{:S(2)}) collective-permute-start(bf16[1,96,768]{2,1,0:T(8,128)(2,1)S(1)} %convert_bitcast_fusion.refs_0_), channel_id=1, source_target_pairs={{0,8},{1,9},{2,10},{3,11},{4,12},{5,13},{6,14},{7,15},{8,0},{9,1},... | collective-permute-start | bytes 442376 | tf_op jit(solution)/shard_map/ppermute | solution.py:55
  32.1 13.0 %collective-permute-start.15 = (bf16[1,96,768]{2,1,0:T(8,128)(2,1)S(1)}, bf16[1,96,768]{2,1,0:T(8,128)(2,1)S(1)}, u32[]{:S(2)}, u32[]{:S(2)}) collective-permute-start(bf16[1,96,768]{2,1,0:T(8,128)(2,1)S(1)} %convert_bitcast_fusion.refs_0_), channel_id=1, source_target_pairs={{0,16},{1,17},{2,18},{3,19},{4,20},{5,21},{6,22},{7,23},{8,24},{9,... | collective-permute-start | bytes 442376 | tf_op jit(solution)/shard_map/ppermute | solution.py:55
  33.0 12.1 %collective-permute-start.16 = (bf16[1,96,768]{2,1,0:T(8,128)(2,1)S(1)}, bf16[1,96,768]{2,1,0:T(8,128)(2,1)S(1)}, u32[]{:S(2)}, u32[]{:S(2)}) collective-permute-start(bf16[1,96,768]{2,1,0:T(8,128)(2,1)S(1)} %convert_bitcast_fusion.refs_0_), channel_id=1, source_target_pairs={{0,24},{1,25},{2,26},{3,27},{4,28},{5,29},{6,30},{7,31},{8,16},{9,... | collective-permute-start | bytes 442376 | tf_op jit(solution)/shard_map/ppermute | solution.py:55
  36.3 16.3 %collective-permute-start.4 = (bf16[4,4,48,384]{3,2,1,0:T(8,128)(2,1)S(1)}, bf16[4,4,48,384]{3,2,1,0:T(8,128)(2,1)S(1)}, u32[]{:S(2)}, u32[]{:S(2)}) collective-permute-start(bf16[4,4,48,384]{3,2,1,0:T(8,128)(2,1)S(1)} %shard_map.354.refs_0_), channel_id=1, source_target_pairs={{0,4},{1,3},{2,6},{3,1},{4,0},{5,7},{6,2},{7,5},{8,12},{9,11},{10,... | collective-permute-start | bytes 1769480 | tf_op jit(solution)/shard_map/ppermute | solution.py:55
  38.4 15.7 %collective-permute-start.10 = (bf16[4,1,48,1536]{3,2,1,0:T(8,128)(2,1)S(1)}, bf16[4,1,48,1536]{3,2,1,0:T(8,128)(2,1)}, u32[]{:S(2)}, u32[]{:S(2)}) collective-permute-start(bf16[4,1,48,1536]{3,2,1,0:T(8,128)(2,1)S(1)} %shard_map.359.refs_0_), channel_id=1, source_target_pairs={{0,2},{1,5},{2,0},{3,7},{4,6},{5,1},{6,4},{7,3},{8,10},{9,13},{10,... | collective-permute-start | bytes 1769480 | tf_op jit(solution)/shard_map/ppermute | solution.py:55
  45.8 16.9 %collective-permute-start.17 = (bf16[4,1,96,768]{3,2,1,0:T(8,128)(2,1)S(1)}, bf16[4,1,96,768]{3,2,1,0:T(8,128)(2,1)}, u32[]{:S(2)}, u32[]{:S(2)}) collective-permute-start(bf16[4,1,96,768]{3,2,1,0:T(8,128)(2,1)S(1)} %shard_map.363.refs_0_), channel_id=1, source_target_pairs={{0,2},{1,5},{2,0},{3,7},{4,6},{5,1},{6,4},{7,3},{8,10},{9,13},{10,... | collective-permute-start | bytes 1769480 | tf_op jit(solution)/shard_map/ppermute | solution.py:55
  47.3 16.4 %collective-permute-start.5 = (bf16[4,4,48,384]{3,2,1,0:T(8,128)(2,1)S(1)}, bf16[4,4,48,384]{3,2,1,0:T(8,128)(2,1)S(1)}, u32[]{:S(2)}, u32[]{:S(2)}) collective-permute-start(bf16[4,4,48,384]{3,2,1,0:T(8,128)(2,1)S(1)} %collective-permute-done.3.refs_1_), channel_id=1, source_target_pairs={{0,4},{1,3},{2,6},{3,1},{4,0},{5,7},{6,2},{7,5},{8,12},{9,11},{10,... | collective-permute-start | bytes 1769480 | tf_op jit(solution)/shard_map/ppermute | solution.py:55
  48.8 19.4 %collective-permute-start.11 = (bf16[4,1,48,1536]{3,2,1,0:T(8,128)(2,1)S(1)}, bf16[4,1,48,1536]{3,2,1,0:T(8,128)(2,1)}, u32[]{:S(2)}, u32[]{:S(2)}) collective-permute-start(bf16[4,1,48,1536]{3,2,1,0:T(8,128)(2,1)S(1)} %shard_map.359.refs_0_), channel_id=1, source_target_pairs={{0,4},{1,3},{2,6},{3,1},{4,0},{5,7},{6,2},{7,5},{8,12},{9,11},{10,... | collective-permute-start | bytes 1769480 | tf_op jit(solution)/shard_map/ppermute | solution.py:55
  52.6 32.3 %collective-permute-start.18 = (bf16[4,1,96,768]{3,2,1,0:T(8,128)(2,1)S(1)}, bf16[4,1,96,768]{3,2,1,0:T(8,128)(2,1)}, u32[]{:S(2)}, u32[]{:S(2)}) collective-permute-start(bf16[4,1,96,768]{3,2,1,0:T(8,128)(2,1)S(1)} %shard_map.363.refs_0_), channel_id=1, source_target_pairs={{0,4},{1,3},{2,6},{3,1},{4,0},{5,7},{6,2},{7,5},{8,12},{9,11},{10,... | collective-permute-start | bytes 1769480 | tf_op jit(solution)/shard_map/ppermute | solution.py:55
  54.1 26.8 %collective-permute-start.12 = (bf16[4,1,48,1536]{3,2,1,0:T(8,128)(2,1)}, bf16[4,1,48,1536]{3,2,1,0:T(8,128)(2,1)}, u32[]{:S(2)}, u32[]{:S(2)}) collective-permute-start(bf16[4,1,48,1536]{3,2,1,0:T(8,128)(2,1)} %collective-permute-done.10.refs_1_), channel_id=1, source_target_pairs={{0,4},{1,3},{2,6},{3,1},{4,0},{5,7},{6,2},{7,5},{8,12},{9,11},{10,... | collective-permute-start | bytes 1769480 | tf_op jit(solution)/shard_map/ppermute | solution.py:55
  62.6 24.6 %collective-permute-start.19 = (bf16[4,1,96,768]{3,2,1,0:T(8,128)(2,1)}, bf16[4,1,96,768]{3,2,1,0:T(8,128)(2,1)}, u32[]{:S(2)}, u32[]{:S(2)}) collective-permute-start(bf16[4,1,96,768]{3,2,1,0:T(8,128)(2,1)} %collective-permute-done.17.refs_1_), channel_id=1, source_target_pairs={{0,4},{1,3},{2,6},{3,1},{4,0},{5,7},{6,2},{7,5},{8,12},{9,11},{10,... | collective-permute-start | bytes 1769480 | tf_op jit(solution)/shard_map/ppermute | solution.py:55
  65.8 23.9 %collective-permute-start.6 = (bf16[4,16,48,384]{3,2,1,0:T(8,128)(2,1)}, bf16[4,16,48,384]{3,2,1,0:T(8,128)(2,1)}, u32[]{:S(2)}, u32[]{:S(2)}) collective-permute-start(bf16[4,16,48,384]{3,2,1,0:T(8,128)(2,1)} %shard_map.355), channel_id=1, source_target_pairs={{0,1},{1,0},{2,3},{3,2},{4,5},{5,4},{6,7},{7,6},{8,9},{9,8},{10,11... | collective-permute-start | bytes 7077896 | tf_op jit(solution)/shard_map/ppermute | solution.py:55
  83.9 21.2 %collective-permute-start.13 = (bf16[1,16,48,1536]{3,2,1,0:T(8,128)(2,1)}, bf16[1,16,48,1536]{3,2,1,0:T(8,128)(2,1)}, u32[]{:S(2)}, u32[]{:S(2)}) collective-permute-start(bf16[1,16,48,1536]{3,2,1,0:T(8,128)(2,1)} %shard_map.360), channel_id=1, source_target_pairs={{0,1},{1,0},{2,3},{3,2},{4,5},{5,4},{6,7},{7,6},{8,9},{9,8},{10,11... | collective-permute-start | bytes 7077896 | tf_op jit(solution)/shard_map/ppermute | solution.py:55
  88.9 26.4 %collective-permute-start.20 = (bf16[1,16,96,768]{3,2,1,0:T(8,128)(2,1)S(1)}, bf16[1,16,96,768]{3,2,1,0:T(8,128)(2,1)}, u32[]{:S(2)}, u32[]{:S(2)}) collective-permute-start(bf16[1,16,96,768]{3,2,1,0:T(8,128)(2,1)S(1)} %shard_map.364), channel_id=1, source_target_pairs={{0,1},{1,0},{2,3},{3,2},{4,5},{5,4},{6,7},{7,6},{8,9},{9,8},{10,11... | collective-permute-start | bytes 7077896 | tf_op jit(solution)/shard_map/ppermute | solution.py:55
  124.6 30.6 %collective-permute-start.41 = (bf16[1,16,96,768]{3,2,1,0:T(8,128)(2,1)S(1)}, bf16[1,16,96,768]{3,2,1,0:T(8,128)(2,1)S(1)}, u32[]{:S(2)}, u32[]{:S(2)}) collective-permute-start(bf16[1,16,96,768]{3,2,1,0:T(8,128)(2,1)S(1)} %bitcast.52), channel_id=1, source_target_pairs={{0,1},{1,0},{2,3},{3,2},{4,5},{5,4},{6,7},{7,6},{8,9},{9,8},{10,11... | collective-permute-start | bytes 7077896 | tf_op jit(solution)/shard_map/ppermute | solution.py:55
  130.7 29.2 %collective-permute-start.35 = (bf16[1,16,48,1536]{3,2,1,0:T(8,128)(2,1)S(1)}, bf16[1,16,48,1536]{3,2,1,0:T(8,128)(2,1)S(1)}, u32[]{:S(2)}, u32[]{:S(2)}) collective-permute-start(bf16[1,16,48,1536]{3,2,1,0:T(8,128)(2,1)S(1)} %bitcast.51), channel_id=1, source_target_pairs={{0,1},{1,0},{2,3},{3,2},{4,5},{5,4},{6,7},{7,6},{8,9},{9,8},{10,11... | collective-permute-start | bytes 7077896 | tf_op jit(solution)/shard_map/ppermute | solution.py:55
  151.4 16.5 %collective-permute-start.29 = (bf16[2,16,48,384]{3,2,1,0:T(8,128)(2,1)S(1)}, bf16[2,16,48,384]{3,2,1,0:T(8,128)(2,1)S(1)}, u32[]{:S(2)}, u32[]{:S(2)}) collective-permute-start(bf16[2,16,48,384]{3,2,1,0:T(8,128)(2,1)S(1)} %bitcast.54), channel_id=1, source_target_pairs={{0,1},{1,0},{2,3},{3,2},{4,5},{5,4},{6,7},{7,6},{8,9},{9,8},{10,11... | collective-permute-start | bytes 3538952 | tf_op jit(solution)/shard_map/ppermute | solution.py:55
  152.5 18.1 %collective-permute-start.23 = (bf16[2,16,48,384]{3,2,1,0:T(8,128)(2,1)S(1)}, bf16[2,16,48,384]{3,2,1,0:T(8,128)(2,1)S(1)}, u32[]{:S(2)}, u32[]{:S(2)}) collective-permute-start(bf16[2,16,48,384]{3,2,1,0:T(8,128)(2,1)S(1)} %bitcast.53), channel_id=1, source_target_pairs={{0,1},{1,0},{2,3},{3,2},{4,5},{5,4},{6,7},{7,6},{8,9},{9,8},{10,11... | collective-permute-start | bytes 3538952 | tf_op jit(solution)/shard_map/ppermute | solution.py:55
  156.4 46.5 %collective-permute-start.42 = (bf16[2,4,1,96,768]{4,3,2,1,0:T(8,128)(2,1)S(1)}, bf16[2,4,1,96,768]{4,3,2,1,0:T(8,128)(2,1)S(1)}, u32[]{:S(2)}, u32[]{:S(2)}) collective-permute-start(bf16[2,4,1,96,768]{4,3,2,1,0:T(8,128)(2,1)S(1)} %get-tuple-element.164), channel_id=1, source_target_pairs={{0,4},{1,3},{2,6},{3,1},{4,0},{5,7},{6,2},{7,5},{8,12},{9,11},{10,... | collective-permute-start | bytes 3538952 | tf_op jit(solution)/shard_map/ppermute | solution.py:55
  161.0 47.9 %collective-permute-start.36 = (bf16[2,4,1,48,1536]{4,3,2,1,0:T(8,128)(2,1)S(1)}, bf16[2,4,1,48,1536]{4,3,2,1,0:T(8,128)(2,1)S(1)}, u32[]{:S(2)}, u32[]{:S(2)}) collective-permute-start(bf16[2,4,1,48,1536]{4,3,2,1,0:T(8,128)(2,1)S(1)} %get-tuple-element.153), channel_id=1, source_target_pairs={{0,4},{1,3},{2,6},{3,1},{4,0},{5,7},{6,2},{7,5},{8,12},{9,11},{10,... | collective-permute-start | bytes 3538952 | tf_op jit(solution)/shard_map/ppermute | solution.py:55
  162.1 10.8 %collective-permute-start.54 = (f32[12,768]{1,0:T(8,128)S(1)}, f32[12,768]{1,0:T(8,128)S(1)}, u32[]{:S(2)}, u32[]{:S(2)}) collective-permute-start(f32[12,768]{1,0:T(8,128)S(1)} %shard_map.401.refs_0_), channel_id=1, source_target_pairs={{0,8},{1,9},{2,10},{3,11},{4,12},{5,13},{6,14},{7,15},{8,0},{9,1},... | collective-permute-start | bytes 110600 | tf_op jit(solution)/shard_map/ppermute | solution.py:55
  167.9 6.0 %collective-permute-start.55 = (f32[12,768]{1,0:T(8,128)S(1)}, f32[12,768]{1,0:T(8,128)S(1)}, u32[]{:S(2)}, u32[]{:S(2)}) collective-permute-start(f32[12,768]{1,0:T(8,128)S(1)} %shard_map.401.refs_0_), channel_id=1, source_target_pairs={{0,16},{1,17},{2,18},{3,19},{4,20},{5,21},{6,22},{7,23},{8,24},{9,... | collective-permute-start | bytes 110600 | tf_op jit(solution)/shard_map/ppermute | solution.py:55
  170.6 9.8 %collective-permute-start.56 = (f32[12,768]{1,0:T(8,128)S(1)}, f32[12,768]{1,0:T(8,128)S(1)}, u32[]{:S(2)}, u32[]{:S(2)}) collective-permute-start(f32[12,768]{1,0:T(8,128)S(1)} %shard_map.401.refs_0_), channel_id=1, source_target_pairs={{0,24},{1,25},{2,26},{3,27},{4,28},{5,29},{6,30},{7,31},{8,16},{9,... | collective-permute-start | bytes 110600 | tf_op jit(solution)/shard_map/ppermute | solution.py:55
  173.0 18.6 %collective-permute-start.30 = (bf16[2,4,2,48,384]{4,3,2,1,0:T(8,128)(2,1)S(1)}, bf16[2,4,2,48,384]{4,3,2,1,0:T(8,128)(2,1)S(1)}, u32[]{:S(2)}, u32[]{:S(2)}) collective-permute-start(bf16[2,4,2,48,384]{4,3,2,1,0:T(8,128)(2,1)S(1)} %get-tuple-element.143), channel_id=1, source_target_pairs={{0,4},{1,3},{2,6},{3,1},{4,0},{5,7},{6,2},{7,5},{8,12},{9,11},{10,... | collective-permute-start | bytes 1769480 | tf_op jit(solution)/shard_map/ppermute | solution.py:55
  173.9 27.3 %collective-permute-start.24 = (bf16[2,4,2,48,384]{4,3,2,1,0:T(8,128)(2,1)S(1)}, bf16[2,4,2,48,384]{4,3,2,1,0:T(8,128)(2,1)S(1)}, u32[]{:S(2)}, u32[]{:S(2)}) collective-permute-start(bf16[2,4,2,48,384]{4,3,2,1,0:T(8,128)(2,1)S(1)} %get-tuple-element.135), channel_id=1, source_target_pairs={{0,4},{1,3},{2,6},{3,1},{4,0},{5,7},{6,2},{7,5},{8,12},{9,11},{10,... | collective-permute-start | bytes 1769480 | tf_op jit(solution)/shard_map/ppermute | solution.py:55
  180.4 141.4 %collective-permute-start.22 = (f32[512,768]{1,0:T(8,128)S(1)}, f32[512,768]{1,0:T(8,128)}, u32[]{:S(2)}, u32[]{:S(2)}) collective-permute-start(f32[512,768]{1,0:T(8,128)S(1)} %shard_map.372.own), channel_id=1, source_target_pairs={{0,1},{1,0},{2,3},{3,2},{4,5},{5,4},{6,7},{7,6},{8,9},{9,8},{10,11... | collective-permute-start | bytes 4718600 | tf_op jit(solution)/shard_map/ppermute | solution.py:55
  191.6 9.1 %collective-permute-start.57 = (f32[12,768]{1,0:T(8,128)S(1)}, f32[12,768]{1,0:T(8,128)S(1)}, u32[]{:S(2)}, u32[]{:S(2)}) collective-permute-start(f32[12,768]{1,0:T(8,128)S(1)} %shard_map.402.refs_0_), channel_id=1, source_target_pairs={{0,4},{1,5},{2,6},{3,7},{4,0},{5,1},{6,2},{7,3},{8,12},{9,13},{10,... | collective-permute-start | bytes 110600 | tf_op jit(solution)/shard_map/ppermute | solution.py:55
  200.7 19.6 %collective-permute-start.31 = (bf16[4,2,48,384]{3,2,1,0:T(8,128)(2,1)S(1)}, bf16[4,2,48,384]{3,2,1,0:T(8,128)(2,1)S(1)}, u32[]{:S(2)}, u32[]{:S(2)}) collective-permute-start(bf16[4,2,48,384]{3,2,1,0:T(8,128)(2,1)S(1)} %get-tuple-element.145), channel_id=1, source_target_pairs={{0,2},{1,5},{2,0},{3,7},{4,6},{5,1},{6,4},{7,3},{8,10},{9,13},{10,... | collective-permute-start | bytes 884744 | tf_op jit(solution)/shard_map/ppermute | solution.py:55
  201.1 7.2 %collective-permute-start.58 = (f32[12,768]{1,0:T(8,128)S(1)}, f32[12,768]{1,0:T(8,128)S(1)}, u32[]{:S(2)}, u32[]{:S(2)}) collective-permute-start(f32[12,768]{1,0:T(8,128)S(1)} %shard_map.402.refs_0_), channel_id=1, source_target_pairs={{0,2},{1,3},{2,0},{3,1},{4,6},{5,7},{6,4},{7,5},{8,10},{9,11},{10,... | collective-permute-start | bytes 110600 | tf_op jit(solution)/shard_map/ppermute | solution.py:55
  202.8 18.0 %collective-permute-start.25 = (bf16[4,2,48,384]{3,2,1,0:T(8,128)(2,1)S(1)}, bf16[4,2,48,384]{3,2,1,0:T(8,128)(2,1)S(1)}, u32[]{:S(2)}, u32[]{:S(2)}) collective-permute-start(bf16[4,2,48,384]{3,2,1,0:T(8,128)(2,1)S(1)} %get-tuple-element.137), channel_id=1, source_target_pairs={{0,2},{1,5},{2,0},{3,7},{4,6},{5,1},{6,4},{7,3},{8,10},{9,13},{10,... | collective-permute-start | bytes 884744 | tf_op jit(solution)/shard_map/ppermute | solution.py:55
  208.3 41.0 %collective-permute-start.43 = (bf16[4,1,96,768]{3,2,1,0:T(8,128)(2,1)S(1)}, bf16[4,1,96,768]{3,2,1,0:T(8,128)(2,1)S(1)}, u32[]{:S(2)}, u32[]{:S(2)}) collective-permute-start(bf16[4,1,96,768]{3,2,1,0:T(8,128)(2,1)S(1)} %get-tuple-element.166), channel_id=1, source_target_pairs={{0,2},{1,5},{2,0},{3,7},{4,6},{5,1},{6,4},{7,3},{8,10},{9,13},{10,... | collective-permute-start | bytes 1769480 | tf_op jit(solution)/shard_map/ppermute | solution.py:55
  208.9 10.8 %collective-permute-start.59 = (f32[12,768]{1,0:T(8,128)S(1)}, f32[12,768]{1,0:T(8,128)S(1)}, u32[]{:S(2)}, u32[]{:S(2)}) collective-permute-start(f32[12,768]{1,0:T(8,128)S(1)} %shard_map.402.refs_0_), channel_id=1, source_target_pairs={{0,6},{1,7},{2,4},{3,5},{4,2},{5,3},{6,0},{7,1},{8,14},{9,15},{10,... | collective-permute-start | bytes 110600 | tf_op jit(solution)/shard_map/ppermute | solution.py:55
  219.7 41.9 %collective-permute-start.37 = (bf16[4,1,48,1536]{3,2,1,0:T(8,128)(2,1)S(1)}, bf16[4,1,48,1536]{3,2,1,0:T(8,128)(2,1)S(1)}, u32[]{:S(2)}, u32[]{:S(2)}) collective-permute-start(bf16[4,1,48,1536]{3,2,1,0:T(8,128)(2,1)S(1)} %get-tuple-element.155), channel_id=1, source_target_pairs={{0,2},{1,5},{2,0},{3,7},{4,6},{5,1},{6,4},{7,3},{8,10},{9,13},{10,... | collective-permute-start | bytes 1769480 | tf_op jit(solution)/shard_map/ppermute | solution.py:55
  220.2 99.1 %collective-permute-start.21 = (bf16[512,768]{1,0:T(8,128)(2,1)}, bf16[512,768]{1,0:T(8,128)(2,1)S(1)}, u32[]{:S(2)}, u32[]{:S(2)}) collective-permute-start(bf16[512,768]{1,0:T(8,128)(2,1)} %get-tuple-element.118.own), channel_id=1, source_target_pairs={{0,1},{1,0},{2,3},{3,2},{4,5},{5,4},{6,7},{7,6},{8,9},{9,8},{10,11... | collective-permute-start | bytes 2359304 | tf_op jit(solution)/shard_map/ppermute | solution.py:55
  220.9 44.3 %copy-start.42 = (f32[2,48,384]{2,1,0:T(8,128)}, f32[2,48,384]{2,1,0:T(8,128)S(1)}, u32[]{:S(2)}) copy-start(f32[2,48,384]{2,1,0:T(8,128)S(1)} %get-tuple-element.146.refs_4_) | copy-start | bytes 442372
  220.9 7.5 %collective-permute-start.32 = (bf16[2,48,384]{2,1,0:T(8,128)(2,1)S(1)}, bf16[2,48,384]{2,1,0:T(8,128)(2,1)S(1)}, u32[]{:S(2)}, u32[]{:S(2)}) collective-permute-start(bf16[2,48,384]{2,1,0:T(8,128)(2,1)S(1)} %get-tuple-element.147), channel_id=1, source_target_pairs={{0,8},{1,9},{2,10},{3,11},{4,12},{5,13},{6,14},{7,15},{8,0},{9,1},... | collective-permute-start | bytes 221192 | tf_op jit(solution)/shard_map/ppermute | solution.py:55
  229.0 6.8 %collective-permute-start.33 = (bf16[2,48,384]{2,1,0:T(8,128)(2,1)S(1)}, bf16[2,48,384]{2,1,0:T(8,128)(2,1)S(1)}, u32[]{:S(2)}, u32[]{:S(2)}) collective-permute-start(bf16[2,48,384]{2,1,0:T(8,128)(2,1)S(1)} %get-tuple-element.148), channel_id=1, source_target_pairs={{0,16},{1,17},{2,18},{3,19},{4,20},{5,21},{6,22},{7,23},{8,24},{9,... | collective-permute-start | bytes 221192 | tf_op jit(solution)/shard_map/ppermute | solution.py:55
  236.4 6.9 %collective-permute-start.34 = (bf16[2,48,384]{2,1,0:T(8,128)(2,1)S(1)}, bf16[2,48,384]{2,1,0:T(8,128)(2,1)S(1)}, u32[]{:S(2)}, u32[]{:S(2)}) collective-permute-start(bf16[2,48,384]{2,1,0:T(8,128)(2,1)S(1)} %get-tuple-element.149), channel_id=1, source_target_pairs={{0,24},{1,25},{2,26},{3,27},{4,28},{5,29},{6,30},{7,31},{8,16},{9,... | collective-permute-start | bytes 221192 | tf_op jit(solution)/shard_map/ppermute | solution.py:55
  243.2 5.1 %collective-permute-start.26 = (bf16[2,48,384]{2,1,0:T(8,128)(2,1)S(1)}, bf16[2,48,384]{2,1,0:T(8,128)(2,1)S(1)}, u32[]{:S(2)}, u32[]{:S(2)}) collective-permute-start(bf16[2,48,384]{2,1,0:T(8,128)(2,1)S(1)} %get-tuple-element.139), channel_id=1, source_target_pairs={{0,8},{1,9},{2,10},{3,11},{4,12},{5,13},{6,14},{7,15},{8,0},{9,1},... | collective-permute-start | bytes 221192 | tf_op jit(solution)/shard_map/ppermute | solution.py:55
  249.0 10.5 %collective-permute-start.27 = (bf16[2,48,384]{2,1,0:T(8,128)(2,1)S(1)}, bf16[2,48,384]{2,1,0:T(8,128)(2,1)S(1)}, u32[]{:S(2)}, u32[]{:S(2)}) collective-permute-start(bf16[2,48,384]{2,1,0:T(8,128)(2,1)S(1)} %get-tuple-element.140), channel_id=1, source_target_pairs={{0,16},{1,17},{2,18},{3,19},{4,20},{5,21},{6,22},{7,23},{8,24},{9,... | collective-permute-start | bytes 221192 | tf_op jit(solution)/shard_map/ppermute | solution.py:55
  249.3 10.8 %collective-permute-start.28 = (bf16[2,48,384]{2,1,0:T(8,128)(2,1)S(1)}, bf16[2,48,384]{2,1,0:T(8,128)(2,1)S(1)}, u32[]{:S(2)}, u32[]{:S(2)}) collective-permute-start(bf16[2,48,384]{2,1,0:T(8,128)(2,1)S(1)} %get-tuple-element.141), channel_id=1, source_target_pairs={{0,24},{1,25},{2,26},{3,27},{4,28},{5,29},{6,30},{7,31},{8,16},{9,... | collective-permute-start | bytes 221192 | tf_op jit(solution)/shard_map/ppermute | solution.py:55
  251.9 30.7 %copy-start.18 = (f32[1,96,768]{2,1,0:T(8,128)}, f32[1,96,768]{2,1,0:T(8,128)S(1)}, u32[]{:S(2)}) copy-start(f32[1,96,768]{2,1,0:T(8,128)S(1)} %get-tuple-element.167.refs_0_) | copy-start | bytes 884740
  260.1 7.1 %collective-permute-start.44 = (bf16[1,96,768]{2,1,0:T(8,128)(2,1)S(1)}, bf16[1,96,768]{2,1,0:T(8,128)(2,1)S(1)}, u32[]{:S(2)}, u32[]{:S(2)}) collective-permute-start(bf16[1,96,768]{2,1,0:T(8,128)(2,1)S(1)} %get-tuple-element.168), channel_id=1, source_target_pairs={{0,8},{1,9},{2,10},{3,11},{4,12},{5,13},{6,14},{7,15},{8,0},{9,1},... | collective-permute-start | bytes 442376 | tf_op jit(solution)/shard_map/ppermute | solution.py:55
  260.7 12.9 %collective-permute-start.45 = (bf16[1,96,768]{2,1,0:T(8,128)(2,1)S(1)}, bf16[1,96,768]{2,1,0:T(8,128)(2,1)S(1)}, u32[]{:S(2)}, u32[]{:S(2)}) collective-permute-start(bf16[1,96,768]{2,1,0:T(8,128)(2,1)S(1)} %get-tuple-element.169), channel_id=1, source_target_pairs={{0,16},{1,17},{2,18},{3,19},{4,20},{5,21},{6,22},{7,23},{8,24},{9,... | collective-permute-start | bytes 442376 | tf_op jit(solution)/shard_map/ppermute | solution.py:55
  261.6 12.7 %collective-permute-start.46 = (bf16[1,96,768]{2,1,0:T(8,128)(2,1)S(1)}, bf16[1,96,768]{2,1,0:T(8,128)(2,1)S(1)}, u32[]{:S(2)}, u32[]{:S(2)}) collective-permute-start(bf16[1,96,768]{2,1,0:T(8,128)(2,1)S(1)} %get-tuple-element.170), channel_id=1, source_target_pairs={{0,24},{1,25},{2,26},{3,27},{4,28},{5,29},{6,30},{7,31},{8,16},{9,... | collective-permute-start | bytes 442376 | tf_op jit(solution)/shard_map/ppermute | solution.py:55
  267.2 10.2 %collective-permute-start.38 = (bf16[1,48,1536]{2,1,0:T(8,128)(2,1)S(1)}, bf16[1,48,1536]{2,1,0:T(8,128)(2,1)S(1)}, u32[]{:S(2)}, u32[]{:S(2)}) collective-permute-start(bf16[1,48,1536]{2,1,0:T(8,128)(2,1)S(1)} %get-tuple-element.157), channel_id=1, source_target_pairs={{0,8},{1,9},{2,10},{3,11},{4,12},{5,13},{6,14},{7,15},{8,0},{9,1},... | collective-permute-start | bytes 442376 | tf_op jit(solution)/shard_map/ppermute | solution.py:55
  274.4 23.8 %collective-permute-start.39 = (bf16[1,48,1536]{2,1,0:T(8,128)(2,1)}, bf16[1,48,1536]{2,1,0:T(8,128)(2,1)}, u32[]{:S(2)}, u32[]{:S(2)}) collective-permute-start(bf16[1,48,1536]{2,1,0:T(8,128)(2,1)} %get-tuple-element.158), channel_id=1, source_target_pairs={{0,16},{1,17},{2,18},{3,19},{4,20},{5,21},{6,22},{7,23},{8,24},{9,... | collective-permute-start | bytes 442376 | tf_op jit(solution)/shard_map/ppermute | solution.py:55
  275.0 23.2 %collective-permute-start.40 = (bf16[1,48,1536]{2,1,0:T(8,128)(2,1)}, bf16[1,48,1536]{2,1,0:T(8,128)(2,1)}, u32[]{:S(2)}, u32[]{:S(2)}) collective-permute-start(bf16[1,48,1536]{2,1,0:T(8,128)(2,1)} %get-tuple-element.159), channel_id=1, source_target_pairs={{0,24},{1,25},{2,26},{3,27},{4,28},{5,29},{6,30},{7,31},{8,16},{9,... | collective-permute-start | bytes 442376 | tf_op jit(solution)/shard_map/ppermute | solution.py:55
  278.1 39.8 %collective-permute-start.60 = (f32[12,768]{1,0:T(8,128)S(1)}, f32[12,768]{1,0:T(8,128)}, u32[]{:S(2)}, u32[]{:S(2)}) collective-permute-start(f32[12,768]{1,0:T(8,128)S(1)} %shard_map.403.own), channel_id=1, source_target_pairs={{0,1},{1,0},{2,3},{3,2},{4,5},{5,4},{6,7},{7,6},{8,9},{9,8},{10,11... | collective-permute-start | bytes 110600 | tf_op jit(solution)/shard_map/ppermute | solution.py:55
  300.6 3.8 %collective-permute-start.47 = (f32[8,128]{1,0:T(8,128)S(1)}, f32[8,128]{1,0:T(8,128)S(1)}, u32[]{:S(2)}, u32[]{:S(2)}) collective-permute-start(f32[8,128]{1,0:T(8,128)S(1)} %shard_map.397.refs_0_), channel_id=1, source_target_pairs={{0,8},{1,9},{2,10},{3,11},{4,12},{5,13},{6,14},{7,15},{8,0},{9,1},... | collective-permute-start | bytes 12296 | tf_op jit(solution)/shard_map/ppermute | solution.py:55
  302.7 4.5 %collective-permute-start.48 = (f32[8,128]{1,0:T(8,128)S(1)}, f32[8,128]{1,0:T(8,128)S(1)}, u32[]{:S(2)}, u32[]{:S(2)}) collective-permute-start(f32[8,128]{1,0:T(8,128)S(1)} %shard_map.397.refs_0_), channel_id=1, source_target_pairs={{0,16},{1,17},{2,18},{3,19},{4,20},{5,21},{6,22},{7,23},{8,24},{9,... | collective-permute-start | bytes 12296 | tf_op jit(solution)/shard_map/ppermute | solution.py:55
  304.3 5.4 %collective-permute-start.49 = (f32[8,128]{1,0:T(8,128)S(1)}, f32[8,128]{1,0:T(8,128)S(1)}, u32[]{:S(2)}, u32[]{:S(2)}) collective-permute-start(f32[8,128]{1,0:T(8,128)S(1)} %shard_map.397.refs_0_), channel_id=1, source_target_pairs={{0,24},{1,25},{2,26},{3,27},{4,28},{5,29},{6,30},{7,31},{8,16},{9,... | collective-permute-start | bytes 12296 | tf_op jit(solution)/shard_map/ppermute | solution.py:55
  309.7 3.6 %collective-permute-start.50 = (f32[8,128]{1,0:T(8,128)S(1)}, f32[8,128]{1,0:T(8,128)S(1)}, u32[]{:S(2)}, u32[]{:S(2)}) collective-permute-start(f32[8,128]{1,0:T(8,128)S(1)} %shard_map.398.refs_0_), channel_id=1, source_target_pairs={{0,4},{1,5},{2,6},{3,7},{4,0},{5,1},{6,2},{7,3},{8,12},{9,13},{10,... | collective-permute-start | bytes 12296 | tf_op jit(solution)/shard_map/ppermute | solution.py:55
  311.1 3.6 %collective-permute-start.51 = (f32[8,128]{1,0:T(8,128)S(1)}, f32[8,128]{1,0:T(8,128)S(1)}, u32[]{:S(2)}, u32[]{:S(2)}) collective-permute-start(f32[8,128]{1,0:T(8,128)S(1)} %shard_map.398.refs_0_), channel_id=1, source_target_pairs={{0,2},{1,3},{2,0},{3,1},{4,6},{5,7},{6,4},{7,5},{8,10},{9,11},{10,... | collective-permute-start | bytes 12296 | tf_op jit(solution)/shard_map/ppermute | solution.py:55
  313.3 4.5 %collective-permute-start.52 = (f32[8,128]{1,0:T(8,128)S(1)}, f32[8,128]{1,0:T(8,128)S(1)}, u32[]{:S(2)}, u32[]{:S(2)}) collective-permute-start(f32[8,128]{1,0:T(8,128)S(1)} %shard_map.398.refs_0_), channel_id=1, source_target_pairs={{0,6},{1,7},{2,4},{3,5},{4,2},{5,3},{6,0},{7,1},{8,14},{9,15},{10,... | collective-permute-start | bytes 12296 | tf_op jit(solution)/shard_map/ppermute | solution.py:55
  317.8 10.7 %collective-permute-start.53 = (f32[8,128]{1,0:T(8,128)S(1)}, f32[8,128]{1,0:T(8,128)S(1)}, u32[]{:S(2)}, u32[]{:S(2)}) collective-permute-start(f32[8,128]{1,0:T(8,128)S(1)} %shard_map.399.own), channel_id=1, source_target_pairs={{0,1},{1,0},{2,3},{3,2},{4,5},{5,4},{6,7},{7,6},{8,9},{9,8},{10,11... | collective-permute-start | bytes 12296 | tf_op jit(solution)/shard_map/ppermute | solution.py:55
  (60 other events, 399.4 us)

commit v2 on v1

v2 whole, which is shorter than its diff:
```python
import math

import jax
import jax.numpy as jnp
import numpy as np
from jax import lax
from jax.experimental import pallas as pl
from jax.experimental.pallas import tpu as pltpu
from jax.sharding import PartitionSpec as P

HEAD_DIM = 64
STEP = 10
NORM_EPS = 1e-05
BETA_ONE = 0.9
BETA_TWO = 0.999
ADAM_EPS = 1e-06
RATE = 0.3
DECAY = 0.01
MASKED = -1e30
AXES = ("dp", "tensor")
F32, BF16 = jnp.float32, jnp.bfloat16
VMEM = pltpu.VMEM
LANES = 128
NT = (((1,), (1,)), ((), ()))
TN = (((0,), (0,)), ((), ()))
MIB = 1 << 20


class Grid:
    def __init__(self, mesh):
        self.dp, self.cores = mesh.shape["dp"], mesh.shape["tensor"]
        chips = mesh.devices.reshape(self.dp, self.cores)[:, 0]
        spots = [tuple(getattr(chip, "coords", ())) for chip in chips]
        if any(len(spot) != 3 for spot in spots) or len(set(spots)) != self.dp:
            side = 1 << ((self.dp.bit_length() - 1) // 3)
            spots = [(i % side, i // side % side, i // (side * side)) for i in range(self.dp)]
        spots = np.array(spots) - np.min(spots, axis=0)
        sizes = spots.max(axis=0) + 1
        order = sorted(range(3), key=lambda k: -sizes[k])
        order = order[:1] + sorted(order[1:])
        self.spots = spots[:, order].tolist()
        self.long, self.side, _ = (int(sizes[k]) for k in order)
        self.at = {tuple(spot): i for i, spot in enumerate(self.spots)}
        unit = [tuple(int(j == k) for j in range(3)) for k in range(3)]
        self.stride = [self.at.get(u, 0) for u in unit]
        self.sizes = [int(sizes[k]) for k in order]

    def send(self, value, hop):
        pairs = []
        for i, spot in enumerate(self.spots):
            for core in range(self.cores):
                offsets, turn = hop(core)
                target = self.at[tuple(u ^ v for u, v in zip(spot, offsets))]
                pairs.append((i * self.cores + core, target * self.cores + (core ^ turn)))
        return lax.ppermute(value, AXES, pairs)

    def place(self):
        index = lax.axis_index("dp")
        spot = [lax.rem(lax.div(index, s), n) if n > 1 else index * 0 for s, n in zip(self.stride, self.sizes)]
        return jnp.stack(spot + [lax.axis_index("tensor")]).astype(jnp.int32)

    def first(self, k):
        return lambda core: ((0, k, 0) if core == 0 else (0, 0, k), 0)

    def second(self, k):
        return lambda core: ((0, 0, k) if core == 0 else (0, k, 0), 0)

    def along(self, k):
        return lambda core: ((k, 0, 0), 0)

    def cross(self, j, k):
        return lambda core: ((0, j, k), 0)

    def core(self, value):
        return self.send(value, lambda core: ((0, 0, 0), 1))

    def slot(self, s, k, m, a):
        zero = s[3] == 0
        b = s[1] ^ jnp.where(zero, k, m)
        c = s[2] ^ jnp.where(zero, m, k)
        return self.stride[0] * a + self.stride[1] * b + self.stride[2] * c


class Tape:
    def __init__(self, place):
        self.place = place
        self.token = None

    def run(self, body, outs, ins, place=False, limit=4, flops=0, moved=0, exps=0, scratch=(), spill=(), plain=(), name=None):
        ins = [v if i in plain else pltpu.with_memory_space_constraint(v, VMEM) for i, v in enumerate(ins)]
        specs = [pl.BlockSpec(memory_space=VMEM)] * len(ins)
        first = []
        if place:
            first.append((self.place, pltpu.SMEM))
        if self.token is not None:
            first.append((pltpu.with_memory_space_constraint(self.token, VMEM), VMEM))
        chained = self.token is not None
        count, results = len(ins), len(outs)

        def chain(*refs):
            refs = list(refs)
            head = [refs.pop(0)] if place else []
            if chained:
                refs.pop(0)
            last = refs.pop(count + results)
            last[...] = jnp.zeros_like(last)
            body(*head, *refs)

        shapes = [
            jax.ShapeDtypeStruct(s, d) if i in spill else VMEM(s, d) for i, (s, d) in enumerate(outs)
        ] + [VMEM((8, LANES), F32)]
        *values, self.token = pl.pallas_call(
            chain,
            out_shape=shapes,
            in_specs=[pl.BlockSpec(memory_space=m) for _, m in first] + specs,
            out_specs=[pl.BlockSpec(memory_space=VMEM)] * len(shapes),
            scratch_shapes=list(scratch),
            name=name or body.__name__,
            cost_estimate=pl.CostEstimate(flops=flops, bytes_accessed=moved, transcendentals=exps),
            compiler_params=pltpu.CompilerParams(vmem_limit_bytes=limit * MIB),
        )(*[v for v, _ in first], *ins)
        return values


class Gather:
    def __init__(self, grid, tape, shard):
        self.grid, self.tape = grid, tape
        self.many, self.rows, self.width = shard.shape
        self.got = [shard] + [grid.send(shard, grid.along(k)) for k in range(1, grid.long)]

    def line(self):
        grid = self.grid
        long, side = grid.long, grid.side

        def body(s, *refs):
            for k in range(long):
                refs[-1][s[0] ^ k] = refs[k][...]

        block = self.tape.run(body, [((long, self.many, self.rows, self.width), BF16)], self.got, True)[0]
        self.pieces = {(0, 0): block}
        for k in range(1, side):
            self.pieces[k, 0] = grid.send(block, grid.first(k))
        for m in range(1, side):
            for k in range(side):
                self.pieces[k, m] = grid.send(self.pieces[k, 0], grid.second(m))

    def whole(self):
        grid = self.grid
        keys = list(self.pieces)

        def body(s, *refs):
            for (k, m), ref in zip(keys, refs[:-1]):
                for a in range(grid.long):
                    spot = grid.slot(s, k, m, a)
                    for j in range(self.many):
                        refs[-1][j, spot] = ref[a, j]

        full = self.tape.run(
            body, [((self.many, grid.dp, self.rows, self.width), BF16)], [self.pieces[key] for key in keys], True
        )[0]
        return full, grid.core(full)


class Scatter:
    def __init__(self, grid, tape, other):
        self.grid, self.tape = grid, tape
        self.many, _, self.rows, self.width = other.shape
        self.got = grid.core(other)
        self.block = (grid.side, grid.long, self.many, self.rows, self.width)

    def pair(self, own):
        grid, side = self.grid, self.grid.side

        def body(s, own_ref, got_ref, keep, *sends):
            for m in range(side):
                out = keep if m == 0 else sends[m - 1]
                for k in range(side):
                    for a in range(grid.long):
                        spot = grid.slot(s, k, m, a)
                        for j in range(self.many):
                            total = own_ref[j, spot] + got_ref[j, spot].astype(F32)
                            out[k, a, j] = total.astype(out.dtype)

        self.keep, *sends = self.tape.run(
            body, [(self.block, F32)] + [(self.block, BF16)] * (side - 1), [own, self.got], True
        )
        self.came = [grid.send(v, grid.second(m + 1)) for m, v in enumerate(sends)]

    def sides(self):
        grid, side = self.grid, self.grid.side

        def body(*refs):
            outs = refs[side:]
            for k in range(side):
                total = refs[0][k]
                for ref in refs[1:side]:
                    total = total + ref[k].astype(F32)
                outs[k][...] = total.astype(outs[k].dtype)

        shape = self.block[1:]
        self.keep, *sends = self.tape.run(
            body, [(shape, F32)] + [(shape, BF16)] * (side - 1), [self.keep] + self.came
        )
        self.came = [grid.send(v, grid.first(k + 1)) for k, v in enumerate(sends)]

    def line(self):
        grid, side, long = self.grid, self.grid.side, self.grid.long

        def body(s, *refs):
            outs = refs[side:]
            for k in range(long):
                total = refs[0][s[0] ^ k]
                for ref in refs[1:side]:
                    total = total + ref[s[0] ^ k].astype(F32)
                outs[k][...] = total.astype(outs[k].dtype)

        shape = self.block[2:]
        keep, *sends = self.tape.run(
            body, [(shape, F32)] + [(shape, BF16)] * (long - 1), [self.keep] + self.came, True
        )
        self.parts = [keep] + [grid.send(v, grid.along(k + 1)) for k, v in enumerate(sends)]


def tree(values):
    values = list(values)
    while len(values) > 1:
        values = [a + b for a, b in zip(values[::2], values[1::2])]
    return values[0]


class Total:
    def __init__(self, grid, tape, value):
        self.grid, self.tape = grid, tape
        self.got = [value] + [grid.send(value, grid.along(k)) for k in range(1, grid.long)]

    def add(self):
        def body(*refs):
            refs[-1][...] = tree(ref[...] for ref in refs[:-1])

        return self.tape.run(body, [(self.got[0].shape, F32)], self.got)[0]

    def line(self):
        grid, value = self.grid, self.add()
        offsets = [(j, k) for j in range(grid.side) for k in range(grid.side)]
        self.got = [value] + [grid.send(value, grid.cross(j, k)) for j, k in offsets[1:]]

    def sides(self):
        value = self.add()
        self.pair = [value, self.grid.core(value)]


def normed_of(values):
    center = values - jnp.mean(values, axis=-1, keepdims=True)
    inverse = lax.rsqrt(jnp.mean(center * center, axis=-1, keepdims=True) + NORM_EPS)
    return center * inverse, inverse


def norm_back(upstream, normed, inverse, gain):
    scaled = upstream * gain
    inner = jnp.mean(scaled * normed, axis=-1, keepdims=True)
    return inverse * (scaled - jnp.mean(scaled, axis=-1, keepdims=True) - normed * inner)


def sum_rows(values):
    return jnp.sum(values, axis=0, keepdims=True)


def adam(grad, first, second):
    first_new = BETA_ONE * first + (1.0 - BETA_ONE) * grad
    second_new = BETA_TWO * second + (1.0 - BETA_TWO) * grad * grad
    corrected = first_new / (1.0 - BETA_ONE**STEP)
    spread = jnp.sqrt(second_new / (1.0 - BETA_TWO**STEP))
    return first_new, second_new, corrected / (spread + ADAM_EPS)


def squares(values):
    return jnp.sum(sum_rows(values * values), axis=1, keepdims=True)


def norm_tile(entries):
    row = lax.broadcasted_iota(jnp.int32, (8, LANES), 0)
    lane = lax.broadcasted_iota(jnp.int32, (8, LANES), 1)
    tile = jnp.zeros((8, LANES), F32)
    for index, weight, direction in entries:
        tile = jnp.where((row == index) & (lane == 0), squares(weight), tile)
        tile = jnp.where((row == index) & (lane == 1), squares(direction), tile)
    return tile


def make_body(grid):
    def body(
        states, cotangent, word_counts, region_counts,
        attend_in, attend_out, expand_up, expand_down,
        first_in, first_out, first_up, first_down,
        second_in, second_out, second_up, second_down,
        vectors, vector_first, vector_second,
    ):
        cores = grid.cores
        pairs, length, width = states.shape
        mine = pairs // cores
        rows = mine * length
        cols = attend_in.shape[2]
        units = expand_up.shape[1]
        twins = width // LANES
        scale = HEAD_DIM**-0.5
        rank = lax.axis_index("tensor")
        counts = lax.dynamic_slice_in_dim(word_counts + region_counts, rank * mine, mine, 0)
        tape = Tape(jnp.concatenate([grid.place(), counts]))
        attend_out, first_out, second_out = (v.T[None] for v in (attend_out, first_out, second_out))

        def cast(*refs):
            spot = 0
            for ref in refs[:-1]:
                refs[-1][spot : spot + ref.shape[0]] = ref[...].astype(BF16)
                spot += ref.shape[0]

        def casted(*mats):
            many = sum(m.shape[0] for m in mats)
            shape = (many,) + mats[0].shape[1:]
            return tape.run(cast, [(shape, BF16)], mats, plain=range(len(mats)))[0]

        gather_a = Gather(grid, tape, casted(attend_in, attend_out))
        gather_b = Gather(grid, tape, casted(expand_up[None]))

        def prepare(s, states_ref, cot_ref, vec, x_ref, x_t, mine_cot, bias_in, bias_up):
            @pl.loop(0, mine)
            def _(p):
                at = pl.ds(pl.multiple_of(p * length, length), length)
                x_ref[at, :] = states_ref[s[3] * mine + p]
                mine_cot[at, :] = cot_ref[s[3] * mine + p]

            x_t[...] = x_ref[...].T
            bias_in[1:2] = jnp.zeros((1, width), F32)
            for t in range(cores):

                @pl.when(s[3] == t)
                def _():
                    for h in range(2):
                        at, source = slice(h * cols, (h + 1) * cols), slice((h ^ t) * cols, ((h ^ t) + 1) * cols)
                        bias_in[0:1, at] = vec[0:1, source]
                        bias_in[2:3, at] = vec[1:2, source]
                        for i in range(units // width):
                            row = 8 + (h ^ t) * (units // width) + i
                            spot = h * units + i * width
                            bias_up[:, spot : spot + width] = vec[row : row + 1]

        x, x_t, cot, bias_in, bias_up = tape.run(
            prepare,
            [((rows, width), BF16), ((width, rows), BF16), ((rows, width), BF16), ((3, width), F32),
             ((1, 2 * units), F32)],
            [states, cotangent, vectors], True, limit=12, moved=6 * MIB, plain=(0, 1),
        )
        gather_a.line()
        gather_c = Gather(grid, tape, casted(expand_down[None]))
        gather_b.line()
        a_own, a_oth = (v.reshape(4, width, cols) for v in gather_a.whole())
        gather_c.line()

        def project(x_ref, own, oth, bias, out):
            @pl.loop(0, 3)
            def _(j):
                for h, ref in enumerate((own, oth)):
                    at = slice(h * cols, (h + 1) * cols)
                    value = jnp.dot(x_ref[...], ref[j], preferred_element_type=F32)
                    out[j, :, at] = (value + bias[pl.ds(j, 1), at]).astype(BF16)

        qkv = tape.run(
            project, [((3, rows, width), BF16)], [x, a_own, a_oth, bias_in],
            limit=8, flops=6 * rows * width * width, moved=8 * MIB,
        )[0]

        def split(v):
            low = lax.broadcasted_iota(jnp.int32, v.shape, 1) < HEAD_DIM
            zero = jnp.zeros_like(v)
            return jnp.concatenate([jnp.where(low, v, zero), jnp.where(low, zero, v)], axis=0)

        def join(v):
            low = lax.broadcasted_iota(jnp.int32, (length, LANES), 1) < HEAD_DIM
            return jnp.where(low, v[:length], v[length:])

        def attend(count, qkv_ref, probs, context):
            @pl.loop(0, mine)
            def _(p):
                at = pl.ds(pl.multiple_of(p * length, length), length)
                known = lax.broadcasted_iota(jnp.int32, (length, length), 1) < count[4 + p]
                for u in range(twins):
                    lanes = slice(u * LANES, (u + 1) * LANES)
                    both = lax.dot_general(
                        qkv_ref[0, at, lanes], split(qkv_ref[1, at, lanes]), NT, preferred_element_type=F32
                    )
                    soft = []
                    for h in range(2):
                        score = jnp.where(known, both[:, h * length : (h + 1) * length] * scale, MASKED)
                        power = jnp.exp(score - jnp.max(score, axis=-1, keepdims=True))
                        soft.append(power / jnp.sum(power, axis=-1, keepdims=True))
                    prob = jnp.concatenate(soft, axis=1).astype(BF16)
                    probs[at, 2 * u * length : 2 * (u + 1) * length] = prob
                    context[at, lanes] = jnp.dot(
                        prob, split(qkv_ref[2, at, lanes]), preferred_element_type=F32
                    ).astype(BF16)

        probs, context = tape.run(
            attend, [((rows, 2 * twins * length), BF16), ((rows, width), BF16)], [qkv], True,
            limit=4, flops=4 * rows * length * width * 4, moved=5 * MIB, exps=rows * twins * 2 * length,
        )

        block = min(rows, 256)

        def hide(context_ref, x_ref, own, oth, vec, hidden, normed, inverse):
            for r in range(0, rows, block):
                at = slice(r, r + block)
                value = x_ref[at].astype(F32) + vec[2:3]
                for h, ref in enumerate((own, oth)):
                    value += lax.dot_general(
                        context_ref[at, h * cols : (h + 1) * cols], ref[3], NT, preferred_element_type=F32
                    )
                normal, spread = normed_of(value)
                normed[at], inverse[at] = normal, spread
                hidden[at] = (normal * vec[3:4] + vec[4:5]).astype(BF16)

        hidden, normed_one, inverse_one = tape.run(
            hide,
            [((rows, width), BF16), ((rows, width), F32), ((rows, 1), F32)],
            [context, x, a_own, a_oth, vectors],
            limit=8, flops=2 * rows * width * width, moved=6 * MIB,
        )

        b_own, b_oth = (v.reshape(width, units) for v in gather_b.whole())
        tile = 256

        def lift(hidden_ref, up, bias, active, active_t, slope):
            @pl.loop(0, units // tile)
            def _(i):
                at = pl.ds(pl.multiple_of(i * tile, tile), tile)
                value = jnp.dot(hidden_ref[...], up[:, at], preferred_element_type=F32) + bias[:, at]
                half = 0.5 * (1.0 + lax.erf(value * math.sqrt(0.5)))
                result = (value * half).astype(BF16)
                active[:, at] = result
                active_t[at, :] = result.T
                bell = jnp.exp(-0.5 * value * value) * (1.0 / math.sqrt(2.0 * math.pi))
                slope[:, at] = (half + value * bell).astype(BF16)

        def lift_half(h, up):
            return tape.run(
                lambda hidden_ref, up_ref, bias, *outs: lift(hidden_ref, up_ref, bias.at[:, h * units : (h + 1) * units], *outs),
                [((rows, units), BF16), ((units, rows), BF16), ((rows, units), BF16)],
                [hidden, up, bias_up],
                limit=8, flops=2 * rows * width * units, moved=8 * MIB, exps=2 * rows * units,
            )

        def turn(value, out):
            out[...] = value[...].T

        lifted = [lift_half(0, b_own), lift_half(1, b_oth)]
        hidden_t = tape.run(turn, [((width, rows), BF16)], [hidden], limit=8, moved=2 * MIB)[0]
        c_own, c_oth = (v.reshape(units, width) for v in gather_c.whole())

        def lower_half(active, down, out):
            @pl.loop(0, width // tile)
            def _(i):
                at = pl.ds(pl.multiple_of(i * tile, tile), tile)
                out[:, at] = jnp.dot(active[...], down[:, at], preferred_element_type=F32)

        lowered = tape.run(
            lower_half, [((rows, width), F32)], [lifted[0][0], c_own],
            limit=6, flops=2 * rows * width * units, moved=6 * MIB,
        )[0]

        def lower(count, lowered_ref, active, down, normed, cot_ref, vec, output, top, top16, sums, work):
            @pl.loop(0, width // tile)
            def _(i):
                at = pl.ds(pl.multiple_of(i * tile, tile), tile)
                work[:, at] = lowered_ref[:, at] + jnp.dot(active[...], down[:, at], preferred_element_type=F32)

            sums[...] = jnp.zeros_like(sums)

            @pl.loop(0, mine)
            def _(p):
                at = pl.ds(pl.multiple_of(p * length, length), length)
                value = normed[at] * vec[3:4] + vec[4:5] + work[at] + vec[5:6]
                normal, spread = normed_of(value)
                output[at] = (normal * vec[6:7] + vec[7:8]).astype(BF16)
                live = lax.broadcasted_iota(jnp.int32, (length, 1), 0) < count[4 + p]
                upstream = jnp.where(live, cot_ref[at].astype(F32), 0.0)
                grad = norm_back(upstream, normal, spread, vec[6:7])
                top[at] = grad
                top16[at] = grad.astype(BF16)
                sums[0:1] += sum_rows(grad)
                sums[1:2] += sum_rows(upstream * normal)
                sums[2:3] += sum_rows(upstream)

        output, top, top16, sums_two = tape.run(
            lower,
            [((rows, width), BF16), ((rows, width), F32), ((rows, width), BF16), ((8, width), F32)],
            [lowered, lifted[1][0], c_oth, normed_one, cot, vectors],
            True, limit=8, flops=2 * rows * width * units, moved=14 * MIB,
            scratch=[VMEM((rows, width), F32)],
        )

        def product(left, right, out):
            step = min(left.shape[0], 256)

            @pl.loop(0, left.shape[0] // step)
            def _(i):
                at = pl.ds(pl.multiple_of(i * step, step), step)
                out[at, :] = jnp.dot(left[at, :], right[...], preferred_element_type=F32).astype(out.dtype)

        def weight_grad(left, right, kind):
            shape = (left.shape[0], right.shape[1])
            return tape.run(
                product, [(shape, kind)], [left, right],
                limit=6, flops=2 * shape[0] * shape[1] * rows, moved=8 * MIB,
            )[0]

        sharded = lambda v, many: v.reshape(many, grid.dp, -1, v.shape[-1])
        scatter_c = Scatter(grid, tape, sharded(weight_grad(lifted[1][1], top16, BF16), 1))
        down_own = weight_grad(lifted[0][1], top16, F32)
        output_oth = grid.core(output)

        def sink(top16_ref, down, slope, grad, sums):
            @pl.loop(0, units // tile)
            def _(i):
                at = pl.ds(pl.multiple_of(i * tile, tile), tile)
                value = lax.dot_general(top16_ref[...], down[at, :], NT, preferred_element_type=F32)
                value = value * slope[:, at].astype(F32)
                grad[:, at] = value.astype(BF16)
                sums[:, at] = sum_rows(value)

        def sink_half(h, down):
            return tape.run(
                sink, [((rows, units), BF16), ((1, units), F32)], [top16, down, lifted[h][2]],
                limit=8, flops=2 * rows * width * units, moved=8 * MIB,
            )

        sunk = [None, sink_half(1, c_oth)]
        scatter_c.pair(sharded(down_own, 1))
        sunk[0] = sink_half(0, c_own)
        scatter_b = Scatter(grid, tape, sharded(weight_grad(hidden_t, sunk[1][0], BF16), 1))
        up_own = weight_grad(hidden_t, sunk[0][0], F32)

        def surface(grad_own, grad_oth, own, oth, top_ref, normed, inverse, vec, a_own_ref, a_oth_ref,
                    mid, mid_t, back, sums, work, mid16):
            @pl.loop(0, width // tile)
            def _(i):
                at = pl.ds(pl.multiple_of(i * tile, tile), tile)
                work[:, at] = (
                    top_ref[:, at]
                    + lax.dot_general(grad_own[...], own[at, :], NT, preferred_element_type=F32)
                    + lax.dot_general(grad_oth[...], oth[at, :], NT, preferred_element_type=F32)
                )

            sums[...] = jnp.zeros_like(sums)

            @pl.loop(0, mine)
            def _(p):
                at = pl.ds(pl.multiple_of(p * length, length), length)
                upstream, normal = work[at], normed[at]
                grad = norm_back(upstream, normal, inverse[at], vec[3:4])
                mid[at] = grad
                mid16[at] = grad.astype(BF16)
                sums[0:1] += sum_rows(grad)
                sums[1:2] += sum_rows(upstream * normal)
                sums[2:3] += sum_rows(upstream)

            mid_t[...] = mid16[...].T
            for h, ref in enumerate((a_own_ref, a_oth_ref)):
                back[:, h * cols : (h + 1) * cols] = jnp.dot(
                    mid16[...], ref[3], preferred_element_type=F32
                ).astype(BF16)

        mid, mid_t, back, sums_one = tape.run(
            surface,
            [((rows, width), F32), ((width, rows), BF16), ((rows, width), BF16), ((8, width), F32)],
            [sunk[0][0], sunk[1][0], b_own, b_oth, top, normed_one, inverse_one, vectors, a_own, a_oth],
            limit=14, flops=4 * rows * width * units + 2 * rows * width * width, moved=14 * MIB,
            scratch=[VMEM((rows, width), F32), VMEM((rows, width), BF16)],
        )

        scatter_b.pair(sharded(up_own, 1))
        scatter_c.sides()

        def values_back(probs_ref, back_ref, grad, sums):
            sums[...] = jnp.zeros_like(sums)

            @pl.loop(0, mine)
            def _(p):
                at = pl.ds(pl.multiple_of(p * length, length), length)
                for u in range(twins):
                    lanes = slice(u * LANES, (u + 1) * LANES)
                    value = join(lax.dot_general(
                        probs_ref[at, 2 * u * length : 2 * (u + 1) * length], back_ref[at, lanes], TN,
                        preferred_element_type=F32,
                    ))
                    grad[at, lanes] = value.astype(BF16)
                    sums[:, lanes] += sum_rows(value)

        grad_v, sum_v = tape.run(
            values_back, [((rows, width), BF16), ((1, width), F32)], [probs, back],
            limit=4, flops=4 * rows * length * width, moved=3 * MIB,
        )

        def halves(left_v, right_v, h, kind, left_w, right_w):
            def both(left_v_ref, right_v_ref, left_w_ref, right_w_ref, out):
                at = slice(h * cols, (h + 1) * cols)
                for j, (left, right) in enumerate(((left_v_ref, right_v_ref), (left_w_ref, right_w_ref))):
                    out[j] = jnp.dot(left[...], right[:, at], preferred_element_type=F32).astype(out.dtype)

            return tape.run(
                both, [((2, width, cols), kind)], [left_v, right_v, left_w, right_w],
                limit=6, flops=4 * rows * width * cols, moved=5 * MIB,
            )[0]

        scatter_vo = Scatter(grid, tape, sharded(halves(x_t, grad_v, 1, BF16, mid_t, context), 2))
        vo_own = halves(x_t, grad_v, 0, F32, mid_t, context)

        def attend_back(probs_ref, back_ref, qkv_ref, grad_q, grad_k, sums):
            sums[...] = jnp.zeros_like(sums)

            @pl.loop(0, mine)
            def _(p):
                at = pl.ds(pl.multiple_of(p * length, length), length)
                for u in range(twins):
                    lanes = slice(u * LANES, (u + 1) * LANES)
                    prob = probs_ref[at, 2 * u * length : 2 * (u + 1) * length].astype(F32)
                    both = lax.dot_general(
                        back_ref[at, lanes], split(qkv_ref[2, at, lanes]), NT, preferred_element_type=F32
                    )
                    parts = []
                    for h in range(2):
                        half = slice(h * length, (h + 1) * length)
                        inner = jnp.sum(prob[:, half] * both[:, half], axis=-1, keepdims=True)
                        parts.append(prob[:, half] * (both[:, half] - inner))
                    grad = jnp.concatenate(parts, axis=1).astype(BF16)
                    value = jnp.dot(grad, split(qkv_ref[1, at, lanes]), preferred_element_type=F32) * scale
                    grad_q[at, lanes] = value.astype(BF16)
                    sums[:, lanes] += sum_rows(value)
                    value = join(lax.dot_general(grad, qkv_ref[0, at, lanes], TN, preferred_element_type=F32))
                    grad_k[at, lanes] = (value * scale).astype(BF16)

        grad_q, grad_k, sum_q = tape.run(
            attend_back, [((rows, width), BF16), ((rows, width), BF16), ((1, width), F32)], [probs, back, qkv],
            limit=4, flops=16 * rows * length * width, moved=6 * MIB,
        )
        scatter_vo.pair(sharded(vo_own, 2))
        scatter_b.sides()
        scatter_c.line()
        scatter_qk = Scatter(grid, tape, sharded(halves(x_t, grad_q, 1, BF16, x_t, grad_k), 2))
        qk_own = halves(x_t, grad_q, 0, F32, x_t, grad_k)

        def states_back(grad_q_ref, grad_k_ref, grad_v_ref, own, oth, mid_ref, out):
            @pl.loop(0, width // tile)
            def _(i):
                at = pl.ds(pl.multiple_of(i * tile, tile), tile)
                value = mid_ref[:, at]
                for j, ref in enumerate((grad_q_ref, grad_k_ref, grad_v_ref)):
                    for h, weight in enumerate((own, oth)):
                        value += lax.dot_general(
                            ref[:, h * cols : (h + 1) * cols], weight[j, at, :], NT, preferred_element_type=F32
                        )
                out[:, at] = value

        states_own = tape.run(
            states_back, [((rows, width), F32)], [grad_q, grad_k, grad_v, a_own, a_oth, mid],
            limit=8, flops=6 * rows * width * width, moved=8 * MIB,
        )[0]

        states_oth = grid.core(states_own)
        scatter_qk.pair(sharded(qk_own, 2))

        def collect(s, sum_q_ref, sum_v_ref, one, two, up_own_ref, up_oth_ref, out):
            for t in range(cores):

                @pl.when(s[3] == t)
                def _():
                    for row, ref in enumerate((sum_q_ref, sum_v_ref)):
                        for h in range(2):
                            out[row : row + 1, (h ^ t) * cols : ((h ^ t) + 1) * cols] = ref[
                                :, h * cols : (h + 1) * cols
                            ]
                    for h, ref in enumerate((up_own_ref, up_oth_ref)):
                        for i in range(units // width):
                            row = 8 + (h ^ t) * (units // width) + i
                            out[row : row + 1] = ref[:, i * width : (i + 1) * width]

            out[2:5] = one[0:3]
            out[5:8] = two[0:3]

        vector_part = tape.run(
            collect, [(vectors.shape, F32)], [sum_q, sum_v, sums_one, sums_two, sunk[0][1], sunk[1][1]], True
        )[0]
        vector_total = Total(grid, tape, vector_part)
        scatter_vo.sides()
        scatter_b.line()

        def pair_up(s, own, oth, out):
            out[s[3]] = own[...]
            out[1 - s[3]] = oth[...]

        def paired(own, oth):
            shape = ((cores,) + own.shape, own.dtype)
            result = tape.run(pair_up, [shape], [own, oth], True, limit=8, spill=(0,))[0]
            return result.reshape(pairs, length, width)

        layer_output = paired(output, output_oth)
        states_grad = paired(states_own, states_oth)
        vector_total.line()
        scatter_qk.sides()
        scatter_vo.line()
        vector_total.sides()

        def vector_step(own, oth, vec, first, second, out, moment, square):
            one, two, direction = adam(own[...] + oth[...], first[...], second[...])
            moment[...], square[...] = one, two
            out[...] = vec[...] - RATE * direction

        def matrix_step(index):
            def step(*refs):
                grad = sum((ref[...].astype(F32) for ref in refs[1 : grid.long]), refs[0][...])
                master, first, second, moment, square, way, kept, tile_ref = refs[grid.long :]
                moment[...], square[...], value = adam(grad, first[...], second[...])
                kept[...] = master[...]
                way[...] = value + DECAY * kept[...]
                tile_ref[...] = norm_tile([(index, kept[0], way[0])])

            return step

        def stepped(step, parts, masters, shapes):
            outs = [(s, F32) for _ in range(4) for s in shapes] + [((8, LANES), F32)]
            n, m = len(parts), len(masters)
            return tape.run(
                step, outs, parts + masters, limit=6, spill=range(2 * len(shapes)), plain=range(n, n + m), moved=2 * MIB
            )

        ups = [v[None] for v in (expand_up, first_up, second_up)]
        downs = [v[None] for v in (expand_down, first_down, second_down)]
        moment_down, square_down, way_down, kept_down, tile_down = stepped(
            matrix_step(5), scatter_c.parts, downs, [downs[0].shape]
        )
        scatter_qk.line()
        moment_up, square_up, way_up, kept_up, tile_up = stepped(
            matrix_step(4), scatter_b.parts, ups, [ups[0].shape]
        )
        updated_vectors, moment_vectors, square_vectors = tape.run(
            vector_step, [(vectors.shape, F32)] * 3,
            vector_total.pair + [vectors, vector_first, vector_second], spill=(0, 1, 2), plain=(2, 3, 4),
        )

        def attend_step(*refs):
            n = grid.long
            vo, qk = refs[:n], refs[n : 2 * n]
            m_in, f_in, s_in, m_out, f_out, s_out, tile_up_ref, tile_down_ref = refs[2 * n : 2 * n + 8]
            mo_in, mo_out, sq_in, sq_out, way_in, way_out, kept_in, kept_out, tile_ref = refs[2 * n + 8 :]
            whole = lambda parts, j: sum((ref[j].astype(F32) for ref in parts[1:]), parts[0][j])
            entries = []
            for j, grad in enumerate((whole(qk, 0), whole(qk, 1), whole(vo, 0), whole(vo, 1))):
                i = j if j < 3 else 0
                m, f, s, mo, sq, kept, way = (
                    (m_in, f_in, s_in, mo_in, sq_in, kept_in, way_in)
                    if j < 3
                    else (m_out, f_out, s_out, mo_out, sq_out, kept_out, way_out)
                )
                mo[i], sq[i], value = adam(grad, f[i], s[i])
                kept[i] = m[i]
                way[i] = value + DECAY * kept[i]
                entries.append((j, kept[i], way[i]))
            tile_ref[...] = norm_tile(entries) + tile_up_ref[...] + tile_down_ref[...]

        ins = scatter_vo.parts + scatter_qk.parts + [attend_in, first_in, second_in, attend_out, first_out, second_out]
        shapes = [attend_in.shape, attend_out.shape]
        (
            moment_in, moment_out, square_in, square_out, way_in, way_out, kept_in, kept_out, tiles
        ) = tape.run(
            attend_step, [(s, F32) for _ in range(4) for s in shapes] + [((8, LANES), F32)], ins + [tile_up, tile_down],
            limit=6, spill=range(4), plain=range(2 * grid.long, 2 * grid.long + 6), moved=2 * MIB,
        )
        tile_total = Total(grid, tape, tiles)
        tile_total.line()
        tile_total.sides()

        def update(own, oth, *refs):
            masters, ways, outs = refs[:4], refs[4:8], refs[8:]
            norms = jnp.sqrt(own[...] + oth[...])
            outs[8][...] = norms.T[0:2, 0:6]
            trust = RATE * (norms[:, 0:1] / norms[:, 1:2])
            for i, first in enumerate((0, 3, 4, 5)):
                for j in range(masters[i].shape[0]):
                    value = masters[i][j] - trust[first + j : first + j + 1] * ways[i][j]
                    outs[i][j], outs[4 + i][j] = value, value.astype(BF16)

        masters = [kept_in, kept_out, kept_up, kept_down]
        results = tape.run(
            update,
            [(m.shape, F32) for m in masters] + [(m.shape, BF16) for m in masters] + [((2, 6), F32)],
            tile_total.pair + masters + [way_in, way_out, way_up, way_down],
            limit=6, spill=range(9), moved=2 * MIB,
        )

        def native(values):
            values = list(values)
            return (values[0], values[1][0].T, values[2][0], values[3][0])

        return (
            layer_output, states_grad, *native(results[:4]),
            *native([moment_in, moment_out, moment_up, moment_down]),
            *native([square_in, square_out, square_up, square_down]),
            *native(results[4:8]), updated_vectors, moment_vectors, square_vectors, results[8].T,
        )

    return body


def solution(mesh):
    rows = P("dp", None, None)
    matrices = (P(None, "dp", "tensor"), P("tensor", "dp"), P("dp", "tensor"), P(("tensor", "dp"), None))
    in_specs = (rows, rows, P("dp"), P("dp")) + matrices * 3 + (P(), P(), P())
    out_specs = (rows, rows) + matrices * 4 + (P(), P(), P(), P())
    body = make_body(Grid(mesh))
    return jax.shard_map(body, mesh=mesh, in_specs=in_specs, out_specs=out_specs, check_vma=False)
```

time: 340 us -> 273 us (0.80)
  local copies, waits for them, and re-layouts: 38.3 us -> 6.63 us
  Pallas kernels: 102 us -> 76.2 us
  starting transfers between devices: 83.5 us -> 70.8 us
  waiting for transfers between devices: 110 us -> 117 us
    unnamed x136 -> x42, local copies, waits for them, and re-layouts: 37.1 us -> 6.46 us
    pallas_call x51 -> x56, Pallas kernels: 102 us -> 76.2 us  [run(): pl.pallas_call(chain, out_shape=shapes, in_specs=[pl.BlockSpec(memory_spa...]
    ppermute x61, starting transfers between devices: 83.5 us -> 70.8 us  [send(): return lax.ppermute(value, AXES, pairs)]
    ppermute x61, waiting for transfers between devices: 110 us -> 117 us  [send(): return lax.ppermute(value, AXES, pairs)]
  transfers between devices with their start and end apart: 61 -> 61, of which waited for: 22 -> 24; matrix products, arithmetic and copies ran while one was open for 3% -> 0% of each run, Pallas kernels for 27% -> 20%
where the time goes in v2:
time: 273 us
  waiting for transfers between devices  117 us (43%)
  Pallas kernels  76.2 us (28%)
  starting transfers between devices  70.8 us (26%)
  local copies, waits for them, and re-layouts  6.63 us (2%)
    ppermute x61, waiting for transfers between devices, send(): return lax.ppermute(value, AXES, pairs)  117 us
    pallas_call x56, Pallas kernels, run(): pl.pallas_call(chain, out_shape=shapes, in_specs=[pl.BlockSpec(memory_spa...  76.2 us
    ppermute x61, starting transfers between devices, send(): return lax.ppermute(value, AXES, pairs)  70.8 us
    unnamed x42, local copies, waits for them, and re-layouts  6.46 us
  transfers between devices with their start and end apart: 61, of which 24 were waited for; matrix products, arithmetic and copies ran while one was open for 0% of the time, Pallas kernels for 20%

profile of v2, /device:TPU:0, one launch (start us, length us, event | category | flops | bytes accessed | tf_op | source)
XLA Modules:
  0.0 272.7 jit_solution(5598526249602300473)
XLA Ops:
  2.5 3.1 %collective-permute-start = (bf16[4,48,384]{2,1,0:T(8,128)(2,1)S(1)}, bf16[4,48,384]{2,1,0:T(8,128)(2,1)S(1)}, u32[]{:S(2)}, u32[]{:S(2)}) collective-permute-start(bf16[4,48,384]{2,1,0:T(8,128)(2,1)S(1)} %get-tuple-element.204.refs_2_), channel_id=1, source_target_pairs={{0,8},{1,9},{2,10},{3,11},{4,12},{5,13},{6,14},{7,15},{8,0},{9,1},... | collective-permute-start | bytes 442376 | tf_op jit(solution)/shard_map/ppermute | solution.py:55
  5.6 2.6 collective-permute-start.1
  10.0 1.4 copy-done
  11.4 1.4 copy-done.1
  14.6 5.0 %collective-permute-done.1.refs_4_ = bf16[4,48,384]{2,1,0:T(8,128)(2,1)S(1)} collective-permute-done((bf16[4,48,384]{2,1,0:T(8,128)(2,1)S(1)}, bf16[4,48,384]{2,1,0:T(8,128)(2,1)S(1)}, u32[]{:S(2)}, u32[]{:S(2)}) %collective-permute-start.1) | collective-permute-done | bytes 147488 | tf_op jit(solution)/shard_map/ppermute | solution.py:55
  20.2 1.6 collective-permute-start.6
  21.8 1.5 collective-permute-start.7
  23.3 13.3 %collective-permute-done.6.refs_3_ = bf16[4,4,48,384]{3,2,1,0:T(8,128)(2,1)S(1)} collective-permute-done((bf16[4,4,48,384]{3,2,1,0:T(8,128)(2,1)S(1)}, bf16[4,4,48,384]{3,2,1,0:T(8,128)(2,1)S(1)}, u32[]{:S(2)}, u32[]{:S(2)}) %collective-permute-start.6) | collective-permute-done | bytes 589856 | tf_op jit(solution)/shard_map/ppermute | solution.py:55
  36.5 2.3 collective-permute-start.3
  39.8 1.5 collective-permute-start.5
  41.3 2.3 collective-permute-done.3.refs_3_
  43.6 5.6 %collective-permute-done.4.refs_4_ = bf16[1,48,1536]{2,1,0:T(8,128)(2,1)S(1)} collective-permute-done((bf16[1,48,1536]{2,1,0:T(8,128)(2,1)S(1)}, bf16[1,48,1536]{2,1,0:T(8,128)(2,1)S(1)}, u32[]{:S(2)}, u32[]{:S(2)}) %collective-permute-start.4) | collective-permute-done | bytes 147488 | tf_op jit(solution)/shard_map/ppermute | solution.py:55
  51.1 3.4 %collective-permute-start.10 = (bf16[1,96,768]{2,1,0:T(8,128)(2,1)S(1)}, bf16[1,96,768]{2,1,0:T(8,128)(2,1)S(1)}, u32[]{:S(2)}, u32[]{:S(2)}) collective-permute-start(bf16[1,96,768]{2,1,0:T(8,128)(2,1)S(1)} %get-tuple-element.211.refs_2_), channel_id=1, source_target_pairs={{0,16},{1,17},{2,18},{3,19},{4,20},{5,21},{6,22},{7,23},{8,24},{9,... | collective-permute-start | bytes 442376 | tf_op jit(solution)/shard_map/ppermute | solution.py:55
  54.5 1.7 collective-permute-start.14
  56.1 7.0 %collective-permute-done.13.refs_3_ = bf16[4,1,48,1536]{3,2,1,0:T(8,128)(2,1)S(1)} collective-permute-done((bf16[4,1,48,1536]{3,2,1,0:T(8,128)(2,1)S(1)}, bf16[4,1,48,1536]{3,2,1,0:T(8,128)(2,1)S(1)}, u32[]{:S(2)}, u32[]{:S(2)}) %collective-permute-start.13) | collective-permute-done | bytes 589856 | tf_op jit(solution)/shard_map/ppermute | solution.py:55
  63.1 2.5 collective-permute-start.15
  65.7 4.3 %collective-permute-start.11 = (bf16[1,96,768]{2,1,0:T(8,128)(2,1)S(1)}, bf16[1,96,768]{2,1,0:T(8,128)(2,1)S(1)}, u32[]{:S(2)}, u32[]{:S(2)}) collective-permute-start(bf16[1,96,768]{2,1,0:T(8,128)(2,1)S(1)} %get-tuple-element.211.refs_2_), channel_id=1, source_target_pairs={{0,24},{1,25},{2,26},{3,27},{4,28},{5,29},{6,30},{7,31},{8,16},{9,... | collective-permute-start | bytes 442376 | tf_op jit(solution)/shard_map/ppermute | solution.py:55
  70.0 2.2 collective-permute-start.9
  72.2 2.4 collective-permute-done.11.refs_5_
  76.4 3.0 %project.1 = (bf16[3,512,768]{2,1,0:T(8,128)(2,1)S(1)}, f32[8,128]{1,0:T(8,128)S(1)}) custom-call(f32[8,128]{1,0:T(8,128)S(1)} %get-tuple-element.212.refs_0_, bf16[512,768]{1,0:T(8,128)(2,1)S(1)} %get-tuple-element.213.refs_1_.refs_2_, bf16[4,768,384]{2,1,0:T(8,128)(2,1)S(1)} %bitcast.56, bf16[4,768,384]{2,1,0:T(8,128)(2,1)S(1)} %bitcast.60, ...), custom_call_target="tpu_custom_call" | custom-call | flops 1811939328 | bytes 8388608 | tf_op jit(solution)/shard_map/project/pallas_call | solution.py:112
  79.4 4.6 %attend.1 = (bf16[512,1536]{1,0:T(8,128)(2,1)S(1)}, bf16[512,768]{1,0:T(8,128)(2,1)S(1)}, f32[8,128]{1,0:T(8,128)S(1)}) custom-call(s32[8]{0:T(128)S(1)} %concatenate.3.refs_0_, f32[8,128]{1,0:T(8,128)S(1)} %get-tuple-element.216.refs_1_, bf16[3,512,768]{2,1,0:T(8,128)(2,1)S(1)} %get-tuple-element.217.refs_2_.refs_3_), custom_call_target="tpu_custom_call" | custom-call | flops 805306368 | bytes 5242880 | tf_op jit(solution)/shard_map/attend/pallas_call | solution.py:112
  84.0 1.3 hide.1
  87.3 14.9 %collective-permute-done.17.refs_3_ = bf16[4,1,96,768]{3,2,1,0:T(8,128)(2,1)S(1)} collective-permute-done((bf16[4,1,96,768]{3,2,1,0:T(8,128)(2,1)S(1)}, bf16[4,1,96,768]{3,2,1,0:T(8,128)(2,1)S(1)}, u32[]{:S(2)}, u32[]{:S(2)}) %collective-permute-start.17) | collective-permute-done | bytes 589856 | tf_op jit(solution)/shard_map/ppermute | solution.py:55
  102.5 3.4 %_lambda_.2 = (bf16[512,1536]{1,0:T(8,128)(2,1)S(1)}, bf16[1536,512]{1,0:T(8,128)(2,1)S(1)}, bf16[512,1536]{1,0:T(8,128)(2,1)S(1)}, f32[8,128]{1,0:T(8,128)S(1)}) custom-call(f32[8,128]{1,0:T(8,128)S(1)} %get-tuple-element.222.refs_0_, bf16[512,768]{1,0:T(8,128)(2,1)S(1)} %get-tuple-element.223.refs_1_, bf16[768,1536]{1,0:T(8,128)(2,1)S(1)} %bitcast.72, ...), custom_call_target="tpu_custom_call" | custom-call | flops 1207959552 | bytes 8388608 | tf_op jit(solution)/shard_map/<lambda>/pallas_call | solution.py:112
  105.8 3.4 %_lambda_.3 = (bf16[512,1536]{1,0:T(8,128)(2,1)S(1)}, bf16[1536,512]{1,0:T(8,128)(2,1)S(1)}, bf16[512,1536]{1,0:T(8,128)(2,1)S(1)}, f32[8,128]{1,0:T(8,128)S(1)}) custom-call(f32[8,128]{1,0:T(8,128)S(1)} %get-tuple-element.226.refs_0_, bf16[512,768]{1,0:T(8,128)(2,1)S(1)} %get-tuple-element.223.refs_1_, bf16[768,1536]{1,0:T(8,128)(2,1)S(1)} %bitcast.74, ...), custom_call_target="tpu_custom_call" | custom-call | flops 1207959552 | bytes 8388608 | tf_op jit(solution)/shard_map/<lambda>/pallas_call | solution.py:112
  109.5 2.6 collective-permute-done.19.refs_5_
  112.9 1.7 lower_half.1
  114.6 2.8 %collective-permute-done.20 = bf16[1,16,96,768]{3,2,1,0:T(8,128)(2,1)S(1)} collective-permute-done((bf16[1,16,96,768]{3,2,1,0:T(8,128)(2,1)S(1)}, bf16[1,16,96,768]{3,2,1,0:T(8,128)(2,1)S(1)}, u32[]{:S(2)}, u32[]{:S(2)}) %collective-permute-start.20) | collective-permute-done | bytes 2359328 | tf_op jit(solution)/shard_map/ppermute | solution.py:55
  117.4 4.0 %lower.1 = (bf16[512,768]{1,0:T(8,128)(2,1)S(1)}, f32[512,768]{1,0:T(8,128)S(1)}, bf16[512,768]{1,0:T(8,128)(2,1)S(1)}, f32[8,768]{1,0:T(8,128)S(1)}, f32[8,128]{1,0:T(8,128)S(1)}) custom-call(s32[8]{0:T(128)S(1)} %concatenate.3.refs_0_, f32[8,128]{1,0:T(8,128)S(1)} %get-tuple-element.233.refs_1_, f32[512,768]{1,0:T(8,128)S(1)} %get-tuple-element.234.refs_2_, ...), custom_call_target="tpu_custom_call" | custom-call | flops 1207959552 | bytes 14680064 | tf_op jit(solution)/shard_map/lower/pallas_call | solution.py:112
  121.4 2.2 product.4
  123.8 2.2 product.5
  126.1 2.5 sink.2
  129.7 2.5 sink.3
  132.2 1.7 product.6
  134.6 1.7 product.7
  136.4 5.1 %surface.1 = (f32[512,768]{1,0:T(8,128)S(1)}, bf16[768,512]{1,0:T(8,128)(2,1)S(1)}, bf16[512,768]{1,0:T(8,128)(2,1)S(1)}, f32[8,768]{1,0:T(8,128)S(1)}, f32[8,128]{1,0:T(8,128)S(1)}) custom-call(f32[8,128]{1,0:T(8,128)S(1)} %get-tuple-element.255.refs_0_, bf16[512,1536]{1,0:T(8,128)(2,1)S(1)} %get-tuple-element.254.refs_2_.refs_1_, ...), custom_call_target="tpu_custom_call" | custom-call | flops 3019898880 | bytes 14680064 | tf_op jit(solution)/shard_map/surface/pallas_call | solution.py:112
  142.5 8.0 %collective-permute-done.23.refs_2_ = bf16[2,4,1,96,768]{4,3,2,1,0:T(8,128)(2,1)S(1)} collective-permute-done((bf16[2,4,1,96,768]{4,3,2,1,0:T(8,128)(2,1)S(1)}, bf16[2,4,1,96,768]{4,3,2,1,0:T(8,128)(2,1)S(1)}, u32[]{:S(2)}, u32[]{:S(2)}) %collective-permute-start.23) | collective-permute-done | bytes 1179680 | tf_op jit(solution)/shard_map/ppermute | solution.py:55
  150.8 1.4 values_back.1
  155.1 6.6 %attend_back.1 = (bf16[512,768]{1,0:T(8,128)(2,1)S(1)}, bf16[512,768]{1,0:T(8,128)(2,1)S(1)}, f32[1,768]{1,0:T(1,128)S(1)}, f32[8,128]{1,0:T(8,128)S(1)}) custom-call(f32[8,128]{1,0:T(8,128)S(1)} %get-tuple-element.272.refs_0_, bf16[512,1536]{1,0:T(8,128)(2,1)S(1)} %get-tuple-element.265.refs_1_, bf16[512,768]{1,0:T(8,128)(2,1)S(1)} %get-tuple-element.266.refs_2_, ...), custom_call_target="tpu_custom_call" | custom-call | flops 805306368 | bytes 6291456 | tf_op jit(solution)/shard_map/attend_back/pallas_call | solution.py:112
  162.5 13.2 %collective-permute-done.25.refs_2_ = bf16[2,4,1,48,1536]{4,3,2,1,0:T(8,128)(2,1)S(1)} collective-permute-done((bf16[2,4,1,48,1536]{4,3,2,1,0:T(8,128)(2,1)S(1)}, bf16[2,4,1,48,1536]{4,3,2,1,0:T(8,128)(2,1)S(1)}, u32[]{:S(2)}, u32[]{:S(2)}) %collective-permute-start.25) | collective-permute-done | bytes 1179680 | tf_op jit(solution)/shard_map/ppermute | solution.py:55
  178.7 3.0 %states_back.1 = (f32[512,768]{1,0:T(8,128)S(1)}, f32[8,128]{1,0:T(8,128)S(1)}) custom-call(f32[8,128]{1,0:T(8,128)S(1)} %get-tuple-element.286.refs_0_, bf16[512,768]{1,0:T(8,128)(2,1)S(1)} %get-tuple-element.283.refs_2_.refs_1_, bf16[512,768]{1,0:T(8,128)(2,1)S(1)} %get-tuple-element.284.refs_4_.refs_2_, ...), custom_call_target="tpu_custom_call" | custom-call | flops 1811939328 | bytes 8388608 | tf_op jit(solution)/shard_map/states_back/pallas_call | solution.py:112
  184.0 2.1 collective-permute-start.35
  186.6 11.9 %collective-permute-done.28.refs_2_ = bf16[2,4,2,48,384]{4,3,2,1,0:T(8,128)(2,1)S(1)} collective-permute-done((bf16[2,4,2,48,384]{4,3,2,1,0:T(8,128)(2,1)S(1)}, bf16[2,4,2,48,384]{4,3,2,1,0:T(8,128)(2,1)S(1)}, u32[]{:S(2)}, u32[]{:S(2)}) %collective-permute-start.28) | collective-permute-done | bytes 589856 | tf_op jit(solution)/shard_map/ppermute | solution.py:55
  199.2 1.7 collective-permute-start.32
  201.0 1.4 collective-permute-start.33
  202.4 1.2 collective-permute-start.34
  204.3 1.8 pair_up.2
  206.1 2.4 pair_up.3
  209.5 1.6 collective-permute-start.43
  211.1 1.7 collective-permute-start.41
  212.8 1.8 collective-permute-start.42
  215.8 7.2 %collective-permute-done.41.refs_3_ = bf16[1,96,768]{2,1,0:T(8,128)(2,1)S(1)} collective-permute-done((bf16[1,96,768]{2,1,0:T(8,128)(2,1)S(1)}, bf16[1,96,768]{2,1,0:T(8,128)(2,1)S(1)}, u32[]{:S(2)}, u32[]{:S(2)}) %collective-permute-start.41) | collective-permute-done | bytes 147488 | tf_op jit(solution)/shard_map/ppermute | solution.py:55
  223.0 3.2 %collective-permute-start.45 = (bf16[1,48,1536]{2,1,0:T(8,128)(2,1)S(1)}, bf16[1,48,1536]{2,1,0:T(8,128)(2,1)S(1)}, u32[]{:S(2)}, u32[]{:S(2)}) collective-permute-start(bf16[1,48,1536]{2,1,0:T(8,128)(2,1)S(1)} %get-tuple-element.331), channel_id=1, source_target_pairs={{0,16},{1,17},{2,18},{3,19},{4,20},{5,21},{6,22},{7,23},{8,24},{9,... | collective-permute-start | bytes 442376 | tf_op jit(solution)/shard_map/ppermute | solution.py:55
  226.2 3.9 %collective-permute-start.46 = (bf16[1,48,1536]{2,1,0:T(8,128)(2,1)S(1)}, bf16[1,48,1536]{2,1,0:T(8,128)(2,1)S(1)}, u32[]{:S(2)}, u32[]{:S(2)}) collective-permute-start(bf16[1,48,1536]{2,1,0:T(8,128)(2,1)S(1)} %get-tuple-element.332), channel_id=1, source_target_pairs={{0,24},{1,25},{2,26},{3,27},{4,28},{5,29},{6,30},{7,31},{8,16},{9,... | collective-permute-start | bytes 442376 | tf_op jit(solution)/shard_map/ppermute | solution.py:55
  230.1 4.1 %collective-permute-done.38.refs_3_ = f32[12,768]{1,0:T(8,128)S(1)} collective-permute-done((f32[12,768]{1,0:T(8,128)S(1)}, f32[12,768]{1,0:T(8,128)S(1)}, u32[]{:S(2)}, u32[]{:S(2)}) %collective-permute-start.38) | collective-permute-done | bytes 36896 | tf_op jit(solution)/shard_map/ppermute | solution.py:55
  234.8 4.3 %collective-permute-done.39.refs_4_ = f32[12,768]{1,0:T(8,128)S(1)} collective-permute-done((f32[12,768]{1,0:T(8,128)S(1)}, f32[12,768]{1,0:T(8,128)S(1)}, u32[]{:S(2)}, u32[]{:S(2)}) %collective-permute-start.39) | collective-permute-done | bytes 36896 | tf_op jit(solution)/shard_map/ppermute | solution.py:55
  241.7 3.8 %collective-permute-start.50 = (bf16[2,48,384]{2,1,0:T(8,128)(2,1)S(1)}, bf16[2,48,384]{2,1,0:T(8,128)(2,1)S(1)}, u32[]{:S(2)}, u32[]{:S(2)}) collective-permute-start(bf16[2,48,384]{2,1,0:T(8,128)(2,1)S(1)} %get-tuple-element.339), channel_id=1, source_target_pairs={{0,24},{1,25},{2,26},{3,27},{4,28},{5,29},{6,30},{7,31},{8,16},{9,... | collective-permute-start | bytes 221192 | tf_op jit(solution)/shard_map/ppermute | solution.py:55
  246.1 3.8 %collective-permute-start.53 = (bf16[2,48,384]{2,1,0:T(8,128)(2,1)S(1)}, bf16[2,48,384]{2,1,0:T(8,128)(2,1)S(1)}, u32[]{:S(2)}, u32[]{:S(2)}) collective-permute-start(bf16[2,48,384]{2,1,0:T(8,128)(2,1)S(1)} %get-tuple-element.343), channel_id=1, source_target_pairs={{0,24},{1,25},{2,26},{3,27},{4,28},{5,29},{6,30},{7,31},{8,16},{9,... | collective-permute-start | bytes 221192 | tf_op jit(solution)/shard_map/ppermute | solution.py:55
  251.6 4.9 %collective-permute-done.52.refs_7_ = bf16[2,48,384]{2,1,0:T(8,128)(2,1)S(1)} collective-permute-done((bf16[2,48,384]{2,1,0:T(8,128)(2,1)S(1)}, bf16[2,48,384]{2,1,0:T(8,128)(2,1)S(1)}, u32[]{:S(2)}, u32[]{:S(2)}) %collective-permute-start.52) | collective-permute-done | bytes 73760 | tf_op jit(solution)/shard_map/ppermute | solution.py:55
  257.7 1.7 collective-permute-start.54
  259.5 2.6 collective-permute-start.56
  262.1 1.8 collective-permute-done.55.refs_3_
  265.8 2.6 collective-permute-start.59
  268.6 1.7 collective-permute-done.59.refs_4_
  (159 shorter events, 41.2 us)
Async XLA Ops:
  2.5 12.1 %collective-permute-start = (bf16[4,48,384]{2,1,0:T(8,128)(2,1)S(1)}, bf16[4,48,384]{2,1,0:T(8,128)(2,1)S(1)}, u32[]{:S(2)}, u32[]{:S(2)}) collective-permute-start(bf16[4,48,384]{2,1,0:T(8,128)(2,1)S(1)} %get-tuple-element.204.refs_2_), channel_id=1, source_target_pairs={{0,8},{1,9},{2,10},{3,11},{4,12},{5,13},{6,14},{7,15},{8,0},{9,1},... | collective-permute-start | bytes 442376 | tf_op jit(solution)/shard_map/ppermute | solution.py:55
  5.6 14.0 %collective-permute-start.1 = (bf16[4,48,384]{2,1,0:T(8,128)(2,1)S(1)}, bf16[4,48,384]{2,1,0:T(8,128)(2,1)S(1)}, u32[]{:S(2)}, u32[]{:S(2)}) collective-permute-start(bf16[4,48,384]{2,1,0:T(8,128)(2,1)S(1)} %get-tuple-element.204.refs_2_), channel_id=1, source_target_pairs={{0,16},{1,17},{2,18},{3,19},{4,20},{5,21},{6,22},{7,23},{8,24},{9,... | collective-permute-start | bytes 442376 | tf_op jit(solution)/shard_map/ppermute | solution.py:55
  8.2 11.4 %collective-permute-start.2 = (bf16[4,48,384]{2,1,0:T(8,128)(2,1)S(1)}, bf16[4,48,384]{2,1,0:T(8,128)(2,1)S(1)}, u32[]{:S(2)}, u32[]{:S(2)}) collective-permute-start(bf16[4,48,384]{2,1,0:T(8,128)(2,1)S(1)} %get-tuple-element.204.refs_2_), channel_id=1, source_target_pairs={{0,24},{1,25},{2,26},{3,27},{4,28},{5,29},{6,30},{7,31},{8,16},{9,... | collective-permute-start | bytes 442376 | tf_op jit(solution)/shard_map/ppermute | solution.py:55
  13.6 27.7 %copy-start.4 = (f32[96,768]{1,0:T(8,128)S(1)}, f32[96,768]{1,0:T(8,128)}, u32[]{:S(2)}) copy-start(f32[96,768]{1,0:T(8,128)} %param.26) | copy-start | bytes 884740
  20.2 16.3 %collective-permute-start.6 = (bf16[4,4,48,384]{3,2,1,0:T(8,128)(2,1)S(1)}, bf16[4,4,48,384]{3,2,1,0:T(8,128)(2,1)S(1)}, u32[]{:S(2)}, u32[]{:S(2)}) collective-permute-start(bf16[4,4,48,384]{3,2,1,0:T(8,128)(2,1)S(1)} %get-tuple-element.209.refs_2_), channel_id=1, source_target_pairs={{0,2},{1,5},{2,0},{3,7},{4,6},{5,1},{6,4},{7,3},{8,10},{9,13},{10,... | collective-permute-start | bytes 1769480 | tf_op jit(solution)/shard_map/ppermute | solution.py:55
  21.8 28.1 %collective-permute-start.7 = (bf16[4,4,48,384]{3,2,1,0:T(8,128)(2,1)S(1)}, bf16[4,4,48,384]{3,2,1,0:T(8,128)(2,1)S(1)}, u32[]{:S(2)}, u32[]{:S(2)}) collective-permute-start(bf16[4,4,48,384]{3,2,1,0:T(8,128)(2,1)S(1)} %get-tuple-element.209.refs_2_), channel_id=1, source_target_pairs={{0,4},{1,3},{2,6},{3,1},{4,0},{5,7},{6,2},{7,5},{8,12},{9,11},{10,... | collective-permute-start | bytes 1769480 | tf_op jit(solution)/shard_map/ppermute | solution.py:55
  36.5 13.4 %collective-permute-start.8 = (bf16[4,4,48,384]{3,2,1,0:T(8,128)(2,1)S(1)}, bf16[4,4,48,384]{3,2,1,0:T(8,128)(2,1)S(1)}, u32[]{:S(2)}, u32[]{:S(2)}) collective-permute-start(bf16[4,4,48,384]{3,2,1,0:T(8,128)(2,1)S(1)} %collective-permute-done.6.refs_3_), channel_id=1, source_target_pairs={{0,4},{1,3},{2,6},{3,1},{4,0},{5,7},{6,2},{7,5},{8,12},{9,11},{10,... | collective-permute-start | bytes 1769480 | tf_op jit(solution)/shard_map/ppermute | solution.py:55
  36.5 7.1 %collective-permute-start.3 = (bf16[1,48,1536]{2,1,0:T(8,128)(2,1)S(1)}, bf16[1,48,1536]{2,1,0:T(8,128)(2,1)S(1)}, u32[]{:S(2)}, u32[]{:S(2)}) collective-permute-start(bf16[1,48,1536]{2,1,0:T(8,128)(2,1)S(1)} %get-tuple-element.207.refs_2_), channel_id=1, source_target_pairs={{0,8},{1,9},{2,10},{3,11},{4,12},{5,13},{6,14},{7,15},{8,0},{9,1},... | collective-permute-start | bytes 442376 | tf_op jit(solution)/shard_map/ppermute | solution.py:55
  38.8 10.5 %collective-permute-start.4 = (bf16[1,48,1536]{2,1,0:T(8,128)(2,1)S(1)}, bf16[1,48,1536]{2,1,0:T(8,128)(2,1)S(1)}, u32[]{:S(2)}, u32[]{:S(2)}) collective-permute-start(bf16[1,48,1536]{2,1,0:T(8,128)(2,1)S(1)} %get-tuple-element.207.refs_2_), channel_id=1, source_target_pairs={{0,16},{1,17},{2,18},{3,19},{4,20},{5,21},{6,22},{7,23},{8,24},{9,... | collective-permute-start | bytes 442376 | tf_op jit(solution)/shard_map/ppermute | solution.py:55
  39.8 9.5 %collective-permute-start.5 = (bf16[1,48,1536]{2,1,0:T(8,128)(2,1)S(1)}, bf16[1,48,1536]{2,1,0:T(8,128)(2,1)S(1)}, u32[]{:S(2)}, u32[]{:S(2)}) collective-permute-start(bf16[1,48,1536]{2,1,0:T(8,128)(2,1)S(1)} %get-tuple-element.207.refs_2_), channel_id=1, source_target_pairs={{0,24},{1,25},{2,26},{3,27},{4,28},{5,29},{6,30},{7,31},{8,16},{9,... | collective-permute-start | bytes 442376 | tf_op jit(solution)/shard_map/ppermute | solution.py:55
  50.7 25.7 %collective-permute-start.12 = (bf16[4,16,48,384]{3,2,1,0:T(8,128)(2,1)S(1)}, bf16[4,16,48,384]{3,2,1,0:T(8,128)(2,1)S(1)}, u32[]{:S(2)}, u32[]{:S(2)}) collective-permute-start(bf16[4,16,48,384]{3,2,1,0:T(8,128)(2,1)S(1)} %get-tuple-element.214), channel_id=1, source_target_pairs={{0,1},{1,0},{2,3},{3,2},{4,5},{5,4},{6,7},{7,6},{8,9},{9,8},{10,11... | collective-permute-start | bytes 7077896 | tf_op jit(solution)/shard_map/ppermute | solution.py:55
  50.7 12.4 %collective-permute-start.13 = (bf16[4,1,48,1536]{3,2,1,0:T(8,128)(2,1)S(1)}, bf16[4,1,48,1536]{3,2,1,0:T(8,128)(2,1)S(1)}, u32[]{:S(2)}, u32[]{:S(2)}) collective-permute-start(bf16[4,1,48,1536]{3,2,1,0:T(8,128)(2,1)S(1)} %get-tuple-element.221.refs_2_), channel_id=1, source_target_pairs={{0,2},{1,5},{2,0},{3,7},{4,6},{5,1},{6,4},{7,3},{8,10},{9,13},{10,... | collective-permute-start | bytes 1769480 | tf_op jit(solution)/shard_map/ppermute | solution.py:55
  51.1 18.9 %collective-permute-start.10 = (bf16[1,96,768]{2,1,0:T(8,128)(2,1)S(1)}, bf16[1,96,768]{2,1,0:T(8,128)(2,1)S(1)}, u32[]{:S(2)}, u32[]{:S(2)}) collective-permute-start(bf16[1,96,768]{2,1,0:T(8,128)(2,1)S(1)} %get-tuple-element.211.refs_2_), channel_id=1, source_target_pairs={{0,16},{1,17},{2,18},{3,19},{4,20},{5,21},{6,22},{7,23},{8,24},{9,... | collective-permute-start | bytes 442376 | tf_op jit(solution)/shard_map/ppermute | solution.py:55
  54.5 30.9 %collective-permute-start.14 = (bf16[4,1,48,1536]{3,2,1,0:T(8,128)(2,1)S(1)}, bf16[4,1,48,1536]{3,2,1,0:T(8,128)(2,1)S(1)}, u32[]{:S(2)}, u32[]{:S(2)}) collective-permute-start(bf16[4,1,48,1536]{3,2,1,0:T(8,128)(2,1)S(1)} %get-tuple-element.221.refs_2_), channel_id=1, source_target_pairs={{0,4},{1,3},{2,6},{3,1},{4,0},{5,7},{6,2},{7,5},{8,12},{9,11},{10,... | collective-permute-start | bytes 1769480 | tf_op jit(solution)/shard_map/ppermute | solution.py:55
  63.1 22.2 %collective-permute-start.15 = (bf16[4,1,48,1536]{3,2,1,0:T(8,128)(2,1)S(1)}, bf16[4,1,48,1536]{3,2,1,0:T(8,128)(2,1)S(1)}, u32[]{:S(2)}, u32[]{:S(2)}) collective-permute-start(bf16[4,1,48,1536]{3,2,1,0:T(8,128)(2,1)S(1)} %collective-permute-done.13.refs_3_), channel_id=1, source_target_pairs={{0,4},{1,3},{2,6},{3,1},{4,0},{5,7},{6,2},{7,5},{8,12},{9,11},{10,... | collective-permute-start | bytes 1769480 | tf_op jit(solution)/shard_map/ppermute | solution.py:55
  65.7 8.9 %collective-permute-start.11 = (bf16[1,96,768]{2,1,0:T(8,128)(2,1)S(1)}, bf16[1,96,768]{2,1,0:T(8,128)(2,1)S(1)}, u32[]{:S(2)}, u32[]{:S(2)}) collective-permute-start(bf16[1,96,768]{2,1,0:T(8,128)(2,1)S(1)} %get-tuple-element.211.refs_2_), channel_id=1, source_target_pairs={{0,24},{1,25},{2,26},{3,27},{4,28},{5,29},{6,30},{7,31},{8,16},{9,... | collective-permute-start | bytes 442376 | tf_op jit(solution)/shard_map/ppermute | solution.py:55
  70.0 5.8 %collective-permute-start.9 = (bf16[1,96,768]{2,1,0:T(8,128)(2,1)S(1)}, bf16[1,96,768]{2,1,0:T(8,128)(2,1)S(1)}, u32[]{:S(2)}, u32[]{:S(2)}) collective-permute-start(bf16[1,96,768]{2,1,0:T(8,128)(2,1)S(1)} %get-tuple-element.211.refs_2_), channel_id=1, source_target_pairs={{0,8},{1,9},{2,10},{3,11},{4,12},{5,13},{6,14},{7,15},{8,0},{9,1},... | collective-permute-start | bytes 442376 | tf_op jit(solution)/shard_map/ppermute | solution.py:55
  86.1 19.8 %collective-permute-start.16 = (bf16[1,16,48,1536]{3,2,1,0:T(8,128)(2,1)S(1)}, bf16[1,16,48,1536]{3,2,1,0:T(8,128)(2,1)S(1)}, u32[]{:S(2)}, u32[]{:S(2)}) collective-permute-start(bf16[1,16,48,1536]{3,2,1,0:T(8,128)(2,1)S(1)} %get-tuple-element.224), channel_id=1, source_target_pairs={{0,1},{1,0},{2,3},{3,2},{4,5},{5,4},{6,7},{7,6},{8,9},{9,8},{10,11... | collective-permute-start | bytes 7077896 | tf_op jit(solution)/shard_map/ppermute | solution.py:55
  86.2 16.1 %collective-permute-start.17 = (bf16[4,1,96,768]{3,2,1,0:T(8,128)(2,1)S(1)}, bf16[4,1,96,768]{3,2,1,0:T(8,128)(2,1)S(1)}, u32[]{:S(2)}, u32[]{:S(2)}) collective-permute-start(bf16[4,1,96,768]{3,2,1,0:T(8,128)(2,1)S(1)} %get-tuple-element.229.refs_2_), channel_id=1, source_target_pairs={{0,2},{1,5},{2,0},{3,7},{4,6},{5,1},{6,4},{7,3},{8,10},{9,13},{10,... | collective-permute-start | bytes 1769480 | tf_op jit(solution)/shard_map/ppermute | solution.py:55
  87.3 22.2 %collective-permute-start.18 = (bf16[4,1,96,768]{3,2,1,0:T(8,128)(2,1)S(1)}, bf16[4,1,96,768]{3,2,1,0:T(8,128)(2,1)S(1)}, u32[]{:S(2)}, u32[]{:S(2)}) collective-permute-start(bf16[4,1,96,768]{3,2,1,0:T(8,128)(2,1)S(1)} %get-tuple-element.229.refs_2_), channel_id=1, source_target_pairs={{0,4},{1,3},{2,6},{3,1},{4,0},{5,7},{6,2},{7,5},{8,12},{9,11},{10,... | collective-permute-start | bytes 1769480 | tf_op jit(solution)/shard_map/ppermute | solution.py:55
  102.2 9.9 %collective-permute-start.19 = (bf16[4,1,96,768]{3,2,1,0:T(8,128)(2,1)S(1)}, bf16[4,1,96,768]{3,2,1,0:T(8,128)(2,1)S(1)}, u32[]{:S(2)}, u32[]{:S(2)}) collective-permute-start(bf16[4,1,96,768]{3,2,1,0:T(8,128)(2,1)S(1)} %collective-permute-done.17.refs_3_), channel_id=1, source_target_pairs={{0,4},{1,3},{2,6},{3,1},{4,0},{5,7},{6,2},{7,5},{8,12},{9,11},{10,... | collective-permute-start | bytes 1769480 | tf_op jit(solution)/shard_map/ppermute | solution.py:55
  112.8 4.6 %collective-permute-start.20 = (bf16[1,16,96,768]{3,2,1,0:T(8,128)(2,1)S(1)}, bf16[1,16,96,768]{3,2,1,0:T(8,128)(2,1)S(1)}, u32[]{:S(2)}, u32[]{:S(2)}) collective-permute-start(bf16[1,16,96,768]{3,2,1,0:T(8,128)(2,1)S(1)} %get-tuple-element.232), channel_id=1, source_target_pairs={{0,1},{1,0},{2,3},{3,2},{4,5},{5,4},{6,7},{7,6},{8,9},{9,8},{10,11... | collective-permute-start | bytes 7077896 | tf_op jit(solution)/shard_map/ppermute | solution.py:55
  123.6 4.9 %collective-permute-start.21 = (bf16[1,16,96,768]{3,2,1,0:T(8,128)(2,1)S(1)}, bf16[1,16,96,768]{3,2,1,0:T(8,128)(2,1)S(1)}, u32[]{:S(2)}, u32[]{:S(2)}) collective-permute-start(bf16[1,16,96,768]{3,2,1,0:T(8,128)(2,1)S(1)} %bitcast.89), channel_id=1, source_target_pairs={{0,1},{1,0},{2,3},{3,2},{4,5},{5,4},{6,7},{7,6},{8,9},{9,8},{10,11... | collective-permute-start | bytes 7077896 | tf_op jit(solution)/shard_map/ppermute | solution.py:55
  133.9 7.5 %collective-permute-start.22 = (bf16[1,16,48,1536]{3,2,1,0:T(8,128)(2,1)S(1)}, bf16[1,16,48,1536]{3,2,1,0:T(8,128)(2,1)S(1)}, u32[]{:S(2)}, u32[]{:S(2)}) collective-permute-start(bf16[1,16,48,1536]{3,2,1,0:T(8,128)(2,1)S(1)} %bitcast.88), channel_id=1, source_target_pairs={{0,1},{1,0},{2,3},{3,2},{4,5},{5,4},{6,7},{7,6},{8,9},{9,8},{10,11... | collective-permute-start | bytes 7077896 | tf_op jit(solution)/shard_map/ppermute | solution.py:55
  134.4 16.2 %collective-permute-start.23 = (bf16[2,4,1,96,768]{4,3,2,1,0:T(8,128)(2,1)S(1)}, bf16[2,4,1,96,768]{4,3,2,1,0:T(8,128)(2,1)S(1)}, u32[]{:S(2)}, u32[]{:S(2)}) collective-permute-start(bf16[2,4,1,96,768]{4,3,2,1,0:T(8,128)(2,1)S(1)} %get-tuple-element.263), channel_id=1, source_target_pairs={{0,4},{1,3},{2,6},{3,1},{4,0},{5,7},{6,2},{7,5},{8,12},{9,11},{10,... | collective-permute-start | bytes 3538952 | tf_op jit(solution)/shard_map/ppermute | solution.py:55
  153.2 8.6 %collective-permute-start.24 = (bf16[2,16,48,384]{3,2,1,0:T(8,128)(2,1)S(1)}, bf16[2,16,48,384]{3,2,1,0:T(8,128)(2,1)S(1)}, u32[]{:S(2)}, u32[]{:S(2)}) collective-permute-start(bf16[2,16,48,384]{3,2,1,0:T(8,128)(2,1)S(1)} %bitcast.91), channel_id=1, source_target_pairs={{0,1},{1,0},{2,3},{3,2},{4,5},{5,4},{6,7},{7,6},{8,9},{9,8},{10,11... | collective-permute-start | bytes 3538952 | tf_op jit(solution)/shard_map/ppermute | solution.py:55
  153.2 22.5 %collective-permute-start.25 = (bf16[2,4,1,48,1536]{4,3,2,1,0:T(8,128)(2,1)S(1)}, bf16[2,4,1,48,1536]{4,3,2,1,0:T(8,128)(2,1)S(1)}, u32[]{:S(2)}, u32[]{:S(2)}) collective-permute-start(bf16[2,4,1,48,1536]{4,3,2,1,0:T(8,128)(2,1)S(1)} %get-tuple-element.278), channel_id=1, source_target_pairs={{0,4},{1,3},{2,6},{3,1},{4,0},{5,7},{6,2},{7,5},{8,12},{9,11},{10,... | collective-permute-start | bytes 3538952 | tf_op jit(solution)/shard_map/ppermute | solution.py:55
  153.6 22.4 %collective-permute-start.26 = (bf16[4,1,96,768]{3,2,1,0:T(8,128)(2,1)S(1)}, bf16[4,1,96,768]{3,2,1,0:T(8,128)(2,1)S(1)}, u32[]{:S(2)}, u32[]{:S(2)}) collective-permute-start(bf16[4,1,96,768]{3,2,1,0:T(8,128)(2,1)S(1)} %get-tuple-element.281), channel_id=1, source_target_pairs={{0,2},{1,5},{2,0},{3,7},{4,6},{5,1},{6,4},{7,3},{8,10},{9,13},{10,... | collective-permute-start | bytes 1769480 | tf_op jit(solution)/shard_map/ppermute | solution.py:55
  178.7 4.5 %collective-permute-start.27 = (bf16[2,16,48,384]{3,2,1,0:T(8,128)(2,1)S(1)}, bf16[2,16,48,384]{3,2,1,0:T(8,128)(2,1)S(1)}, u32[]{:S(2)}, u32[]{:S(2)}) collective-permute-start(bf16[2,16,48,384]{3,2,1,0:T(8,128)(2,1)S(1)} %bitcast.90), channel_id=1, source_target_pairs={{0,1},{1,0},{2,3},{3,2},{4,5},{5,4},{6,7},{7,6},{8,9},{9,8},{10,11... | collective-permute-start | bytes 3538952 | tf_op jit(solution)/shard_map/ppermute | solution.py:55
  181.7 20.7 %collective-permute-start.31 = (f32[512,768]{1,0:T(8,128)S(1)}, f32[512,768]{1,0:T(8,128)S(1)}, u32[]{:S(2)}, u32[]{:S(2)}) collective-permute-start(f32[512,768]{1,0:T(8,128)S(1)} %get-tuple-element.308.refs_2_), channel_id=1, source_target_pairs={{0,1},{1,0},{2,3},{3,2},{4,5},{5,4},{6,7},{7,6},{8,9},{9,8},{10,11... | collective-permute-start | bytes 4718600 | tf_op jit(solution)/shard_map/ppermute | solution.py:55
  182.3 17.0 %collective-permute-start.30 = (bf16[512,768]{1,0:T(8,128)(2,1)S(1)}, bf16[512,768]{1,0:T(8,128)(2,1)S(1)}, u32[]{:S(2)}, u32[]{:S(2)}) collective-permute-start(bf16[512,768]{1,0:T(8,128)(2,1)S(1)} %get-tuple-element.305.refs_2_), channel_id=1, source_target_pairs={{0,1},{1,0},{2,3},{3,2},{4,5},{5,4},{6,7},{7,6},{8,9},{9,8},{10,11... | collective-permute-start | bytes 2359304 | tf_op jit(solution)/shard_map/ppermute | solution.py:55
  182.3 16.2 %collective-permute-start.28 = (bf16[2,4,2,48,384]{4,3,2,1,0:T(8,128)(2,1)S(1)}, bf16[2,4,2,48,384]{4,3,2,1,0:T(8,128)(2,1)S(1)}, u32[]{:S(2)}, u32[]{:S(2)}) collective-permute-start(bf16[2,4,2,48,384]{4,3,2,1,0:T(8,128)(2,1)S(1)} %get-tuple-element.300), channel_id=1, source_target_pairs={{0,4},{1,3},{2,6},{3,1},{4,0},{5,7},{6,2},{7,5},{8,12},{9,11},{10,... | collective-permute-start | bytes 1769480 | tf_op jit(solution)/shard_map/ppermute | solution.py:55
  182.6 18.4 %collective-permute-start.29 = (bf16[4,1,48,1536]{3,2,1,0:T(8,128)(2,1)S(1)}, bf16[4,1,48,1536]{3,2,1,0:T(8,128)(2,1)S(1)}, u32[]{:S(2)}, u32[]{:S(2)}) collective-permute-start(bf16[4,1,48,1536]{3,2,1,0:T(8,128)(2,1)S(1)} %get-tuple-element.303), channel_id=1, source_target_pairs={{0,2},{1,5},{2,0},{3,7},{4,6},{5,1},{6,4},{7,3},{8,10},{9,13},{10,... | collective-permute-start | bytes 1769480 | tf_op jit(solution)/shard_map/ppermute | solution.py:55
  184.0 25.5 %collective-permute-start.35 = (bf16[2,4,2,48,384]{4,3,2,1,0:T(8,128)(2,1)S(1)}, bf16[2,4,2,48,384]{4,3,2,1,0:T(8,128)(2,1)S(1)}, u32[]{:S(2)}, u32[]{:S(2)}) collective-permute-start(bf16[2,4,2,48,384]{4,3,2,1,0:T(8,128)(2,1)S(1)} %get-tuple-element.314), channel_id=1, source_target_pairs={{0,4},{1,3},{2,6},{3,1},{4,0},{5,7},{6,2},{7,5},{8,12},{9,11},{10,... | collective-permute-start | bytes 1769480 | tf_op jit(solution)/shard_map/ppermute | solution.py:55
  198.6 27.6 %collective-permute-start.36 = (bf16[4,2,48,384]{3,2,1,0:T(8,128)(2,1)S(1)}, bf16[4,2,48,384]{3,2,1,0:T(8,128)(2,1)S(1)}, u32[]{:S(2)}, u32[]{:S(2)}) collective-permute-start(bf16[4,2,48,384]{3,2,1,0:T(8,128)(2,1)S(1)} %get-tuple-element.317), channel_id=1, source_target_pairs={{0,2},{1,5},{2,0},{3,7},{4,6},{5,1},{6,4},{7,3},{8,10},{9,13},{10,... | collective-permute-start | bytes 884744 | tf_op jit(solution)/shard_map/ppermute | solution.py:55
  199.2 9.3 %collective-permute-start.32 = (f32[12,768]{1,0:T(8,128)S(1)}, f32[12,768]{1,0:T(8,128)S(1)}, u32[]{:S(2)}, u32[]{:S(2)}) collective-permute-start(f32[12,768]{1,0:T(8,128)S(1)} %get-tuple-element.311.refs_1_), channel_id=1, source_target_pairs={{0,8},{1,9},{2,10},{3,11},{4,12},{5,13},{6,14},{7,15},{8,0},{9,1},... | collective-permute-start | bytes 110600 | tf_op jit(solution)/shard_map/ppermute | solution.py:55
  201.0 8.4 %collective-permute-start.33 = (f32[12,768]{1,0:T(8,128)S(1)}, f32[12,768]{1,0:T(8,128)S(1)}, u32[]{:S(2)}, u32[]{:S(2)}) collective-permute-start(f32[12,768]{1,0:T(8,128)S(1)} %get-tuple-element.311.refs_1_), channel_id=1, source_target_pairs={{0,16},{1,17},{2,18},{3,19},{4,20},{5,21},{6,22},{7,23},{8,24},{9,... | collective-permute-start | bytes 110600 | tf_op jit(solution)/shard_map/ppermute | solution.py:55
  202.4 7.0 %collective-permute-start.34 = (f32[12,768]{1,0:T(8,128)S(1)}, f32[12,768]{1,0:T(8,128)S(1)}, u32[]{:S(2)}, u32[]{:S(2)}) collective-permute-start(f32[12,768]{1,0:T(8,128)S(1)} %get-tuple-element.311.refs_1_), channel_id=1, source_target_pairs={{0,24},{1,25},{2,26},{3,27},{4,28},{5,29},{6,30},{7,31},{8,16},{9,... | collective-permute-start | bytes 110600 | tf_op jit(solution)/shard_map/ppermute | solution.py:55
  208.5 30.8 %copy-start.9 = (f32[96,768]{1,0:T(8,128)S(1)}, f32[96,768]{1,0:T(8,128)}, u32[]{:S(2)}) copy-start(f32[96,768]{1,0:T(8,128)} %param.30) | copy-start | bytes 884740
  208.5 30.8 %copy-start.10 = (f32[96,768]{1,0:T(8,128)S(1)}, f32[96,768]{1,0:T(8,128)}, u32[]{:S(2)}) copy-start(f32[96,768]{1,0:T(8,128)} %param.34) | copy-start | bytes 884740
  208.5 6.4 %collective-permute-start.40 = (bf16[1,96,768]{2,1,0:T(8,128)(2,1)S(1)}, bf16[1,96,768]{2,1,0:T(8,128)(2,1)S(1)}, u32[]{:S(2)}, u32[]{:S(2)}) collective-permute-start(bf16[1,96,768]{2,1,0:T(8,128)(2,1)S(1)} %get-tuple-element.322), channel_id=1, source_target_pairs={{0,8},{1,9},{2,10},{3,11},{4,12},{5,13},{6,14},{7,15},{8,0},{9,1},... | collective-permute-start | bytes 442376 | tf_op jit(solution)/shard_map/ppermute | solution.py:55
  209.5 29.7 %collective-permute-start.43 = (bf16[4,2,48,384]{3,2,1,0:T(8,128)(2,1)S(1)}, bf16[4,2,48,384]{3,2,1,0:T(8,128)(2,1)S(1)}, u32[]{:S(2)}, u32[]{:S(2)}) collective-permute-start(bf16[4,2,48,384]{3,2,1,0:T(8,128)(2,1)S(1)} %get-tuple-element.327), channel_id=1, source_target_pairs={{0,2},{1,5},{2,0},{3,7},{4,6},{5,1},{6,4},{7,3},{8,10},{9,13},{10,... | collective-permute-start | bytes 884744 | tf_op jit(solution)/shard_map/ppermute | solution.py:55
  211.1 11.9 %collective-permute-start.41 = (bf16[1,96,768]{2,1,0:T(8,128)(2,1)S(1)}, bf16[1,96,768]{2,1,0:T(8,128)(2,1)S(1)}, u32[]{:S(2)}, u32[]{:S(2)}) collective-permute-start(bf16[1,96,768]{2,1,0:T(8,128)(2,1)S(1)} %get-tuple-element.323), channel_id=1, source_target_pairs={{0,16},{1,17},{2,18},{3,19},{4,20},{5,21},{6,22},{7,23},{8,24},{9,... | collective-permute-start | bytes 442376 | tf_op jit(solution)/shard_map/ppermute | solution.py:55
  212.8 10.2 %collective-permute-start.42 = (bf16[1,96,768]{2,1,0:T(8,128)(2,1)S(1)}, bf16[1,96,768]{2,1,0:T(8,128)(2,1)S(1)}, u32[]{:S(2)}, u32[]{:S(2)}) collective-permute-start(bf16[1,96,768]{2,1,0:T(8,128)(2,1)S(1)} %get-tuple-element.324), channel_id=1, source_target_pairs={{0,24},{1,25},{2,26},{3,27},{4,28},{5,29},{6,30},{7,31},{8,16},{9,... | collective-permute-start | bytes 442376 | tf_op jit(solution)/shard_map/ppermute | solution.py:55
  214.9 15.2 %collective-permute-start.37 = (f32[12,768]{1,0:T(8,128)S(1)}, f32[12,768]{1,0:T(8,128)S(1)}, u32[]{:S(2)}, u32[]{:S(2)}) collective-permute-start(f32[12,768]{1,0:T(8,128)S(1)} %get-tuple-element.319.refs_1_), channel_id=1, source_target_pairs={{0,4},{1,5},{2,6},{3,7},{4,0},{5,1},{6,2},{7,3},{8,12},{9,13},{10,... | collective-permute-start | bytes 110600 | tf_op jit(solution)/shard_map/ppermute | solution.py:55
  223.0 18.0 %collective-permute-start.44 = (bf16[1,48,1536]{2,1,0:T(8,128)(2,1)S(1)}, bf16[1,48,1536]{2,1,0:T(8,128)(2,1)S(1)}, u32[]{:S(2)}, u32[]{:S(2)}) collective-permute-start(bf16[1,48,1536]{2,1,0:T(8,128)(2,1)S(1)} %get-tuple-element.330), channel_id=1, source_target_pairs={{0,8},{1,9},{2,10},{3,11},{4,12},{5,13},{6,14},{7,15},{8,0},{9,1},... | collective-permute-start | bytes 442376 | tf_op jit(solution)/shard_map/ppermute | solution.py:55
  223.0 18.7 %collective-permute-start.45 = (bf16[1,48,1536]{2,1,0:T(8,128)(2,1)S(1)}, bf16[1,48,1536]{2,1,0:T(8,128)(2,1)S(1)}, u32[]{:S(2)}, u32[]{:S(2)}) collective-permute-start(bf16[1,48,1536]{2,1,0:T(8,128)(2,1)S(1)} %get-tuple-element.331), channel_id=1, source_target_pairs={{0,16},{1,17},{2,18},{3,19},{4,20},{5,21},{6,22},{7,23},{8,24},{9,... | collective-permute-start | bytes 442376 | tf_op jit(solution)/shard_map/ppermute | solution.py:55
  226.2 19.2 %collective-permute-start.46 = (bf16[1,48,1536]{2,1,0:T(8,128)(2,1)S(1)}, bf16[1,48,1536]{2,1,0:T(8,128)(2,1)S(1)}, u32[]{:S(2)}, u32[]{:S(2)}) collective-permute-start(bf16[1,48,1536]{2,1,0:T(8,128)(2,1)S(1)} %get-tuple-element.332), channel_id=1, source_target_pairs={{0,24},{1,25},{2,26},{3,27},{4,28},{5,29},{6,30},{7,31},{8,16},{9,... | collective-permute-start | bytes 442376 | tf_op jit(solution)/shard_map/ppermute | solution.py:55
  230.1 4.1 %collective-permute-start.38 = (f32[12,768]{1,0:T(8,128)S(1)}, f32[12,768]{1,0:T(8,128)S(1)}, u32[]{:S(2)}, u32[]{:S(2)}) collective-permute-start(f32[12,768]{1,0:T(8,128)S(1)} %get-tuple-element.319.refs_1_), channel_id=1, source_target_pairs={{0,2},{1,3},{2,0},{3,1},{4,6},{5,7},{6,4},{7,5},{8,10},{9,11},{10,... | collective-permute-start | bytes 110600 | tf_op jit(solution)/shard_map/ppermute | solution.py:55
  234.2 5.0 %collective-permute-start.39 = (f32[12,768]{1,0:T(8,128)S(1)}, f32[12,768]{1,0:T(8,128)S(1)}, u32[]{:S(2)}, u32[]{:S(2)}) collective-permute-start(f32[12,768]{1,0:T(8,128)S(1)} %get-tuple-element.319.refs_1_), channel_id=1, source_target_pairs={{0,6},{1,7},{2,4},{3,5},{4,2},{5,3},{6,0},{7,1},{8,14},{9,15},{10,... | collective-permute-start | bytes 110600 | tf_op jit(solution)/shard_map/ppermute | solution.py:55
  239.2 6.9 %collective-permute-start.48 = (bf16[2,48,384]{2,1,0:T(8,128)(2,1)S(1)}, bf16[2,48,384]{2,1,0:T(8,128)(2,1)S(1)}, u32[]{:S(2)}, u32[]{:S(2)}) collective-permute-start(bf16[2,48,384]{2,1,0:T(8,128)(2,1)S(1)} %get-tuple-element.337), channel_id=1, source_target_pairs={{0,8},{1,9},{2,10},{3,11},{4,12},{5,13},{6,14},{7,15},{8,0},{9,1},... | collective-permute-start | bytes 221192 | tf_op jit(solution)/shard_map/ppermute | solution.py:55
  239.2 6.3 %collective-permute-start.47 = (f32[12,768]{1,0:T(8,128)S(1)}, f32[12,768]{1,0:T(8,128)S(1)}, u32[]{:S(2)}, u32[]{:S(2)}) collective-permute-start(f32[12,768]{1,0:T(8,128)S(1)} %get-tuple-element.334.refs_1_), channel_id=1, source_target_pairs={{0,1},{1,0},{2,3},{3,2},{4,5},{5,4},{6,7},{7,6},{8,9},{9,8},{10,11... | collective-permute-start | bytes 110600 | tf_op jit(solution)/shard_map/ppermute | solution.py:55
  241.0 10.6 %collective-permute-start.49 = (bf16[2,48,384]{2,1,0:T(8,128)(2,1)S(1)}, bf16[2,48,384]{2,1,0:T(8,128)(2,1)S(1)}, u32[]{:S(2)}, u32[]{:S(2)}) collective-permute-start(bf16[2,48,384]{2,1,0:T(8,128)(2,1)S(1)} %get-tuple-element.338), channel_id=1, source_target_pairs={{0,16},{1,17},{2,18},{3,19},{4,20},{5,21},{6,22},{7,23},{8,24},{9,... | collective-permute-start | bytes 221192 | tf_op jit(solution)/shard_map/ppermute | solution.py:55
  241.7 9.9 %collective-permute-start.50 = (bf16[2,48,384]{2,1,0:T(8,128)(2,1)S(1)}, bf16[2,48,384]{2,1,0:T(8,128)(2,1)S(1)}, u32[]{:S(2)}, u32[]{:S(2)}) collective-permute-start(bf16[2,48,384]{2,1,0:T(8,128)(2,1)S(1)} %get-tuple-element.339), channel_id=1, source_target_pairs={{0,24},{1,25},{2,26},{3,27},{4,28},{5,29},{6,30},{7,31},{8,16},{9,... | collective-permute-start | bytes 221192 | tf_op jit(solution)/shard_map/ppermute | solution.py:55
  245.5 6.1 %collective-permute-start.51 = (bf16[2,48,384]{2,1,0:T(8,128)(2,1)S(1)}, bf16[2,48,384]{2,1,0:T(8,128)(2,1)S(1)}, u32[]{:S(2)}, u32[]{:S(2)}) collective-permute-start(bf16[2,48,384]{2,1,0:T(8,128)(2,1)S(1)} %get-tuple-element.341), channel_id=1, source_target_pairs={{0,8},{1,9},{2,10},{3,11},{4,12},{5,13},{6,14},{7,15},{8,0},{9,1},... | collective-permute-start | bytes 221192 | tf_op jit(solution)/shard_map/ppermute | solution.py:55
  245.5 11.0 %collective-permute-start.52 = (bf16[2,48,384]{2,1,0:T(8,128)(2,1)S(1)}, bf16[2,48,384]{2,1,0:T(8,128)(2,1)S(1)}, u32[]{:S(2)}, u32[]{:S(2)}) collective-permute-start(bf16[2,48,384]{2,1,0:T(8,128)(2,1)S(1)} %get-tuple-element.342), channel_id=1, source_target_pairs={{0,16},{1,17},{2,18},{3,19},{4,20},{5,21},{6,22},{7,23},{8,24},{9,... | collective-permute-start | bytes 221192 | tf_op jit(solution)/shard_map/ppermute | solution.py:55
  246.1 10.4 %collective-permute-start.53 = (bf16[2,48,384]{2,1,0:T(8,128)(2,1)S(1)}, bf16[2,48,384]{2,1,0:T(8,128)(2,1)S(1)}, u32[]{:S(2)}, u32[]{:S(2)}) collective-permute-start(bf16[2,48,384]{2,1,0:T(8,128)(2,1)S(1)} %get-tuple-element.343), channel_id=1, source_target_pairs={{0,24},{1,25},{2,26},{3,27},{4,28},{5,29},{6,30},{7,31},{8,16},{9,... | collective-permute-start | bytes 221192 | tf_op jit(solution)/shard_map/ppermute | solution.py:55
  257.7 4.4 %collective-permute-start.54 = (f32[8,128]{1,0:T(8,128)S(1)}, f32[8,128]{1,0:T(8,128)S(1)}, u32[]{:S(2)}, u32[]{:S(2)}) collective-permute-start(f32[8,128]{1,0:T(8,128)S(1)} %get-tuple-element.347.refs_1_), channel_id=1, source_target_pairs={{0,8},{1,9},{2,10},{3,11},{4,12},{5,13},{6,14},{7,15},{8,0},{9,1},... | collective-permute-start | bytes 12296 | tf_op jit(solution)/shard_map/ppermute | solution.py:55
  259.4 4.5 %collective-permute-start.55 = (f32[8,128]{1,0:T(8,128)S(1)}, f32[8,128]{1,0:T(8,128)S(1)}, u32[]{:S(2)}, u32[]{:S(2)}) collective-permute-start(f32[8,128]{1,0:T(8,128)S(1)} %get-tuple-element.347.refs_1_), channel_id=1, source_target_pairs={{0,16},{1,17},{2,18},{3,19},{4,20},{5,21},{6,22},{7,23},{8,24},{9,... | collective-permute-start | bytes 12296 | tf_op jit(solution)/shard_map/ppermute | solution.py:55
  259.5 5.4 %collective-permute-start.56 = (f32[8,128]{1,0:T(8,128)S(1)}, f32[8,128]{1,0:T(8,128)S(1)}, u32[]{:S(2)}, u32[]{:S(2)}) collective-permute-start(f32[8,128]{1,0:T(8,128)S(1)} %get-tuple-element.347.refs_1_), channel_id=1, source_target_pairs={{0,24},{1,25},{2,26},{3,27},{4,28},{5,29},{6,30},{7,31},{8,16},{9,... | collective-permute-start | bytes 12296 | tf_op jit(solution)/shard_map/ppermute | solution.py:55
  264.9 3.6 %collective-permute-start.57 = (f32[8,128]{1,0:T(8,128)S(1)}, f32[8,128]{1,0:T(8,128)S(1)}, u32[]{:S(2)}, u32[]{:S(2)}) collective-permute-start(f32[8,128]{1,0:T(8,128)S(1)} %get-tuple-element.349.refs_1_), channel_id=1, source_target_pairs={{0,4},{1,5},{2,6},{3,7},{4,0},{5,1},{6,2},{7,3},{8,12},{9,13},{10,... | collective-permute-start | bytes 12296 | tf_op jit(solution)/shard_map/ppermute | solution.py:55
  264.9 3.7 %collective-permute-start.58 = (f32[8,128]{1,0:T(8,128)S(1)}, f32[8,128]{1,0:T(8,128)S(1)}, u32[]{:S(2)}, u32[]{:S(2)}) collective-permute-start(f32[8,128]{1,0:T(8,128)S(1)} %get-tuple-element.349.refs_1_), channel_id=1, source_target_pairs={{0,2},{1,3},{2,0},{3,1},{4,6},{5,7},{6,4},{7,5},{8,10},{9,11},{10,... | collective-permute-start | bytes 12296 | tf_op jit(solution)/shard_map/ppermute | solution.py:55
  265.8 4.5 %collective-permute-start.59 = (f32[8,128]{1,0:T(8,128)S(1)}, f32[8,128]{1,0:T(8,128)S(1)}, u32[]{:S(2)}, u32[]{:S(2)}) collective-permute-start(f32[8,128]{1,0:T(8,128)S(1)} %get-tuple-element.349.refs_1_), channel_id=1, source_target_pairs={{0,6},{1,7},{2,4},{3,5},{4,2},{5,3},{6,0},{7,1},{8,14},{9,15},{10,... | collective-permute-start | bytes 12296 | tf_op jit(solution)/shard_map/ppermute | solution.py:55
  270.3 1.2 collective-permute-start.60
  (18 other events, 171.6 us)

commit v3 on v2

--- a/solution.py
+++ b/solution.py
@@ -1,3 +1,4 @@
+import itertools
 import math
 
 import jax
@@ -59,11 +60,33 @@
         spot = [lax.rem(lax.div(index, s), n) if n > 1 else index * 0 for s, n in zip(self.stride, self.sizes)]
         return jnp.stack(spot + [lax.axis_index("tensor")]).astype(jnp.int32)
 
-    def first(self, k):
-        return lambda core: ((0, k, 0) if core == 0 else (0, 0, k), 0)
-
-    def second(self, k):
-        return lambda core: ((0, 0, k) if core == 0 else (0, k, 0), 0)
+    def path(self):
+        bits = [[1 << b for b in reversed(range((n - 1).bit_length()))] for n in (self.long, self.side, self.side)]
+        return [(side, k) for side in range(3) for k in bits[side]]
+
+    def exchange(self, value, step):
+        side, k = step
+        offsets = [(k, 0, 0), (0, k, 0), (0, 0, k)]
+        return self.send(value, lambda core: (offsets[side if core == 0 else (0, 2, 1)[side]], 0))
+
+    def bit(self, s, step):
+        side, k = step
+        spot = s[0] if side == 0 else jnp.where(s[3] == 0, s[side], s[3 - side])
+        return lax.rem(lax.div(spot, k), 2)
+
+    def spot(self, s, steps, bits):
+        place = 0
+        for (side, k), bit in zip(steps, bits):
+            stride = self.stride[0] if side == 0 else jnp.where(s[3] == 0, self.stride[side], self.stride[3 - side])
+            place = place + bit * k * stride
+        return place
+
+    def long_steps(self):
+        return [step for step in self.path() if step[0] == 0]
+
+    def long_bits(self, s, k):
+        spot = s[0] ^ k
+        return tuple(lax.rem(lax.div(spot, distance), 2) for _, distance in reversed(self.long_steps()))
 
     def along(self, k):
         return lambda core: ((k, 0, 0), 0)
@@ -73,12 +96,6 @@
 
     def core(self, value):
         return self.send(value, lambda core: ((0, 0, 0), 1))
-
-    def slot(self, s, k, m, a):
-        zero = s[3] == 0
-        b = s[1] ^ jnp.where(zero, k, m)
-        c = s[2] ^ jnp.where(zero, m, k)
-        return self.stride[0] * a + self.stride[1] * b + self.stride[2] * c
 
 
 class Tape:
@@ -116,109 +133,136 @@
             out_specs=[pl.BlockSpec(memory_space=VMEM)] * len(shapes),
             scratch_shapes=list(scratch),
             name=name or body.__name__,
-            cost_estimate=pl.CostEstimate(flops=flops, bytes_accessed=moved, transcendentals=exps),
+            cost_estimate=pl.CostEstimate(flops=flops, bytes_accessed=moved, transcendentals=0),
             compiler_params=pltpu.CompilerParams(vmem_limit_bytes=limit * MIB),
         )(*[v for v, _ in first], *ins)
         return values
 
 
+def part(count, group, groups=3):
+    return range(count * group // groups, count * (group + 1) // groups)
+
+
 class Gather:
-    def __init__(self, grid, tape, shard):
-        self.grid, self.tape = grid, tape
-        self.many, self.rows, self.width = shard.shape
-        self.got = [shard] + [grid.send(shard, grid.along(k)) for k in range(1, grid.long)]
-
-    def line(self):
+    def __init__(self, grid, tape, shard, direct=False):
+        self.grid, self.tape, self.block = grid, tape, shard
+        self.path = grid.path()
+        if direct:
+            self.got = [grid.send(shard, grid.along(k)) for k in range(1, grid.long)]
+        else:
+            self.got = grid.exchange(shard, self.path[0])
+
+    def merge_long(self):
         grid = self.grid
-        long, side = grid.long, grid.side
-
-        def body(s, *refs):
-            for k in range(long):
-                refs[-1][s[0] ^ k] = refs[k][...]
-
-        block = self.tape.run(body, [((long, self.many, self.rows, self.width), BF16)], self.got, True)[0]
-        self.pieces = {(0, 0): block}
-        for k in range(1, side):
-            self.pieces[k, 0] = grid.send(block, grid.first(k))
-        for m in range(1, side):
-            for k in range(side):
-                self.pieces[k, m] = grid.send(self.pieces[k, 0], grid.second(m))
+        steps = grid.long_steps()
+
+        def gather_long(s, *refs):
+            for k, ref in enumerate(refs[:-1]):
+                refs[-1][grid.long_bits(s, k)] = ref[...]
+
+        shape = (2,) * len(steps) + self.block.shape
+        self.block = self.tape.run(gather_long, [(shape, BF16)], [self.block] + self.got, True)[0]
+        self.got = grid.exchange(self.block, self.path[len(steps)])
+
+    def merge(self, group):
+        self.merges(part(len(self.path) - 1, group))
+
+    def merge_short(self):
+        self.merges(range(len(self.grid.long_steps()), len(self.path) - 1))
+
+    def merges(self, steps):
+        grid = self.grid
+        for i in steps:
+            step = self.path[i]
+
+            def gather_merge(s, own, got, out):
+                bit = grid.bit(s, step)
+                out[bit] = own[...]
+                out[1 - bit] = got[...]
+
+            shape = (2,) + self.block.shape
+            self.block = self.tape.run(gather_merge, [(shape, BF16)], [self.block, self.got], True)[0]
+            self.got = grid.exchange(self.block, self.path[i + 1])
 
     def whole(self):
-        grid = self.grid
-        keys = list(self.pieces)
-
-        def body(s, *refs):
-            for (k, m), ref in zip(keys, refs[:-1]):
-                for a in range(grid.long):
-                    spot = grid.slot(s, k, m, a)
-                    for j in range(self.many):
-                        refs[-1][j, spot] = ref[a, j]
-
-        full = self.tape.run(
-            body, [((self.many, grid.dp, self.rows, self.width), BF16)], [self.pieces[key] for key in keys], True
-        )[0]
+        grid, path = self.grid, self.path
+        many, rows, width = self.block.shape[-3:]
+
+        def gather_whole(s, own, got, out):
+            last = grid.bit(s, path[-1])
+            for bits in itertools.product(range(2), repeat=len(path) - 1):
+                for ref, bit in ((own, last), (got, 1 - last)):
+                    spot = grid.spot(s, path, bits[::-1] + (bit,))
+                    for j in range(many):
+                        out[j, spot] = ref[bits + (j,)]
+
+        shape = (many, grid.dp, rows, width)
+        full = self.tape.run(gather_whole, [(shape, BF16)], [self.block, self.got], True)[0]
         return full, grid.core(full)
 
 
 class Scatter:
     def __init__(self, grid, tape, other):
         self.grid, self.tape = grid, tape
-        self.many, _, self.rows, self.width = other.shape
-        self.got = grid.core(other)
-        self.block = (grid.side, grid.long, self.many, self.rows, self.width)
+        self.path = grid.path()
+        self.got = [grid.core(v) for v in other]
 
     def pair(self, own):
-        grid, side = self.grid, self.grid.side
-
-        def body(s, own_ref, got_ref, keep, *sends):
-            for m in range(side):
-                out = keep if m == 0 else sends[m - 1]
-                for k in range(side):
-                    for a in range(grid.long):
-                        spot = grid.slot(s, k, m, a)
-                        for j in range(self.many):
-                            total = own_ref[j, spot] + got_ref[j, spot].astype(F32)
-                            out[k, a, j] = total.astype(out.dtype)
-
-        self.keep, *sends = self.tape.run(
-            body, [(self.block, F32)] + [(self.block, BF16)] * (side - 1), [own, self.got], True
-        )
-        self.came = [grid.send(v, grid.second(m + 1)) for m, v in enumerate(sends)]
-
-    def sides(self):
-        grid, side = self.grid, self.grid.side
-
-        def body(*refs):
-            outs = refs[side:]
-            for k in range(side):
-                total = refs[0][k]
-                for ref in refs[1:side]:
-                    total = total + ref[k].astype(F32)
-                outs[k][...] = total.astype(outs[k].dtype)
-
-        shape = self.block[1:]
-        self.keep, *sends = self.tape.run(
-            body, [(shape, F32)] + [(shape, BF16)] * (side - 1), [self.keep] + self.came
-        )
-        self.came = [grid.send(v, grid.first(k + 1)) for k, v in enumerate(sends)]
-
-    def line(self):
-        grid, side, long = self.grid, self.grid.side, self.grid.long
-
-        def body(s, *refs):
-            outs = refs[side:]
-            for k in range(long):
-                total = refs[0][s[0] ^ k]
-                for ref in refs[1:side]:
-                    total = total + ref[s[0] ^ k].astype(F32)
-                outs[k][...] = total.astype(outs[k].dtype)
-
-        shape = self.block[2:]
-        keep, *sends = self.tape.run(
-            body, [(shape, F32)] + [(shape, BF16)] * (long - 1), [self.keep] + self.came, True
-        )
-        self.parts = [keep] + [grid.send(v, grid.along(k + 1)) for k, v in enumerate(sends)]
+        grid, path = self.grid, self.path
+        each, _, rows, width = own[0].shape
+        many, pieces = each * len(own), len(own)
+        shape = (2,) * (len(path) - 1) + (many, rows, width)
+
+        def scatter_pair(s, *refs):
+            own_refs, got_refs, (keep, send) = refs[:pieces], refs[pieces : 2 * pieces], refs[2 * pieces :]
+            last = grid.bit(s, path[-1])
+            for bits in itertools.product(range(2), repeat=len(path) - 1):
+                for out, bit in ((keep, last), (send, 1 - last)):
+                    spot = grid.spot(s, path, bits[::-1] + (bit,))
+                    for j in range(many):
+                        g, i = divmod(j, each)
+                        total = own_refs[g][i, spot] + got_refs[g][i, spot].astype(F32)
+                        out[bits + (j,)] = total.astype(out.dtype)
+
+        self.keep, value = self.tape.run(scatter_pair, [(shape, F32), (shape, BF16)], own + self.got, True)
+        self.got = grid.exchange(value, path[-1])
+
+    def split(self, group):
+        self.splits(part(len(self.path) - 1, group))
+
+    def split_short(self):
+        self.splits(range(len(self.path) - 1 - len(self.grid.long_steps())))
+
+    def split_long(self):
+        grid, count = self.grid, len(self.grid.long_steps())
+
+        def scatter_long(s, own, got, *outs):
+            for k, out in enumerate(outs):
+                at = grid.long_bits(s, k)
+                out[...] = (own[at] + got[at].astype(F32)).astype(out.dtype)
+
+        shape = self.keep.shape[count:]
+        keep, *values = self.tape.run(
+            scatter_long, [(shape, F32)] + [(shape, BF16)] * (grid.long - 1), [self.keep, self.got], True
+        )
+        self.parts = [keep] + [grid.send(v, grid.along(k + 1)) for k, v in enumerate(values)]
+
+    def splits(self, steps):
+        grid = self.grid
+        for i in steps:
+            step = self.path[len(self.path) - 2 - i]
+
+            def scatter_split(s, own, got, keep, send):
+                bit = grid.bit(s, step)
+                keep[...] = own[bit] + got[bit].astype(F32)
+                send[...] = (own[1 - bit] + got[1 - bit].astype(F32)).astype(BF16)
+
+            shape = self.keep.shape[1:]
+            self.keep, value = self.tape.run(
+                scatter_split, [(shape, F32), (shape, BF16)], [self.keep, self.got], True
+            )
+            self.got = grid.exchange(value, step)
+        self.parts = [self.keep, self.got]
 
 
 def tree(values):
@@ -277,14 +321,13 @@
     return jnp.sum(sum_rows(values * values), axis=1, keepdims=True)
 
 
-def norm_tile(entries):
-    row = lax.broadcasted_iota(jnp.int32, (8, LANES), 0)
-    lane = lax.broadcasted_iota(jnp.int32, (8, LANES), 1)
-    tile = jnp.zeros((8, LANES), F32)
+def norm_row(entries):
+    lane = lax.broadcasted_iota(jnp.int32, (1, LANES), 1)
+    row = jnp.zeros((1, LANES), F32)
     for index, weight, direction in entries:
-        tile = jnp.where((row == index) & (lane == 0), squares(weight), tile)
-        tile = jnp.where((row == index) & (lane == 1), squares(direction), tile)
-    return tile
+        row = jnp.where(lane == index, squares(weight), row)
+        row = jnp.where(lane == index + 6, squares(direction), row)
+    return row
 
 
 def make_body(grid):
@@ -319,8 +362,7 @@
             shape = (many,) + mats[0].shape[1:]
             return tape.run(cast, [(shape, BF16)], mats, plain=range(len(mats)))[0]
 
-        gather_a = Gather(grid, tape, casted(attend_in, attend_out))
-        gather_b = Gather(grid, tape, casted(expand_up[None]))
+        gather_a = Gather(grid, tape, casted(attend_in, attend_out), direct=True)
 
         def prepare(s, states_ref, cot_ref, vec, x_ref, x_t, mine_cot, bias_in, bias_up):
             @pl.loop(0, mine)
@@ -350,11 +392,16 @@
              ((1, 2 * units), F32)],
             [states, cotangent, vectors], True, limit=12, moved=6 * MIB, plain=(0, 1),
         )
-        gather_a.line()
+        gather_b = Gather(grid, tape, casted(expand_up[None]))
+        gather_a.merge_long()
+        gather_b.merge(0)
+        gather_a.merge_short()
         gather_c = Gather(grid, tape, casted(expand_down[None]))
-        gather_b.line()
+        gather_b.merge(1)
+        gather_c.merge(0)
+        gather_b.merge(2)
+        gather_c.merge(1)
         a_own, a_oth = (v.reshape(4, width, cols) for v in gather_a.whole())
-        gather_c.line()
 
         def project(x_ref, own, oth, bias, out):
             @pl.loop(0, 3)
@@ -404,6 +451,8 @@
             limit=4, flops=4 * rows * length * width * 4, moved=5 * MIB, exps=rows * twins * 2 * length,
         )
 
+        gather_c.merge(2)
+        b_own, b_oth = (v.reshape(width, units) for v in gather_b.whole())
         block = min(rows, 256)
 
         def hide(context_ref, x_ref, own, oth, vec, hidden, normed, inverse):
@@ -425,7 +474,6 @@
             limit=8, flops=2 * rows * width * width, moved=6 * MIB,
         )
 
-        b_own, b_oth = (v.reshape(width, units) for v in gather_b.whole())
         tile = 256
 
         def lift(hidden_ref, up, bias, active, active_t, slope):
@@ -497,22 +545,25 @@
             scratch=[VMEM((rows, width), F32)],
         )
 
-        def product(left, right, out):
+        def product(left, right, *outs):
             step = min(left.shape[0], 256)
 
             @pl.loop(0, left.shape[0] // step)
             def _(i):
                 at = pl.ds(pl.multiple_of(i * step, step), step)
-                out[at, :] = jnp.dot(left[at, :], right[...], preferred_element_type=F32).astype(out.dtype)
-
-        def weight_grad(left, right, kind):
+                value = jnp.dot(left[at, :], right[...], preferred_element_type=F32)
+                share = value.shape[1] // len(outs)
+                for g, out in enumerate(outs):
+                    out[at, :] = value[:, g * share : (g + 1) * share].astype(out.dtype)
+
+        def weight_grad(left, right, kind, pieces=1):
             shape = (left.shape[0], right.shape[1])
             return tape.run(
-                product, [(shape, kind)], [left, right],
+                product, [((shape[0], shape[1] // pieces), kind)] * pieces, [left, right],
                 limit=6, flops=2 * shape[0] * shape[1] * rows, moved=8 * MIB,
-            )[0]
-
-        sharded = lambda v, many: v.reshape(many, grid.dp, -1, v.shape[-1])
+            )
+
+        sharded = lambda values, many: [v.reshape(many, grid.dp, -1, v.shape[-1]) for v in values]
         scatter_c = Scatter(grid, tape, sharded(weight_grad(lifted[1][1], top16, BF16), 1))
         down_own = weight_grad(lifted[0][1], top16, F32)
         output_oth = grid.core(output)
@@ -533,9 +584,9 @@
             )
 
         sunk = [None, sink_half(1, c_oth)]
+        scatter_b = Scatter(grid, tape, sharded(weight_grad(hidden_t, sunk[1][0], BF16), 1))
         scatter_c.pair(sharded(down_own, 1))
         sunk[0] = sink_half(0, c_own)
-        scatter_b = Scatter(grid, tape, sharded(weight_grad(hidden_t, sunk[1][0], BF16), 1))
         up_own = weight_grad(hidden_t, sunk[0][0], F32)
 
         def surface(grad_own, grad_oth, own, oth, top_ref, normed, inverse, vec, a_own_ref, a_oth_ref,
@@ -576,8 +627,14 @@
             scratch=[VMEM((rows, width), F32), VMEM((rows, width), BF16)],
         )
 
-        scatter_b.pair(sharded(up_own, 1))
-        scatter_c.sides()
+        def pair_up(s, own, oth, out):
+            out[s[3]] = own[...]
+            out[1 - s[3]] = oth[...]
+
+        def paired(own, oth):
+            shape = ((cores,) + own.shape, own.dtype)
+            result = tape.run(pair_up, [shape], [own, oth], True, limit=8, spill=(0,))[0]
+            return result.reshape(pairs, length, width)
 
         def values_back(probs_ref, back_ref, grad, sums):
             sums[...] = jnp.zeros_like(sums)
@@ -599,19 +656,22 @@
             limit=4, flops=4 * rows * length * width, moved=3 * MIB,
         )
 
-        def halves(left_v, right_v, h, kind, left_w, right_w):
-            def both(left_v_ref, right_v_ref, left_w_ref, right_w_ref, out):
+        def attend_grad(h, kind, lefts, rights):
+            def attend_grad_half(*refs):
                 at = slice(h * cols, (h + 1) * cols)
-                for j, (left, right) in enumerate(((left_v_ref, right_v_ref), (left_w_ref, right_w_ref))):
-                    out[j] = jnp.dot(left[...], right[:, at], preferred_element_type=F32).astype(out.dtype)
+                for left, right, out in zip(refs[:2], refs[2:4], refs[4:]):
+                    out[...] = jnp.dot(left[...], right[:, at], preferred_element_type=F32).astype(out.dtype)
 
             return tape.run(
-                both, [((2, width, cols), kind)], [left_v, right_v, left_w, right_w],
+                attend_grad_half, [((width, cols), kind)] * 2, lefts + rights,
                 limit=6, flops=4 * rows * width * cols, moved=5 * MIB,
-            )[0]
-
-        scatter_vo = Scatter(grid, tape, sharded(halves(x_t, grad_v, 1, BF16, mid_t, context), 2))
-        vo_own = halves(x_t, grad_v, 0, F32, mid_t, context)
+            )
+
+        lefts_vo, rights_vo = [x_t, mid_t], [grad_v, context]
+        vo_oth = attend_grad(1, BF16, lefts_vo, rights_vo)
+        layer_output = paired(output, output_oth)
+        scatter_c.split(0)
+        scatter_b.pair(sharded(up_own, 1))
 
         def attend_back(probs_ref, back_ref, qkv_ref, grad_q, grad_k, sums):
             sums[...] = jnp.zeros_like(sums)
@@ -641,11 +701,36 @@
             attend_back, [((rows, width), BF16), ((rows, width), BF16), ((1, width), F32)], [probs, back, qkv],
             limit=4, flops=16 * rows * length * width, moved=6 * MIB,
         )
-        scatter_vo.pair(sharded(vo_own, 2))
-        scatter_b.sides()
-        scatter_c.line()
-        scatter_qk = Scatter(grid, tape, sharded(halves(x_t, grad_q, 1, BF16, x_t, grad_k), 2))
-        qk_own = halves(x_t, grad_q, 0, F32, x_t, grad_k)
+        qk_oth = attend_grad(1, BF16, [x_t, x_t], [grad_q, grad_k])
+        scatter_a = Scatter(grid, tape, sharded([*qk_oth, *vo_oth], 1))
+        scatter_c.split(1)
+        qk_own = attend_grad(0, F32, [x_t, x_t], [grad_q, grad_k])
+        vo_own = attend_grad(0, F32, lefts_vo, rights_vo)
+
+
+        def matrix_step(index):
+            def step(*refs):
+                grad = refs[0][...] + refs[1][...].astype(F32)
+                master, first, second, moment, square, way, kept, tile_ref = refs[2:]
+                moment[...], square[...], value = adam(grad, first[...], second[...])
+                kept[...] = master[...]
+                way[...] = value + DECAY * kept[...]
+                tile_ref[...] = norm_row([(index, kept[0], way[0])])
+
+            return step
+
+        def stepped(step, parts, masters, shapes):
+            outs = [(s, F32) for _ in range(4) for s in shapes] + [((1, LANES), F32)]
+            n, m = len(parts), len(masters)
+            return tape.run(
+                step, outs, parts + masters, limit=6, spill=range(2 * len(shapes)), plain=range(n, n + m), moved=2 * MIB
+            )
+
+        ups = [v[None] for v in (expand_up, first_up, second_up)]
+        downs = [v[None] for v in (expand_down, first_down, second_down)]
+        scatter_b.split(0)
+        scatter_a.pair(sharded([*qk_own, *vo_own], 1))
+        scatter_c.split(2)
 
         def states_back(grad_q_ref, grad_k_ref, grad_v_ref, own, oth, mid_ref, out):
             @pl.loop(0, width // tile)
@@ -665,8 +750,6 @@
         )[0]
 
         states_oth = grid.core(states_own)
-        scatter_qk.pair(sharded(qk_own, 2))
-
         def collect(s, sum_q_ref, sum_v_ref, one, two, up_own_ref, up_oth_ref, out):
             for t in range(cores):
 
@@ -688,71 +771,37 @@
         vector_part = tape.run(
             collect, [(vectors.shape, F32)], [sum_q, sum_v, sums_one, sums_two, sunk[0][1], sunk[1][1]], True
         )[0]
-        vector_total = Total(grid, tape, vector_part)
-        scatter_vo.sides()
-        scatter_b.line()
-
-        def pair_up(s, own, oth, out):
-            out[s[3]] = own[...]
-            out[1 - s[3]] = oth[...]
-
-        def paired(own, oth):
-            shape = ((cores,) + own.shape, own.dtype)
-            result = tape.run(pair_up, [shape], [own, oth], True, limit=8, spill=(0,))[0]
-            return result.reshape(pairs, length, width)
-
-        layer_output = paired(output, output_oth)
-        states_grad = paired(states_own, states_oth)
-        vector_total.line()
-        scatter_qk.sides()
-        scatter_vo.line()
-        vector_total.sides()
-
-        def vector_step(own, oth, vec, first, second, out, moment, square):
-            one, two, direction = adam(own[...] + oth[...], first[...], second[...])
-            moment[...], square[...] = one, two
-            out[...] = vec[...] - RATE * direction
-
-        def matrix_step(index):
-            def step(*refs):
-                grad = sum((ref[...].astype(F32) for ref in refs[1 : grid.long]), refs[0][...])
-                master, first, second, moment, square, way, kept, tile_ref = refs[grid.long :]
-                moment[...], square[...], value = adam(grad, first[...], second[...])
-                kept[...] = master[...]
-                way[...] = value + DECAY * kept[...]
-                tile_ref[...] = norm_tile([(index, kept[0], way[0])])
-
-            return step
-
-        def stepped(step, parts, masters, shapes):
-            outs = [(s, F32) for _ in range(4) for s in shapes] + [((8, LANES), F32)]
-            n, m = len(parts), len(masters)
-            return tape.run(
-                step, outs, parts + masters, limit=6, spill=range(2 * len(shapes)), plain=range(n, n + m), moved=2 * MIB
-            )
-
-        ups = [v[None] for v in (expand_up, first_up, second_up)]
-        downs = [v[None] for v in (expand_down, first_down, second_down)]
+        vector_oth = grid.core(vector_part)
+        half = vectors.shape[0] // cores
+
+        def vector_half(s, own, oth, out):
+            for t in range(cores):
+
+                @pl.when(s[3] == t)
+                def _():
+                    at = slice(t * half, (t + 1) * half)
+                    out[...] = own[at] + oth[at]
+
+        vector_share = tape.run(vector_half, [((half, width), F32)], [vector_part, vector_oth], True)[0]
         moment_down, square_down, way_down, kept_down, tile_down = stepped(
             matrix_step(5), scatter_c.parts, downs, [downs[0].shape]
         )
-        scatter_qk.line()
+        scatter_b.split(1)
+        scatter_a.split_short()
+        states_grad = paired(states_own, states_oth)
+        scatter_b.split(2)
+        scatter_a.split_long()
         moment_up, square_up, way_up, kept_up, tile_up = stepped(
             matrix_step(4), scatter_b.parts, ups, [ups[0].shape]
         )
-        updated_vectors, moment_vectors, square_vectors = tape.run(
-            vector_step, [(vectors.shape, F32)] * 3,
-            vector_total.pair + [vectors, vector_first, vector_second], spill=(0, 1, 2), plain=(2, 3, 4),
-        )
 
         def attend_step(*refs):
-            n = grid.long
-            vo, qk = refs[:n], refs[n : 2 * n]
-            m_in, f_in, s_in, m_out, f_out, s_out, tile_up_ref, tile_down_ref = refs[2 * n : 2 * n + 8]
-            mo_in, mo_out, sq_in, sq_out, way_in, way_out, kept_in, kept_out, tile_ref = refs[2 * n + 8 :]
-            whole = lambda parts, j: sum((ref[j].astype(F32) for ref in parts[1:]), parts[0][j])
+            n = len(scatter_a.parts)
+            m_in, f_in, s_in, m_out, f_out, s_out, tile_up_ref, tile_down_ref, share = refs[n : n + 9]
+            mo_in, mo_out, sq_in, sq_out, way_in, way_out, kept_in, kept_out, load = refs[n + 9 :]
             entries = []
-            for j, grad in enumerate((whole(qk, 0), whole(qk, 1), whole(vo, 0), whole(vo, 1))):
+            for j in range(4):
+                grad = sum((ref[j].astype(F32) for ref in refs[1:n]), refs[0][j])
                 i = j if j < 3 else 0
                 m, f, s, mo, sq, kept, way = (
                     (m_in, f_in, s_in, mo_in, sq_in, kept_in, way_in)
@@ -763,37 +812,52 @@
                 kept[i] = m[i]
                 way[i] = value + DECAY * kept[i]
                 entries.append((j, kept[i], way[i]))
-            tile_ref[...] = norm_tile(entries) + tile_up_ref[...] + tile_down_ref[...]
-
-        ins = scatter_vo.parts + scatter_qk.parts + [attend_in, first_in, second_in, attend_out, first_out, second_out]
+            load[...] = jnp.zeros_like(load)
+            load[0:half] = share[...]
+            load[half : half + 1, 0:LANES] = norm_row(entries) + tile_up_ref[...] + tile_down_ref[...]
+
         shapes = [attend_in.shape, attend_out.shape]
-        (
-            moment_in, moment_out, square_in, square_out, way_in, way_out, kept_in, kept_out, tiles
-        ) = tape.run(
-            attend_step, [(s, F32) for _ in range(4) for s in shapes] + [((8, LANES), F32)], ins + [tile_up, tile_down],
-            limit=6, spill=range(4), plain=range(2 * grid.long, 2 * grid.long + 6), moved=2 * MIB,
-        )
-        tile_total = Total(grid, tape, tiles)
-        tile_total.line()
-        tile_total.sides()
-
-        def update(own, oth, *refs):
-            masters, ways, outs = refs[:4], refs[4:8], refs[8:]
-            norms = jnp.sqrt(own[...] + oth[...])
-            outs[8][...] = norms.T[0:2, 0:6]
-            trust = RATE * (norms[:, 0:1] / norms[:, 1:2])
+        masters = [attend_in, first_in, second_in, attend_out, first_out, second_out]
+        moment_in, moment_out, square_in, square_out, way_in, way_out, kept_in, kept_out, load = tape.run(
+            attend_step, [(s, F32) for _ in range(4) for s in shapes] + [((8, width), F32)],
+            scatter_a.parts + masters + [tile_up, tile_down, vector_share],
+            limit=6, spill=range(4), plain=range(grid.long, grid.long + 6), moved=2 * MIB,
+        )
+        total = Total(grid, tape, load)
+        total.line()
+        total.sides()
+
+        def update(s, own, oth, vec, vec_first, vec_second, *refs):
+            masters, ways, outs, grad = refs[:4], refs[4:8], refs[8:-1], refs[-1]
+            norms = jnp.sqrt(own[half : half + 1, 0:LANES] + oth[half : half + 1, 0:LANES])
+            outs[8][0:1] = norms[:, 0:6]
+            outs[8][1:2] = norms[:, 6:12]
             for i, first in enumerate((0, 3, 4, 5)):
                 for j in range(masters[i].shape[0]):
-                    value = masters[i][j] - trust[first + j : first + j + 1] * ways[i][j]
+                    m = first + j
+                    trust = RATE * (norms[:, m : m + 1] / norms[:, 6 + m : 7 + m])
+                    value = masters[i][j] - trust * ways[i][j]
                     outs[i][j], outs[4 + i][j] = value, value.astype(BF16)
+            for t in range(cores):
+
+                @pl.when(s[3] == t)
+                def _():
+                    grad[t * half : (t + 1) * half] = own[0:half]
+                    grad[(1 - t) * half : (2 - t) * half] = oth[0:half]
+
+            outs[10][...], outs[11][...], direction = adam(grad[...], vec_first[...], vec_second[...])
+            outs[9][...] = vec[...] - RATE * direction
 
         masters = [kept_in, kept_out, kept_up, kept_down]
         results = tape.run(
             update,
-            [(m.shape, F32) for m in masters] + [(m.shape, BF16) for m in masters] + [((2, 6), F32)],
-            tile_total.pair + masters + [way_in, way_out, way_up, way_down],
-            limit=6, spill=range(9), moved=2 * MIB,
-        )
+            [(m.shape, F32) for m in masters] + [(m.shape, BF16) for m in masters] + [((2, 6), F32)]
+            + [(vectors.shape, F32)] * 3,
+            total.pair + [vectors, vector_first, vector_second] + masters + [way_in, way_out, way_up, way_down],
+            True, limit=6, spill=range(12), plain=(2, 3, 4), moved=2 * MIB,
+            scratch=[VMEM(vectors.shape, F32)],
+        )
+        updated_vectors, moment_vectors, square_vectors = results[9:12]
 
         def native(values):
             values = list(values)

time: 273 us -> 237 us (0.87)
  starting transfers between devices: 70.8 us -> 47.5 us
  waiting for transfers between devices: 117 us -> 99.8 us
  Pallas kernels: 76.2 us -> 81.9 us
    ppermute x61 -> x45, starting transfers between devices: 70.8 us -> 47.5 us  [send(): return lax.ppermute(value, AXES, pairs)]
    ppermute x61 -> x45, waiting for transfers between devices: 117 us -> 99.8 us  [send(): return lax.ppermute(value, AXES, pairs)]
    pallas_call x56 -> x58, Pallas kernels: 76.2 us -> 81.9 us  [run(): pl.pallas_call(chain, out_shape=shapes, in_specs=[pl.BlockSpec(memory_spa...]
    unnamed x42 -> x40, local copies, waits for them, and re-layouts: 6.46 us -> 5.52 us
  transfers between devices with their start and end apart: 61 -> 45, of which waited for: 24 -> 26; matrix products, arithmetic and copies ran while one was open for 0% -> 0% of each run, Pallas kernels for 20% -> 29%
where the time goes in v3:
time: 237 us
  waiting for transfers between devices  99.8 us (42%)
  Pallas kernels  81.9 us (35%)
  starting transfers between devices  47.5 us (20%)
  local copies, waits for them, and re-layouts  5.68 us (2%)
    ppermute x45, waiting for transfers between devices, send(): return lax.ppermute(value, AXES, pairs)  99.8 us
    pallas_call x58, Pallas kernels, run(): pl.pallas_call(chain, out_shape=shapes, in_specs=[pl.BlockSpec(memory_spa...  81.9 us
    ppermute x45, starting transfers between devices, send(): return lax.ppermute(value, AXES, pairs)  47.5 us
    unnamed x40, local copies, waits for them, and re-layouts  5.52 us
  transfers between devices with their start and end apart: 45, of which 26 were waited for; matrix products, arithmetic and copies ran while one was open for 0% of the time, Pallas kernels for 29%

profile of v3, /device:TPU:0, one launch (start us, length us, event | category | flops | bytes accessed | tf_op | source)
XLA Modules:
  0.0 237.0 jit_solution(5059436237437529823)
XLA Ops:
  2.5 3.1 %collective-permute-start = (bf16[4,48,384]{2,1,0:T(8,128)(2,1)S(1)}, bf16[4,48,384]{2,1,0:T(8,128)(2,1)S(1)}, u32[]{:S(2)}, u32[]{:S(2)}) collective-permute-start(bf16[4,48,384]{2,1,0:T(8,128)(2,1)S(1)} %get-tuple-element.206.refs_2_), channel_id=1, source_target_pairs={{0,8},{1,9},{2,10},{3,11},{4,12},{5,13},{6,14},{7,15},{8,0},{9,1},... | collective-permute-start | bytes 442376 | tf_op jit(solution)/shard_map/ppermute | solution.py:56
  5.6 2.6 %collective-permute-start.1 = (bf16[4,48,384]{2,1,0:T(8,128)(2,1)S(1)}, bf16[4,48,384]{2,1,0:T(8,128)(2,1)S(1)}, u32[]{:S(2)}, u32[]{:S(2)}) collective-permute-start(bf16[4,48,384]{2,1,0:T(8,128)(2,1)S(1)} %get-tuple-element.206.refs_2_), channel_id=1, source_target_pairs={{0,16},{1,17},{2,18},{3,19},{4,20},{5,21},{6,22},{7,23},{8,24},{9,... | collective-permute-start | bytes 442376 | tf_op jit(solution)/shard_map/ppermute | solution.py:56
  9.0 1.4 copy-done
  10.4 1.4 copy-done.1
  13.6 6.0 %collective-permute-done.1.refs_4_ = bf16[4,48,384]{2,1,0:T(8,128)(2,1)S(1)} collective-permute-done((bf16[4,48,384]{2,1,0:T(8,128)(2,1)S(1)}, bf16[4,48,384]{2,1,0:T(8,128)(2,1)S(1)}, u32[]{:S(2)}, u32[]{:S(2)}) %collective-permute-start.1) | collective-permute-done | bytes 147488 | tf_op jit(solution)/shard_map/ppermute | solution.py:56
  20.2 1.6 collective-permute-start.4
  21.8 3.3 %collective-permute-start.3 = (bf16[1,48,1536]{2,1,0:T(8,128)(2,1)S(1)}, bf16[1,48,1536]{2,1,0:T(8,128)(2,1)S(1)}, u32[]{:S(2)}, u32[]{:S(2)}) collective-permute-start(bf16[1,48,1536]{2,1,0:T(8,128)(2,1)S(1)} %get-tuple-element.208.refs_2_), channel_id=1, source_target_pairs={{0,16},{1,17},{2,18},{3,19},{4,20},{5,21},{6,22},{7,23},{8,24},{9,... | collective-permute-start | bytes 442376 | tf_op jit(solution)/shard_map/ppermute | solution.py:56
  25.1 5.8 %collective-permute-done.3.refs_3_ = bf16[1,48,1536]{2,1,0:T(8,128)(2,1)S(1)} collective-permute-done((bf16[1,48,1536]{2,1,0:T(8,128)(2,1)S(1)}, bf16[1,48,1536]{2,1,0:T(8,128)(2,1)S(1)}, u32[]{:S(2)}, u32[]{:S(2)}) %collective-permute-start.3) | collective-permute-done | bytes 147488 | tf_op jit(solution)/shard_map/ppermute | solution.py:56
  32.7 2.0 collective-permute-start.5
  34.7 6.7 %collective-permute-done.5.refs_3_ = bf16[2,1,48,1536]{3,2,1,0:T(8,128)(2,1)S(1)} collective-permute-done((bf16[2,1,48,1536]{3,2,1,0:T(8,128)(2,1)S(1)}, bf16[2,1,48,1536]{3,2,1,0:T(8,128)(2,1)S(1)}, u32[]{:S(2)}, u32[]{:S(2)}) %collective-permute-start.5) | collective-permute-done | bytes 294944 | tf_op jit(solution)/shard_map/ppermute | solution.py:56
  42.6 2.0 collective-permute-start.6
  44.6 5.7 %collective-permute-done.6.refs_3_ = bf16[1,96,768]{2,1,0:T(8,128)(2,1)S(1)} collective-permute-done((bf16[1,96,768]{2,1,0:T(8,128)(2,1)S(1)}, bf16[1,96,768]{2,1,0:T(8,128)(2,1)S(1)}, u32[]{:S(2)}, u32[]{:S(2)}) %collective-permute-start.6) | collective-permute-done | bytes 147488 | tf_op jit(solution)/shard_map/ppermute | solution.py:56
  50.9 1.9 collective-permute-done.7.refs_3_
  53.4 4.2 %collective-permute-done.8.refs_3_ = bf16[2,1,96,768]{3,2,1,0:T(8,128)(2,1)S(1)} collective-permute-done((bf16[2,1,96,768]{3,2,1,0:T(8,128)(2,1)S(1)}, bf16[2,1,96,768]{3,2,1,0:T(8,128)(2,1)S(1)}, u32[]{:S(2)}, u32[]{:S(2)}) %collective-permute-start.8) | collective-permute-done | bytes 294944 | tf_op jit(solution)/shard_map/ppermute | solution.py:56
  59.0 3.0 %collective-permute-start.12 = (bf16[2,2,2,1,48,1536]{5,4,3,2,1,0:T(8,128)(2,1)S(1)}, bf16[2,2,2,1,48,1536]{5,4,3,2,1,0:T(8,128)(2,1)S(1)}, u32[]{:S(2)}, u32[]{:S(2)}) collective-permute-start(bf16[2,2,2,1,48,1536]{5,4,3,2,1,0:T(8,128)(2,1)S(1)} %get-tuple-element.231.refs_2_), channel_id=1, source_target_pairs={{0,4},{1,3},{2,6},{3,1},{4,0},{5,7},{6,2},{7,5},{8,12},{9,11},{10,... | collective-permute-start | bytes 3538952 | tf_op jit(solution)/shard_map/ppermute | solution.py:56
  62.0 1.5 collective-permute-done.10
  63.6 3.0 %project.1 = (bf16[3,512,768]{2,1,0:T(8,128)(2,1)S(1)}, f32[8,128]{1,0:T(8,128)S(1)}) custom-call(f32[8,128]{1,0:T(8,128)S(1)} %get-tuple-element.222.refs_0_, bf16[512,768]{1,0:T(8,128)(2,1)S(1)} %get-tuple-element.223.refs_1_.refs_2_, bf16[4,768,384]{2,1,0:T(8,128)(2,1)S(1)} %bitcast.60, bf16[4,768,384]{2,1,0:T(8,128)(2,1)S(1)} %bitcast.64, ...), custom_call_target="tpu_custom_call" | custom-call | flops 1811939328 | bytes 8388608 | tf_op jit(solution)/shard_map/project/pallas_call | solution.py:129
  66.5 4.6 %attend.1 = (bf16[512,1536]{1,0:T(8,128)(2,1)S(1)}, bf16[512,768]{1,0:T(8,128)(2,1)S(1)}, f32[8,128]{1,0:T(8,128)S(1)}) custom-call(s32[8]{0:T(128)S(1)} %concatenate.3.refs_0_, f32[8,128]{1,0:T(8,128)S(1)} %get-tuple-element.226.refs_1_, bf16[3,512,768]{2,1,0:T(8,128)(2,1)S(1)} %get-tuple-element.227.refs_2_.refs_3_), custom_call_target="tpu_custom_call" | custom-call | flops 805306368 | bytes 5242880 | tf_op jit(solution)/shard_map/attend/pallas_call | solution.py:129
  71.2 7.1 %collective-permute-done.11.refs_3_ = bf16[2,2,1,96,768]{4,3,2,1,0:T(8,128)(2,1)S(1)} collective-permute-done((bf16[2,2,1,96,768]{4,3,2,1,0:T(8,128)(2,1)S(1)}, bf16[2,2,1,96,768]{4,3,2,1,0:T(8,128)(2,1)S(1)}, u32[]{:S(2)}, u32[]{:S(2)}) %collective-permute-start.11) | collective-permute-done | bytes 589856 | tf_op jit(solution)/shard_map/ppermute | solution.py:56
  78.9 3.3 %collective-permute-done.12.refs_3_ = bf16[2,2,2,1,48,1536]{5,4,3,2,1,0:T(8,128)(2,1)S(1)} collective-permute-done((bf16[2,2,2,1,48,1536]{5,4,3,2,1,0:T(8,128)(2,1)S(1)}, bf16[2,2,2,1,48,1536]{5,4,3,2,1,0:T(8,128)(2,1)S(1)}, u32[]{:S(2)}, u32[]{:S(2)}) %collective-permute-start.12) | collective-permute-done | bytes 1179680 | tf_op jit(solution)/shard_map/ppermute | solution.py:56
  83.1 1.8 collective-permute-start.14
  84.9 1.3 hide.1
  86.2 3.4 %_lambda_.2 = (bf16[512,1536]{1,0:T(8,128)(2,1)S(1)}, bf16[1536,512]{1,0:T(8,128)(2,1)S(1)}, bf16[512,1536]{1,0:T(8,128)(2,1)S(1)}, f32[8,128]{1,0:T(8,128)S(1)}) custom-call(f32[8,128]{1,0:T(8,128)S(1)} %get-tuple-element.234.refs_0_, bf16[512,768]{1,0:T(8,128)(2,1)S(1)} %get-tuple-element.235.refs_1_, bf16[768,1536]{1,0:T(8,128)(2,1)S(1)} %bitcast.74, ...), custom_call_target="tpu_custom_call" | custom-call | flops 1207959552 | bytes 8388608 | tf_op jit(solution)/shard_map/<lambda>/pallas_call | solution.py:129
  89.6 3.4 %_lambda_.3 = (bf16[512,1536]{1,0:T(8,128)(2,1)S(1)}, bf16[1536,512]{1,0:T(8,128)(2,1)S(1)}, bf16[512,1536]{1,0:T(8,128)(2,1)S(1)}, f32[8,128]{1,0:T(8,128)S(1)}) custom-call(f32[8,128]{1,0:T(8,128)S(1)} %get-tuple-element.238.refs_0_, bf16[512,768]{1,0:T(8,128)(2,1)S(1)} %get-tuple-element.235.refs_1_, bf16[768,1536]{1,0:T(8,128)(2,1)S(1)} %bitcast.76, ...), custom_call_target="tpu_custom_call" | custom-call | flops 1207959552 | bytes 8388608 | tf_op jit(solution)/shard_map/<lambda>/pallas_call | solution.py:129
  93.2 6.1 %collective-permute-done.14.refs_3_ = bf16[2,2,2,1,96,768]{5,4,3,2,1,0:T(8,128)(2,1)S(1)} collective-permute-done((bf16[2,2,2,1,96,768]{5,4,3,2,1,0:T(8,128)(2,1)S(1)}, bf16[2,2,2,1,96,768]{5,4,3,2,1,0:T(8,128)(2,1)S(1)}, u32[]{:S(2)}, u32[]{:S(2)}) %collective-permute-start.14) | collective-permute-done | bytes 1179680 | tf_op jit(solution)/shard_map/ppermute | solution.py:56
  100.1 1.7 lower_half.1
  101.9 2.8 %collective-permute-done.15 = bf16[1,16,96,768]{3,2,1,0:T(8,128)(2,1)S(1)} collective-permute-done((bf16[1,16,96,768]{3,2,1,0:T(8,128)(2,1)S(1)}, bf16[1,16,96,768]{3,2,1,0:T(8,128)(2,1)S(1)}, u32[]{:S(2)}, u32[]{:S(2)}) %collective-permute-start.15) | collective-permute-done | bytes 2359328 | tf_op jit(solution)/shard_map/ppermute | solution.py:56
  104.6 4.0 %lower.1 = (bf16[512,768]{1,0:T(8,128)(2,1)S(1)}, f32[512,768]{1,0:T(8,128)S(1)}, bf16[512,768]{1,0:T(8,128)(2,1)S(1)}, f32[8,768]{1,0:T(8,128)S(1)}, f32[8,128]{1,0:T(8,128)S(1)}) custom-call(s32[8]{0:T(128)S(1)} %concatenate.3.refs_0_, f32[8,128]{1,0:T(8,128)S(1)} %get-tuple-element.245.refs_1_, f32[512,768]{1,0:T(8,128)S(1)} %get-tuple-element.246.refs_2_, ...), custom_call_target="tpu_custom_call" | custom-call | flops 1207959552 | bytes 14680064 | tf_op jit(solution)/shard_map/lower/pallas_call | solution.py:129
  108.6 2.2 product.4
  111.1 2.2 product.5
  113.3 2.5 %sink.2 = (bf16[512,1536]{1,0:T(8,128)(2,1)S(1)}, f32[1,1536]{1,0:T(1,128)S(1)}, f32[8,128]{1,0:T(8,128)S(1)}) custom-call(f32[8,128]{1,0:T(8,128)S(1)} %get-tuple-element.255.refs_0_, bf16[512,768]{1,0:T(8,128)(2,1)S(1)} %get-tuple-element.252.refs_2_.refs_1_, bf16[1536,768]{1,0:T(8,128)(2,1)S(1)} %bitcast.69, bf16[512,1536]{1,0:T(8,128)(2,1)S(1)} %get-tuple-element.256.refs_3_), custom_call_target="tpu_custom_call" | custom-call | flops 1207959552 | bytes 8388608 | tf_op jit(solution)/shard_map/sink/pallas_call | solution.py:129
  115.8 1.7 product.6
  118.9 1.9 collective-permute-start.18
  120.8 2.5 %sink.3 = (bf16[512,1536]{1,0:T(8,128)(2,1)S(1)}, f32[1,1536]{1,0:T(1,128)S(1)}, f32[8,128]{1,0:T(8,128)S(1)}) custom-call(f32[8,128]{1,0:T(8,128)S(1)} %get-tuple-element.263.refs_0_, bf16[512,768]{1,0:T(8,128)(2,1)S(1)} %get-tuple-element.252.refs_2_.refs_1_, bf16[1536,768]{1,0:T(8,128)(2,1)S(1)} %bitcast.73, bf16[512,1536]{1,0:T(8,128)(2,1)S(1)} %get-tuple-element.264.refs_3_), custom_call_target="tpu_custom_call" | custom-call | flops 1207959552 | bytes 8388608 | tf_op jit(solution)/shard_map/sink/pallas_call | solution.py:129
  123.3 1.7 product.7
  125.0 5.1 %surface.1 = (f32[512,768]{1,0:T(8,128)S(1)}, bf16[768,512]{1,0:T(8,128)(2,1)S(1)}, bf16[512,768]{1,0:T(8,128)(2,1)S(1)}, f32[8,768]{1,0:T(8,128)S(1)}, f32[8,128]{1,0:T(8,128)S(1)}) custom-call(f32[8,128]{1,0:T(8,128)S(1)} %get-tuple-element.267.refs_0_, bf16[512,1536]{1,0:T(8,128)(2,1)S(1)} %get-tuple-element.266.refs_2_.refs_1_, ...), custom_call_target="tpu_custom_call" | custom-call | flops 3019898880 | bytes 14680064 | tf_op jit(solution)/shard_map/surface/pallas_call | solution.py:129
  130.1 1.2 values_back.1
  132.4 1.8 pair_up.2
  137.0 1.9 collective-permute-start.21
  139.4 6.6 %attend_back.1 = (bf16[512,768]{1,0:T(8,128)(2,1)S(1)}, bf16[512,768]{1,0:T(8,128)(2,1)S(1)}, f32[1,768]{1,0:T(1,128)S(1)}, f32[8,128]{1,0:T(8,128)S(1)}) custom-call(f32[8,128]{1,0:T(8,128)S(1)} %get-tuple-element.286.refs_0_, bf16[512,1536]{1,0:T(8,128)(2,1)S(1)} %get-tuple-element.271.refs_1_, bf16[512,768]{1,0:T(8,128)(2,1)S(1)} %get-tuple-element.272.refs_2_, ...), custom_call_target="tpu_custom_call" | custom-call | flops 805306368 | bytes 6291456 | tf_op jit(solution)/shard_map/attend_back/pallas_call | solution.py:129
  147.1 8.1 %collective-permute-done.20.refs_3_ = bf16[2,2,1,96,768]{4,3,2,1,0:T(8,128)(2,1)S(1)} collective-permute-done((bf16[2,2,1,96,768]{4,3,2,1,0:T(8,128)(2,1)S(1)}, bf16[2,2,1,96,768]{4,3,2,1,0:T(8,128)(2,1)S(1)}, u32[]{:S(2)}, u32[]{:S(2)}) %collective-permute-start.20) | collective-permute-done | bytes 589856 | tf_op jit(solution)/shard_map/ppermute | solution.py:56
  155.8 2.5 %collective-permute-done.21.refs_3_ = bf16[2,2,2,1,48,1536]{5,4,3,2,1,0:T(8,128)(2,1)S(1)} collective-permute-done((bf16[2,2,2,1,48,1536]{5,4,3,2,1,0:T(8,128)(2,1)S(1)}, bf16[2,2,2,1,48,1536]{5,4,3,2,1,0:T(8,128)(2,1)S(1)}, u32[]{:S(2)}, u32[]{:S(2)}) %collective-permute-start.21) | collective-permute-done | bytes 1179680 | tf_op jit(solution)/shard_map/ppermute | solution.py:56
  162.4 1.7 collective-permute-start.30
  164.0 3.1 %collective-permute-done.26.refs_3_ = bf16[2,1,96,768]{3,2,1,0:T(8,128)(2,1)S(1)} collective-permute-done((bf16[2,1,96,768]{3,2,1,0:T(8,128)(2,1)S(1)}, bf16[2,1,96,768]{3,2,1,0:T(8,128)(2,1)S(1)}, u32[]{:S(2)}, u32[]{:S(2)}) %collective-permute-start.26) | collective-permute-done | bytes 294944 | tf_op jit(solution)/shard_map/ppermute | solution.py:56
  167.8 3.0 %states_back.1 = (f32[512,768]{1,0:T(8,128)S(1)}, f32[8,128]{1,0:T(8,128)S(1)}) custom-call(f32[8,128]{1,0:T(8,128)S(1)} %get-tuple-element.310.refs_0_, bf16[512,768]{1,0:T(8,128)(2,1)S(1)} %get-tuple-element.288.refs_3_.refs_1_, bf16[512,768]{1,0:T(8,128)(2,1)S(1)} %get-tuple-element.289.refs_4_.refs_2_, bf16[512,768]{1,0:T(8,128)(2,1)S(1)} %get-tuple-element.276.refs_3_, ...), custom_call_target="tpu_custom_call" | custom-call | flops 1811939328 | bytes 8388608 | tf_op jit(solution)/shard_map/states_back/pallas_call | solution.py:129
  172.0 1.3 collective-permute-start.27
  174.9 7.0 %collective-permute-done.28.refs_2_ = bf16[1,96,768]{2,1,0:T(8,128)(2,1)S(1)} collective-permute-done((bf16[1,96,768]{2,1,0:T(8,128)(2,1)S(1)}, bf16[1,96,768]{2,1,0:T(8,128)(2,1)S(1)}, u32[]{:S(2)}, u32[]{:S(2)}) %collective-permute-start.28) | collective-permute-done | bytes 147488 | tf_op jit(solution)/shard_map/ppermute | solution.py:56
  181.9 1.2 step.2
  185.2 1.7 collective-permute-start.33
  186.9 2.3 collective-permute-start.32
  189.2 2.4 %pair_up.3 = (f32[2,512,768]{2,1,0:T(8,128)}, f32[8,128]{1,0:T(8,128)S(1)}) custom-call(s32[8]{0:T(128)S(1)} %concatenate.3.refs_0_, f32[8,128]{1,0:T(8,128)S(1)} %get-tuple-element.330.refs_1_, f32[512,768]{1,0:T(8,128)S(1)} %get-tuple-element.331.refs_2_, f32[512,768]{1,0:T(8,128)S(1)} %collective-permute-done.31.refs_3_), custom_call_target="tpu_custom_call" | custom-call | tf_op jit(solution)/shard_map/pair_up/pallas_call | solution.py:129
  191.6 5.0 %collective-permute-done.32.refs_3_ = bf16[2,1,48,1536]{3,2,1,0:T(8,128)(2,1)S(1)} collective-permute-done((bf16[2,1,48,1536]{3,2,1,0:T(8,128)(2,1)S(1)}, bf16[2,1,48,1536]{3,2,1,0:T(8,128)(2,1)S(1)}, u32[]{:S(2)}, u32[]{:S(2)}) %collective-permute-start.32) | collective-permute-done | bytes 294944 | tf_op jit(solution)/shard_map/ppermute | solution.py:56
  199.9 2.9 %collective-permute-start.36 = (bf16[4,48,384]{2,1,0:T(8,128)(2,1)S(1)}, bf16[4,48,384]{2,1,0:T(8,128)(2,1)S(1)}, u32[]{:S(2)}, u32[]{:S(2)}) collective-permute-start(bf16[4,48,384]{2,1,0:T(8,128)(2,1)S(1)} %get-tuple-element.345), channel_id=1, source_target_pairs={{0,16},{1,17},{2,18},{3,19},{4,20},{5,21},{6,22},{7,23},{8,24},{9,... | collective-permute-start | bytes 442376 | tf_op jit(solution)/shard_map/ppermute | solution.py:56
  203.3 10.9 %collective-permute-done.34.refs_2_ = bf16[1,48,1536]{2,1,0:T(8,128)(2,1)S(1)} collective-permute-done((bf16[1,48,1536]{2,1,0:T(8,128)(2,1)S(1)}, bf16[1,48,1536]{2,1,0:T(8,128)(2,1)S(1)}, u32[]{:S(2)}, u32[]{:S(2)}) %collective-permute-start.34) | collective-permute-done | bytes 147488 | tf_op jit(solution)/shard_map/ppermute | solution.py:56
  214.2 1.2 step.3
  215.5 1.9 collective-permute-done.36.refs_3_
  217.4 1.2 attend_step.1
  218.6 2.7 %collective-permute-start.38 = (f32[8,768]{1,0:T(8,128)S(1)}, f32[8,768]{1,0:T(8,128)S(1)}, u32[]{:S(2)}, u32[]{:S(2)}) collective-permute-start(f32[8,768]{1,0:T(8,128)S(1)} %get-tuple-element.351.refs_1_), channel_id=1, source_target_pairs={{0,8},{1,9},{2,10},{3,11},{4,12},{5,13},{6,14},{7,15},{8,0},{9,1},... | collective-permute-start | bytes 73736 | tf_op jit(solution)/shard_map/ppermute | solution.py:56
  221.4 2.4 collective-permute-start.40
  223.7 2.4 collective-permute-done.39.refs_3_
  227.1 1.8 collective-permute-start.42
  228.9 1.6 collective-permute-start.43
  231.0 2.6 %collective-permute-done.43.refs_4_ = f32[8,768]{1,0:T(8,128)S(1)} collective-permute-done((f32[8,768]{1,0:T(8,128)S(1)}, f32[8,768]{1,0:T(8,128)S(1)}, u32[]{:S(2)}, u32[]{:S(2)}) %collective-permute-start.43) | collective-permute-done | bytes 24608 | tf_op jit(solution)/shard_map/ppermute | solution.py:56
  234.9 2.0 update.1
  (127 shorter events, 36.7 us)
Async XLA Ops:
  0.7 0.9 copy-start.6
  1.6 0.9 copy-start.8
  2.5 11.1 %collective-permute-start = (bf16[4,48,384]{2,1,0:T(8,128)(2,1)S(1)}, bf16[4,48,384]{2,1,0:T(8,128)(2,1)S(1)}, u32[]{:S(2)}, u32[]{:S(2)}) collective-permute-start(bf16[4,48,384]{2,1,0:T(8,128)(2,1)S(1)} %get-tuple-element.206.refs_2_), channel_id=1, source_target_pairs={{0,8},{1,9},{2,10},{3,11},{4,12},{5,13},{6,14},{7,15},{8,0},{9,1},... | collective-permute-start | bytes 442376 | tf_op jit(solution)/shard_map/ppermute | solution.py:56
  5.6 14.0 %collective-permute-start.1 = (bf16[4,48,384]{2,1,0:T(8,128)(2,1)S(1)}, bf16[4,48,384]{2,1,0:T(8,128)(2,1)S(1)}, u32[]{:S(2)}, u32[]{:S(2)}) collective-permute-start(bf16[4,48,384]{2,1,0:T(8,128)(2,1)S(1)} %get-tuple-element.206.refs_2_), channel_id=1, source_target_pairs={{0,16},{1,17},{2,18},{3,19},{4,20},{5,21},{6,22},{7,23},{8,24},{9,... | collective-permute-start | bytes 442376 | tf_op jit(solution)/shard_map/ppermute | solution.py:56
  8.2 11.4 %collective-permute-start.2 = (bf16[4,48,384]{2,1,0:T(8,128)(2,1)S(1)}, bf16[4,48,384]{2,1,0:T(8,128)(2,1)S(1)}, u32[]{:S(2)}, u32[]{:S(2)}) collective-permute-start(bf16[4,48,384]{2,1,0:T(8,128)(2,1)S(1)} %get-tuple-element.206.refs_2_), channel_id=1, source_target_pairs={{0,24},{1,25},{2,26},{3,27},{4,28},{5,29},{6,30},{7,31},{8,16},{9,... | collective-permute-start | bytes 442376 | tf_op jit(solution)/shard_map/ppermute | solution.py:56
  9.0 1.4 copy-start
  10.4 1.4 copy-start.1
  12.6 1.0 copy-start.5
  13.6 21.1 %copy-start.4 = (f32[96,768]{1,0:T(8,128)S(1)}, f32[96,768]{1,0:T(8,128)}, u32[]{:S(2)}) copy-start(f32[96,768]{1,0:T(8,128)} %param.26) | copy-start | bytes 884740
  20.2 11.2 %collective-permute-start.4 = (bf16[2,2,4,48,384]{4,3,2,1,0:T(8,128)(2,1)S(1)}, bf16[2,2,4,48,384]{4,3,2,1,0:T(8,128)(2,1)S(1)}, u32[]{:S(2)}, u32[]{:S(2)}) collective-permute-start(bf16[2,2,4,48,384]{4,3,2,1,0:T(8,128)(2,1)S(1)} %get-tuple-element.210.refs_2_), channel_id=1, source_target_pairs={{0,2},{1,5},{2,0},{3,7},{4,6},{5,1},{6,4},{7,3},{8,10},{9,13},{10,... | collective-permute-start | bytes 1769480 | tf_op jit(solution)/shard_map/ppermute | solution.py:56
  21.8 9.1 %collective-permute-start.3 = (bf16[1,48,1536]{2,1,0:T(8,128)(2,1)S(1)}, bf16[1,48,1536]{2,1,0:T(8,128)(2,1)S(1)}, u32[]{:S(2)}, u32[]{:S(2)}) collective-permute-start(bf16[1,48,1536]{2,1,0:T(8,128)(2,1)S(1)} %get-tuple-element.208.refs_2_), channel_id=1, source_target_pairs={{0,16},{1,17},{2,18},{3,19},{4,20},{5,21},{6,22},{7,23},{8,24},{9,... | collective-permute-start | bytes 442376 | tf_op jit(solution)/shard_map/ppermute | solution.py:56
  32.1 26.1 %collective-permute-start.9 = (bf16[2,2,2,4,48,384]{5,4,3,2,1,0:T(8,128)(2,1)S(1)}, bf16[2,2,2,4,48,384]{5,4,3,2,1,0:T(8,128)(2,1)S(1)}, u32[]{:S(2)}, u32[]{:S(2)}) collective-permute-start(bf16[2,2,2,4,48,384]{5,4,3,2,1,0:T(8,128)(2,1)S(1)} %get-tuple-element.221.refs_2_), channel_id=1, source_target_pairs={{0,4},{1,3},{2,6},{3,1},{4,0},{5,7},{6,2},{7,5},{8,12},{9,11},{10,... | collective-permute-start | bytes 3538952 | tf_op jit(solution)/shard_map/ppermute | solution.py:56
  32.7 8.7 %collective-permute-start.5 = (bf16[2,1,48,1536]{3,2,1,0:T(8,128)(2,1)S(1)}, bf16[2,1,48,1536]{3,2,1,0:T(8,128)(2,1)S(1)}, u32[]{:S(2)}, u32[]{:S(2)}) collective-permute-start(bf16[2,1,48,1536]{3,2,1,0:T(8,128)(2,1)S(1)} %get-tuple-element.213.refs_2_), channel_id=1, source_target_pairs={{0,8},{1,9},{2,10},{3,11},{4,12},{5,13},{6,14},{7,15},{8,0},{9,1},... | collective-permute-start | bytes 884744 | tf_op jit(solution)/shard_map/ppermute | solution.py:56
  42.0 10.8 %collective-permute-start.7 = (bf16[2,2,1,48,1536]{4,3,2,1,0:T(8,128)(2,1)S(1)}, bf16[2,2,1,48,1536]{4,3,2,1,0:T(8,128)(2,1)S(1)}, u32[]{:S(2)}, u32[]{:S(2)}) collective-permute-start(bf16[2,2,1,48,1536]{4,3,2,1,0:T(8,128)(2,1)S(1)} %get-tuple-element.217.refs_2_), channel_id=1, source_target_pairs={{0,2},{1,5},{2,0},{3,7},{4,6},{5,1},{6,4},{7,3},{8,10},{9,13},{10,... | collective-permute-start | bytes 1769480 | tf_op jit(solution)/shard_map/ppermute | solution.py:56
  42.6 7.7 %collective-permute-start.6 = (bf16[1,96,768]{2,1,0:T(8,128)(2,1)S(1)}, bf16[1,96,768]{2,1,0:T(8,128)(2,1)S(1)}, u32[]{:S(2)}, u32[]{:S(2)}) collective-permute-start(bf16[1,96,768]{2,1,0:T(8,128)(2,1)S(1)} %get-tuple-element.215.refs_2_), channel_id=1, source_target_pairs={{0,16},{1,17},{2,18},{3,19},{4,20},{5,21},{6,22},{7,23},{8,24},{9,... | collective-permute-start | bytes 442376 | tf_op jit(solution)/shard_map/ppermute | solution.py:56
  50.8 6.8 %collective-permute-start.8 = (bf16[2,1,96,768]{3,2,1,0:T(8,128)(2,1)S(1)}, bf16[2,1,96,768]{3,2,1,0:T(8,128)(2,1)S(1)}, u32[]{:S(2)}, u32[]{:S(2)}) collective-permute-start(bf16[2,1,96,768]{3,2,1,0:T(8,128)(2,1)S(1)} %get-tuple-element.219.refs_2_), channel_id=1, source_target_pairs={{0,8},{1,9},{2,10},{3,11},{4,12},{5,13},{6,14},{7,15},{8,0},{9,1},... | collective-permute-start | bytes 884744 | tf_op jit(solution)/shard_map/ppermute | solution.py:56
  59.0 4.6 %collective-permute-start.10 = (bf16[4,16,48,384]{3,2,1,0:T(8,128)(2,1)S(1)}, bf16[4,16,48,384]{3,2,1,0:T(8,128)(2,1)S(1)}, u32[]{:S(2)}, u32[]{:S(2)}) collective-permute-start(bf16[4,16,48,384]{3,2,1,0:T(8,128)(2,1)S(1)} %get-tuple-element.224), channel_id=1, source_target_pairs={{0,1},{1,0},{2,3},{3,2},{4,5},{5,4},{6,7},{7,6},{8,9},{9,8},{10,11... | collective-permute-start | bytes 7077896 | tf_op jit(solution)/shard_map/ppermute | solution.py:56
  59.0 23.2 %collective-permute-start.12 = (bf16[2,2,2,1,48,1536]{5,4,3,2,1,0:T(8,128)(2,1)S(1)}, bf16[2,2,2,1,48,1536]{5,4,3,2,1,0:T(8,128)(2,1)S(1)}, u32[]{:S(2)}, u32[]{:S(2)}) collective-permute-start(bf16[2,2,2,1,48,1536]{5,4,3,2,1,0:T(8,128)(2,1)S(1)} %get-tuple-element.231.refs_2_), channel_id=1, source_target_pairs={{0,4},{1,3},{2,6},{3,1},{4,0},{5,7},{6,2},{7,5},{8,12},{9,11},{10,... | collective-permute-start | bytes 3538952 | tf_op jit(solution)/shard_map/ppermute | solution.py:56
  62.0 16.3 %collective-permute-start.11 = (bf16[2,2,1,96,768]{4,3,2,1,0:T(8,128)(2,1)S(1)}, bf16[2,2,1,96,768]{4,3,2,1,0:T(8,128)(2,1)S(1)}, u32[]{:S(2)}, u32[]{:S(2)}) collective-permute-start(bf16[2,2,1,96,768]{4,3,2,1,0:T(8,128)(2,1)S(1)} %get-tuple-element.229.refs_2_), channel_id=1, source_target_pairs={{0,2},{1,5},{2,0},{3,7},{4,6},{5,1},{6,4},{7,3},{8,10},{9,13},{10,... | collective-permute-start | bytes 1769480 | tf_op jit(solution)/shard_map/ppermute | solution.py:56
  83.0 6.6 %collective-permute-start.13 = (bf16[1,16,48,1536]{3,2,1,0:T(8,128)(2,1)S(1)}, bf16[1,16,48,1536]{3,2,1,0:T(8,128)(2,1)S(1)}, u32[]{:S(2)}, u32[]{:S(2)}) collective-permute-start(bf16[1,16,48,1536]{3,2,1,0:T(8,128)(2,1)S(1)} %get-tuple-element.236), channel_id=1, source_target_pairs={{0,1},{1,0},{2,3},{3,2},{4,5},{5,4},{6,7},{7,6},{8,9},{9,8},{10,11... | collective-permute-start | bytes 7077896 | tf_op jit(solution)/shard_map/ppermute | solution.py:56
  83.1 16.3 %collective-permute-start.14 = (bf16[2,2,2,1,96,768]{5,4,3,2,1,0:T(8,128)(2,1)S(1)}, bf16[2,2,2,1,96,768]{5,4,3,2,1,0:T(8,128)(2,1)S(1)}, u32[]{:S(2)}, u32[]{:S(2)}) collective-permute-start(bf16[2,2,2,1,96,768]{5,4,3,2,1,0:T(8,128)(2,1)S(1)} %get-tuple-element.241.refs_2_), channel_id=1, source_target_pairs={{0,4},{1,3},{2,6},{3,1},{4,0},{5,7},{6,2},{7,5},{8,12},{9,11},{10,... | collective-permute-start | bytes 3538952 | tf_op jit(solution)/shard_map/ppermute | solution.py:56
  100.0 4.6 %collective-permute-start.15 = (bf16[1,16,96,768]{3,2,1,0:T(8,128)(2,1)S(1)}, bf16[1,16,96,768]{3,2,1,0:T(8,128)(2,1)S(1)}, u32[]{:S(2)}, u32[]{:S(2)}) collective-permute-start(bf16[1,16,96,768]{3,2,1,0:T(8,128)(2,1)S(1)} %get-tuple-element.244), channel_id=1, source_target_pairs={{0,1},{1,0},{2,3},{3,2},{4,5},{5,4},{6,7},{7,6},{8,9},{9,8},{10,11... | collective-permute-start | bytes 7077896 | tf_op jit(solution)/shard_map/ppermute | solution.py:56
  100.1 4.5 %copy-start.3 = (f32[12,768]{1,0:T(8,128)S(1)}, f32[12,768]{1,0:T(8,128)}, u32[]{:S(2)}) copy-start(f32[12,768]{1,0:T(8,128)} %refs_4_.3) | copy-start | bytes 110596
  110.9 7.1 %collective-permute-start.16 = (bf16[1,16,96,768]{3,2,1,0:T(8,128)(2,1)S(1)}, bf16[1,16,96,768]{3,2,1,0:T(8,128)(2,1)S(1)}, u32[]{:S(2)}, u32[]{:S(2)}) collective-permute-start(bf16[1,16,96,768]{3,2,1,0:T(8,128)(2,1)S(1)} %bitcast.95), channel_id=1, source_target_pairs={{0,1},{1,0},{2,3},{3,2},{4,5},{5,4},{6,7},{7,6},{8,9},{9,8},{10,11... | collective-permute-start | bytes 7077896 | tf_op jit(solution)/shard_map/ppermute | solution.py:56
  117.6 18.4 %collective-permute-start.19 = (bf16[1,16,48,1536]{3,2,1,0:T(8,128)(2,1)S(1)}, bf16[1,16,48,1536]{3,2,1,0:T(8,128)(2,1)S(1)}, u32[]{:S(2)}, u32[]{:S(2)}) collective-permute-start(bf16[1,16,48,1536]{3,2,1,0:T(8,128)(2,1)S(1)} %bitcast.94), channel_id=1, source_target_pairs={{0,1},{1,0},{2,3},{3,2},{4,5},{5,4},{6,7},{7,6},{8,9},{9,8},{10,11... | collective-permute-start | bytes 7077896 | tf_op jit(solution)/shard_map/ppermute | solution.py:56
  118.9 16.3 %collective-permute-start.18 = (bf16[2,2,2,1,96,768]{5,4,3,2,1,0:T(8,128)(2,1)S(1)}, bf16[2,2,2,1,96,768]{5,4,3,2,1,0:T(8,128)(2,1)S(1)}, u32[]{:S(2)}, u32[]{:S(2)}) collective-permute-start(bf16[2,2,2,1,96,768]{5,4,3,2,1,0:T(8,128)(2,1)S(1)} %get-tuple-element.282), channel_id=1, source_target_pairs={{0,4},{1,3},{2,6},{3,1},{4,0},{5,7},{6,2},{7,5},{8,12},{9,11},{10,... | collective-permute-start | bytes 3538952 | tf_op jit(solution)/shard_map/ppermute | solution.py:56
  120.8 11.6 %collective-permute-start.17 = (bf16[512,768]{1,0:T(8,128)(2,1)S(1)}, bf16[512,768]{1,0:T(8,128)(2,1)S(1)}, u32[]{:S(2)}, u32[]{:S(2)}) collective-permute-start(bf16[512,768]{1,0:T(8,128)(2,1)S(1)} %get-tuple-element.278.refs_2_), channel_id=1, source_target_pairs={{0,1},{1,0},{2,3},{3,2},{4,5},{5,4},{6,7},{7,6},{8,9},{9,8},{10,11... | collective-permute-start | bytes 2359304 | tf_op jit(solution)/shard_map/ppermute | solution.py:56
  137.0 21.3 %collective-permute-start.21 = (bf16[2,2,2,1,48,1536]{5,4,3,2,1,0:T(8,128)(2,1)S(1)}, bf16[2,2,2,1,48,1536]{5,4,3,2,1,0:T(8,128)(2,1)S(1)}, u32[]{:S(2)}, u32[]{:S(2)}) collective-permute-start(bf16[2,2,2,1,48,1536]{5,4,3,2,1,0:T(8,128)(2,1)S(1)} %get-tuple-element.297), channel_id=1, source_target_pairs={{0,4},{1,3},{2,6},{3,1},{4,0},{5,7},{6,2},{7,5},{8,12},{9,11},{10,... | collective-permute-start | bytes 3538952 | tf_op jit(solution)/shard_map/ppermute | solution.py:56
  138.9 16.3 %collective-permute-start.20 = (bf16[2,2,1,96,768]{4,3,2,1,0:T(8,128)(2,1)S(1)}, bf16[2,2,1,96,768]{4,3,2,1,0:T(8,128)(2,1)S(1)}, u32[]{:S(2)}, u32[]{:S(2)}) collective-permute-start(bf16[2,2,1,96,768]{4,3,2,1,0:T(8,128)(2,1)S(1)} %get-tuple-element.292), channel_id=1, source_target_pairs={{0,2},{1,5},{2,0},{3,7},{4,6},{5,1},{6,4},{7,3},{8,10},{9,13},{10,... | collective-permute-start | bytes 1769480 | tf_op jit(solution)/shard_map/ppermute | solution.py:56
  138.9 22.4 %collective-permute-start.24 = (bf16[1,16,48,384]{3,2,1,0:T(8,128)(2,1)S(1)}, bf16[1,16,48,384]{3,2,1,0:T(8,128)(2,1)S(1)}, u32[]{:S(2)}, u32[]{:S(2)}) collective-permute-start(bf16[1,16,48,384]{3,2,1,0:T(8,128)(2,1)S(1)} %bitcast.97), channel_id=1, source_target_pairs={{0,1},{1,0},{2,3},{3,2},{4,5},{5,4},{6,7},{7,6},{8,9},{9,8},{10,11... | collective-permute-start | bytes 1769480 | tf_op jit(solution)/shard_map/ppermute | solution.py:56
  138.9 22.4 %collective-permute-start.25 = (bf16[1,16,48,384]{3,2,1,0:T(8,128)(2,1)S(1)}, bf16[1,16,48,384]{3,2,1,0:T(8,128)(2,1)S(1)}, u32[]{:S(2)}, u32[]{:S(2)}) collective-permute-start(bf16[1,16,48,384]{3,2,1,0:T(8,128)(2,1)S(1)} %bitcast.96), channel_id=1, source_target_pairs={{0,1},{1,0},{2,3},{3,2},{4,5},{5,4},{6,7},{7,6},{8,9},{9,8},{10,11... | collective-permute-start | bytes 1769480 | tf_op jit(solution)/shard_map/ppermute | solution.py:56
  147.0 14.3 %collective-permute-start.22 = (bf16[1,16,48,384]{3,2,1,0:T(8,128)(2,1)S(1)}, bf16[1,16,48,384]{3,2,1,0:T(8,128)(2,1)S(1)}, u32[]{:S(2)}, u32[]{:S(2)}) collective-permute-start(bf16[1,16,48,384]{3,2,1,0:T(8,128)(2,1)S(1)} %bitcast.99), channel_id=1, source_target_pairs={{0,1},{1,0},{2,3},{3,2},{4,5},{5,4},{6,7},{7,6},{8,9},{9,8},{10,11... | collective-permute-start | bytes 1769480 | tf_op jit(solution)/shard_map/ppermute | solution.py:56
  155.2 6.2 %collective-permute-start.23 = (bf16[1,16,48,384]{3,2,1,0:T(8,128)(2,1)S(1)}, bf16[1,16,48,384]{3,2,1,0:T(8,128)(2,1)S(1)}, u32[]{:S(2)}, u32[]{:S(2)}) collective-permute-start(bf16[1,16,48,384]{3,2,1,0:T(8,128)(2,1)S(1)} %bitcast.98), channel_id=1, source_target_pairs={{0,1},{1,0},{2,3},{3,2},{4,5},{5,4},{6,7},{7,6},{8,9},{9,8},{10,11... | collective-permute-start | bytes 1769480 | tf_op jit(solution)/shard_map/ppermute | solution.py:56
  158.4 8.8 %collective-permute-start.26 = (bf16[2,1,96,768]{3,2,1,0:T(8,128)(2,1)S(1)}, bf16[2,1,96,768]{3,2,1,0:T(8,128)(2,1)S(1)}, u32[]{:S(2)}, u32[]{:S(2)}) collective-permute-start(bf16[2,1,96,768]{3,2,1,0:T(8,128)(2,1)S(1)} %get-tuple-element.309), channel_id=1, source_target_pairs={{0,8},{1,9},{2,10},{3,11},{4,12},{5,13},{6,14},{7,15},{8,0},{9,1},... | collective-permute-start | bytes 884744 | tf_op jit(solution)/shard_map/ppermute | solution.py:56
  162.4 22.0 %collective-permute-start.30 = (bf16[2,2,2,4,48,384]{5,4,3,2,1,0:T(8,128)(2,1)S(1)}, bf16[2,2,2,4,48,384]{5,4,3,2,1,0:T(8,128)(2,1)S(1)}, u32[]{:S(2)}, u32[]{:S(2)}) collective-permute-start(bf16[2,2,2,4,48,384]{5,4,3,2,1,0:T(8,128)(2,1)S(1)} %get-tuple-element.329), channel_id=1, source_target_pairs={{0,4},{1,3},{2,6},{3,1},{4,0},{5,7},{6,2},{7,5},{8,12},{9,11},{10,... | collective-permute-start | bytes 3538952 | tf_op jit(solution)/shard_map/ppermute | solution.py:56
  167.8 14.2 %copy-start.10 = (f32[96,768]{1,0:T(8,128)S(1)}, f32[96,768]{1,0:T(8,128)}, u32[]{:S(2)}) copy-start(f32[96,768]{1,0:T(8,128)} %param.30) | copy-start | bytes 884740
  167.8 14.1 %copy-start.11 = (f32[96,768]{1,0:T(8,128)S(1)}, f32[96,768]{1,0:T(8,128)}, u32[]{:S(2)}) copy-start(f32[96,768]{1,0:T(8,128)} %param.34) | copy-start | bytes 884740
  170.8 18.5 %collective-permute-start.31 = (f32[512,768]{1,0:T(8,128)S(1)}, f32[512,768]{1,0:T(8,128)S(1)}, u32[]{:S(2)}, u32[]{:S(2)}) collective-permute-start(f32[512,768]{1,0:T(8,128)S(1)} %get-tuple-element.331.refs_2_), channel_id=1, source_target_pairs={{0,1},{1,0},{2,3},{3,2},{4,5},{5,4},{6,7},{7,6},{8,9},{9,8},{10,11... | collective-permute-start | bytes 4718600 | tf_op jit(solution)/shard_map/ppermute | solution.py:56
  170.8 12.9 %collective-permute-start.29 = (bf16[2,2,1,48,1536]{4,3,2,1,0:T(8,128)(2,1)S(1)}, bf16[2,2,1,48,1536]{4,3,2,1,0:T(8,128)(2,1)S(1)}, u32[]{:S(2)}, u32[]{:S(2)}) collective-permute-start(bf16[2,2,1,48,1536]{4,3,2,1,0:T(8,128)(2,1)S(1)} %get-tuple-element.326), channel_id=1, source_target_pairs={{0,2},{1,5},{2,0},{3,7},{4,6},{5,1},{6,4},{7,3},{8,10},{9,13},{10,... | collective-permute-start | bytes 1769480 | tf_op jit(solution)/shard_map/ppermute | solution.py:56
  171.4 10.5 %collective-permute-start.28 = (bf16[1,96,768]{2,1,0:T(8,128)(2,1)S(1)}, bf16[1,96,768]{2,1,0:T(8,128)(2,1)S(1)}, u32[]{:S(2)}, u32[]{:S(2)}) collective-permute-start(bf16[1,96,768]{2,1,0:T(8,128)(2,1)S(1)} %get-tuple-element.323), channel_id=1, source_target_pairs={{0,16},{1,17},{2,18},{3,19},{4,20},{5,21},{6,22},{7,23},{8,24},{9,... | collective-permute-start | bytes 442376 | tf_op jit(solution)/shard_map/ppermute | solution.py:56
  172.0 2.3 collective-permute-start.27
  185.2 13.0 %collective-permute-start.33 = (bf16[2,2,4,48,384]{4,3,2,1,0:T(8,128)(2,1)S(1)}, bf16[2,2,4,48,384]{4,3,2,1,0:T(8,128)(2,1)S(1)}, u32[]{:S(2)}, u32[]{:S(2)}) collective-permute-start(bf16[2,2,4,48,384]{4,3,2,1,0:T(8,128)(2,1)S(1)} %get-tuple-element.338), channel_id=1, source_target_pairs={{0,2},{1,5},{2,0},{3,7},{4,6},{5,1},{6,4},{7,3},{8,10},{9,13},{10,... | collective-permute-start | bytes 1769480 | tf_op jit(solution)/shard_map/ppermute | solution.py:56
  186.9 9.7 %collective-permute-start.32 = (bf16[2,1,48,1536]{3,2,1,0:T(8,128)(2,1)S(1)}, bf16[2,1,48,1536]{3,2,1,0:T(8,128)(2,1)S(1)}, u32[]{:S(2)}, u32[]{:S(2)}) collective-permute-start(bf16[2,1,48,1536]{3,2,1,0:T(8,128)(2,1)S(1)} %get-tuple-element.335), channel_id=1, source_target_pairs={{0,8},{1,9},{2,10},{3,11},{4,12},{5,13},{6,14},{7,15},{8,0},{9,1},... | collective-permute-start | bytes 884744 | tf_op jit(solution)/shard_map/ppermute | solution.py:56
  191.6 22.6 %copy-start.12 = (f32[48,1536]{1,0:T(8,128)S(1)}, f32[48,1536]{1,0:T(8,128)}, u32[]{:S(2)}) copy-start(f32[48,1536]{1,0:T(8,128)} %param.29) | copy-start | bytes 884740
  191.6 22.6 %copy-start.13 = (f32[48,1536]{1,0:T(8,128)S(1)}, f32[48,1536]{1,0:T(8,128)}, u32[]{:S(2)}) copy-start(f32[48,1536]{1,0:T(8,128)} %param.33) | copy-start | bytes 884740
  197.2 20.2 %copy-start.7 = (f32[3,48,384]{2,1,0:T(8,128)S(1)}, f32[3,48,384]{2,1,0:T(8,128)}, u32[]{:S(2)}) copy-start(f32[3,48,384]{2,1,0:T(8,128)} %refs_5_.4) | copy-start | bytes 663556
  197.3 20.1 %copy-start.9 = (f32[384,48]{0,1:T(8,128)S(1)}, f32[384,48]{0,1:T(8,128)}, u32[]{:S(2)}) copy-start(f32[384,48]{0,1:T(8,128)} %param.24) | copy-start | bytes 221188
  197.3 20.1 %copy-start.14 = (f32[3,48,384]{2,1,0:T(8,128)S(1)}, f32[3,48,384]{2,1,0:T(8,128)}, u32[]{:S(2)}) copy-start(f32[3,48,384]{2,1,0:T(8,128)} %refs_6_.2) | copy-start | bytes 663556
  197.3 20.1 %copy-start.15 = (f32[3,48,384]{2,1,0:T(8,128)S(1)}, f32[3,48,384]{2,1,0:T(8,128)}, u32[]{:S(2)}) copy-start(f32[3,48,384]{2,1,0:T(8,128)} %refs_7_.3) | copy-start | bytes 663556
  197.3 20.1 %copy-start.16 = (f32[384,48]{0,1:T(8,128)S(1)}, f32[384,48]{0,1:T(8,128)}, u32[]{:S(2)}) copy-start(f32[384,48]{0,1:T(8,128)} %param.28) | copy-start | bytes 221188
  197.3 20.1 %copy-start.17 = (f32[384,48]{0,1:T(8,128)S(1)}, f32[384,48]{0,1:T(8,128)}, u32[]{:S(2)}) copy-start(f32[384,48]{0,1:T(8,128)} %param.32) | copy-start | bytes 221188
  197.3 16.9 %collective-permute-start.34 = (bf16[1,48,1536]{2,1,0:T(8,128)(2,1)S(1)}, bf16[1,48,1536]{2,1,0:T(8,128)(2,1)S(1)}, u32[]{:S(2)}, u32[]{:S(2)}) collective-permute-start(bf16[1,48,1536]{2,1,0:T(8,128)(2,1)S(1)} %get-tuple-element.341), channel_id=1, source_target_pairs={{0,16},{1,17},{2,18},{3,19},{4,20},{5,21},{6,22},{7,23},{8,24},{9,... | collective-permute-start | bytes 442376 | tf_op jit(solution)/shard_map/ppermute | solution.py:56
  198.9 16.6 %collective-permute-start.35 = (bf16[4,48,384]{2,1,0:T(8,128)(2,1)S(1)}, bf16[4,48,384]{2,1,0:T(8,128)(2,1)S(1)}, u32[]{:S(2)}, u32[]{:S(2)}) collective-permute-start(bf16[4,48,384]{2,1,0:T(8,128)(2,1)S(1)} %get-tuple-element.344), channel_id=1, source_target_pairs={{0,8},{1,9},{2,10},{3,11},{4,12},{5,13},{6,14},{7,15},{8,0},{9,1},... | collective-permute-start | bytes 442376 | tf_op jit(solution)/shard_map/ppermute | solution.py:56
  199.9 17.5 %collective-permute-start.36 = (bf16[4,48,384]{2,1,0:T(8,128)(2,1)S(1)}, bf16[4,48,384]{2,1,0:T(8,128)(2,1)S(1)}, u32[]{:S(2)}, u32[]{:S(2)}) collective-permute-start(bf16[4,48,384]{2,1,0:T(8,128)(2,1)S(1)} %get-tuple-element.345), channel_id=1, source_target_pairs={{0,16},{1,17},{2,18},{3,19},{4,20},{5,21},{6,22},{7,23},{8,24},{9,... | collective-permute-start | bytes 442376 | tf_op jit(solution)/shard_map/ppermute | solution.py:56
  202.8 14.6 %collective-permute-start.37 = (bf16[4,48,384]{2,1,0:T(8,128)(2,1)S(1)}, bf16[4,48,384]{2,1,0:T(8,128)(2,1)S(1)}, u32[]{:S(2)}, u32[]{:S(2)}) collective-permute-start(bf16[4,48,384]{2,1,0:T(8,128)(2,1)S(1)} %get-tuple-element.346), channel_id=1, source_target_pairs={{0,24},{1,25},{2,26},{3,27},{4,28},{5,29},{6,30},{7,31},{8,16},{9,... | collective-permute-start | bytes 442376 | tf_op jit(solution)/shard_map/ppermute | solution.py:56
  214.2 20.7 %copy-start.18 = (f32[12,768]{1,0:T(8,128)S(1)}, f32[12,768]{1,0:T(8,128)}, u32[]{:S(2)}) copy-start(f32[12,768]{1,0:T(8,128)} %refs_5_.5) | copy-start | bytes 110596
  214.2 20.7 %copy-start.19 = (f32[12,768]{1,0:T(8,128)S(1)}, f32[12,768]{1,0:T(8,128)}, u32[]{:S(2)}) copy-start(f32[12,768]{1,0:T(8,128)} %refs_6_.3) | copy-start | bytes 110596
  218.6 5.1 %collective-permute-start.38 = (f32[8,768]{1,0:T(8,128)S(1)}, f32[8,768]{1,0:T(8,128)S(1)}, u32[]{:S(2)}, u32[]{:S(2)}) collective-permute-start(f32[8,768]{1,0:T(8,128)S(1)} %get-tuple-element.351.refs_1_), channel_id=1, source_target_pairs={{0,8},{1,9},{2,10},{3,11},{4,12},{5,13},{6,14},{7,15},{8,0},{9,1},... | collective-permute-start | bytes 73736 | tf_op jit(solution)/shard_map/ppermute | solution.py:56
  221.4 4.7 %collective-permute-start.39 = (f32[8,768]{1,0:T(8,128)S(1)}, f32[8,768]{1,0:T(8,128)S(1)}, u32[]{:S(2)}, u32[]{:S(2)}) collective-permute-start(f32[8,768]{1,0:T(8,128)S(1)} %get-tuple-element.351.refs_1_), channel_id=1, source_target_pairs={{0,16},{1,17},{2,18},{3,19},{4,20},{5,21},{6,22},{7,23},{8,24},{9,... | collective-permute-start | bytes 73736 | tf_op jit(solution)/shard_map/ppermute | solution.py:56
  221.4 5.6 %collective-permute-start.40 = (f32[8,768]{1,0:T(8,128)S(1)}, f32[8,768]{1,0:T(8,128)S(1)}, u32[]{:S(2)}, u32[]{:S(2)}) collective-permute-start(f32[8,768]{1,0:T(8,128)S(1)} %get-tuple-element.351.refs_1_), channel_id=1, source_target_pairs={{0,24},{1,25},{2,26},{3,27},{4,28},{5,29},{6,30},{7,31},{8,16},{9,... | collective-permute-start | bytes 73736 | tf_op jit(solution)/shard_map/ppermute | solution.py:56
  227.0 4.0 %collective-permute-start.41 = (f32[8,768]{1,0:T(8,128)S(1)}, f32[8,768]{1,0:T(8,128)S(1)}, u32[]{:S(2)}, u32[]{:S(2)}) collective-permute-start(f32[8,768]{1,0:T(8,128)S(1)} %get-tuple-element.353.refs_1_), channel_id=1, source_target_pairs={{0,4},{1,5},{2,6},{3,7},{4,0},{5,1},{6,2},{7,3},{8,12},{9,13},{10,... | collective-permute-start | bytes 73736 | tf_op jit(solution)/shard_map/ppermute | solution.py:56
  227.1 3.9 %collective-permute-start.42 = (f32[8,768]{1,0:T(8,128)S(1)}, f32[8,768]{1,0:T(8,128)S(1)}, u32[]{:S(2)}, u32[]{:S(2)}) collective-permute-start(f32[8,768]{1,0:T(8,128)S(1)} %get-tuple-element.353.refs_1_), channel_id=1, source_target_pairs={{0,2},{1,3},{2,0},{3,1},{4,6},{5,7},{6,4},{7,5},{8,10},{9,11},{10,... | collective-permute-start | bytes 73736 | tf_op jit(solution)/shard_map/ppermute | solution.py:56
  228.9 4.7 %collective-permute-start.43 = (f32[8,768]{1,0:T(8,128)S(1)}, f32[8,768]{1,0:T(8,128)S(1)}, u32[]{:S(2)}, u32[]{:S(2)}) collective-permute-start(f32[8,768]{1,0:T(8,128)S(1)} %get-tuple-element.353.refs_1_), channel_id=1, source_target_pairs={{0,6},{1,7},{2,4},{3,5},{4,2},{5,3},{6,0},{7,1},{8,14},{9,15},{10,... | collective-permute-start | bytes 73736 | tf_op jit(solution)/shard_map/ppermute | solution.py:56
  233.7 1.3 collective-permute-start.44
  (1 other events, 0.8 us)

commit v4 on v3

--- a/solution.py
+++ b/solution.py
@@ -1,5 +1,6 @@
 import itertools
 import math
+import types
 
 import jax
 import jax.numpy as jnp
@@ -25,6 +26,15 @@
 NT = (((1,), (1,)), ((), ()))
 TN = (((0,), (0,)), ((), ()))
 MIB = 1 << 20
+PATHS = ("zzab", "azzb", "azzb", "azzb")
+COUNTS = (1, 4)
+ORDER = (
+    "castA", "prep", "castB", "a0", "b0", "a1", "castC", "c0", "b1", "c1", "b2", "wholeA", "project",
+    "attend", "c2", "wholeB", "hide", "liftOwn", "liftOth", "turn", "wholeC", "lowerOwn", "lower", "sinkOth",
+    "downOth", "downOwn", "upOth", "pairC", "sinkOwn", "upOwn", "pairB", "surface", "values", "voOth", "C0",
+    "back", "qkOth", "qkOwn", "voOwn", "voSum", "B0", "C1", "pairA", "states", "collect", "share", "C2", "A0",
+    "B1", "A1", "A2", "stepC", "B2", "pairS", "pairO", "stepB", "stepA",
+)
 
 
 class Grid:
@@ -60,9 +70,11 @@
         spot = [lax.rem(lax.div(index, s), n) if n > 1 else index * 0 for s, n in zip(self.stride, self.sizes)]
         return jnp.stack(spot + [lax.axis_index("tensor")]).astype(jnp.int32)
 
-    def path(self):
+    def path(self, order="zzab"):
         bits = [[1 << b for b in reversed(range((n - 1).bit_length()))] for n in (self.long, self.side, self.side)]
-        return [(side, k) for side in range(3) for k in bits[side]]
+        steps = [[(side, k) for k in bits[side]] for side in range(3)]
+        stock = {"z": [steps[0][:-1], steps[0][-1:]], "a": [steps[1]], "b": [steps[2]]}
+        return sum((stock[kind].pop(0) for kind in order), [])
 
     def exchange(self, value, step):
         side, k = step
@@ -144,9 +156,9 @@
 
 
 class Gather:
-    def __init__(self, grid, tape, shard, direct=False):
+    def __init__(self, grid, tape, shard, direct=False, order="zzab"):
         self.grid, self.tape, self.block = grid, tape, shard
-        self.path = grid.path()
+        self.path = grid.path(order)
         if direct:
             self.got = [grid.send(shard, grid.along(k)) for k in range(1, grid.long)]
         else:
@@ -202,27 +214,36 @@
 
 
 class Scatter:
-    def __init__(self, grid, tape, other):
+    def __init__(self, grid, tape, other, order="zzab"):
         self.grid, self.tape = grid, tape
-        self.path = grid.path()
-        self.got = [grid.core(v) for v in other]
+        self.path = grid.path(order)
+        self.got = [grid.core(v) for v, _, _ in other]
+        self.spots = [(j, c) for _, j, c in other]
 
     def pair(self, own):
         grid, path = self.grid, self.path
-        each, _, rows, width = own[0].shape
-        many, pieces = each * len(own), len(own)
+        _, _, rows, width = own[0].shape
+        own_spots = [(g, i) for g, v in enumerate(own) for i in range(v.shape[0])]
+        many, pieces, got = len(own_spots), len(own), len(self.got)
+        shapes = [v.shape for v in self.got]
         shape = (2,) * (len(path) - 1) + (many, rows, width)
 
         def scatter_pair(s, *refs):
-            own_refs, got_refs, (keep, send) = refs[:pieces], refs[pieces : 2 * pieces], refs[2 * pieces :]
+            own_refs, got_refs, (keep, send) = refs[:pieces], refs[pieces : pieces + got], refs[pieces + got :]
             last = grid.bit(s, path[-1])
             for bits in itertools.product(range(2), repeat=len(path) - 1):
                 for out, bit in ((keep, last), (send, 1 - last)):
                     spot = grid.spot(s, path, bits[::-1] + (bit,))
-                    for j in range(many):
-                        g, i = divmod(j, each)
-                        total = own_refs[g][i, spot] + got_refs[g][i, spot].astype(F32)
-                        out[bits + (j,)] = total.astype(out.dtype)
+                    for j, (g, i) in enumerate(own_spots):
+                        found = False
+                        for ref, (first, column), piece in zip(got_refs, self.spots, shapes):
+                            if first <= j < first + piece[0]:
+                                at = slice(column, column + piece[3])
+                                total = own_refs[g][i, spot, :, at] + ref[j - first, spot].astype(F32)
+                                out[bits + (j, slice(None), at)] = total.astype(out.dtype)
+                                found = True
+                        if not found:
+                            out[bits + (j,)] = own_refs[g][i, spot].astype(out.dtype)
 
         self.keep, value = self.tape.run(scatter_pair, [(shape, F32), (shape, BF16)], own + self.got, True)
         self.got = grid.exchange(value, path[-1])
@@ -338,6 +359,8 @@
         second_in, second_out, second_up, second_down,
         vectors, vector_first, vector_second,
     ):
+        w = types.SimpleNamespace()
+        paths, counts_of = PATHS, COUNTS
         cores = grid.cores
         pairs, length, width = states.shape
         mine = pairs // cores
@@ -362,7 +385,15 @@
             shape = (many,) + mats[0].shape[1:]
             return tape.run(cast, [(shape, BF16)], mats, plain=range(len(mats)))[0]
 
-        gather_a = Gather(grid, tape, casted(attend_in, attend_out), direct=True)
+        def cast_a():
+            w.gather_a = Gather(grid, tape, casted(attend_in, attend_out), direct=True)
+
+        def cast_b():
+            w.gather_b = Gather(grid, tape, casted(expand_up[None]), order=paths[0])
+
+        def cast_c():
+            w.gather_c = Gather(grid, tape, casted(expand_down[None]), order=paths[1])
+
 
         def prepare(s, states_ref, cot_ref, vec, x_ref, x_t, mine_cot, bias_in, bias_up):
             @pl.loop(0, mine)
@@ -386,22 +417,22 @@
                             spot = h * units + i * width
                             bias_up[:, spot : spot + width] = vec[row : row + 1]
 
-        x, x_t, cot, bias_in, bias_up = tape.run(
-            prepare,
-            [((rows, width), BF16), ((width, rows), BF16), ((rows, width), BF16), ((3, width), F32),
-             ((1, 2 * units), F32)],
-            [states, cotangent, vectors], True, limit=12, moved=6 * MIB, plain=(0, 1),
-        )
-        gather_b = Gather(grid, tape, casted(expand_up[None]))
-        gather_a.merge_long()
-        gather_b.merge(0)
-        gather_a.merge_short()
-        gather_c = Gather(grid, tape, casted(expand_down[None]))
-        gather_b.merge(1)
-        gather_c.merge(0)
-        gather_b.merge(2)
-        gather_c.merge(1)
-        a_own, a_oth = (v.reshape(4, width, cols) for v in gather_a.whole())
+        def prepared():
+            w.x, w.x_t, w.cot, w.bias_in, w.bias_up = tape.run(
+                prepare,
+                [((rows, width), BF16), ((width, rows), BF16), ((rows, width), BF16), ((3, width), F32),
+                 ((1, 2 * units), F32)],
+                [states, cotangent, vectors], True, limit=12, moved=6 * MIB, plain=(0, 1),
+            )
+
+        def whole_a():
+            w.a_own, w.a_oth = (v.reshape(4, width, cols) for v in w.gather_a.whole())
+
+        def whole_b():
+            w.b_own, w.b_oth = (v.reshape(width, units) for v in w.gather_b.whole())
+
+        def whole_c():
+            w.c_own, w.c_oth = (v.reshape(units, width) for v in w.gather_c.whole())
 
         def project(x_ref, own, oth, bias, out):
             @pl.loop(0, 3)
@@ -411,10 +442,11 @@
                     value = jnp.dot(x_ref[...], ref[j], preferred_element_type=F32)
                     out[j, :, at] = (value + bias[pl.ds(j, 1), at]).astype(BF16)
 
-        qkv = tape.run(
-            project, [((3, rows, width), BF16)], [x, a_own, a_oth, bias_in],
-            limit=8, flops=6 * rows * width * width, moved=8 * MIB,
-        )[0]
+        def projected():
+            w.qkv = tape.run(
+                project, [((3, rows, width), BF16)], [w.x, w.a_own, w.a_oth, w.bias_in],
+                limit=8, flops=6 * rows * width * width, moved=8 * MIB,
+            )[0]
 
         def split(v):
             low = lax.broadcasted_iota(jnp.int32, v.shape, 1) < HEAD_DIM
@@ -446,13 +478,12 @@
                         prob, split(qkv_ref[2, at, lanes]), preferred_element_type=F32
                     ).astype(BF16)
 
-        probs, context = tape.run(
-            attend, [((rows, 2 * twins * length), BF16), ((rows, width), BF16)], [qkv], True,
-            limit=4, flops=4 * rows * length * width * 4, moved=5 * MIB, exps=rows * twins * 2 * length,
-        )
-
-        gather_c.merge(2)
-        b_own, b_oth = (v.reshape(width, units) for v in gather_b.whole())
+        def attended():
+            w.probs, w.context = tape.run(
+                attend, [((rows, 2 * twins * length), BF16), ((rows, width), BF16)], [w.qkv], True,
+                limit=4, flops=4 * rows * length * width * 4, moved=5 * MIB, exps=rows * twins * 2 * length,
+            )
+
         block = min(rows, 256)
 
         def hide(context_ref, x_ref, own, oth, vec, hidden, normed, inverse):
@@ -467,12 +498,13 @@
                 normed[at], inverse[at] = normal, spread
                 hidden[at] = (normal * vec[3:4] + vec[4:5]).astype(BF16)
 
-        hidden, normed_one, inverse_one = tape.run(
-            hide,
-            [((rows, width), BF16), ((rows, width), F32), ((rows, 1), F32)],
-            [context, x, a_own, a_oth, vectors],
-            limit=8, flops=2 * rows * width * width, moved=6 * MIB,
-        )
+        def hid():
+            w.hidden, w.normed_one, w.inverse_one = tape.run(
+                hide,
+                [((rows, width), BF16), ((rows, width), F32), ((rows, 1), F32)],
+                [w.context, w.x, w.a_own, w.a_oth, vectors],
+                limit=8, flops=2 * rows * width * width, moved=6 * MIB,
+            )
 
         tile = 256
 
@@ -492,16 +524,21 @@
             return tape.run(
                 lambda hidden_ref, up_ref, bias, *outs: lift(hidden_ref, up_ref, bias.at[:, h * units : (h + 1) * units], *outs),
                 [((rows, units), BF16), ((units, rows), BF16), ((rows, units), BF16)],
-                [hidden, up, bias_up],
+                [w.hidden, up, w.bias_up],
                 limit=8, flops=2 * rows * width * units, moved=8 * MIB, exps=2 * rows * units,
             )
 
         def turn(value, out):
             out[...] = value[...].T
 
-        lifted = [lift_half(0, b_own), lift_half(1, b_oth)]
-        hidden_t = tape.run(turn, [((width, rows), BF16)], [hidden], limit=8, moved=2 * MIB)[0]
-        c_own, c_oth = (v.reshape(units, width) for v in gather_c.whole())
+        def lift_own():
+            w.lift_own = lift_half(0, w.b_own)
+
+        def lift_oth():
+            w.lift_oth = lift_half(1, w.b_oth)
+
+        def turned():
+            w.hidden_t = tape.run(turn, [((width, rows), BF16)], [w.hidden], limit=8)[0]
 
         def lower_half(active, down, out):
             @pl.loop(0, width // tile)
@@ -509,10 +546,11 @@
                 at = pl.ds(pl.multiple_of(i * tile, tile), tile)
                 out[:, at] = jnp.dot(active[...], down[:, at], preferred_element_type=F32)
 
-        lowered = tape.run(
-            lower_half, [((rows, width), F32)], [lifted[0][0], c_own],
-            limit=6, flops=2 * rows * width * units, moved=6 * MIB,
-        )[0]
+        def lowered_own():
+            w.lowered = tape.run(
+                lower_half, [((rows, width), F32)], [w.lift_own[0], w.c_own],
+                limit=6, flops=2 * rows * width * units, moved=6 * MIB,
+            )[0]
 
         def lower(count, lowered_ref, active, down, normed, cot_ref, vec, output, top, top16, sums, work):
             @pl.loop(0, width // tile)
@@ -537,13 +575,14 @@
                 sums[1:2] += sum_rows(upstream * normal)
                 sums[2:3] += sum_rows(upstream)
 
-        output, top, top16, sums_two = tape.run(
-            lower,
-            [((rows, width), BF16), ((rows, width), F32), ((rows, width), BF16), ((8, width), F32)],
-            [lowered, lifted[1][0], c_oth, normed_one, cot, vectors],
-            True, limit=8, flops=2 * rows * width * units, moved=14 * MIB,
-            scratch=[VMEM((rows, width), F32)],
-        )
+        def lowered_all():
+            w.output, w.top, w.top16, w.sums_two = tape.run(
+                lower,
+                [((rows, width), BF16), ((rows, width), F32), ((rows, width), BF16), ((8, width), F32)],
+                [w.lowered, w.lift_oth[0], w.c_oth, w.normed_one, w.cot, vectors],
+                True, limit=8, flops=2 * rows * width * units, moved=14 * MIB,
+                scratch=[VMEM((rows, width), F32)],
+            )
 
         def product(left, right, *outs):
             step = min(left.shape[0], 256)
@@ -556,7 +595,7 @@
                 for g, out in enumerate(outs):
                     out[at, :] = value[:, g * share : (g + 1) * share].astype(out.dtype)
 
-        def weight_grad(left, right, kind, pieces=1):
+        def weight_grad(left, right, kind, pieces=2):
             shape = (left.shape[0], right.shape[1])
             return tape.run(
                 product, [((shape[0], shape[1] // pieces), kind)] * pieces, [left, right],
@@ -564,9 +603,27 @@
             )
 
         sharded = lambda values, many: [v.reshape(many, grid.dp, -1, v.shape[-1]) for v in values]
-        scatter_c = Scatter(grid, tape, sharded(weight_grad(lifted[1][1], top16, BF16), 1))
-        down_own = weight_grad(lifted[0][1], top16, F32)
-        output_oth = grid.core(output)
+        numbered = lambda values: [(v, i, 0) for i, v in enumerate(values)]
+
+        def down_oth():
+            other = sharded(weight_grad(w.lift_oth[1], w.top16, BF16, counts_of[0]), 1)
+            w.scatter_c = Scatter(grid, tape, numbered(other), order=paths[3])
+
+        def down_own():
+            w.down_own = weight_grad(w.lift_own[1], w.top16, F32, counts_of[0])
+
+        def pair_c():
+            w.scatter_c.pair(sharded(w.down_own, 1))
+
+        def up_oth():
+            other = sharded(weight_grad(w.hidden_t, w.sink_oth[0], BF16, counts_of[1]), 1)
+            w.scatter_b = Scatter(grid, tape, numbered(other), order=paths[2])
+
+        def up_own():
+            w.up_own = weight_grad(w.hidden_t, w.sink_own[0], F32, counts_of[1])
+
+        def pair_b():
+            w.scatter_b.pair(sharded(w.up_own, 1))
 
         def sink(top16_ref, down, slope, grad, sums):
             @pl.loop(0, units // tile)
@@ -577,17 +634,16 @@
                 grad[:, at] = value.astype(BF16)
                 sums[:, at] = sum_rows(value)
 
-        def sink_half(h, down):
+        def sink_half(lifted, down):
             return tape.run(
-                sink, [((rows, units), BF16), ((1, units), F32)], [top16, down, lifted[h][2]],
-                limit=8, flops=2 * rows * width * units, moved=8 * MIB,
-            )
-
-        sunk = [None, sink_half(1, c_oth)]
-        scatter_b = Scatter(grid, tape, sharded(weight_grad(hidden_t, sunk[1][0], BF16), 1))
-        scatter_c.pair(sharded(down_own, 1))
-        sunk[0] = sink_half(0, c_own)
-        up_own = weight_grad(hidden_t, sunk[0][0], F32)
+                sink, [((rows, units), BF16), ((1, units), F32)], [w.top16, down, lifted[2]], limit=8
+            )
+
+        def sink_own():
+            w.sink_own = sink_half(w.lift_own, w.c_own)
+
+        def sink_oth():
+            w.sink_oth = sink_half(w.lift_oth, w.c_oth)
 
         def surface(grad_own, grad_oth, own, oth, top_ref, normed, inverse, vec, a_own_ref, a_oth_ref,
                     mid, mid_t, back, sums, work, mid16):
@@ -619,20 +675,22 @@
                     mid16[...], ref[3], preferred_element_type=F32
                 ).astype(BF16)
 
-        mid, mid_t, back, sums_one = tape.run(
-            surface,
-            [((rows, width), F32), ((width, rows), BF16), ((rows, width), BF16), ((8, width), F32)],
-            [sunk[0][0], sunk[1][0], b_own, b_oth, top, normed_one, inverse_one, vectors, a_own, a_oth],
-            limit=14, flops=4 * rows * width * units + 2 * rows * width * width, moved=14 * MIB,
-            scratch=[VMEM((rows, width), F32), VMEM((rows, width), BF16)],
-        )
+        def surfaced():
+            w.mid, w.mid_t, w.back, w.sums_one = tape.run(
+                surface,
+                [((rows, width), F32), ((width, rows), BF16), ((rows, width), BF16), ((8, width), F32)],
+                [w.sink_own[0], w.sink_oth[0], w.b_own, w.b_oth, w.top, w.normed_one, w.inverse_one, vectors,
+                 w.a_own, w.a_oth],
+                limit=14, flops=4 * rows * width * units + 2 * rows * width * width, moved=14 * MIB,
+                scratch=[VMEM((rows, width), F32), VMEM((rows, width), BF16)],
+            )
 
         def pair_up(s, own, oth, out):
-            out[s[3]] = own[...]
-            out[1 - s[3]] = oth[...]
-
-        def paired(own, oth):
-            shape = ((cores,) + own.shape, own.dtype)
+            out[s[3]] = own[...].astype(out.dtype)
+            out[1 - s[3]] = oth[...].astype(out.dtype)
+
+        def paired(own, oth, kind):
+            shape = ((cores,) + own.shape, kind)
             result = tape.run(pair_up, [shape], [own, oth], True, limit=8, spill=(0,))[0]
             return result.reshape(pairs, length, width)
 
@@ -651,27 +709,44 @@
                     grad[at, lanes] = value.astype(BF16)
                     sums[:, lanes] += sum_rows(value)
 
-        grad_v, sum_v = tape.run(
-            values_back, [((rows, width), BF16), ((1, width), F32)], [probs, back],
-            limit=4, flops=4 * rows * length * width, moved=3 * MIB,
-        )
-
-        def attend_grad(h, kind, lefts, rights):
+        def valued():
+            w.grad_v, w.sum_v = tape.run(
+                values_back, [((rows, width), BF16), ((1, width), F32)], [w.probs, w.back],
+                limit=4, flops=4 * rows * length * width, moved=3 * MIB,
+            )
+
+        def attend_grad(h, kind, lefts, rights, pieces=1):
             def attend_grad_half(*refs):
                 at = slice(h * cols, (h + 1) * cols)
-                for left, right, out in zip(refs[:2], refs[2:4], refs[4:]):
-                    out[...] = jnp.dot(left[...], right[:, at], preferred_element_type=F32).astype(out.dtype)
+                share = cols // pieces
+                for j, (left, right) in enumerate(zip(refs[:2], refs[2:4])):
+                    value = jnp.dot(left[...], right[:, at], preferred_element_type=F32)
+                    for g, out in enumerate(refs[4:]):
+                        out[j] = value[:, g * share : (g + 1) * share].astype(kind)
 
             return tape.run(
-                attend_grad_half, [((width, cols), kind)] * 2, lefts + rights,
-                limit=6, flops=4 * rows * width * cols, moved=5 * MIB,
-            )
-
-        lefts_vo, rights_vo = [x_t, mid_t], [grad_v, context]
-        vo_oth = attend_grad(1, BF16, lefts_vo, rights_vo)
-        layer_output = paired(output, output_oth)
-        scatter_c.split(0)
-        scatter_b.pair(sharded(up_own, 1))
+                attend_grad_half, [((2, width, cols // pieces), kind)] * pieces, lefts + rights, limit=6
+            )
+
+        def vo_oth():
+            w.vo_oth = grid.core(attend_grad(1, BF16, [w.x_t, w.mid_t], [w.grad_v, w.context])[0])
+
+        def vo_own():
+            w.vo_own = attend_grad(0, F32, [w.x_t, w.mid_t], [w.grad_v, w.context])
+
+        def qk_oth():
+            pieces = cols // LANES
+            other = sharded(attend_grad(1, BF16, [w.x_t, w.x_t], [w.grad_q, w.grad_k], pieces), 2)
+            w.scatter_a = Scatter(grid, tape, [(v, 0, LANES * i) for i, v in enumerate(other)])
+
+        def qk_own():
+            w.qk_own = attend_grad(0, F32, [w.x_t, w.x_t], [w.grad_q, w.grad_k])
+
+        def vo_sum():
+            w.vo_sum = tape.run(add_up, [((2, width, cols), F32)], [w.vo_own[0], w.vo_oth])
+
+        def pair_a():
+            w.scatter_a.pair(sharded(w.qk_own + w.vo_sum, 2))
 
         def attend_back(probs_ref, back_ref, qkv_ref, grad_q, grad_k, sums):
             sums[...] = jnp.zeros_like(sums)
@@ -697,40 +772,13 @@
                     value = join(lax.dot_general(grad, qkv_ref[0, at, lanes], TN, preferred_element_type=F32))
                     grad_k[at, lanes] = (value * scale).astype(BF16)
 
-        grad_q, grad_k, sum_q = tape.run(
-            attend_back, [((rows, width), BF16), ((rows, width), BF16), ((1, width), F32)], [probs, back, qkv],
-            limit=4, flops=16 * rows * length * width, moved=6 * MIB,
-        )
-        qk_oth = attend_grad(1, BF16, [x_t, x_t], [grad_q, grad_k])
-        scatter_a = Scatter(grid, tape, sharded([*qk_oth, *vo_oth], 1))
-        scatter_c.split(1)
-        qk_own = attend_grad(0, F32, [x_t, x_t], [grad_q, grad_k])
-        vo_own = attend_grad(0, F32, lefts_vo, rights_vo)
-
-
-        def matrix_step(index):
-            def step(*refs):
-                grad = refs[0][...] + refs[1][...].astype(F32)
-                master, first, second, moment, square, way, kept, tile_ref = refs[2:]
-                moment[...], square[...], value = adam(grad, first[...], second[...])
-                kept[...] = master[...]
-                way[...] = value + DECAY * kept[...]
-                tile_ref[...] = norm_row([(index, kept[0], way[0])])
-
-            return step
-
-        def stepped(step, parts, masters, shapes):
-            outs = [(s, F32) for _ in range(4) for s in shapes] + [((1, LANES), F32)]
-            n, m = len(parts), len(masters)
-            return tape.run(
-                step, outs, parts + masters, limit=6, spill=range(2 * len(shapes)), plain=range(n, n + m), moved=2 * MIB
-            )
-
-        ups = [v[None] for v in (expand_up, first_up, second_up)]
-        downs = [v[None] for v in (expand_down, first_down, second_down)]
-        scatter_b.split(0)
-        scatter_a.pair(sharded([*qk_own, *vo_own], 1))
-        scatter_c.split(2)
+        def attended_back():
+            w.grad_q, w.grad_k, w.sum_q = tape.run(
+                attend_back, [((rows, width), BF16), ((rows, width), BF16), ((1, width), F32)], [w.probs, w.back, w.qkv],
+                limit=4, flops=16 * rows * length * width, moved=6 * MIB,
+            )
+        def add_up(own, oth, out):
+            out[...] = own[...] + oth[...].astype(F32)
 
         def states_back(grad_q_ref, grad_k_ref, grad_v_ref, own, oth, mid_ref, out):
             @pl.loop(0, width // tile)
@@ -742,14 +790,36 @@
                         value += lax.dot_general(
                             ref[:, h * cols : (h + 1) * cols], weight[j, at, :], NT, preferred_element_type=F32
                         )
-                out[:, at] = value
-
-        states_own = tape.run(
-            states_back, [((rows, width), F32)], [grad_q, grad_k, grad_v, a_own, a_oth, mid],
-            limit=8, flops=6 * rows * width * width, moved=8 * MIB,
-        )[0]
-
-        states_oth = grid.core(states_own)
+                out[:, at] = value.astype(BF16)
+
+        def states_own():
+            w.states_own = tape.run(
+                states_back, [((rows, width), BF16)], [w.grad_q, w.grad_k, w.grad_v, w.a_own, w.a_oth, w.mid],
+                limit=8, flops=6 * rows * width * width, moved=8 * MIB,
+            )[0]
+
+        def matrix_step(index):
+            def step(*refs):
+                grad = refs[0][...] + refs[1][...].astype(F32)
+                grad = jnp.concatenate([grad[j] for j in range(grad.shape[0])], axis=-1)[None]
+                master, first, second, moment, square, way, kept, tile_ref = refs[2:]
+                moment[...], square[...], value = adam(grad, first[...], second[...])
+                kept[...] = master[...]
+                way[...] = value + DECAY * kept[...]
+                tile_ref[...] = norm_row([(index, kept[0], way[0])])
+
+            return step
+
+        def stepped(step, parts, masters, shapes):
+            outs = [(s, F32) for _ in range(4) for s in shapes] + [((1, LANES), F32)]
+            n, m = len(parts), len(masters)
+            return tape.run(
+                step, outs, parts + masters, limit=6, spill=range(2 * len(shapes)), plain=range(n, n + m), moved=2 * MIB
+            )
+
+        ups = [v[None] for v in (expand_up, first_up, second_up)]
+        downs = [v[None] for v in (expand_down, first_down, second_down)]
+
         def collect(s, sum_q_ref, sum_v_ref, one, two, up_own_ref, up_oth_ref, out):
             for t in range(cores):
 
@@ -768,11 +838,13 @@
             out[2:5] = one[0:3]
             out[5:8] = two[0:3]
 
-        vector_part = tape.run(
-            collect, [(vectors.shape, F32)], [sum_q, sum_v, sums_one, sums_two, sunk[0][1], sunk[1][1]], True
-        )[0]
-        vector_oth = grid.core(vector_part)
         half = vectors.shape[0] // cores
+
+        def collected():
+            w.vector_part = tape.run(
+                    collect, [(vectors.shape, F32)],
+                    [w.sum_q, w.sum_v, w.sums_one, w.sums_two, w.sink_own[1], w.sink_oth[1]], True,
+            )[0]
 
         def vector_half(s, own, oth, out):
             for t in range(cores):
@@ -782,21 +854,24 @@
                     at = slice(t * half, (t + 1) * half)
                     out[...] = own[at] + oth[at]
 
-        vector_share = tape.run(vector_half, [((half, width), F32)], [vector_part, vector_oth], True)[0]
-        moment_down, square_down, way_down, kept_down, tile_down = stepped(
-            matrix_step(5), scatter_c.parts, downs, [downs[0].shape]
-        )
-        scatter_b.split(1)
-        scatter_a.split_short()
-        states_grad = paired(states_own, states_oth)
-        scatter_b.split(2)
-        scatter_a.split_long()
-        moment_up, square_up, way_up, kept_up, tile_up = stepped(
-            matrix_step(4), scatter_b.parts, ups, [ups[0].shape]
-        )
+        def vector_shared():
+            parts = [w.vector_part, grid.core(w.vector_part)]
+            w.vector_share = tape.run(vector_half, [((half, width), F32)], parts, True)[0]
+
+        def step_c():
+            w.step_c = stepped(matrix_step(5), w.scatter_c.parts, downs, [downs[0].shape])
+
+        def step_b():
+            w.step_b = stepped(matrix_step(4), w.scatter_b.parts, ups, [ups[0].shape])
+
+        def states_pair():
+            w.states_grad = paired(w.states_own, grid.core(w.states_own), F32)
+
+        def output_pair():
+            w.layer_output = paired(w.output, grid.core(w.output), BF16)
 
         def attend_step(*refs):
-            n = len(scatter_a.parts)
+            n = len(w.scatter_a.parts)
             m_in, f_in, s_in, m_out, f_out, s_out, tile_up_ref, tile_down_ref, share = refs[n : n + 9]
             mo_in, mo_out, sq_in, sq_out, way_in, way_out, kept_in, kept_out, load = refs[n + 9 :]
             entries = []
@@ -818,11 +893,34 @@
 
         shapes = [attend_in.shape, attend_out.shape]
         masters = [attend_in, first_in, second_in, attend_out, first_out, second_out]
-        moment_in, moment_out, square_in, square_out, way_in, way_out, kept_in, kept_out, load = tape.run(
-            attend_step, [(s, F32) for _ in range(4) for s in shapes] + [((8, width), F32)],
-            scatter_a.parts + masters + [tile_up, tile_down, vector_share],
-            limit=6, spill=range(4), plain=range(grid.long, grid.long + 6), moved=2 * MIB,
-        )
+        def step_a():
+            w.step_a = tape.run(
+                attend_step, [(s, F32) for _ in range(4) for s in shapes] + [((8, width), F32)],
+                w.scatter_a.parts + masters + [w.step_b[4], w.step_c[4], w.vector_share],
+                limit=6, spill=range(4), plain=range(len(w.scatter_a.parts), len(w.scatter_a.parts) + 6),
+            )
+
+        stages = {
+            "a0": lambda: w.gather_a.merge_long(), "a1": lambda: w.gather_a.merge_short(),
+            "b0": lambda: w.gather_b.merge(0), "b1": lambda: w.gather_b.merge(1), "b2": lambda: w.gather_b.merge(2),
+            "c0": lambda: w.gather_c.merge(0), "c1": lambda: w.gather_c.merge(1), "c2": lambda: w.gather_c.merge(2),
+            "A0": lambda: w.scatter_a.split(0), "A1": lambda: w.scatter_a.split(1), "A2": lambda: w.scatter_a.split(2),
+            "B0": lambda: w.scatter_b.split(0), "B1": lambda: w.scatter_b.split(1), "B2": lambda: w.scatter_b.split(2),
+            "C0": lambda: w.scatter_c.split(0), "C1": lambda: w.scatter_c.split(1), "C2": lambda: w.scatter_c.split(2),
+            "castA": cast_a, "castB": cast_b, "castC": cast_c, "prep": prepared, "wholeA": whole_a, "wholeB": whole_b,
+            "wholeC": whole_c, "project": projected, "attend": attended, "hide": hid, "liftOwn": lift_own,
+            "liftOth": lift_oth, "turn": turned, "lowerOwn": lowered_own, "lower": lowered_all, "downOth": down_oth,
+            "downOwn": down_own, "pairC": pair_c, "upOth": up_oth, "upOwn": up_own, "pairB": pair_b, "sinkOwn": sink_own,
+            "sinkOth": sink_oth, "surface": surfaced, "values": valued, "voOth": vo_oth, "voOwn": vo_own,
+            "qkOth": qk_oth, "qkOwn": qk_own, "voSum": vo_sum, "pairA": pair_a, "back": attended_back,
+            "states": states_own, "collect": collected, "share": vector_shared, "stepC": step_c, "stepB": step_b,
+            "pairS": states_pair, "pairO": output_pair, "stepA": step_a,
+        }
+        for name in ORDER:
+            stages[name]()
+        moment_down, square_down, way_down, kept_down, _ = w.step_c
+        moment_up, square_up, way_up, kept_up, _ = w.step_b
+        moment_in, moment_out, square_in, square_out, way_in, way_out, kept_in, kept_out, load = w.step_a
         total = Total(grid, tape, load)
         total.line()
         total.sides()
@@ -864,7 +962,7 @@
             return (values[0], values[1][0].T, values[2][0], values[3][0])
 
         return (
-            layer_output, states_grad, *native(results[:4]),
+            w.layer_output, w.states_grad, *native(results[:4]),
             *native([moment_in, moment_out, moment_up, moment_down]),
             *native([square_in, square_out, square_up, square_down]),
             *native(results[4:8]), updated_vectors, moment_vectors, square_vectors, results[8].T,

time: 237 us -> 221 us (0.932)
  waiting for transfers between devices: 99.8 us -> 87.3 us
  starting transfers between devices: 47.5 us -> 42.8 us
    ppermute x45 -> x47, waiting for transfers between devices: 99.8 us -> 87.3 us  [send(): return lax.ppermute(value, AXES, pairs)]
    ppermute x45 -> x47, starting transfers between devices: 47.5 us -> 42.8 us  [send(): return lax.ppermute(value, AXES, pairs)]
    pallas_call x58 -> x60, Pallas kernels: 81.9 us -> 82.6 us  [run(): pl.pallas_call(chain, out_shape=shapes, in_specs=[pl.BlockSpec(memory_spa...]
  transfers between devices with their start and end apart: 45 -> 47, of which waited for: 26 -> 21; matrix products, arithmetic and copies ran while one was open for 0% -> 0% of each run, Pallas kernels for 29% -> 30%
where the time goes in v4:
time: 221 us; the launch traced here: 220 us
  waiting for transfers between devices  87.3 us (40%)
  Pallas kernels  82.6 us (37%)
  starting transfers between devices  42.8 us (19%)
  local copies, waits for them, and re-layouts  5.67 us (3%)
    ppermute x47, waiting for transfers between devices, send(): return lax.ppermute(value, AXES, pairs)  87.3 us
    pallas_call x60, Pallas kernels, run(): pl.pallas_call(chain, out_shape=shapes, in_specs=[pl.BlockSpec(memory_spa...  82.6 us
    ppermute x47, starting transfers between devices, send(): return lax.ppermute(value, AXES, pairs)  42.8 us
    unnamed x40, local copies, waits for them, and re-layouts  5.51 us
  transfers between devices with their start and end apart: 47, of which 21 were waited for; matrix products, arithmetic and copies ran while one was open for 0% of the time, Pallas kernels for 30%

profile of v4, /device:TPU:0, one launch (start us, length us, event | category | flops | bytes accessed | tf_op | source)
XLA Modules:
  0.0 220.4 jit_solution(2802317084831785690)
XLA Ops:
  2.5 3.1 %collective-permute-start = (bf16[4,48,384]{2,1,0:T(8,128)(2,1)S(1)}, bf16[4,48,384]{2,1,0:T(8,128)(2,1)S(1)}, u32[]{:S(2)}, u32[]{:S(2)}) collective-permute-start(bf16[4,48,384]{2,1,0:T(8,128)(2,1)S(1)} %get-tuple-element.213.refs_2_), channel_id=1, source_target_pairs={{0,8},{1,9},{2,10},{3,11},{4,12},{5,13},{6,14},{7,15},{8,0},{9,1},... | collective-permute-start | bytes 442376 | tf_op jit(solution)/shard_map/ppermute | solution.py:66
  5.6 2.6 %collective-permute-start.1 = (bf16[4,48,384]{2,1,0:T(8,128)(2,1)S(1)}, bf16[4,48,384]{2,1,0:T(8,128)(2,1)S(1)}, u32[]{:S(2)}, u32[]{:S(2)}) collective-permute-start(bf16[4,48,384]{2,1,0:T(8,128)(2,1)S(1)} %get-tuple-element.213.refs_2_), channel_id=1, source_target_pairs={{0,16},{1,17},{2,18},{3,19},{4,20},{5,21},{6,22},{7,23},{8,24},{9,... | collective-permute-start | bytes 442376 | tf_op jit(solution)/shard_map/ppermute | solution.py:66
  9.0 1.4 copy-done
  10.4 1.4 copy-done.1
  13.6 6.0 %collective-permute-done.1.refs_4_ = bf16[4,48,384]{2,1,0:T(8,128)(2,1)S(1)} collective-permute-done((bf16[4,48,384]{2,1,0:T(8,128)(2,1)S(1)}, bf16[4,48,384]{2,1,0:T(8,128)(2,1)S(1)}, u32[]{:S(2)}, u32[]{:S(2)}) %collective-permute-start.1) | collective-permute-done | bytes 147488 | tf_op jit(solution)/shard_map/ppermute | solution.py:66
  20.2 1.6 collective-permute-start.4
  21.8 3.3 %collective-permute-start.3 = (bf16[1,48,1536]{2,1,0:T(8,128)(2,1)S(1)}, bf16[1,48,1536]{2,1,0:T(8,128)(2,1)S(1)}, u32[]{:S(2)}, u32[]{:S(2)}) collective-permute-start(bf16[1,48,1536]{2,1,0:T(8,128)(2,1)S(1)} %get-tuple-element.215.refs_2_), channel_id=1, source_target_pairs={{0,16},{1,17},{2,18},{3,19},{4,20},{5,21},{6,22},{7,23},{8,24},{9,... | collective-permute-start | bytes 442376 | tf_op jit(solution)/shard_map/ppermute | solution.py:66
  25.1 5.8 %collective-permute-done.3.refs_3_ = bf16[1,48,1536]{2,1,0:T(8,128)(2,1)S(1)} collective-permute-done((bf16[1,48,1536]{2,1,0:T(8,128)(2,1)S(1)}, bf16[1,48,1536]{2,1,0:T(8,128)(2,1)S(1)}, u32[]{:S(2)}, u32[]{:S(2)}) %collective-permute-start.3) | collective-permute-done | bytes 147488 | tf_op jit(solution)/shard_map/ppermute | solution.py:66
  32.7 2.0 collective-permute-start.6
  34.7 1.6 collective-permute-start.5
  36.3 5.3 %collective-permute-done.5.refs_3_ = bf16[1,96,768]{2,1,0:T(8,128)(2,1)S(1)} collective-permute-done((bf16[1,96,768]{2,1,0:T(8,128)(2,1)S(1)}, bf16[1,96,768]{2,1,0:T(8,128)(2,1)S(1)}, u32[]{:S(2)}, u32[]{:S(2)}) %collective-permute-start.5) | collective-permute-done | bytes 147488 | tf_op jit(solution)/shard_map/ppermute | solution.py:66
  42.8 1.6 collective-permute-start.8
  44.3 1.0 collective-permute-start.7
  45.3 11.8 %collective-permute-done.7.refs_3_ = bf16[2,1,96,768]{3,2,1,0:T(8,128)(2,1)S(1)} collective-permute-done((bf16[2,1,96,768]{3,2,1,0:T(8,128)(2,1)S(1)}, bf16[2,1,96,768]{3,2,1,0:T(8,128)(2,1)S(1)}, u32[]{:S(2)}, u32[]{:S(2)}) %collective-permute-start.7) | collective-permute-done | bytes 294944 | tf_op jit(solution)/shard_map/ppermute | solution.py:66
  59.2 1.7 collective-permute-start.12
  60.9 2.8 %collective-permute-done.10 = bf16[4,16,48,384]{3,2,1,0:T(8,128)(2,1)S(1)} collective-permute-done((bf16[4,16,48,384]{3,2,1,0:T(8,128)(2,1)S(1)}, bf16[4,16,48,384]{3,2,1,0:T(8,128)(2,1)S(1)}, u32[]{:S(2)}, u32[]{:S(2)}) %collective-permute-start.10) | collective-permute-done | bytes 2359328 | tf_op jit(solution)/shard_map/ppermute | solution.py:66
  63.7 3.0 %project.1 = (bf16[3,512,768]{2,1,0:T(8,128)(2,1)S(1)}, f32[8,128]{1,0:T(8,128)S(1)}) custom-call(f32[8,128]{1,0:T(8,128)S(1)} %get-tuple-element.229.refs_0_, bf16[512,768]{1,0:T(8,128)(2,1)S(1)} %get-tuple-element.230.refs_1_.refs_2_, bf16[4,768,384]{2,1,0:T(8,128)(2,1)S(1)} %bitcast.63, bf16[4,768,384]{2,1,0:T(8,128)(2,1)S(1)} %bitcast.67, ...), custom_call_target="tpu_custom_call" | custom-call | flops 1811939328 | bytes 8388608 | tf_op jit(solution)/shard_map/project/pallas_call | solution.py:141
  66.7 4.6 %attend.1 = (bf16[512,1536]{1,0:T(8,128)(2,1)S(1)}, bf16[512,768]{1,0:T(8,128)(2,1)S(1)}, f32[8,128]{1,0:T(8,128)S(1)}) custom-call(s32[8]{0:T(128)S(1)} %concatenate.3.refs_0_, f32[8,128]{1,0:T(8,128)S(1)} %get-tuple-element.233.refs_1_, bf16[3,512,768]{2,1,0:T(8,128)(2,1)S(1)} %get-tuple-element.234.refs_2_.refs_3_), custom_call_target="tpu_custom_call" | custom-call | flops 805306368 | bytes 5242880 | tf_op jit(solution)/shard_map/attend/pallas_call | solution.py:141
  71.3 3.6 %collective-permute-done.11.refs_3_ = bf16[2,2,1,96,768]{4,3,2,1,0:T(8,128)(2,1)S(1)} collective-permute-done((bf16[2,2,1,96,768]{4,3,2,1,0:T(8,128)(2,1)S(1)}, bf16[2,2,1,96,768]{4,3,2,1,0:T(8,128)(2,1)S(1)}, u32[]{:S(2)}, u32[]{:S(2)}) %collective-permute-start.11) | collective-permute-done | bytes 589856 | tf_op jit(solution)/shard_map/ppermute | solution.py:66
  76.4 1.7 collective-permute-start.14
  78.1 1.3 hide.1
  79.4 3.4 %_lambda_.2 = (bf16[512,1536]{1,0:T(8,128)(2,1)S(1)}, bf16[1536,512]{1,0:T(8,128)(2,1)S(1)}, bf16[512,1536]{1,0:T(8,128)(2,1)S(1)}, f32[8,128]{1,0:T(8,128)S(1)}) custom-call(f32[8,128]{1,0:T(8,128)S(1)} %get-tuple-element.241.refs_0_, bf16[512,768]{1,0:T(8,128)(2,1)S(1)} %get-tuple-element.242.refs_1_, bf16[768,1536]{1,0:T(8,128)(2,1)S(1)} %bitcast.76, ...), custom_call_target="tpu_custom_call" | custom-call | flops 1207959552 | bytes 8388608 | tf_op jit(solution)/shard_map/<lambda>/pallas_call | solution.py:141
  82.8 3.4 %_lambda_.3 = (bf16[512,1536]{1,0:T(8,128)(2,1)S(1)}, bf16[1536,512]{1,0:T(8,128)(2,1)S(1)}, bf16[512,1536]{1,0:T(8,128)(2,1)S(1)}, f32[8,128]{1,0:T(8,128)S(1)}) custom-call(f32[8,128]{1,0:T(8,128)S(1)} %get-tuple-element.245.refs_0_, bf16[512,768]{1,0:T(8,128)(2,1)S(1)} %get-tuple-element.242.refs_1_, bf16[768,1536]{1,0:T(8,128)(2,1)S(1)} %bitcast.78, ...), custom_call_target="tpu_custom_call" | custom-call | flops 1207959552 | bytes 8388608 | tf_op jit(solution)/shard_map/<lambda>/pallas_call | solution.py:141
  86.5 6.2 %collective-permute-done.14.refs_3_ = bf16[2,2,2,1,96,768]{5,4,3,2,1,0:T(8,128)(2,1)S(1)} collective-permute-done((bf16[2,2,2,1,96,768]{5,4,3,2,1,0:T(8,128)(2,1)S(1)}, bf16[2,2,2,1,96,768]{5,4,3,2,1,0:T(8,128)(2,1)S(1)}, u32[]{:S(2)}, u32[]{:S(2)}) %collective-permute-start.14) | collective-permute-done | bytes 1179680 | tf_op jit(solution)/shard_map/ppermute | solution.py:66
  93.4 1.7 lower_half.1
  95.2 2.8 %collective-permute-done.15 = bf16[1,16,96,768]{3,2,1,0:T(8,128)(2,1)S(1)} collective-permute-done((bf16[1,16,96,768]{3,2,1,0:T(8,128)(2,1)S(1)}, bf16[1,16,96,768]{3,2,1,0:T(8,128)(2,1)S(1)}, u32[]{:S(2)}, u32[]{:S(2)}) %collective-permute-start.15) | collective-permute-done | bytes 2359328 | tf_op jit(solution)/shard_map/ppermute | solution.py:66
  98.0 4.0 %lower.1 = (bf16[512,768]{1,0:T(8,128)(2,1)S(1)}, f32[512,768]{1,0:T(8,128)S(1)}, bf16[512,768]{1,0:T(8,128)(2,1)S(1)}, f32[8,768]{1,0:T(8,128)S(1)}, f32[8,128]{1,0:T(8,128)S(1)}) custom-call(s32[8]{0:T(128)S(1)} %concatenate.3.refs_0_, f32[8,128]{1,0:T(8,128)S(1)} %get-tuple-element.252.refs_1_, f32[512,768]{1,0:T(8,128)S(1)} %get-tuple-element.253.refs_2_, ...), custom_call_target="tpu_custom_call" | custom-call | flops 1207959552 | bytes 14680064 | tf_op jit(solution)/shard_map/lower/pallas_call | solution.py:141
  102.0 2.5 %sink.2 = (bf16[512,1536]{1,0:T(8,128)(2,1)S(1)}, f32[1,1536]{1,0:T(1,128)S(1)}, f32[8,128]{1,0:T(8,128)S(1)}) custom-call(f32[8,128]{1,0:T(8,128)S(1)} %get-tuple-element.257.refs_0_, bf16[512,768]{1,0:T(8,128)(2,1)S(1)} %get-tuple-element.258.refs_1_.refs_2_, bf16[1536,768]{1,0:T(8,128)(2,1)S(1)} %bitcast.72, bf16[512,1536]{1,0:T(8,128)(2,1)S(1)} %get-tuple-element.259.refs_3_), custom_call_target="tpu_custom_call" | custom-call | tf_op jit(solution)/shard_map/sink/pallas_call | solution.py:141
  104.5 2.2 %product.4 = (bf16[1536,768]{1,0:T(8,128)(2,1)S(1)}, f32[8,128]{1,0:T(8,128)S(1)}) custom-call(f32[8,128]{1,0:T(8,128)S(1)} %get-tuple-element.260.refs_0_, bf16[1536,512]{1,0:T(8,128)(2,1)S(1)} %get-tuple-element.261.refs_1_, bf16[512,768]{1,0:T(8,128)(2,1)S(1)} %get-tuple-element.258.refs_1_.refs_2_), custom_call_target="tpu_custom_call" | custom-call | flops 1207959552 | bytes 8388608 | tf_op jit(solution)/shard_map/product/pallas_call | solution.py:141
  106.9 2.2 %product.5 = (f32[1536,768]{1,0:T(8,128)S(1)}, f32[8,128]{1,0:T(8,128)S(1)}) custom-call(f32[8,128]{1,0:T(8,128)S(1)} %get-tuple-element.262.refs_0_, bf16[1536,512]{1,0:T(8,128)(2,1)S(1)} %get-tuple-element.263.refs_1_, bf16[512,768]{1,0:T(8,128)(2,1)S(1)} %get-tuple-element.258.refs_1_.refs_2_), custom_call_target="tpu_custom_call" | custom-call | flops 1207959552 | bytes 8388608 | tf_op jit(solution)/shard_map/product/pallas_call | solution.py:141
  109.1 1.7 product.6
  112.0 1.1 scatter_pair.3
  113.0 1.7 collective-permute-start.21
  114.8 2.5 %sink.3 = (bf16[512,1536]{1,0:T(8,128)(2,1)S(1)}, f32[1,1536]{1,0:T(1,128)S(1)}, f32[8,128]{1,0:T(8,128)S(1)}) custom-call(f32[8,128]{1,0:T(8,128)S(1)} %get-tuple-element.270.refs_0_, bf16[512,768]{1,0:T(8,128)(2,1)S(1)} %get-tuple-element.258.refs_1_.refs_2_, bf16[1536,768]{1,0:T(8,128)(2,1)S(1)} %bitcast.75, bf16[512,1536]{1,0:T(8,128)(2,1)S(1)} %get-tuple-element.271.refs_3_), custom_call_target="tpu_custom_call" | custom-call | tf_op jit(solution)/shard_map/sink/pallas_call | solution.py:141
  117.3 1.7 product.7
  119.1 1.0 scatter_pair.4
  120.1 5.1 %surface.1 = (f32[512,768]{1,0:T(8,128)S(1)}, bf16[768,512]{1,0:T(8,128)(2,1)S(1)}, bf16[512,768]{1,0:T(8,128)(2,1)S(1)}, f32[8,768]{1,0:T(8,128)S(1)}, f32[8,128]{1,0:T(8,128)S(1)}) custom-call(f32[8,128]{1,0:T(8,128)S(1)} %get-tuple-element.283.refs_0_, bf16[512,1536]{1,0:T(8,128)(2,1)S(1)} %get-tuple-element.273.refs_2_.refs_1_, ...), custom_call_target="tpu_custom_call" | custom-call | flops 3019898880 | bytes 14680064 | tf_op jit(solution)/shard_map/surface/pallas_call | solution.py:141
  125.2 1.2 values_back.1
  127.9 1.4 collective-permute-done.21.refs_3_
  130.4 6.6 %attend_back.1 = (bf16[512,768]{1,0:T(8,128)(2,1)S(1)}, bf16[512,768]{1,0:T(8,128)(2,1)S(1)}, f32[1,768]{1,0:T(1,128)S(1)}, f32[8,128]{1,0:T(8,128)S(1)}) custom-call(f32[8,128]{1,0:T(8,128)S(1)} %get-tuple-element.296.refs_0_, bf16[512,1536]{1,0:T(8,128)(2,1)S(1)} %get-tuple-element.287.refs_1_, bf16[512,768]{1,0:T(8,128)(2,1)S(1)} %get-tuple-element.288.refs_2_, ...), custom_call_target="tpu_custom_call" | custom-call | flops 805306368 | bytes 6291456 | tf_op jit(solution)/shard_map/attend_back/pallas_call | solution.py:141
  140.9 3.0 %collective-permute-done.23.refs_3_ = bf16[2,2,2,4,48,384]{5,4,3,2,1,0:T(8,128)(2,1)S(1)} collective-permute-done((bf16[2,2,2,4,48,384]{5,4,3,2,1,0:T(8,128)(2,1)S(1)}, bf16[2,2,2,4,48,384]{5,4,3,2,1,0:T(8,128)(2,1)S(1)}, u32[]{:S(2)}, u32[]{:S(2)}) %collective-permute-start.23) | collective-permute-done | bytes 1179680 | tf_op jit(solution)/shard_map/ppermute | solution.py:66
  146.5 1.7 collective-permute-start.30
  148.3 3.0 %states_back.1 = (bf16[512,768]{1,0:T(8,128)(2,1)S(1)}, f32[8,128]{1,0:T(8,128)S(1)}) custom-call(f32[8,128]{1,0:T(8,128)S(1)} %get-tuple-element.317.refs_0_, bf16[512,768]{1,0:T(8,128)(2,1)S(1)} %get-tuple-element.298.refs_3_.refs_1_, bf16[512,768]{1,0:T(8,128)(2,1)S(1)} %get-tuple-element.299.refs_4_.refs_2_, ...), custom_call_target="tpu_custom_call" | custom-call | flops 1811939328 | bytes 8388608 | tf_op jit(solution)/shard_map/states_back/pallas_call | solution.py:141
  151.9 1.3 collective-permute-start.31
  153.8 9.1 %collective-permute-done.29.refs_3_ = bf16[2,1,96,768]{3,2,1,0:T(8,128)(2,1)S(1)} collective-permute-done((bf16[2,1,96,768]{3,2,1,0:T(8,128)(2,1)S(1)}, bf16[2,1,96,768]{3,2,1,0:T(8,128)(2,1)S(1)}, u32[]{:S(2)}, u32[]{:S(2)}) %collective-permute-start.29) | collective-permute-done | bytes 294944 | tf_op jit(solution)/shard_map/ppermute | solution.py:66
  164.3 1.1 collective-permute-start.32
  165.9 7.9 %collective-permute-done.31.refs_3_ = bf16[2,2,4,48,384]{4,3,2,1,0:T(8,128)(2,1)S(1)} collective-permute-done((bf16[2,2,4,48,384]{4,3,2,1,0:T(8,128)(2,1)S(1)}, bf16[2,2,4,48,384]{4,3,2,1,0:T(8,128)(2,1)S(1)}, u32[]{:S(2)}, u32[]{:S(2)}) %collective-permute-start.31) | collective-permute-done | bytes 589856 | tf_op jit(solution)/shard_map/ppermute | solution.py:66
  175.3 3.2 %collective-permute-start.35 = (bf16[2,4,48,384]{3,2,1,0:T(8,128)(2,1)S(1)}, bf16[2,4,48,384]{3,2,1,0:T(8,128)(2,1)S(1)}, u32[]{:S(2)}, u32[]{:S(2)}) collective-permute-start(bf16[2,4,48,384]{3,2,1,0:T(8,128)(2,1)S(1)} %get-tuple-element.348), channel_id=1, source_target_pairs={{0,16},{1,17},{2,18},{3,19},{4,20},{5,21},{6,22},{7,23},{8,24},{9,... | collective-permute-start | bytes 884744 | tf_op jit(solution)/shard_map/ppermute | solution.py:66
  178.8 11.1 %collective-permute-done.33.refs_3_ = bf16[2,4,48,384]{3,2,1,0:T(8,128)(2,1)S(1)} collective-permute-done((bf16[2,4,48,384]{3,2,1,0:T(8,128)(2,1)S(1)}, bf16[2,4,48,384]{3,2,1,0:T(8,128)(2,1)S(1)}, u32[]{:S(2)}, u32[]{:S(2)}) %collective-permute-start.33) | collective-permute-done | bytes 294944 | tf_op jit(solution)/shard_map/ppermute | solution.py:66
  190.6 1.2 step.2
  193.5 2.4 %pair_up.2 = (f32[2,512,768]{2,1,0:T(8,128)}, f32[8,128]{1,0:T(8,128)S(1)}) custom-call(s32[8]{0:T(128)S(1)} %concatenate.3.refs_0_, f32[8,128]{1,0:T(8,128)S(1)} %get-tuple-element.349.refs_1_, bf16[512,768]{1,0:T(8,128)(2,1)S(1)} %get-tuple-element.350.refs_2_, bf16[512,768]{1,0:T(8,128)(2,1)S(1)} %collective-permute-done.36.refs_3_), custom_call_target="tpu_custom_call" | custom-call | tf_op jit(solution)/shard_map/pair_up/pallas_call | solution.py:141
  195.9 1.8 pair_up.3
  197.7 1.2 step.3
  198.9 2.4 %collective-permute-done.39.refs_2_ = bf16[4,48,384]{2,1,0:T(8,128)(2,1)S(1)} collective-permute-done((bf16[4,48,384]{2,1,0:T(8,128)(2,1)S(1)}, bf16[4,48,384]{2,1,0:T(8,128)(2,1)S(1)}, u32[]{:S(2)}, u32[]{:S(2)}) %collective-permute-start.39) | collective-permute-done | bytes 147488 | tf_op jit(solution)/shard_map/ppermute | solution.py:66
  201.4 1.1 attend_step.1
  202.5 2.0 collective-permute-start.41
  204.5 2.4 %collective-permute-start.42 = (f32[8,768]{1,0:T(8,128)S(1)}, f32[8,768]{1,0:T(8,128)S(1)}, u32[]{:S(2)}, u32[]{:S(2)}) collective-permute-start(f32[8,768]{1,0:T(8,128)S(1)} %get-tuple-element.365.refs_1_), channel_id=1, source_target_pairs={{0,24},{1,25},{2,26},{3,27},{4,28},{5,29},{6,30},{7,31},{8,16},{9,... | collective-permute-start | bytes 73736 | tf_op jit(solution)/shard_map/ppermute | solution.py:66
  207.2 2.9 %collective-permute-done.42.refs_4_ = f32[8,768]{1,0:T(8,128)S(1)} collective-permute-done((f32[8,768]{1,0:T(8,128)S(1)}, f32[8,768]{1,0:T(8,128)S(1)}, u32[]{:S(2)}, u32[]{:S(2)}) %collective-permute-start.42) | collective-permute-done | bytes 24608 | tf_op jit(solution)/shard_map/ppermute | solution.py:66
  210.2 1.3 collective-permute-start.43
  212.4 1.3 collective-permute-start.45
  214.1 1.2 collective-permute-done.44.refs_3_
  215.2 1.9 collective-permute-done.45.refs_4_
  217.2 1.2 collective-permute-done.46.refs_3_
  218.4 2.0 update.1
  (133 shorter events, 31.7 us)
Async XLA Ops:
  2.5 11.1 %collective-permute-start = (bf16[4,48,384]{2,1,0:T(8,128)(2,1)S(1)}, bf16[4,48,384]{2,1,0:T(8,128)(2,1)S(1)}, u32[]{:S(2)}, u32[]{:S(2)}) collective-permute-start(bf16[4,48,384]{2,1,0:T(8,128)(2,1)S(1)} %get-tuple-element.213.refs_2_), channel_id=1, source_target_pairs={{0,8},{1,9},{2,10},{3,11},{4,12},{5,13},{6,14},{7,15},{8,0},{9,1},... | collective-permute-start | bytes 442376 | tf_op jit(solution)/shard_map/ppermute | solution.py:66
  5.6 14.0 %collective-permute-start.1 = (bf16[4,48,384]{2,1,0:T(8,128)(2,1)S(1)}, bf16[4,48,384]{2,1,0:T(8,128)(2,1)S(1)}, u32[]{:S(2)}, u32[]{:S(2)}) collective-permute-start(bf16[4,48,384]{2,1,0:T(8,128)(2,1)S(1)} %get-tuple-element.213.refs_2_), channel_id=1, source_target_pairs={{0,16},{1,17},{2,18},{3,19},{4,20},{5,21},{6,22},{7,23},{8,24},{9,... | collective-permute-start | bytes 442376 | tf_op jit(solution)/shard_map/ppermute | solution.py:66
  8.2 11.4 %collective-permute-start.2 = (bf16[4,48,384]{2,1,0:T(8,128)(2,1)S(1)}, bf16[4,48,384]{2,1,0:T(8,128)(2,1)S(1)}, u32[]{:S(2)}, u32[]{:S(2)}) collective-permute-start(bf16[4,48,384]{2,1,0:T(8,128)(2,1)S(1)} %get-tuple-element.213.refs_2_), channel_id=1, source_target_pairs={{0,24},{1,25},{2,26},{3,27},{4,28},{5,29},{6,30},{7,31},{8,16},{9,... | collective-permute-start | bytes 442376 | tf_op jit(solution)/shard_map/ppermute | solution.py:66
  9.0 1.4 copy-start
  10.4 1.4 copy-start.1
  12.6 1.0 copy-start.5
  13.6 21.1 %copy-start.4 = (f32[96,768]{1,0:T(8,128)S(1)}, f32[96,768]{1,0:T(8,128)}, u32[]{:S(2)}) copy-start(f32[96,768]{1,0:T(8,128)} %param.26) | copy-start | bytes 884740
  20.2 11.2 %collective-permute-start.4 = (bf16[2,2,4,48,384]{4,3,2,1,0:T(8,128)(2,1)S(1)}, bf16[2,2,4,48,384]{4,3,2,1,0:T(8,128)(2,1)S(1)}, u32[]{:S(2)}, u32[]{:S(2)}) collective-permute-start(bf16[2,2,4,48,384]{4,3,2,1,0:T(8,128)(2,1)S(1)} %get-tuple-element.217.refs_2_), channel_id=1, source_target_pairs={{0,2},{1,5},{2,0},{3,7},{4,6},{5,1},{6,4},{7,3},{8,10},{9,13},{10,... | collective-permute-start | bytes 1769480 | tf_op jit(solution)/shard_map/ppermute | solution.py:66
  21.8 9.1 %collective-permute-start.3 = (bf16[1,48,1536]{2,1,0:T(8,128)(2,1)S(1)}, bf16[1,48,1536]{2,1,0:T(8,128)(2,1)S(1)}, u32[]{:S(2)}, u32[]{:S(2)}) collective-permute-start(bf16[1,48,1536]{2,1,0:T(8,128)(2,1)S(1)} %get-tuple-element.215.refs_2_), channel_id=1, source_target_pairs={{0,16},{1,17},{2,18},{3,19},{4,20},{5,21},{6,22},{7,23},{8,24},{9,... | collective-permute-start | bytes 442376 | tf_op jit(solution)/shard_map/ppermute | solution.py:66
  32.1 26.2 %collective-permute-start.9 = (bf16[2,2,2,4,48,384]{5,4,3,2,1,0:T(8,128)(2,1)S(1)}, bf16[2,2,2,4,48,384]{5,4,3,2,1,0:T(8,128)(2,1)S(1)}, u32[]{:S(2)}, u32[]{:S(2)}) collective-permute-start(bf16[2,2,2,4,48,384]{5,4,3,2,1,0:T(8,128)(2,1)S(1)} %get-tuple-element.228.refs_2_), channel_id=1, source_target_pairs={{0,4},{1,3},{2,6},{3,1},{4,0},{5,7},{6,2},{7,5},{8,12},{9,11},{10,... | collective-permute-start | bytes 3538952 | tf_op jit(solution)/shard_map/ppermute | solution.py:66
  32.7 9.5 %collective-permute-start.6 = (bf16[2,1,48,1536]{3,2,1,0:T(8,128)(2,1)S(1)}, bf16[2,1,48,1536]{3,2,1,0:T(8,128)(2,1)S(1)}, u32[]{:S(2)}, u32[]{:S(2)}) collective-permute-start(bf16[2,1,48,1536]{3,2,1,0:T(8,128)(2,1)S(1)} %get-tuple-element.222.refs_2_), channel_id=1, source_target_pairs={{0,8},{1,9},{2,10},{3,11},{4,12},{5,13},{6,14},{7,15},{8,0},{9,1},... | collective-permute-start | bytes 884744 | tf_op jit(solution)/shard_map/ppermute | solution.py:66
  34.7 6.9 %collective-permute-start.5 = (bf16[1,96,768]{2,1,0:T(8,128)(2,1)S(1)}, bf16[1,96,768]{2,1,0:T(8,128)(2,1)S(1)}, u32[]{:S(2)}, u32[]{:S(2)}) collective-permute-start(bf16[1,96,768]{2,1,0:T(8,128)(2,1)S(1)} %get-tuple-element.220.refs_2_), channel_id=1, source_target_pairs={{0,2},{1,5},{2,0},{3,7},{4,6},{5,1},{6,4},{7,3},{8,10},{9,13},{10,... | collective-permute-start | bytes 442376 | tf_op jit(solution)/shard_map/ppermute | solution.py:66
  42.8 15.0 %collective-permute-start.8 = (bf16[2,2,1,48,1536]{4,3,2,1,0:T(8,128)(2,1)S(1)}, bf16[2,2,1,48,1536]{4,3,2,1,0:T(8,128)(2,1)S(1)}, u32[]{:S(2)}, u32[]{:S(2)}) collective-permute-start(bf16[2,2,1,48,1536]{4,3,2,1,0:T(8,128)(2,1)S(1)} %get-tuple-element.226.refs_2_), channel_id=1, source_target_pairs={{0,2},{1,5},{2,0},{3,7},{4,6},{5,1},{6,4},{7,3},{8,10},{9,13},{10,... | collective-permute-start | bytes 1769480 | tf_op jit(solution)/shard_map/ppermute | solution.py:66
  44.3 12.8 %collective-permute-start.7 = (bf16[2,1,96,768]{3,2,1,0:T(8,128)(2,1)S(1)}, bf16[2,1,96,768]{3,2,1,0:T(8,128)(2,1)S(1)}, u32[]{:S(2)}, u32[]{:S(2)}) collective-permute-start(bf16[2,1,96,768]{3,2,1,0:T(8,128)(2,1)S(1)} %get-tuple-element.224.refs_2_), channel_id=1, source_target_pairs={{0,16},{1,17},{2,18},{3,19},{4,20},{5,21},{6,22},{7,23},{8,24},{9,... | collective-permute-start | bytes 884744 | tf_op jit(solution)/shard_map/ppermute | solution.py:66
  59.1 4.6 %collective-permute-start.10 = (bf16[4,16,48,384]{3,2,1,0:T(8,128)(2,1)S(1)}, bf16[4,16,48,384]{3,2,1,0:T(8,128)(2,1)S(1)}, u32[]{:S(2)}, u32[]{:S(2)}) collective-permute-start(bf16[4,16,48,384]{3,2,1,0:T(8,128)(2,1)S(1)} %get-tuple-element.231), channel_id=1, source_target_pairs={{0,1},{1,0},{2,3},{3,2},{4,5},{5,4},{6,7},{7,6},{8,9},{9,8},{10,11... | collective-permute-start | bytes 7077896 | tf_op jit(solution)/shard_map/ppermute | solution.py:66
  59.2 16.4 %collective-permute-start.12 = (bf16[2,2,2,1,48,1536]{5,4,3,2,1,0:T(8,128)(2,1)S(1)}, bf16[2,2,2,1,48,1536]{5,4,3,2,1,0:T(8,128)(2,1)S(1)}, u32[]{:S(2)}, u32[]{:S(2)}) collective-permute-start(bf16[2,2,2,1,48,1536]{5,4,3,2,1,0:T(8,128)(2,1)S(1)} %get-tuple-element.238.refs_2_), channel_id=1, source_target_pairs={{0,4},{1,3},{2,6},{3,1},{4,0},{5,7},{6,2},{7,5},{8,12},{9,11},{10,... | collective-permute-start | bytes 3538952 | tf_op jit(solution)/shard_map/ppermute | solution.py:66
  60.9 14.0 %collective-permute-start.11 = (bf16[2,2,1,96,768]{4,3,2,1,0:T(8,128)(2,1)S(1)}, bf16[2,2,1,96,768]{4,3,2,1,0:T(8,128)(2,1)S(1)}, u32[]{:S(2)}, u32[]{:S(2)}) collective-permute-start(bf16[2,2,1,96,768]{4,3,2,1,0:T(8,128)(2,1)S(1)} %get-tuple-element.236.refs_2_), channel_id=1, source_target_pairs={{0,8},{1,9},{2,10},{3,11},{4,12},{5,13},{6,14},{7,15},{8,0},{9,1},... | collective-permute-start | bytes 1769480 | tf_op jit(solution)/shard_map/ppermute | solution.py:66
  76.3 6.5 %collective-permute-start.13 = (bf16[1,16,48,1536]{3,2,1,0:T(8,128)(2,1)S(1)}, bf16[1,16,48,1536]{3,2,1,0:T(8,128)(2,1)S(1)}, u32[]{:S(2)}, u32[]{:S(2)}) collective-permute-start(bf16[1,16,48,1536]{3,2,1,0:T(8,128)(2,1)S(1)} %get-tuple-element.243), channel_id=1, source_target_pairs={{0,1},{1,0},{2,3},{3,2},{4,5},{5,4},{6,7},{7,6},{8,9},{9,8},{10,11... | collective-permute-start | bytes 7077896 | tf_op jit(solution)/shard_map/ppermute | solution.py:66
  76.4 16.3 %collective-permute-start.14 = (bf16[2,2,2,1,96,768]{5,4,3,2,1,0:T(8,128)(2,1)S(1)}, bf16[2,2,2,1,96,768]{5,4,3,2,1,0:T(8,128)(2,1)S(1)}, u32[]{:S(2)}, u32[]{:S(2)}) collective-permute-start(bf16[2,2,2,1,96,768]{5,4,3,2,1,0:T(8,128)(2,1)S(1)} %get-tuple-element.248.refs_2_), channel_id=1, source_target_pairs={{0,4},{1,3},{2,6},{3,1},{4,0},{5,7},{6,2},{7,5},{8,12},{9,11},{10,... | collective-permute-start | bytes 3538952 | tf_op jit(solution)/shard_map/ppermute | solution.py:66
  93.4 4.6 %collective-permute-start.15 = (bf16[1,16,96,768]{3,2,1,0:T(8,128)(2,1)S(1)}, bf16[1,16,96,768]{3,2,1,0:T(8,128)(2,1)S(1)}, u32[]{:S(2)}, u32[]{:S(2)}) collective-permute-start(bf16[1,16,96,768]{3,2,1,0:T(8,128)(2,1)S(1)} %get-tuple-element.251), channel_id=1, source_target_pairs={{0,1},{1,0},{2,3},{3,2},{4,5},{5,4},{6,7},{7,6},{8,9},{9,8},{10,11... | collective-permute-start | bytes 7077896 | tf_op jit(solution)/shard_map/ppermute | solution.py:66
  93.4 4.5 %copy-start.3 = (f32[12,768]{1,0:T(8,128)S(1)}, f32[12,768]{1,0:T(8,128)}, u32[]{:S(2)}) copy-start(f32[12,768]{1,0:T(8,128)} %refs_4_.5) | copy-start | bytes 110596
  106.7 5.3 %collective-permute-start.16 = (bf16[1,16,96,768]{3,2,1,0:T(8,128)(2,1)S(1)}, bf16[1,16,96,768]{3,2,1,0:T(8,128)(2,1)S(1)}, u32[]{:S(2)}, u32[]{:S(2)}) collective-permute-start(bf16[1,16,96,768]{3,2,1,0:T(8,128)(2,1)S(1)} %bitcast.98), channel_id=1, source_target_pairs={{0,1},{1,0},{2,3},{3,2},{4,5},{5,4},{6,7},{7,6},{8,9},{9,8},{10,11... | collective-permute-start | bytes 7077896 | tf_op jit(solution)/shard_map/ppermute | solution.py:66
  110.9 8.2 %collective-permute-start.17 = (bf16[1,16,48,384]{3,2,1,0:T(8,128)(2,1)S(1)}, bf16[1,16,48,384]{3,2,1,0:T(8,128)(2,1)S(1)}, u32[]{:S(2)}, u32[]{:S(2)}) collective-permute-start(bf16[1,16,48,384]{3,2,1,0:T(8,128)(2,1)S(1)} %bitcast.102), channel_id=1, source_target_pairs={{0,1},{1,0},{2,3},{3,2},{4,5},{5,4},{6,7},{7,6},{8,9},{9,8},{10,11... | collective-permute-start | bytes 1769480 | tf_op jit(solution)/shard_map/ppermute | solution.py:66
  111.3 7.7 %collective-permute-start.18 = (bf16[1,16,48,384]{3,2,1,0:T(8,128)(2,1)S(1)}, bf16[1,16,48,384]{3,2,1,0:T(8,128)(2,1)S(1)}, u32[]{:S(2)}, u32[]{:S(2)}) collective-permute-start(bf16[1,16,48,384]{3,2,1,0:T(8,128)(2,1)S(1)} %bitcast.101), channel_id=1, source_target_pairs={{0,1},{1,0},{2,3},{3,2},{4,5},{5,4},{6,7},{7,6},{8,9},{9,8},{10,11... | collective-permute-start | bytes 1769480 | tf_op jit(solution)/shard_map/ppermute | solution.py:66
  111.4 7.6 %collective-permute-start.19 = (bf16[1,16,48,384]{3,2,1,0:T(8,128)(2,1)S(1)}, bf16[1,16,48,384]{3,2,1,0:T(8,128)(2,1)S(1)}, u32[]{:S(2)}, u32[]{:S(2)}) collective-permute-start(bf16[1,16,48,384]{3,2,1,0:T(8,128)(2,1)S(1)} %bitcast.100), channel_id=1, source_target_pairs={{0,1},{1,0},{2,3},{3,2},{4,5},{5,4},{6,7},{7,6},{8,9},{9,8},{10,11... | collective-permute-start | bytes 1769480 | tf_op jit(solution)/shard_map/ppermute | solution.py:66
  111.8 7.2 %collective-permute-start.20 = (bf16[1,16,48,384]{3,2,1,0:T(8,128)(2,1)S(1)}, bf16[1,16,48,384]{3,2,1,0:T(8,128)(2,1)S(1)}, u32[]{:S(2)}, u32[]{:S(2)}) collective-permute-start(bf16[1,16,48,384]{3,2,1,0:T(8,128)(2,1)S(1)} %bitcast.99), channel_id=1, source_target_pairs={{0,1},{1,0},{2,3},{3,2},{4,5},{5,4},{6,7},{7,6},{8,9},{9,8},{10,11... | collective-permute-start | bytes 1769480 | tf_op jit(solution)/shard_map/ppermute | solution.py:66
  113.0 16.3 %collective-permute-start.21 = (bf16[2,2,2,1,96,768]{5,4,3,2,1,0:T(8,128)(2,1)S(1)}, bf16[2,2,2,1,96,768]{5,4,3,2,1,0:T(8,128)(2,1)S(1)}, u32[]{:S(2)}, u32[]{:S(2)}) collective-permute-start(bf16[2,2,2,1,96,768]{5,4,3,2,1,0:T(8,128)(2,1)S(1)} %get-tuple-element.295), channel_id=1, source_target_pairs={{0,4},{1,3},{2,6},{3,1},{4,0},{5,7},{6,2},{7,5},{8,12},{9,11},{10,... | collective-permute-start | bytes 3538952 | tf_op jit(solution)/shard_map/ppermute | solution.py:66
  127.4 11.2 %collective-permute-start.22 = (bf16[2,768,384]{2,1,0:T(8,128)(2,1)S(1)}, bf16[2,768,384]{2,1,0:T(8,128)(2,1)S(1)}, u32[]{:S(2)}, u32[]{:S(2)}) collective-permute-start(bf16[2,768,384]{2,1,0:T(8,128)(2,1)S(1)} %get-tuple-element.304), channel_id=1, source_target_pairs={{0,1},{1,0},{2,3},{3,2},{4,5},{5,4},{6,7},{7,6},{8,9},{9,8},{10,11... | collective-permute-start | bytes 3538952 | tf_op jit(solution)/shard_map/ppermute | solution.py:66
  127.7 16.2 %collective-permute-start.23 = (bf16[2,2,2,4,48,384]{5,4,3,2,1,0:T(8,128)(2,1)S(1)}, bf16[2,2,2,4,48,384]{5,4,3,2,1,0:T(8,128)(2,1)S(1)}, u32[]{:S(2)}, u32[]{:S(2)}) collective-permute-start(bf16[2,2,2,4,48,384]{5,4,3,2,1,0:T(8,128)(2,1)S(1)} %get-tuple-element.307), channel_id=1, source_target_pairs={{0,4},{1,3},{2,6},{3,1},{4,0},{5,7},{6,2},{7,5},{8,12},{9,11},{10,... | collective-permute-start | bytes 3538952 | tf_op jit(solution)/shard_map/ppermute | solution.py:66
  130.0 14.8 %collective-permute-start.24 = (bf16[2,2,1,96,768]{4,3,2,1,0:T(8,128)(2,1)S(1)}, bf16[2,2,1,96,768]{4,3,2,1,0:T(8,128)(2,1)S(1)}, u32[]{:S(2)}, u32[]{:S(2)}) collective-permute-start(bf16[2,2,1,96,768]{4,3,2,1,0:T(8,128)(2,1)S(1)} %get-tuple-element.310), channel_id=1, source_target_pairs={{0,8},{1,9},{2,10},{3,11},{4,12},{5,13},{6,14},{7,15},{8,0},{9,1},... | collective-permute-start | bytes 1769480 | tf_op jit(solution)/shard_map/ppermute | solution.py:66
  138.0 7.6 %collective-permute-start.25 = (bf16[2,16,48,128]{3,2,1,0:T(8,128)(2,1)S(1)}, bf16[2,16,48,128]{3,2,1,0:T(8,128)(2,1)S(1)}, u32[]{:S(2)}, u32[]{:S(2)}) collective-permute-start(bf16[2,16,48,128]{3,2,1,0:T(8,128)(2,1)S(1)} %bitcast.105), channel_id=1, source_target_pairs={{0,1},{1,0},{2,3},{3,2},{4,5},{5,4},{6,7},{7,6},{8,9},{9,8},{10,11... | collective-permute-start | bytes 1179656 | tf_op jit(solution)/shard_map/ppermute | solution.py:66
  138.1 7.5 %collective-permute-start.26 = (bf16[2,16,48,128]{3,2,1,0:T(8,128)(2,1)S(1)}, bf16[2,16,48,128]{3,2,1,0:T(8,128)(2,1)S(1)}, u32[]{:S(2)}, u32[]{:S(2)}) collective-permute-start(bf16[2,16,48,128]{3,2,1,0:T(8,128)(2,1)S(1)} %bitcast.104), channel_id=1, source_target_pairs={{0,1},{1,0},{2,3},{3,2},{4,5},{5,4},{6,7},{7,6},{8,9},{9,8},{10,11... | collective-permute-start | bytes 1179656 | tf_op jit(solution)/shard_map/ppermute | solution.py:66
  138.6 7.0 %collective-permute-start.27 = (bf16[2,16,48,128]{3,2,1,0:T(8,128)(2,1)S(1)}, bf16[2,16,48,128]{3,2,1,0:T(8,128)(2,1)S(1)}, u32[]{:S(2)}, u32[]{:S(2)}) collective-permute-start(bf16[2,16,48,128]{3,2,1,0:T(8,128)(2,1)S(1)} %bitcast.103), channel_id=1, source_target_pairs={{0,1},{1,0},{2,3},{3,2},{4,5},{5,4},{6,7},{7,6},{8,9},{9,8},{10,11... | collective-permute-start | bytes 1179656 | tf_op jit(solution)/shard_map/ppermute | solution.py:66
  146.5 17.0 %collective-permute-start.30 = (bf16[2,2,2,4,48,384]{5,4,3,2,1,0:T(8,128)(2,1)S(1)}, bf16[2,2,2,4,48,384]{5,4,3,2,1,0:T(8,128)(2,1)S(1)}, u32[]{:S(2)}, u32[]{:S(2)}) collective-permute-start(bf16[2,2,2,4,48,384]{5,4,3,2,1,0:T(8,128)(2,1)S(1)} %get-tuple-element.333), channel_id=1, source_target_pairs={{0,4},{1,3},{2,6},{3,1},{4,0},{5,7},{6,2},{7,5},{8,12},{9,11},{10,... | collective-permute-start | bytes 3538952 | tf_op jit(solution)/shard_map/ppermute | solution.py:66
  148.3 14.6 %collective-permute-start.29 = (bf16[2,1,96,768]{3,2,1,0:T(8,128)(2,1)S(1)}, bf16[2,1,96,768]{3,2,1,0:T(8,128)(2,1)S(1)}, u32[]{:S(2)}, u32[]{:S(2)}) collective-permute-start(bf16[2,1,96,768]{3,2,1,0:T(8,128)(2,1)S(1)} %get-tuple-element.330), channel_id=1, source_target_pairs={{0,16},{1,17},{2,18},{3,19},{4,20},{5,21},{6,22},{7,23},{8,24},{9,... | collective-permute-start | bytes 884744 | tf_op jit(solution)/shard_map/ppermute | solution.py:66
  151.8 1.4 collective-permute-start.28
  151.9 21.9 %collective-permute-start.31 = (bf16[2,2,4,48,384]{4,3,2,1,0:T(8,128)(2,1)S(1)}, bf16[2,2,4,48,384]{4,3,2,1,0:T(8,128)(2,1)S(1)}, u32[]{:S(2)}, u32[]{:S(2)}) collective-permute-start(bf16[2,2,4,48,384]{4,3,2,1,0:T(8,128)(2,1)S(1)} %get-tuple-element.336), channel_id=1, source_target_pairs={{0,8},{1,9},{2,10},{3,11},{4,12},{5,13},{6,14},{7,15},{8,0},{9,1},... | collective-permute-start | bytes 1769480 | tf_op jit(solution)/shard_map/ppermute | solution.py:66
  164.3 10.2 %collective-permute-start.32 = (bf16[2,2,4,48,384]{4,3,2,1,0:T(8,128)(2,1)S(1)}, bf16[2,2,4,48,384]{4,3,2,1,0:T(8,128)(2,1)S(1)}, u32[]{:S(2)}, u32[]{:S(2)}) collective-permute-start(bf16[2,2,4,48,384]{4,3,2,1,0:T(8,128)(2,1)S(1)} %get-tuple-element.339), channel_id=1, source_target_pairs={{0,2},{1,5},{2,0},{3,7},{4,6},{5,1},{6,4},{7,3},{8,10},{9,13},{10,... | collective-permute-start | bytes 1769480 | tf_op jit(solution)/shard_map/ppermute | solution.py:66
  165.4 28.1 %collective-permute-start.36 = (bf16[512,768]{1,0:T(8,128)(2,1)S(1)}, bf16[512,768]{1,0:T(8,128)(2,1)S(1)}, u32[]{:S(2)}, u32[]{:S(2)}) collective-permute-start(bf16[512,768]{1,0:T(8,128)(2,1)S(1)} %get-tuple-element.350.refs_2_), channel_id=1, source_target_pairs={{0,1},{1,0},{2,3},{3,2},{4,5},{5,4},{6,7},{7,6},{8,9},{9,8},{10,11... | collective-permute-start | bytes 2359304 | tf_op jit(solution)/shard_map/ppermute | solution.py:66
  165.4 30.5 %collective-permute-start.37 = (bf16[512,768]{1,0:T(8,128)(2,1)S(1)}, bf16[512,768]{1,0:T(8,128)(2,1)S(1)}, u32[]{:S(2)}, u32[]{:S(2)}) collective-permute-start(bf16[512,768]{1,0:T(8,128)(2,1)S(1)} %get-tuple-element.352.refs_2_), channel_id=1, source_target_pairs={{0,1},{1,0},{2,3},{3,2},{4,5},{5,4},{6,7},{7,6},{8,9},{9,8},{10,11... | collective-permute-start | bytes 2359304 | tf_op jit(solution)/shard_map/ppermute | solution.py:66
  174.5 16.1 %copy-start.10 = (f32[96,768]{1,0:T(8,128)S(1)}, f32[96,768]{1,0:T(8,128)}, u32[]{:S(2)}) copy-start(f32[96,768]{1,0:T(8,128)} %param.30) | copy-start | bytes 884740
  174.5 16.1 %copy-start.11 = (f32[96,768]{1,0:T(8,128)S(1)}, f32[96,768]{1,0:T(8,128)}, u32[]{:S(2)}) copy-start(f32[96,768]{1,0:T(8,128)} %param.34) | copy-start | bytes 884740
  175.2 14.7 %collective-permute-start.33 = (bf16[2,4,48,384]{3,2,1,0:T(8,128)(2,1)S(1)}, bf16[2,4,48,384]{3,2,1,0:T(8,128)(2,1)S(1)}, u32[]{:S(2)}, u32[]{:S(2)}) collective-permute-start(bf16[2,4,48,384]{3,2,1,0:T(8,128)(2,1)S(1)} %get-tuple-element.342), channel_id=1, source_target_pairs={{0,8},{1,9},{2,10},{3,11},{4,12},{5,13},{6,14},{7,15},{8,0},{9,1},... | collective-permute-start | bytes 884744 | tf_op jit(solution)/shard_map/ppermute | solution.py:66
  175.3 16.5 %collective-permute-start.35 = (bf16[2,4,48,384]{3,2,1,0:T(8,128)(2,1)S(1)}, bf16[2,4,48,384]{3,2,1,0:T(8,128)(2,1)S(1)}, u32[]{:S(2)}, u32[]{:S(2)}) collective-permute-start(bf16[2,4,48,384]{3,2,1,0:T(8,128)(2,1)S(1)} %get-tuple-element.348), channel_id=1, source_target_pairs={{0,16},{1,17},{2,18},{3,19},{4,20},{5,21},{6,22},{7,23},{8,24},{9,... | collective-permute-start | bytes 884744 | tf_op jit(solution)/shard_map/ppermute | solution.py:66
  178.5 12.0 %collective-permute-start.34 = (bf16[1,96,768]{2,1,0:T(8,128)(2,1)S(1)}, bf16[1,96,768]{2,1,0:T(8,128)(2,1)S(1)}, u32[]{:S(2)}, u32[]{:S(2)}) collective-permute-start(bf16[1,96,768]{2,1,0:T(8,128)(2,1)S(1)} %get-tuple-element.345), channel_id=1, source_target_pairs={{0,2},{1,5},{2,0},{3,7},{4,6},{5,1},{6,4},{7,3},{8,10},{9,13},{10,... | collective-permute-start | bytes 442376 | tf_op jit(solution)/shard_map/ppermute | solution.py:66
  192.4 5.3 %collective-permute-start.38 = (bf16[4,48,384]{2,1,0:T(8,128)(2,1)S(1)}, bf16[4,48,384]{2,1,0:T(8,128)(2,1)S(1)}, u32[]{:S(2)}, u32[]{:S(2)}) collective-permute-start(bf16[4,48,384]{2,1,0:T(8,128)(2,1)S(1)} %get-tuple-element.357), channel_id=1, source_target_pairs={{0,2},{1,5},{2,0},{3,7},{4,6},{5,1},{6,4},{7,3},{8,10},{9,13},{10,... | collective-permute-start | bytes 442376 | tf_op jit(solution)/shard_map/ppermute | solution.py:66
  193.2 8.1 %collective-permute-start.39 = (bf16[4,48,384]{2,1,0:T(8,128)(2,1)S(1)}, bf16[4,48,384]{2,1,0:T(8,128)(2,1)S(1)}, u32[]{:S(2)}, u32[]{:S(2)}) collective-permute-start(bf16[4,48,384]{2,1,0:T(8,128)(2,1)S(1)} %get-tuple-element.360), channel_id=1, source_target_pairs={{0,16},{1,17},{2,18},{3,19},{4,20},{5,21},{6,22},{7,23},{8,24},{9,... | collective-permute-start | bytes 442376 | tf_op jit(solution)/shard_map/ppermute | solution.py:66
  193.5 4.3 %copy-start.12 = (f32[48,1536]{1,0:T(8,128)S(1)}, f32[48,1536]{1,0:T(8,128)}, u32[]{:S(2)}) copy-start(f32[48,1536]{1,0:T(8,128)} %param.29) | copy-start | bytes 884740
  193.5 4.3 %copy-start.13 = (f32[48,1536]{1,0:T(8,128)S(1)}, f32[48,1536]{1,0:T(8,128)}, u32[]{:S(2)}) copy-start(f32[48,1536]{1,0:T(8,128)} %param.33) | copy-start | bytes 884740
  195.9 5.5 %copy-start.7 = (f32[3,48,384]{2,1,0:T(8,128)S(1)}, f32[3,48,384]{2,1,0:T(8,128)}, u32[]{:S(2)}) copy-start(f32[3,48,384]{2,1,0:T(8,128)} %refs_3_.3) | copy-start | bytes 663556
  195.9 5.5 %copy-start.9 = (f32[384,48]{0,1:T(8,128)S(1)}, f32[384,48]{0,1:T(8,128)}, u32[]{:S(2)}) copy-start(f32[384,48]{0,1:T(8,128)} %param.24) | copy-start | bytes 221188
  195.9 5.5 %copy-start.14 = (f32[3,48,384]{2,1,0:T(8,128)S(1)}, f32[3,48,384]{2,1,0:T(8,128)}, u32[]{:S(2)}) copy-start(f32[3,48,384]{2,1,0:T(8,128)} %refs_4_.4) | copy-start | bytes 663556
  195.9 5.5 %copy-start.15 = (f32[3,48,384]{2,1,0:T(8,128)S(1)}, f32[3,48,384]{2,1,0:T(8,128)}, u32[]{:S(2)}) copy-start(f32[3,48,384]{2,1,0:T(8,128)} %refs_5_.4) | copy-start | bytes 663556
  195.9 5.5 %copy-start.16 = (f32[384,48]{0,1:T(8,128)S(1)}, f32[384,48]{0,1:T(8,128)}, u32[]{:S(2)}) copy-start(f32[384,48]{0,1:T(8,128)} %param.28) | copy-start | bytes 221188
  195.9 5.5 %copy-start.17 = (f32[384,48]{0,1:T(8,128)S(1)}, f32[384,48]{0,1:T(8,128)}, u32[]{:S(2)}) copy-start(f32[384,48]{0,1:T(8,128)} %param.32) | copy-start | bytes 221188
  197.7 20.7 %copy-start.18 = (f32[12,768]{1,0:T(8,128)S(1)}, f32[12,768]{1,0:T(8,128)}, u32[]{:S(2)}) copy-start(f32[12,768]{1,0:T(8,128)} %refs_5_.5) | copy-start | bytes 110596
  197.7 20.7 %copy-start.19 = (f32[12,768]{1,0:T(8,128)S(1)}, f32[12,768]{1,0:T(8,128)}, u32[]{:S(2)}) copy-start(f32[12,768]{1,0:T(8,128)} %refs_6_.1) | copy-start | bytes 110596
  202.5 4.4 %collective-permute-start.40 = (f32[8,768]{1,0:T(8,128)S(1)}, f32[8,768]{1,0:T(8,128)S(1)}, u32[]{:S(2)}, u32[]{:S(2)}) collective-permute-start(f32[8,768]{1,0:T(8,128)S(1)} %get-tuple-element.365.refs_1_), channel_id=1, source_target_pairs={{0,8},{1,9},{2,10},{3,11},{4,12},{5,13},{6,14},{7,15},{8,0},{9,1},... | collective-permute-start | bytes 73736 | tf_op jit(solution)/shard_map/ppermute | solution.py:66
  202.5 4.7 %collective-permute-start.41 = (f32[8,768]{1,0:T(8,128)S(1)}, f32[8,768]{1,0:T(8,128)S(1)}, u32[]{:S(2)}, u32[]{:S(2)}) collective-permute-start(f32[8,768]{1,0:T(8,128)S(1)} %get-tuple-element.365.refs_1_), channel_id=1, source_target_pairs={{0,16},{1,17},{2,18},{3,19},{4,20},{5,21},{6,22},{7,23},{8,24},{9,... | collective-permute-start | bytes 73736 | tf_op jit(solution)/shard_map/ppermute | solution.py:66
  204.5 5.6 %collective-permute-start.42 = (f32[8,768]{1,0:T(8,128)S(1)}, f32[8,768]{1,0:T(8,128)S(1)}, u32[]{:S(2)}, u32[]{:S(2)}) collective-permute-start(f32[8,768]{1,0:T(8,128)S(1)} %get-tuple-element.365.refs_1_), channel_id=1, source_target_pairs={{0,24},{1,25},{2,26},{3,27},{4,28},{5,29},{6,30},{7,31},{8,16},{9,... | collective-permute-start | bytes 73736 | tf_op jit(solution)/shard_map/ppermute | solution.py:66
  210.2 3.9 %collective-permute-start.43 = (f32[8,768]{1,0:T(8,128)S(1)}, f32[8,768]{1,0:T(8,128)S(1)}, u32[]{:S(2)}, u32[]{:S(2)}) collective-permute-start(f32[8,768]{1,0:T(8,128)S(1)} %get-tuple-element.367.refs_1_), channel_id=1, source_target_pairs={{0,4},{1,5},{2,6},{3,7},{4,0},{5,1},{6,2},{7,3},{8,12},{9,13},{10,... | collective-permute-start | bytes 73736 | tf_op jit(solution)/shard_map/ppermute | solution.py:66
  211.4 3.8 %collective-permute-start.44 = (f32[8,768]{1,0:T(8,128)S(1)}, f32[8,768]{1,0:T(8,128)S(1)}, u32[]{:S(2)}, u32[]{:S(2)}) collective-permute-start(f32[8,768]{1,0:T(8,128)S(1)} %get-tuple-element.367.refs_1_), channel_id=1, source_target_pairs={{0,2},{1,3},{2,0},{3,1},{4,6},{5,7},{6,4},{7,5},{8,10},{9,11},{10,... | collective-permute-start | bytes 73736 | tf_op jit(solution)/shard_map/ppermute | solution.py:66
  212.4 4.7 %collective-permute-start.45 = (f32[8,768]{1,0:T(8,128)S(1)}, f32[8,768]{1,0:T(8,128)S(1)}, u32[]{:S(2)}, u32[]{:S(2)}) collective-permute-start(f32[8,768]{1,0:T(8,128)S(1)} %get-tuple-element.367.refs_1_), channel_id=1, source_target_pairs={{0,6},{1,7},{2,4},{3,5},{4,2},{5,3},{6,0},{7,1},{8,14},{9,15},{10,... | collective-permute-start | bytes 73736 | tf_op jit(solution)/shard_map/ppermute | solution.py:66
  217.1 1.3 collective-permute-start.46
  (3 other events, 2.6 us)

commit v5 on v4

--- a/solution.py
+++ b/solution.py
@@ -27,13 +27,14 @@
 TN = (((0,), (0,)), ((), ()))
 MIB = 1 << 20
 PATHS = ("zzab", "azzb", "azzb", "azzb")
-COUNTS = (1, 4)
+COUNTS = (1, 3, 1, 1, 2)
 ORDER = (
-    "castA", "prep", "castB", "a0", "b0", "a1", "castC", "c0", "b1", "c1", "b2", "wholeA", "project",
-    "attend", "c2", "wholeB", "hide", "liftOwn", "liftOth", "turn", "wholeC", "lowerOwn", "lower", "sinkOth",
-    "downOth", "downOwn", "upOth", "pairC", "sinkOwn", "upOwn", "pairB", "surface", "values", "voOth", "C0",
-    "back", "qkOth", "qkOwn", "voOwn", "voSum", "B0", "C1", "pairA", "states", "collect", "share", "C2", "A0",
-    "B1", "A1", "A2", "stepC", "B2", "pairS", "pairO", "stepB", "stepA",
+    "castA", "castB", "prep", "a0", "b0", "a1", "castC", "c0", "b1", "wholeA", "c1", "b2", "otherA",
+    "project", "attend", "c2", "wholeB", "otherB", "hide", "liftOwn", "liftOth", "turn", "wholeC", "lowerOwn",
+    "otherC", "lower", "sinkOth", "downOth", "downOwn", "upOth", "pairC", "sinkOwn", "upOwn", "pairB",
+    "surface", "values", "voOth", "C0", "back", "qkOwn", "qkOth", "voOwn", "voSum", "C1", "B0", "pairA",
+    "states", "collect", "share", "C2", "B1", "A0", "pairO", "A1", "stepC", "B2", "A2", "stepB", "stepA",
+    "pairS",
 )
 
 
@@ -197,10 +198,20 @@
             self.got = grid.exchange(self.block, self.path[i + 1])
 
     def whole(self):
+        full, self.came = self.put_together(self.block, self.got, False)
+        return full
+
+    def other(self):
+        return self.put_together(self.grid.core(self.block), self.grid.core(self.came), True)[0]
+
+    def put_together(self, block, came, other):
         grid, path = self.grid, self.path
-        many, rows, width = self.block.shape[-3:]
-
-        def gather_whole(s, own, got, out):
+        many, rows, width = block.shape[-3:]
+
+        def gather_whole(s, own, got, out, *relay):
+            for ref in relay:
+                ref[...] = got[...]
+            s = [s[0], s[1], s[2], 1 - s[3] if other else s[3]]
             last = grid.bit(s, path[-1])
             for bits in itertools.product(range(2), repeat=len(path) - 1):
                 for ref, bit in ((own, last), (got, 1 - last)):
@@ -208,9 +219,8 @@
                     for j in range(many):
                         out[j, spot] = ref[bits + (j,)]
 
-        shape = (many, grid.dp, rows, width)
-        full = self.tape.run(gather_whole, [(shape, BF16)], [self.block, self.got], True)[0]
-        return full, grid.core(full)
+        shapes = [((many, grid.dp, rows, width), BF16)] + [(came.shape, BF16)] * (not other)
+        return self.tape.run(gather_whole, shapes, [block, came], True)
 
 
 class Scatter:
@@ -220,33 +230,37 @@
         self.got = [grid.core(v) for v, _, _ in other]
         self.spots = [(j, c) for _, j, c in other]
 
-    def pair(self, own):
+    def pair(self, own, cut=1):
         grid, path = self.grid, self.path
         _, _, rows, width = own[0].shape
         own_spots = [(g, i) for g, v in enumerate(own) for i in range(v.shape[0])]
         many, pieces, got = len(own_spots), len(own), len(self.got)
         shapes = [v.shape for v in self.got]
-        shape = (2,) * (len(path) - 1) + (many, rows, width)
+        lead = (2,) * (len(path) - 1)
+        shape = lead + (many, rows, width)
+        each = many // cut
+        sends = [(lead + (each, rows, width), BF16)] * cut
 
         def scatter_pair(s, *refs):
-            own_refs, got_refs, (keep, send) = refs[:pieces], refs[pieces : pieces + got], refs[pieces + got :]
+            own_refs, got_refs, outs = refs[:pieces], refs[pieces : pieces + got], refs[pieces + got :]
             last = grid.bit(s, path[-1])
             for bits in itertools.product(range(2), repeat=len(path) - 1):
-                for out, bit in ((keep, last), (send, 1 - last)):
+                for sent, bit in ((False, last), (True, 1 - last)):
                     spot = grid.spot(s, path, bits[::-1] + (bit,))
                     for j, (g, i) in enumerate(own_spots):
+                        out, m = (outs[1 + j // each], j % each) if sent else (outs[0], j)
                         found = False
                         for ref, (first, column), piece in zip(got_refs, self.spots, shapes):
                             if first <= j < first + piece[0]:
                                 at = slice(column, column + piece[3])
                                 total = own_refs[g][i, spot, :, at] + ref[j - first, spot].astype(F32)
-                                out[bits + (j, slice(None), at)] = total.astype(out.dtype)
+                                out[bits + (m, slice(None), at)] = total.astype(out.dtype)
                                 found = True
                         if not found:
-                            out[bits + (j,)] = own_refs[g][i, spot].astype(out.dtype)
-
-        self.keep, value = self.tape.run(scatter_pair, [(shape, F32), (shape, BF16)], own + self.got, True)
-        self.got = grid.exchange(value, path[-1])
+                            out[bits + (m,)] = own_refs[g][i, spot].astype(out.dtype)
+
+        self.keep, *values = self.tape.run(scatter_pair, [(shape, F32)] + sends, own + self.got, True)
+        self.got = [grid.exchange(v, path[-1]) for v in values]
 
     def split(self, group):
         self.splits(part(len(self.path) - 1, group))
@@ -256,6 +270,8 @@
 
     def split_long(self):
         grid, count = self.grid, len(self.grid.long_steps())
+
+        assert len(self.got) == 1
 
         def scatter_long(s, own, got, *outs):
             for k, out in enumerate(outs):
@@ -264,7 +280,7 @@
 
         shape = self.keep.shape[count:]
         keep, *values = self.tape.run(
-            scatter_long, [(shape, F32)] + [(shape, BF16)] * (grid.long - 1), [self.keep, self.got], True
+            scatter_long, [(shape, F32)] + [(shape, BF16)] * (grid.long - 1), [self.keep] + self.got, True
         )
         self.parts = [keep] + [grid.send(v, grid.along(k + 1)) for k, v in enumerate(values)]
 
@@ -273,17 +289,24 @@
         for i in steps:
             step = self.path[len(self.path) - 2 - i]
 
-            def scatter_split(s, own, got, keep, send):
+            count = len(self.got)
+            each = self.keep.shape[-3] // count
+            free = (slice(None),) * (len(self.keep.shape) - 4)
+
+            def scatter_split(s, own, *refs):
+                keep, send = refs[count:]
                 bit = grid.bit(s, step)
-                keep[...] = own[bit] + got[bit].astype(F32)
-                send[...] = (own[1 - bit] + got[1 - bit].astype(F32)).astype(BF16)
+                for g, got in enumerate(refs[:count]):
+                    at = free + (slice(g * each, (g + 1) * each),)
+                    keep[at] = own[(bit,) + at] + got[bit].astype(F32)
+                    send[at] = (own[(1 - bit,) + at] + got[1 - bit].astype(F32)).astype(BF16)
 
             shape = self.keep.shape[1:]
             self.keep, value = self.tape.run(
-                scatter_split, [(shape, F32), (shape, BF16)], [self.keep, self.got], True
-            )
-            self.got = grid.exchange(value, step)
-        self.parts = [self.keep, self.got]
+                scatter_split, [(shape, F32), (shape, BF16)], [self.keep] + self.got, True
+            )
+            self.got = [grid.exchange(value, step)]
+        self.parts = [self.keep] + self.got
 
 
 def tree(values):
@@ -426,13 +449,22 @@
             )
 
         def whole_a():
-            w.a_own, w.a_oth = (v.reshape(4, width, cols) for v in w.gather_a.whole())
+            w.a_own = w.gather_a.whole().reshape(4, width, cols)
+
+        def other_a():
+            w.a_oth = w.gather_a.other().reshape(4, width, cols)
 
         def whole_b():
-            w.b_own, w.b_oth = (v.reshape(width, units) for v in w.gather_b.whole())
+            w.b_own = w.gather_b.whole().reshape(width, units)
+
+        def other_b():
+            w.b_oth = w.gather_b.other().reshape(width, units)
 
         def whole_c():
-            w.c_own, w.c_oth = (v.reshape(units, width) for v in w.gather_c.whole())
+            w.c_own = w.gather_c.whole().reshape(units, width)
+
+        def other_c():
+            w.c_oth = w.gather_c.other().reshape(units, width)
 
         def project(x_ref, own, oth, bias, out):
             @pl.loop(0, 3)
@@ -560,9 +592,8 @@
 
             sums[...] = jnp.zeros_like(sums)
 
-            @pl.loop(0, mine)
-            def _(p):
-                at = pl.ds(pl.multiple_of(p * length, length), length)
+            for p in range(mine):
+                at = slice(p * length, (p + 1) * length)
                 value = normed[at] * vec[3:4] + vec[4:5] + work[at] + vec[5:6]
                 normal, spread = normed_of(value)
                 output[at] = (normal * vec[6:7] + vec[7:8]).astype(BF16)
@@ -613,7 +644,7 @@
             w.down_own = weight_grad(w.lift_own[1], w.top16, F32, counts_of[0])
 
         def pair_c():
-            w.scatter_c.pair(sharded(w.down_own, 1))
+            w.scatter_c.pair(sharded(w.down_own, 1), counts_of[2])
 
         def up_oth():
             other = sharded(weight_grad(w.hidden_t, w.sink_oth[0], BF16, counts_of[1]), 1)
@@ -623,7 +654,7 @@
             w.up_own = weight_grad(w.hidden_t, w.sink_own[0], F32, counts_of[1])
 
         def pair_b():
-            w.scatter_b.pair(sharded(w.up_own, 1))
+            w.scatter_b.pair(sharded(w.up_own, 1), counts_of[3])
 
         def sink(top16_ref, down, slope, grad, sums):
             @pl.loop(0, units // tile)
@@ -746,7 +777,7 @@
             w.vo_sum = tape.run(add_up, [((2, width, cols), F32)], [w.vo_own[0], w.vo_oth])
 
         def pair_a():
-            w.scatter_a.pair(sharded(w.qk_own + w.vo_sum, 2))
+            w.scatter_a.pair(sharded(w.qk_own + w.vo_sum, 2), counts_of[4])
 
         def attend_back(probs_ref, back_ref, qkv_ref, grad_q, grad_k, sums):
             sums[...] = jnp.zeros_like(sums)
@@ -908,7 +939,7 @@
             "B0": lambda: w.scatter_b.split(0), "B1": lambda: w.scatter_b.split(1), "B2": lambda: w.scatter_b.split(2),
             "C0": lambda: w.scatter_c.split(0), "C1": lambda: w.scatter_c.split(1), "C2": lambda: w.scatter_c.split(2),
             "castA": cast_a, "castB": cast_b, "castC": cast_c, "prep": prepared, "wholeA": whole_a, "wholeB": whole_b,
-            "wholeC": whole_c, "project": projected, "attend": attended, "hide": hid, "liftOwn": lift_own,
+            "wholeC": whole_c, "otherA": other_a, "otherB": other_b, "otherC": other_c, "project": projected, "attend": attended, "hide": hid, "liftOwn": lift_own,
             "liftOth": lift_oth, "turn": turned, "lowerOwn": lowered_own, "lower": lowered_all, "downOth": down_oth,
             "downOwn": down_own, "pairC": pair_c, "upOth": up_oth, "upOwn": up_own, "pairB": pair_b, "sinkOwn": sink_own,
             "sinkOth": sink_oth, "surface": surfaced, "values": valued, "voOth": vo_oth, "voOwn": vo_own,

time: 221 us -> 215 us (0.973)
  waiting for transfers between devices: 87.3 us -> 71.3 us
  starting transfers between devices: 42.8 us -> 49.3 us
  Pallas kernels: 82.6 us -> 85.3 us
    ppermute x47 -> x50, waiting for transfers between devices: 87.3 us -> 71.3 us  [send(): return lax.ppermute(value, AXES, pairs)]
    ppermute x47 -> x50, starting transfers between devices: 42.8 us -> 49.3 us  [send(): return lax.ppermute(value, AXES, pairs)]
    pallas_call x60 -> x63, Pallas kernels: 82.6 us -> 85.3 us  [run(): pl.pallas_call(chain, out_shape=shapes, in_specs=[pl.BlockSpec(memory_spa...]
    unnamed x40 -> x42, local copies, waits for them, and re-layouts: 5.51 us -> 6.47 us
  transfers between devices with their start and end apart: 47 -> 50, of which waited for: 21 -> 25; matrix products, arithmetic and copies ran while one was open for 0% -> 0% of each run, Pallas kernels for 30% -> 34%
where the time goes in v5:
time: 215 us
  Pallas kernels  85.3 us (40%)
  waiting for transfers between devices  71.3 us (33%)
  starting transfers between devices  49.3 us (23%)
  local copies, waits for them, and re-layouts  6.63 us (3%)
    pallas_call x63, Pallas kernels, run(): pl.pallas_call(chain, out_shape=shapes, in_specs=[pl.BlockSpec(memory_spa...  85.3 us
    ppermute x50, waiting for transfers between devices, send(): return lax.ppermute(value, AXES, pairs)  71.3 us
    ppermute x50, starting transfers between devices, send(): return lax.ppermute(value, AXES, pairs)  49.3 us
    unnamed x42, local copies, waits for them, and re-layouts  6.47 us
  transfers between devices with their start and end apart: 50, of which 25 were waited for; matrix products, arithmetic and copies ran while one was open for 0% of the time, Pallas kernels for 34%

profile of v5, /device:TPU:0, one launch (start us, length us, event | category | flops | bytes accessed | tf_op | source)
XLA Modules:
  0.0 214.7 jit_solution(17509012544689116477)
XLA Ops:
  2.5 3.1 %collective-permute-start = (bf16[4,48,384]{2,1,0:T(8,128)(2,1)S(1)}, bf16[4,48,384]{2,1,0:T(8,128)(2,1)S(1)}, u32[]{:S(2)}, u32[]{:S(2)}) collective-permute-start(bf16[4,48,384]{2,1,0:T(8,128)(2,1)S(1)} %get-tuple-element.221.refs_2_), channel_id=1, source_target_pairs={{0,8},{1,9},{2,10},{3,11},{4,12},{5,13},{6,14},{7,15},{8,0},{9,1},... | collective-permute-start | bytes 442376 | tf_op jit(solution)/shard_map/ppermute | solution.py:67
  5.6 2.6 %collective-permute-start.1 = (bf16[4,48,384]{2,1,0:T(8,128)(2,1)S(1)}, bf16[4,48,384]{2,1,0:T(8,128)(2,1)S(1)}, u32[]{:S(2)}, u32[]{:S(2)}) collective-permute-start(bf16[4,48,384]{2,1,0:T(8,128)(2,1)S(1)} %get-tuple-element.221.refs_2_), channel_id=1, source_target_pairs={{0,16},{1,17},{2,18},{3,19},{4,20},{5,21},{6,22},{7,23},{8,24},{9,... | collective-permute-start | bytes 442376 | tf_op jit(solution)/shard_map/ppermute | solution.py:67
  10.0 1.4 copy-done
  11.4 1.4 copy-done.1
  14.6 5.0 %collective-permute-done.1.refs_4_ = bf16[4,48,384]{2,1,0:T(8,128)(2,1)S(1)} collective-permute-done((bf16[4,48,384]{2,1,0:T(8,128)(2,1)S(1)}, bf16[4,48,384]{2,1,0:T(8,128)(2,1)S(1)}, u32[]{:S(2)}, u32[]{:S(2)}) %collective-permute-start.1) | collective-permute-done | bytes 147488 | tf_op jit(solution)/shard_map/ppermute | solution.py:67
  20.2 1.6 collective-permute-start.4
  21.8 3.3 %collective-permute-start.3 = (bf16[1,48,1536]{2,1,0:T(8,128)(2,1)S(1)}, bf16[1,48,1536]{2,1,0:T(8,128)(2,1)S(1)}, u32[]{:S(2)}, u32[]{:S(2)}) collective-permute-start(bf16[1,48,1536]{2,1,0:T(8,128)(2,1)S(1)} %get-tuple-element.223.refs_2_), channel_id=1, source_target_pairs={{0,16},{1,17},{2,18},{3,19},{4,20},{5,21},{6,22},{7,23},{8,24},{9,... | collective-permute-start | bytes 442376 | tf_op jit(solution)/shard_map/ppermute | solution.py:67
  25.1 5.8 %collective-permute-done.3.refs_3_ = bf16[1,48,1536]{2,1,0:T(8,128)(2,1)S(1)} collective-permute-done((bf16[1,48,1536]{2,1,0:T(8,128)(2,1)S(1)}, bf16[1,48,1536]{2,1,0:T(8,128)(2,1)S(1)}, u32[]{:S(2)}, u32[]{:S(2)}) %collective-permute-start.3) | collective-permute-done | bytes 147488 | tf_op jit(solution)/shard_map/ppermute | solution.py:67
  32.7 2.0 collective-permute-start.6
  34.7 1.6 collective-permute-start.5
  36.3 5.3 %collective-permute-done.5.refs_3_ = bf16[1,96,768]{2,1,0:T(8,128)(2,1)S(1)} collective-permute-done((bf16[1,96,768]{2,1,0:T(8,128)(2,1)S(1)}, bf16[1,96,768]{2,1,0:T(8,128)(2,1)S(1)}, u32[]{:S(2)}, u32[]{:S(2)}) %collective-permute-start.5) | collective-permute-done | bytes 147488 | tf_op jit(solution)/shard_map/ppermute | solution.py:67
  42.8 1.6 collective-permute-start.9
  45.3 9.8 %collective-permute-done.7.refs_3_ = bf16[2,2,2,4,48,384]{5,4,3,2,1,0:T(8,128)(2,1)S(1)} collective-permute-done((bf16[2,2,2,4,48,384]{5,4,3,2,1,0:T(8,128)(2,1)S(1)}, bf16[2,2,2,4,48,384]{5,4,3,2,1,0:T(8,128)(2,1)S(1)}, u32[]{:S(2)}, u32[]{:S(2)}) %collective-permute-start.7) | collective-permute-done | bytes 1179680 | tf_op jit(solution)/shard_map/ppermute | solution.py:67
  58.4 1.7 collective-permute-start.13
  61.0 3.2 %project.1 = (bf16[3,512,768]{2,1,0:T(8,128)(2,1)S(1)}, f32[8,128]{1,0:T(8,128)S(1)}) custom-call(f32[8,128]{1,0:T(8,128)S(1)} %get-tuple-element.239.refs_0_, bf16[512,768]{1,0:T(8,128)(2,1)S(1)} %get-tuple-element.240.refs_1_.refs_2_, bf16[4,768,384]{2,1,0:T(8,128)(2,1)S(1)} %bitcast.61, bf16[4,768,384]{2,1,0:T(8,128)(2,1)S(1)} %bitcast.65, ...), custom_call_target="tpu_custom_call" | custom-call | flops 1811939328 | bytes 8388608 | tf_op jit(solution)/shard_map/project/pallas_call | solution.py:142
  64.1 4.6 %attend.1 = (bf16[512,1536]{1,0:T(8,128)(2,1)S(1)}, bf16[512,768]{1,0:T(8,128)(2,1)S(1)}, f32[8,128]{1,0:T(8,128)S(1)}) custom-call(s32[8]{0:T(128)S(1)} %concatenate.3.refs_0_, f32[8,128]{1,0:T(8,128)S(1)} %get-tuple-element.244.refs_1_, bf16[3,512,768]{2,1,0:T(8,128)(2,1)S(1)} %get-tuple-element.245.refs_2_.refs_3_), custom_call_target="tpu_custom_call" | custom-call | flops 805306368 | bytes 5242880 | tf_op jit(solution)/shard_map/attend/pallas_call | solution.py:142
  68.8 5.2 %collective-permute-done.12.refs_3_ = bf16[2,2,1,96,768]{4,3,2,1,0:T(8,128)(2,1)S(1)} collective-permute-done((bf16[2,2,1,96,768]{4,3,2,1,0:T(8,128)(2,1)S(1)}, bf16[2,2,1,96,768]{4,3,2,1,0:T(8,128)(2,1)S(1)}, u32[]{:S(2)}, u32[]{:S(2)}) %collective-permute-start.12) | collective-permute-done | bytes 589856 | tf_op jit(solution)/shard_map/ppermute | solution.py:67
  75.5 1.7 collective-permute-start.16
  77.2 1.1 collective-permute-done.15.refs_3_
  79.0 1.3 hide.1
  80.4 3.4 %_lambda_.2 = (bf16[512,1536]{1,0:T(8,128)(2,1)S(1)}, bf16[1536,512]{1,0:T(8,128)(2,1)S(1)}, bf16[512,1536]{1,0:T(8,128)(2,1)S(1)}, f32[8,128]{1,0:T(8,128)S(1)}) custom-call(f32[8,128]{1,0:T(8,128)S(1)} %get-tuple-element.254.refs_0_, bf16[512,768]{1,0:T(8,128)(2,1)S(1)} %get-tuple-element.255.refs_1_, bf16[768,1536]{1,0:T(8,128)(2,1)S(1)} %bitcast.74, ...), custom_call_target="tpu_custom_call" | custom-call | flops 1207959552 | bytes 8388608 | tf_op jit(solution)/shard_map/<lambda>/pallas_call | solution.py:142
  83.8 3.4 %_lambda_.3 = (bf16[512,1536]{1,0:T(8,128)(2,1)S(1)}, bf16[1536,512]{1,0:T(8,128)(2,1)S(1)}, bf16[512,1536]{1,0:T(8,128)(2,1)S(1)}, f32[8,128]{1,0:T(8,128)S(1)}) custom-call(f32[8,128]{1,0:T(8,128)S(1)} %get-tuple-element.258.refs_0_, bf16[512,768]{1,0:T(8,128)(2,1)S(1)} %get-tuple-element.255.refs_1_, bf16[768,1536]{1,0:T(8,128)(2,1)S(1)} %bitcast.76, ...), custom_call_target="tpu_custom_call" | custom-call | flops 1207959552 | bytes 8388608 | tf_op jit(solution)/shard_map/<lambda>/pallas_call | solution.py:142
  87.4 4.4 %collective-permute-done.16.refs_3_ = bf16[2,2,2,1,96,768]{5,4,3,2,1,0:T(8,128)(2,1)S(1)} collective-permute-done((bf16[2,2,2,1,96,768]{5,4,3,2,1,0:T(8,128)(2,1)S(1)}, bf16[2,2,2,1,96,768]{5,4,3,2,1,0:T(8,128)(2,1)S(1)}, u32[]{:S(2)}, u32[]{:S(2)}) %collective-permute-start.16) | collective-permute-done | bytes 1179680 | tf_op jit(solution)/shard_map/ppermute | solution.py:67
  92.6 1.7 lower_half.1
  94.4 1.1 collective-permute-done.18.refs_3_
  96.2 3.9 %lower.1 = (bf16[512,768]{1,0:T(8,128)(2,1)S(1)}, f32[512,768]{1,0:T(8,128)S(1)}, bf16[512,768]{1,0:T(8,128)(2,1)S(1)}, f32[8,768]{1,0:T(8,128)S(1)}, f32[8,128]{1,0:T(8,128)S(1)}) custom-call(s32[8]{0:T(128)S(1)} %concatenate.3.refs_0_, f32[8,128]{1,0:T(8,128)S(1)} %get-tuple-element.268.refs_1_, f32[512,768]{1,0:T(8,128)S(1)} %get-tuple-element.269.refs_2_, ...), custom_call_target="tpu_custom_call" | custom-call | flops 1207959552 | bytes 14680064 | tf_op jit(solution)/shard_map/lower/pallas_call | solution.py:142
  100.1 2.5 %sink.2 = (bf16[512,1536]{1,0:T(8,128)(2,1)S(1)}, f32[1,1536]{1,0:T(1,128)S(1)}, f32[8,128]{1,0:T(8,128)S(1)}) custom-call(f32[8,128]{1,0:T(8,128)S(1)} %get-tuple-element.274.refs_0_, bf16[512,768]{1,0:T(8,128)(2,1)S(1)} %get-tuple-element.275.refs_1_.refs_2_, bf16[1536,768]{1,0:T(8,128)(2,1)S(1)} %bitcast.70, bf16[512,1536]{1,0:T(8,128)(2,1)S(1)} %get-tuple-element.276.refs_3_), custom_call_target="tpu_custom_call" | custom-call | tf_op jit(solution)/shard_map/sink/pallas_call | solution.py:142
  102.6 2.2 %product.4 = (bf16[1536,768]{1,0:T(8,128)(2,1)S(1)}, f32[8,128]{1,0:T(8,128)S(1)}) custom-call(f32[8,128]{1,0:T(8,128)S(1)} %get-tuple-element.277.refs_0_, bf16[1536,512]{1,0:T(8,128)(2,1)S(1)} %get-tuple-element.278.refs_1_, bf16[512,768]{1,0:T(8,128)(2,1)S(1)} %get-tuple-element.275.refs_1_.refs_2_), custom_call_target="tpu_custom_call" | custom-call | flops 1207959552 | bytes 8388608 | tf_op jit(solution)/shard_map/product/pallas_call | solution.py:142
  105.0 2.2 %product.5 = (f32[1536,768]{1,0:T(8,128)S(1)}, f32[8,128]{1,0:T(8,128)S(1)}) custom-call(f32[8,128]{1,0:T(8,128)S(1)} %get-tuple-element.279.refs_0_, bf16[1536,512]{1,0:T(8,128)(2,1)S(1)} %get-tuple-element.280.refs_1_, bf16[512,768]{1,0:T(8,128)(2,1)S(1)} %get-tuple-element.275.refs_1_.refs_2_), custom_call_target="tpu_custom_call" | custom-call | flops 1207959552 | bytes 8388608 | tf_op jit(solution)/shard_map/product/pallas_call | solution.py:142
  107.3 1.7 product.6
  109.9 1.1 scatter_pair.3
  111.0 1.7 collective-permute-start.23
  112.7 2.5 %sink.3 = (bf16[512,1536]{1,0:T(8,128)(2,1)S(1)}, f32[1,1536]{1,0:T(1,128)S(1)}, f32[8,128]{1,0:T(8,128)S(1)}) custom-call(f32[8,128]{1,0:T(8,128)S(1)} %get-tuple-element.287.refs_0_, bf16[512,768]{1,0:T(8,128)(2,1)S(1)} %get-tuple-element.275.refs_1_.refs_2_, bf16[1536,768]{1,0:T(8,128)(2,1)S(1)} %bitcast.73, bf16[512,1536]{1,0:T(8,128)(2,1)S(1)} %get-tuple-element.288.refs_3_), custom_call_target="tpu_custom_call" | custom-call | tf_op jit(solution)/shard_map/sink/pallas_call | solution.py:142
  115.3 1.7 product.7
  118.0 5.1 %surface.1 = (f32[512,768]{1,0:T(8,128)S(1)}, bf16[768,512]{1,0:T(8,128)(2,1)S(1)}, bf16[512,768]{1,0:T(8,128)(2,1)S(1)}, f32[8,768]{1,0:T(8,128)S(1)}, f32[8,128]{1,0:T(8,128)S(1)}) custom-call(f32[8,128]{1,0:T(8,128)S(1)} %get-tuple-element.298.refs_0_, bf16[512,1536]{1,0:T(8,128)(2,1)S(1)} %get-tuple-element.290.refs_2_.refs_1_, ...), custom_call_target="tpu_custom_call" | custom-call | flops 3019898880 | bytes 14680064 | tf_op jit(solution)/shard_map/surface/pallas_call | solution.py:142
  123.1 1.4 values_back.1
  128.1 1.7 collective-permute-start.25
  129.8 6.6 %attend_back.1 = (bf16[512,768]{1,0:T(8,128)(2,1)S(1)}, bf16[512,768]{1,0:T(8,128)(2,1)S(1)}, f32[1,768]{1,0:T(1,128)S(1)}, f32[8,128]{1,0:T(8,128)S(1)}) custom-call(f32[8,128]{1,0:T(8,128)S(1)} %get-tuple-element.311.refs_0_, bf16[512,1536]{1,0:T(8,128)(2,1)S(1)} %get-tuple-element.302.refs_1_, bf16[512,768]{1,0:T(8,128)(2,1)S(1)} %get-tuple-element.303.refs_2_, ...), custom_call_target="tpu_custom_call" | custom-call | flops 805306368 | bytes 6291456 | tf_op jit(solution)/shard_map/attend_back/pallas_call | solution.py:142
  140.3 2.4 %collective-permute-done.25.refs_3_ = bf16[2,2,1,96,768]{4,3,2,1,0:T(8,128)(2,1)S(1)} collective-permute-done((bf16[2,2,1,96,768]{4,3,2,1,0:T(8,128)(2,1)S(1)}, bf16[2,2,1,96,768]{4,3,2,1,0:T(8,128)(2,1)S(1)}, u32[]{:S(2)}, u32[]{:S(2)}) %collective-permute-start.25) | collective-permute-done | bytes 589856 | tf_op jit(solution)/shard_map/ppermute | solution.py:67
  144.2 1.7 collective-permute-start.32
  149.9 3.0 %states_back.1 = (bf16[512,768]{1,0:T(8,128)(2,1)S(1)}, f32[8,128]{1,0:T(8,128)S(1)}) custom-call(f32[8,128]{1,0:T(8,128)S(1)} %get-tuple-element.332.refs_0_, bf16[512,768]{1,0:T(8,128)(2,1)S(1)} %get-tuple-element.313.refs_3_.refs_1_, bf16[512,768]{1,0:T(8,128)(2,1)S(1)} %get-tuple-element.314.refs_4_.refs_2_, ...), custom_call_target="tpu_custom_call" | custom-call | flops 1811939328 | bytes 8388608 | tf_op jit(solution)/shard_map/states_back/pallas_call | solution.py:142
  153.6 1.2 collective-permute-done.30.refs_3_
  155.5 7.8 %collective-permute-done.31.refs_3_ = bf16[2,1,96,768]{3,2,1,0:T(8,128)(2,1)S(1)} collective-permute-done((bf16[2,1,96,768]{3,2,1,0:T(8,128)(2,1)S(1)}, bf16[2,1,96,768]{3,2,1,0:T(8,128)(2,1)S(1)}, u32[]{:S(2)}, u32[]{:S(2)}) %collective-permute-start.31) | collective-permute-done | bytes 294944 | tf_op jit(solution)/shard_map/ppermute | solution.py:67
  165.8 1.2 collective-permute-start.36
  167.0 3.2 %collective-permute-start.38 = (bf16[2,3,48,512]{3,2,1,0:T(8,128)(2,1)S(1)}, bf16[2,3,48,512]{3,2,1,0:T(8,128)(2,1)S(1)}, u32[]{:S(2)}, u32[]{:S(2)}) collective-permute-start(bf16[2,3,48,512]{3,2,1,0:T(8,128)(2,1)S(1)} %get-tuple-element.364), channel_id=1, source_target_pairs={{0,16},{1,17},{2,18},{3,19},{4,20},{5,21},{6,22},{7,23},{8,24},{9,... | collective-permute-start | bytes 884744 | tf_op jit(solution)/shard_map/ppermute | solution.py:67
  170.2 1.8 pair_up.2
  172.0 3.7 %collective-permute-done.36.refs_3_ = bf16[2,2,4,48,384]{4,3,2,1,0:T(8,128)(2,1)S(1)} collective-permute-done((bf16[2,2,4,48,384]{4,3,2,1,0:T(8,128)(2,1)S(1)}, bf16[2,2,4,48,384]{4,3,2,1,0:T(8,128)(2,1)S(1)}, u32[]{:S(2)}, u32[]{:S(2)}) %collective-permute-start.36) | collective-permute-done | bytes 589856 | tf_op jit(solution)/shard_map/ppermute | solution.py:67
  176.4 2.4 %collective-permute-start.39 = (bf16[2,4,48,384]{3,2,1,0:T(8,128)(2,1)S(1)}, bf16[2,4,48,384]{3,2,1,0:T(8,128)(2,1)S(1)}, u32[]{:S(2)}, u32[]{:S(2)}) collective-permute-start(bf16[2,4,48,384]{3,2,1,0:T(8,128)(2,1)S(1)} %get-tuple-element.367), channel_id=1, source_target_pairs={{0,8},{1,9},{2,10},{3,11},{4,12},{5,13},{6,14},{7,15},{8,0},{9,1},... | collective-permute-start | bytes 884744 | tf_op jit(solution)/shard_map/ppermute | solution.py:67
  179.8 4.2 %collective-permute-done.37.refs_2_ = bf16[1,96,768]{2,1,0:T(8,128)(2,1)S(1)} collective-permute-done((bf16[1,96,768]{2,1,0:T(8,128)(2,1)S(1)}, bf16[1,96,768]{2,1,0:T(8,128)(2,1)S(1)}, u32[]{:S(2)}, u32[]{:S(2)}) %collective-permute-start.37) | collective-permute-done | bytes 147488 | tf_op jit(solution)/shard_map/ppermute | solution.py:67
  184.0 1.2 step.2
  188.7 2.4 %collective-permute-done.40.refs_2_ = bf16[3,48,512]{2,1,0:T(8,128)(2,1)S(1)} collective-permute-done((bf16[3,48,512]{2,1,0:T(8,128)(2,1)S(1)}, bf16[3,48,512]{2,1,0:T(8,128)(2,1)S(1)}, u32[]{:S(2)}, u32[]{:S(2)}) %collective-permute-start.40) | collective-permute-done | bytes 147488 | tf_op jit(solution)/shard_map/ppermute | solution.py:67
  191.1 1.2 step.3
  192.3 2.7 %collective-permute-done.41.refs_2_ = bf16[4,48,384]{2,1,0:T(8,128)(2,1)S(1)} collective-permute-done((bf16[4,48,384]{2,1,0:T(8,128)(2,1)S(1)}, bf16[4,48,384]{2,1,0:T(8,128)(2,1)S(1)}, u32[]{:S(2)}, u32[]{:S(2)}) %collective-permute-start.41) | collective-permute-done | bytes 147488 | tf_op jit(solution)/shard_map/ppermute | solution.py:67
  195.1 1.1 attend_step.1
  196.2 2.7 %collective-permute-start.44 = (f32[8,768]{1,0:T(8,128)S(1)}, f32[8,768]{1,0:T(8,128)S(1)}, u32[]{:S(2)}, u32[]{:S(2)}) collective-permute-start(f32[8,768]{1,0:T(8,128)S(1)} %get-tuple-element.381.refs_1_), channel_id=1, source_target_pairs={{0,16},{1,17},{2,18},{3,19},{4,20},{5,21},{6,22},{7,23},{8,24},{9,... | collective-permute-start | bytes 73736 | tf_op jit(solution)/shard_map/ppermute | solution.py:67
  199.0 1.6 collective-permute-start.45
  200.6 2.4 %pair_up.3 = (f32[2,512,768]{2,1,0:T(8,128)}, f32[8,128]{1,0:T(8,128)S(1)}) custom-call(s32[8]{0:T(128)S(1)} %concatenate.3.refs_0_, f32[8,128]{1,0:T(8,128)S(1)} %get-tuple-element.377.refs_1_, bf16[512,768]{1,0:T(8,128)(2,1)S(1)} %get-tuple-element.378.refs_2_, bf16[512,768]{1,0:T(8,128)(2,1)S(1)} %collective-permute-done.42.refs_3_), custom_call_target="tpu_custom_call" | custom-call | tf_op jit(solution)/shard_map/pair_up/pallas_call | solution.py:142
  203.0 1.6 collective-permute-done.45.refs_4_
  204.6 1.1 collective-permute-start.46
  206.6 1.6 collective-permute-start.48
  208.5 1.1 collective-permute-done.47.refs_3_
  209.6 1.7 collective-permute-done.48.refs_4_
  211.4 1.2 collective-permute-done.49.refs_3_
  212.6 2.0 update.1
  (144 shorter events, 43.3 us)
Async XLA Ops:
  2.5 12.1 %collective-permute-start = (bf16[4,48,384]{2,1,0:T(8,128)(2,1)S(1)}, bf16[4,48,384]{2,1,0:T(8,128)(2,1)S(1)}, u32[]{:S(2)}, u32[]{:S(2)}) collective-permute-start(bf16[4,48,384]{2,1,0:T(8,128)(2,1)S(1)} %get-tuple-element.221.refs_2_), channel_id=1, source_target_pairs={{0,8},{1,9},{2,10},{3,11},{4,12},{5,13},{6,14},{7,15},{8,0},{9,1},... | collective-permute-start | bytes 442376 | tf_op jit(solution)/shard_map/ppermute | solution.py:67
  5.6 14.0 %collective-permute-start.1 = (bf16[4,48,384]{2,1,0:T(8,128)(2,1)S(1)}, bf16[4,48,384]{2,1,0:T(8,128)(2,1)S(1)}, u32[]{:S(2)}, u32[]{:S(2)}) collective-permute-start(bf16[4,48,384]{2,1,0:T(8,128)(2,1)S(1)} %get-tuple-element.221.refs_2_), channel_id=1, source_target_pairs={{0,16},{1,17},{2,18},{3,19},{4,20},{5,21},{6,22},{7,23},{8,24},{9,... | collective-permute-start | bytes 442376 | tf_op jit(solution)/shard_map/ppermute | solution.py:67
  8.2 11.4 %collective-permute-start.2 = (bf16[4,48,384]{2,1,0:T(8,128)(2,1)S(1)}, bf16[4,48,384]{2,1,0:T(8,128)(2,1)S(1)}, u32[]{:S(2)}, u32[]{:S(2)}) collective-permute-start(bf16[4,48,384]{2,1,0:T(8,128)(2,1)S(1)} %get-tuple-element.221.refs_2_), channel_id=1, source_target_pairs={{0,24},{1,25},{2,26},{3,27},{4,28},{5,29},{6,30},{7,31},{8,16},{9,... | collective-permute-start | bytes 442376 | tf_op jit(solution)/shard_map/ppermute | solution.py:67
  14.6 20.1 %copy-start.4 = (f32[96,768]{1,0:T(8,128)S(1)}, f32[96,768]{1,0:T(8,128)}, u32[]{:S(2)}) copy-start(f32[96,768]{1,0:T(8,128)} %param.26) | copy-start | bytes 884740
  20.2 11.2 %collective-permute-start.4 = (bf16[2,2,4,48,384]{4,3,2,1,0:T(8,128)(2,1)S(1)}, bf16[2,2,4,48,384]{4,3,2,1,0:T(8,128)(2,1)S(1)}, u32[]{:S(2)}, u32[]{:S(2)}) collective-permute-start(bf16[2,2,4,48,384]{4,3,2,1,0:T(8,128)(2,1)S(1)} %get-tuple-element.225.refs_2_), channel_id=1, source_target_pairs={{0,2},{1,5},{2,0},{3,7},{4,6},{5,1},{6,4},{7,3},{8,10},{9,13},{10,... | collective-permute-start | bytes 1769480 | tf_op jit(solution)/shard_map/ppermute | solution.py:67
  21.8 9.1 %collective-permute-start.3 = (bf16[1,48,1536]{2,1,0:T(8,128)(2,1)S(1)}, bf16[1,48,1536]{2,1,0:T(8,128)(2,1)S(1)}, u32[]{:S(2)}, u32[]{:S(2)}) collective-permute-start(bf16[1,48,1536]{2,1,0:T(8,128)(2,1)S(1)} %get-tuple-element.223.refs_2_), channel_id=1, source_target_pairs={{0,16},{1,17},{2,18},{3,19},{4,20},{5,21},{6,22},{7,23},{8,24},{9,... | collective-permute-start | bytes 442376 | tf_op jit(solution)/shard_map/ppermute | solution.py:67
  32.1 23.1 %collective-permute-start.7 = (bf16[2,2,2,4,48,384]{5,4,3,2,1,0:T(8,128)(2,1)S(1)}, bf16[2,2,2,4,48,384]{5,4,3,2,1,0:T(8,128)(2,1)S(1)}, u32[]{:S(2)}, u32[]{:S(2)}) collective-permute-start(bf16[2,2,2,4,48,384]{5,4,3,2,1,0:T(8,128)(2,1)S(1)} %get-tuple-element.232.refs_2_), channel_id=1, source_target_pairs={{0,4},{1,3},{2,6},{3,1},{4,0},{5,7},{6,2},{7,5},{8,12},{9,11},{10,... | collective-permute-start | bytes 3538952 | tf_op jit(solution)/shard_map/ppermute | solution.py:67
  32.7 9.5 %collective-permute-start.6 = (bf16[2,1,48,1536]{3,2,1,0:T(8,128)(2,1)S(1)}, bf16[2,1,48,1536]{3,2,1,0:T(8,128)(2,1)S(1)}, u32[]{:S(2)}, u32[]{:S(2)}) collective-permute-start(bf16[2,1,48,1536]{3,2,1,0:T(8,128)(2,1)S(1)} %get-tuple-element.230.refs_2_), channel_id=1, source_target_pairs={{0,8},{1,9},{2,10},{3,11},{4,12},{5,13},{6,14},{7,15},{8,0},{9,1},... | collective-permute-start | bytes 884744 | tf_op jit(solution)/shard_map/ppermute | solution.py:67
  34.7 6.9 %collective-permute-start.5 = (bf16[1,96,768]{2,1,0:T(8,128)(2,1)S(1)}, bf16[1,96,768]{2,1,0:T(8,128)(2,1)S(1)}, u32[]{:S(2)}, u32[]{:S(2)}) collective-permute-start(bf16[1,96,768]{2,1,0:T(8,128)(2,1)S(1)} %get-tuple-element.228.refs_2_), channel_id=1, source_target_pairs={{0,2},{1,5},{2,0},{3,7},{4,6},{5,1},{6,4},{7,3},{8,10},{9,13},{10,... | collective-permute-start | bytes 442376 | tf_op jit(solution)/shard_map/ppermute | solution.py:67
  42.8 15.0 %collective-permute-start.9 = (bf16[2,2,1,48,1536]{4,3,2,1,0:T(8,128)(2,1)S(1)}, bf16[2,2,1,48,1536]{4,3,2,1,0:T(8,128)(2,1)S(1)}, u32[]{:S(2)}, u32[]{:S(2)}) collective-permute-start(bf16[2,2,1,48,1536]{4,3,2,1,0:T(8,128)(2,1)S(1)} %get-tuple-element.236.refs_2_), channel_id=1, source_target_pairs={{0,2},{1,5},{2,0},{3,7},{4,6},{5,1},{6,4},{7,3},{8,10},{9,13},{10,... | collective-permute-start | bytes 1769480 | tf_op jit(solution)/shard_map/ppermute | solution.py:67
  44.3 12.8 %collective-permute-start.8 = (bf16[2,1,96,768]{3,2,1,0:T(8,128)(2,1)S(1)}, bf16[2,1,96,768]{3,2,1,0:T(8,128)(2,1)S(1)}, u32[]{:S(2)}, u32[]{:S(2)}) collective-permute-start(bf16[2,1,96,768]{3,2,1,0:T(8,128)(2,1)S(1)} %get-tuple-element.234.refs_2_), channel_id=1, source_target_pairs={{0,16},{1,17},{2,18},{3,19},{4,20},{5,21},{6,22},{7,23},{8,24},{9,... | collective-permute-start | bytes 884744 | tf_op jit(solution)/shard_map/ppermute | solution.py:67
  45.3 14.9 %collective-permute-start.10 = (bf16[2,2,2,4,48,384]{5,4,3,2,1,0:T(8,128)(2,1)S(1)}, bf16[2,2,2,4,48,384]{5,4,3,2,1,0:T(8,128)(2,1)S(1)}, u32[]{:S(2)}, u32[]{:S(2)}) collective-permute-start(bf16[2,2,2,4,48,384]{5,4,3,2,1,0:T(8,128)(2,1)S(1)} %get-tuple-element.232.refs_2_), channel_id=1, source_target_pairs={{0,1},{1,0},{2,3},{3,2},{4,5},{5,4},{6,7},{7,6},{8,9},{9,8},{10,11... | collective-permute-start | bytes 3538952 | tf_op jit(solution)/shard_map/ppermute | solution.py:67
  56.0 4.2 %collective-permute-start.11 = (bf16[2,2,2,4,48,384]{5,4,3,2,1,0:T(8,128)(2,1)S(1)}, bf16[2,2,2,4,48,384]{5,4,3,2,1,0:T(8,128)(2,1)S(1)}, u32[]{:S(2)}, u32[]{:S(2)}) collective-permute-start(bf16[2,2,2,4,48,384]{5,4,3,2,1,0:T(8,128)(2,1)S(1)} %get-tuple-element.238), channel_id=1, source_target_pairs={{0,1},{1,0},{2,3},{3,2},{4,5},{5,4},{6,7},{7,6},{8,9},{9,8},{10,11... | collective-permute-start | bytes 3538952 | tf_op jit(solution)/shard_map/ppermute | solution.py:67
  58.4 16.3 %collective-permute-start.13 = (bf16[2,2,2,1,48,1536]{5,4,3,2,1,0:T(8,128)(2,1)S(1)}, bf16[2,2,2,1,48,1536]{5,4,3,2,1,0:T(8,128)(2,1)S(1)}, u32[]{:S(2)}, u32[]{:S(2)}) collective-permute-start(bf16[2,2,2,1,48,1536]{5,4,3,2,1,0:T(8,128)(2,1)S(1)} %get-tuple-element.249.refs_2_), channel_id=1, source_target_pairs={{0,4},{1,3},{2,6},{3,1},{4,0},{5,7},{6,2},{7,5},{8,12},{9,11},{10,... | collective-permute-start | bytes 3538952 | tf_op jit(solution)/shard_map/ppermute | solution.py:67
  60.1 13.8 %collective-permute-start.12 = (bf16[2,2,1,96,768]{4,3,2,1,0:T(8,128)(2,1)S(1)}, bf16[2,2,1,96,768]{4,3,2,1,0:T(8,128)(2,1)S(1)}, u32[]{:S(2)}, u32[]{:S(2)}) collective-permute-start(bf16[2,2,1,96,768]{4,3,2,1,0:T(8,128)(2,1)S(1)} %get-tuple-element.247.refs_2_), channel_id=1, source_target_pairs={{0,8},{1,9},{2,10},{3,11},{4,12},{5,13},{6,14},{7,15},{8,0},{9,1},... | collective-permute-start | bytes 1769480 | tf_op jit(solution)/shard_map/ppermute | solution.py:67
  60.2 17.0 %collective-permute-start.14 = (bf16[2,2,2,1,48,1536]{5,4,3,2,1,0:T(8,128)(2,1)S(1)}, bf16[2,2,2,1,48,1536]{5,4,3,2,1,0:T(8,128)(2,1)S(1)}, u32[]{:S(2)}, u32[]{:S(2)}) collective-permute-start(bf16[2,2,2,1,48,1536]{5,4,3,2,1,0:T(8,128)(2,1)S(1)} %get-tuple-element.249.refs_2_), channel_id=1, source_target_pairs={{0,1},{1,0},{2,3},{3,2},{4,5},{5,4},{6,7},{7,6},{8,9},{9,8},{10,11... | collective-permute-start | bytes 3538952 | tf_op jit(solution)/shard_map/ppermute | solution.py:67
  75.4 2.9 %collective-permute-start.15 = (bf16[2,2,2,1,48,1536]{5,4,3,2,1,0:T(8,128)(2,1)S(1)}, bf16[2,2,2,1,48,1536]{5,4,3,2,1,0:T(8,128)(2,1)S(1)}, u32[]{:S(2)}, u32[]{:S(2)}) collective-permute-start(bf16[2,2,2,1,48,1536]{5,4,3,2,1,0:T(8,128)(2,1)S(1)} %get-tuple-element.251), channel_id=1, source_target_pairs={{0,1},{1,0},{2,3},{3,2},{4,5},{5,4},{6,7},{7,6},{8,9},{9,8},{10,11... | collective-permute-start | bytes 3538952 | tf_op jit(solution)/shard_map/ppermute | solution.py:67
  75.5 16.3 %collective-permute-start.16 = (bf16[2,2,2,1,96,768]{5,4,3,2,1,0:T(8,128)(2,1)S(1)}, bf16[2,2,2,1,96,768]{5,4,3,2,1,0:T(8,128)(2,1)S(1)}, u32[]{:S(2)}, u32[]{:S(2)}) collective-permute-start(bf16[2,2,2,1,96,768]{5,4,3,2,1,0:T(8,128)(2,1)S(1)} %get-tuple-element.262.refs_2_), channel_id=1, source_target_pairs={{0,4},{1,3},{2,6},{3,1},{4,0},{5,7},{6,2},{7,5},{8,12},{9,11},{10,... | collective-permute-start | bytes 3538952 | tf_op jit(solution)/shard_map/ppermute | solution.py:67
  77.2 17.2 %collective-permute-start.17 = (bf16[2,2,2,1,96,768]{5,4,3,2,1,0:T(8,128)(2,1)S(1)}, bf16[2,2,2,1,96,768]{5,4,3,2,1,0:T(8,128)(2,1)S(1)}, u32[]{:S(2)}, u32[]{:S(2)}) collective-permute-start(bf16[2,2,2,1,96,768]{5,4,3,2,1,0:T(8,128)(2,1)S(1)} %get-tuple-element.262.refs_2_), channel_id=1, source_target_pairs={{0,1},{1,0},{2,3},{3,2},{4,5},{5,4},{6,7},{7,6},{8,9},{9,8},{10,11... | collective-permute-start | bytes 3538952 | tf_op jit(solution)/shard_map/ppermute | solution.py:67
  92.5 2.9 %collective-permute-start.18 = (bf16[2,2,2,1,96,768]{5,4,3,2,1,0:T(8,128)(2,1)S(1)}, bf16[2,2,2,1,96,768]{5,4,3,2,1,0:T(8,128)(2,1)S(1)}, u32[]{:S(2)}, u32[]{:S(2)}) collective-permute-start(bf16[2,2,2,1,96,768]{5,4,3,2,1,0:T(8,128)(2,1)S(1)} %get-tuple-element.267), channel_id=1, source_target_pairs={{0,1},{1,0},{2,3},{3,2},{4,5},{5,4},{6,7},{7,6},{8,9},{9,8},{10,11... | collective-permute-start | bytes 3538952 | tf_op jit(solution)/shard_map/ppermute | solution.py:67
  104.8 5.1 %collective-permute-start.19 = (bf16[1,16,96,768]{3,2,1,0:T(8,128)(2,1)S(1)}, bf16[1,16,96,768]{3,2,1,0:T(8,128)(2,1)S(1)}, u32[]{:S(2)}, u32[]{:S(2)}) collective-permute-start(bf16[1,16,96,768]{3,2,1,0:T(8,128)(2,1)S(1)} %bitcast.95), channel_id=1, source_target_pairs={{0,1},{1,0},{2,3},{3,2},{4,5},{5,4},{6,7},{7,6},{8,9},{9,8},{10,11... | collective-permute-start | bytes 7077896 | tf_op jit(solution)/shard_map/ppermute | solution.py:67
  109.0 8.0 %collective-permute-start.20 = (bf16[1,16,48,512]{3,2,1,0:T(8,128)(2,1)S(1)}, bf16[1,16,48,512]{3,2,1,0:T(8,128)(2,1)S(1)}, u32[]{:S(2)}, u32[]{:S(2)}) collective-permute-start(bf16[1,16,48,512]{3,2,1,0:T(8,128)(2,1)S(1)} %bitcast.98), channel_id=1, source_target_pairs={{0,1},{1,0},{2,3},{3,2},{4,5},{5,4},{6,7},{7,6},{8,9},{9,8},{10,11... | collective-permute-start | bytes 2359304 | tf_op jit(solution)/shard_map/ppermute | solution.py:67
  109.4 7.6 %collective-permute-start.21 = (bf16[1,16,48,512]{3,2,1,0:T(8,128)(2,1)S(1)}, bf16[1,16,48,512]{3,2,1,0:T(8,128)(2,1)S(1)}, u32[]{:S(2)}, u32[]{:S(2)}) collective-permute-start(bf16[1,16,48,512]{3,2,1,0:T(8,128)(2,1)S(1)} %bitcast.97), channel_id=1, source_target_pairs={{0,1},{1,0},{2,3},{3,2},{4,5},{5,4},{6,7},{7,6},{8,9},{9,8},{10,11... | collective-permute-start | bytes 2359304 | tf_op jit(solution)/shard_map/ppermute | solution.py:67
  109.6 7.5 %collective-permute-start.22 = (bf16[1,16,48,512]{3,2,1,0:T(8,128)(2,1)S(1)}, bf16[1,16,48,512]{3,2,1,0:T(8,128)(2,1)S(1)}, u32[]{:S(2)}, u32[]{:S(2)}) collective-permute-start(bf16[1,16,48,512]{3,2,1,0:T(8,128)(2,1)S(1)} %bitcast.96), channel_id=1, source_target_pairs={{0,1},{1,0},{2,3},{3,2},{4,5},{5,4},{6,7},{7,6},{8,9},{9,8},{10,11... | collective-permute-start | bytes 2359304 | tf_op jit(solution)/shard_map/ppermute | solution.py:67
  111.0 16.3 %collective-permute-start.23 = (bf16[2,2,2,1,96,768]{5,4,3,2,1,0:T(8,128)(2,1)S(1)}, bf16[2,2,2,1,96,768]{5,4,3,2,1,0:T(8,128)(2,1)S(1)}, u32[]{:S(2)}, u32[]{:S(2)}) collective-permute-start(bf16[2,2,2,1,96,768]{5,4,3,2,1,0:T(8,128)(2,1)S(1)} %get-tuple-element.310), channel_id=1, source_target_pairs={{0,4},{1,3},{2,6},{3,1},{4,0},{5,7},{6,2},{7,5},{8,12},{9,11},{10,... | collective-permute-start | bytes 3538952 | tf_op jit(solution)/shard_map/ppermute | solution.py:67
  125.5 13.5 %collective-permute-start.24 = (bf16[2,768,384]{2,1,0:T(8,128)(2,1)S(1)}, bf16[2,768,384]{2,1,0:T(8,128)(2,1)S(1)}, u32[]{:S(2)}, u32[]{:S(2)}) collective-permute-start(bf16[2,768,384]{2,1,0:T(8,128)(2,1)S(1)} %get-tuple-element.319), channel_id=1, source_target_pairs={{0,1},{1,0},{2,3},{3,2},{4,5},{5,4},{6,7},{7,6},{8,9},{9,8},{10,11... | collective-permute-start | bytes 3538952 | tf_op jit(solution)/shard_map/ppermute | solution.py:67
  125.6 17.9 %collective-permute-start.26 = (bf16[2,2,2,3,48,512]{5,4,3,2,1,0:T(8,128)(2,1)S(1)}, bf16[2,2,2,3,48,512]{5,4,3,2,1,0:T(8,128)(2,1)S(1)}, u32[]{:S(2)}, u32[]{:S(2)}) collective-permute-start(bf16[2,2,2,3,48,512]{5,4,3,2,1,0:T(8,128)(2,1)S(1)} %get-tuple-element.325), channel_id=1, source_target_pairs={{0,4},{1,3},{2,6},{3,1},{4,0},{5,7},{6,2},{7,5},{8,12},{9,11},{10,... | collective-permute-start | bytes 3538952 | tf_op jit(solution)/shard_map/ppermute | solution.py:67
  128.1 14.7 %collective-permute-start.25 = (bf16[2,2,1,96,768]{4,3,2,1,0:T(8,128)(2,1)S(1)}, bf16[2,2,1,96,768]{4,3,2,1,0:T(8,128)(2,1)S(1)}, u32[]{:S(2)}, u32[]{:S(2)}) collective-permute-start(bf16[2,2,1,96,768]{4,3,2,1,0:T(8,128)(2,1)S(1)} %get-tuple-element.322), channel_id=1, source_target_pairs={{0,8},{1,9},{2,10},{3,11},{4,12},{5,13},{6,14},{7,15},{8,0},{9,1},... | collective-permute-start | bytes 1769480 | tf_op jit(solution)/shard_map/ppermute | solution.py:67
  138.4 7.5 %collective-permute-start.27 = (bf16[2,16,48,128]{3,2,1,0:T(8,128)(2,1)S(1)}, bf16[2,16,48,128]{3,2,1,0:T(8,128)(2,1)S(1)}, u32[]{:S(2)}, u32[]{:S(2)}) collective-permute-start(bf16[2,16,48,128]{3,2,1,0:T(8,128)(2,1)S(1)} %bitcast.101), channel_id=1, source_target_pairs={{0,1},{1,0},{2,3},{3,2},{4,5},{5,4},{6,7},{7,6},{8,9},{9,8},{10,11... | collective-permute-start | bytes 1179656 | tf_op jit(solution)/shard_map/ppermute | solution.py:67
  138.5 7.4 %collective-permute-start.28 = (bf16[2,16,48,128]{3,2,1,0:T(8,128)(2,1)S(1)}, bf16[2,16,48,128]{3,2,1,0:T(8,128)(2,1)S(1)}, u32[]{:S(2)}, u32[]{:S(2)}) collective-permute-start(bf16[2,16,48,128]{3,2,1,0:T(8,128)(2,1)S(1)} %bitcast.100), channel_id=1, source_target_pairs={{0,1},{1,0},{2,3},{3,2},{4,5},{5,4},{6,7},{7,6},{8,9},{9,8},{10,11... | collective-permute-start | bytes 1179656 | tf_op jit(solution)/shard_map/ppermute | solution.py:67
  139.0 6.9 %collective-permute-start.29 = (bf16[2,16,48,128]{3,2,1,0:T(8,128)(2,1)S(1)}, bf16[2,16,48,128]{3,2,1,0:T(8,128)(2,1)S(1)}, u32[]{:S(2)}, u32[]{:S(2)}) collective-permute-start(bf16[2,16,48,128]{3,2,1,0:T(8,128)(2,1)S(1)} %bitcast.99), channel_id=1, source_target_pairs={{0,1},{1,0},{2,3},{3,2},{4,5},{5,4},{6,7},{7,6},{8,9},{9,8},{10,11... | collective-permute-start | bytes 1179656 | tf_op jit(solution)/shard_map/ppermute | solution.py:67
  144.2 20.1 %collective-permute-start.32 = (bf16[2,2,3,48,512]{4,3,2,1,0:T(8,128)(2,1)S(1)}, bf16[2,2,3,48,512]{4,3,2,1,0:T(8,128)(2,1)S(1)}, u32[]{:S(2)}, u32[]{:S(2)}) collective-permute-start(bf16[2,2,3,48,512]{4,3,2,1,0:T(8,128)(2,1)S(1)} %get-tuple-element.348), channel_id=1, source_target_pairs={{0,8},{1,9},{2,10},{3,11},{4,12},{5,13},{6,14},{7,15},{8,0},{9,1},... | collective-permute-start | bytes 1769480 | tf_op jit(solution)/shard_map/ppermute | solution.py:67
  146.8 18.1 %collective-permute-start.33 = (bf16[2,2,2,2,48,384]{5,4,3,2,1,0:T(8,128)(2,1)S(1)}, bf16[2,2,2,2,48,384]{5,4,3,2,1,0:T(8,128)(2,1)S(1)}, u32[]{:S(2)}, u32[]{:S(2)}) collective-permute-start(bf16[2,2,2,2,48,384]{5,4,3,2,1,0:T(8,128)(2,1)S(1)} %get-tuple-element.351), channel_id=1, source_target_pairs={{0,4},{1,3},{2,6},{3,1},{4,0},{5,7},{6,2},{7,5},{8,12},{9,11},{10,... | collective-permute-start | bytes 1769480 | tf_op jit(solution)/shard_map/ppermute | solution.py:67
  147.9 17.1 %collective-permute-start.34 = (bf16[2,2,2,2,48,384]{5,4,3,2,1,0:T(8,128)(2,1)S(1)}, bf16[2,2,2,2,48,384]{5,4,3,2,1,0:T(8,128)(2,1)S(1)}, u32[]{:S(2)}, u32[]{:S(2)}) collective-permute-start(bf16[2,2,2,2,48,384]{5,4,3,2,1,0:T(8,128)(2,1)S(1)} %get-tuple-element.352), channel_id=1, source_target_pairs={{0,4},{1,3},{2,6},{3,1},{4,0},{5,7},{6,2},{7,5},{8,12},{9,11},{10,... | collective-permute-start | bytes 1769480 | tf_op jit(solution)/shard_map/ppermute | solution.py:67
  148.9 14.4 %collective-permute-start.31 = (bf16[2,1,96,768]{3,2,1,0:T(8,128)(2,1)S(1)}, bf16[2,1,96,768]{3,2,1,0:T(8,128)(2,1)S(1)}, u32[]{:S(2)}, u32[]{:S(2)}) collective-permute-start(bf16[2,1,96,768]{3,2,1,0:T(8,128)(2,1)S(1)} %get-tuple-element.345), channel_id=1, source_target_pairs={{0,16},{1,17},{2,18},{3,19},{4,20},{5,21},{6,22},{7,23},{8,24},{9,... | collective-permute-start | bytes 884744 | tf_op jit(solution)/shard_map/ppermute | solution.py:67
  153.5 1.3 collective-permute-start.30
  154.8 15.4 %collective-permute-start.35 = (bf16[512,768]{1,0:T(8,128)(2,1)S(1)}, bf16[512,768]{1,0:T(8,128)(2,1)S(1)}, u32[]{:S(2)}, u32[]{:S(2)}) collective-permute-start(bf16[512,768]{1,0:T(8,128)(2,1)S(1)} %get-tuple-element.354.refs_2_), channel_id=1, source_target_pairs={{0,1},{1,0},{2,3},{3,2},{4,5},{5,4},{6,7},{7,6},{8,9},{9,8},{10,11... | collective-permute-start | bytes 2359304 | tf_op jit(solution)/shard_map/ppermute | solution.py:67
  165.8 9.9 %collective-permute-start.36 = (bf16[2,2,4,48,384]{4,3,2,1,0:T(8,128)(2,1)S(1)}, bf16[2,2,4,48,384]{4,3,2,1,0:T(8,128)(2,1)S(1)}, u32[]{:S(2)}, u32[]{:S(2)}) collective-permute-start(bf16[2,2,4,48,384]{4,3,2,1,0:T(8,128)(2,1)S(1)} %get-tuple-element.358), channel_id=1, source_target_pairs={{0,2},{1,5},{2,0},{3,7},{4,6},{5,1},{6,4},{7,3},{8,10},{9,13},{10,... | collective-permute-start | bytes 1769480 | tf_op jit(solution)/shard_map/ppermute | solution.py:67
  167.0 33.6 %collective-permute-start.42 = (bf16[512,768]{1,0:T(8,128)(2,1)S(1)}, bf16[512,768]{1,0:T(8,128)(2,1)S(1)}, u32[]{:S(2)}, u32[]{:S(2)}) collective-permute-start(bf16[512,768]{1,0:T(8,128)(2,1)S(1)} %get-tuple-element.378.refs_2_), channel_id=1, source_target_pairs={{0,1},{1,0},{2,3},{3,2},{4,5},{5,4},{6,7},{7,6},{8,9},{9,8},{10,11... | collective-permute-start | bytes 2359304 | tf_op jit(solution)/shard_map/ppermute | solution.py:67
  167.0 18.3 %collective-permute-start.38 = (bf16[2,3,48,512]{3,2,1,0:T(8,128)(2,1)S(1)}, bf16[2,3,48,512]{3,2,1,0:T(8,128)(2,1)S(1)}, u32[]{:S(2)}, u32[]{:S(2)}) collective-permute-start(bf16[2,3,48,512]{3,2,1,0:T(8,128)(2,1)S(1)} %get-tuple-element.364), channel_id=1, source_target_pairs={{0,16},{1,17},{2,18},{3,19},{4,20},{5,21},{6,22},{7,23},{8,24},{9,... | collective-permute-start | bytes 884744 | tf_op jit(solution)/shard_map/ppermute | solution.py:67
  170.2 13.8 %copy-start.11 = (f32[96,768]{1,0:T(8,128)S(1)}, f32[96,768]{1,0:T(8,128)}, u32[]{:S(2)}) copy-start(f32[96,768]{1,0:T(8,128)} %param.30) | copy-start | bytes 884740
  170.2 13.8 %copy-start.12 = (f32[96,768]{1,0:T(8,128)S(1)}, f32[96,768]{1,0:T(8,128)}, u32[]{:S(2)}) copy-start(f32[96,768]{1,0:T(8,128)} %param.34) | copy-start | bytes 884740
  176.4 14.7 %copy-start.6 = (f32[48,1536]{1,0:T(8,128)S(1)}, f32[48,1536]{1,0:T(8,128)}, u32[]{:S(2)}) copy-start(f32[48,1536]{1,0:T(8,128)} %param.25) | copy-start | bytes 884740
  176.4 14.7 %copy-start.13 = (f32[48,1536]{1,0:T(8,128)S(1)}, f32[48,1536]{1,0:T(8,128)}, u32[]{:S(2)}) copy-start(f32[48,1536]{1,0:T(8,128)} %param.29) | copy-start | bytes 884740
  176.4 14.7 %copy-start.14 = (f32[48,1536]{1,0:T(8,128)S(1)}, f32[48,1536]{1,0:T(8,128)}, u32[]{:S(2)}) copy-start(f32[48,1536]{1,0:T(8,128)} %param.33) | copy-start | bytes 884740
  176.4 11.3 %collective-permute-start.39 = (bf16[2,4,48,384]{3,2,1,0:T(8,128)(2,1)S(1)}, bf16[2,4,48,384]{3,2,1,0:T(8,128)(2,1)S(1)}, u32[]{:S(2)}, u32[]{:S(2)}) collective-permute-start(bf16[2,4,48,384]{3,2,1,0:T(8,128)(2,1)S(1)} %get-tuple-element.367), channel_id=1, source_target_pairs={{0,8},{1,9},{2,10},{3,11},{4,12},{5,13},{6,14},{7,15},{8,0},{9,1},... | collective-permute-start | bytes 884744 | tf_op jit(solution)/shard_map/ppermute | solution.py:67
  178.8 5.1 %collective-permute-start.37 = (bf16[1,96,768]{2,1,0:T(8,128)(2,1)S(1)}, bf16[1,96,768]{2,1,0:T(8,128)(2,1)S(1)}, u32[]{:S(2)}, u32[]{:S(2)}) collective-permute-start(bf16[1,96,768]{2,1,0:T(8,128)(2,1)S(1)} %get-tuple-element.361), channel_id=1, source_target_pairs={{0,2},{1,5},{2,0},{3,7},{4,6},{5,1},{6,4},{7,3},{8,10},{9,13},{10,... | collective-permute-start | bytes 442376 | tf_op jit(solution)/shard_map/ppermute | solution.py:67
  185.2 9.8 %copy-start.8 = (f32[3,48,384]{2,1,0:T(8,128)S(1)}, f32[3,48,384]{2,1,0:T(8,128)}, u32[]{:S(2)}) copy-start(f32[3,48,384]{2,1,0:T(8,128)} %refs_3_.3) | copy-start | bytes 663556
  185.2 9.8 %copy-start.10 = (f32[384,48]{0,1:T(8,128)S(1)}, f32[384,48]{0,1:T(8,128)}, u32[]{:S(2)}) copy-start(f32[384,48]{0,1:T(8,128)} %param.24) | copy-start | bytes 221188
  185.2 9.8 %copy-start.15 = (f32[3,48,384]{2,1,0:T(8,128)S(1)}, f32[3,48,384]{2,1,0:T(8,128)}, u32[]{:S(2)}) copy-start(f32[3,48,384]{2,1,0:T(8,128)} %refs_4_.4) | copy-start | bytes 663556
  185.2 9.9 %copy-start.16 = (f32[3,48,384]{2,1,0:T(8,128)S(1)}, f32[3,48,384]{2,1,0:T(8,128)}, u32[]{:S(2)}) copy-start(f32[3,48,384]{2,1,0:T(8,128)} %refs_5_.4) | copy-start | bytes 663556
  185.2 9.9 %copy-start.17 = (f32[384,48]{0,1:T(8,128)S(1)}, f32[384,48]{0,1:T(8,128)}, u32[]{:S(2)}) copy-start(f32[384,48]{0,1:T(8,128)} %param.28) | copy-start | bytes 221188
  185.2 9.9 %copy-start.18 = (f32[384,48]{0,1:T(8,128)S(1)}, f32[384,48]{0,1:T(8,128)}, u32[]{:S(2)}) copy-start(f32[384,48]{0,1:T(8,128)} %param.32) | copy-start | bytes 221188
  185.8 5.2 %collective-permute-start.40 = (bf16[3,48,512]{2,1,0:T(8,128)(2,1)S(1)}, bf16[3,48,512]{2,1,0:T(8,128)(2,1)S(1)}, u32[]{:S(2)}, u32[]{:S(2)}) collective-permute-start(bf16[3,48,512]{2,1,0:T(8,128)(2,1)S(1)} %get-tuple-element.370), channel_id=1, source_target_pairs={{0,2},{1,5},{2,0},{3,7},{4,6},{5,1},{6,4},{7,3},{8,10},{9,13},{10,... | collective-permute-start | bytes 442376 | tf_op jit(solution)/shard_map/ppermute | solution.py:67
  188.3 6.7 %collective-permute-start.41 = (bf16[4,48,384]{2,1,0:T(8,128)(2,1)S(1)}, bf16[4,48,384]{2,1,0:T(8,128)(2,1)S(1)}, u32[]{:S(2)}, u32[]{:S(2)}) collective-permute-start(bf16[4,48,384]{2,1,0:T(8,128)(2,1)S(1)} %get-tuple-element.373), channel_id=1, source_target_pairs={{0,16},{1,17},{2,18},{3,19},{4,20},{5,21},{6,22},{7,23},{8,24},{9,... | collective-permute-start | bytes 442376 | tf_op jit(solution)/shard_map/ppermute | solution.py:67
  195.1 17.5 %copy-start.19 = (f32[12,768]{1,0:T(8,128)S(1)}, f32[12,768]{1,0:T(8,128)}, u32[]{:S(2)}) copy-start(f32[12,768]{1,0:T(8,128)} %refs_5_.5) | copy-start | bytes 110596
  195.1 17.5 %copy-start.20 = (f32[12,768]{1,0:T(8,128)S(1)}, f32[12,768]{1,0:T(8,128)}, u32[]{:S(2)}) copy-start(f32[12,768]{1,0:T(8,128)} %refs_6_.1) | copy-start | bytes 110596
  196.2 6.8 %collective-permute-start.43 = (f32[8,768]{1,0:T(8,128)S(1)}, f32[8,768]{1,0:T(8,128)S(1)}, u32[]{:S(2)}, u32[]{:S(2)}) collective-permute-start(f32[8,768]{1,0:T(8,128)S(1)} %get-tuple-element.381.refs_1_), channel_id=1, source_target_pairs={{0,8},{1,9},{2,10},{3,11},{4,12},{5,13},{6,14},{7,15},{8,0},{9,1},... | collective-permute-start | bytes 73736 | tf_op jit(solution)/shard_map/ppermute | solution.py:67
  196.2 6.8 %collective-permute-start.44 = (f32[8,768]{1,0:T(8,128)S(1)}, f32[8,768]{1,0:T(8,128)S(1)}, u32[]{:S(2)}, u32[]{:S(2)}) collective-permute-start(f32[8,768]{1,0:T(8,128)S(1)} %get-tuple-element.381.refs_1_), channel_id=1, source_target_pairs={{0,16},{1,17},{2,18},{3,19},{4,20},{5,21},{6,22},{7,23},{8,24},{9,... | collective-permute-start | bytes 73736 | tf_op jit(solution)/shard_map/ppermute | solution.py:67
  199.0 5.6 %collective-permute-start.45 = (f32[8,768]{1,0:T(8,128)S(1)}, f32[8,768]{1,0:T(8,128)S(1)}, u32[]{:S(2)}, u32[]{:S(2)}) collective-permute-start(f32[8,768]{1,0:T(8,128)S(1)} %get-tuple-element.381.refs_1_), channel_id=1, source_target_pairs={{0,24},{1,25},{2,26},{3,27},{4,28},{5,29},{6,30},{7,31},{8,16},{9,... | collective-permute-start | bytes 73736 | tf_op jit(solution)/shard_map/ppermute | solution.py:67
  204.6 3.9 %collective-permute-start.46 = (f32[8,768]{1,0:T(8,128)S(1)}, f32[8,768]{1,0:T(8,128)S(1)}, u32[]{:S(2)}, u32[]{:S(2)}) collective-permute-start(f32[8,768]{1,0:T(8,128)S(1)} %get-tuple-element.383.refs_1_), channel_id=1, source_target_pairs={{0,4},{1,5},{2,6},{3,7},{4,0},{5,1},{6,2},{7,3},{8,12},{9,13},{10,... | collective-permute-start | bytes 73736 | tf_op jit(solution)/shard_map/ppermute | solution.py:67
  205.7 3.8 %collective-permute-start.47 = (f32[8,768]{1,0:T(8,128)S(1)}, f32[8,768]{1,0:T(8,128)S(1)}, u32[]{:S(2)}, u32[]{:S(2)}) collective-permute-start(f32[8,768]{1,0:T(8,128)S(1)} %get-tuple-element.383.refs_1_), channel_id=1, source_target_pairs={{0,2},{1,3},{2,0},{3,1},{4,6},{5,7},{6,4},{7,5},{8,10},{9,11},{10,... | collective-permute-start | bytes 73736 | tf_op jit(solution)/shard_map/ppermute | solution.py:67
  206.6 4.7 %collective-permute-start.48 = (f32[8,768]{1,0:T(8,128)S(1)}, f32[8,768]{1,0:T(8,128)S(1)}, u32[]{:S(2)}, u32[]{:S(2)}) collective-permute-start(f32[8,768]{1,0:T(8,128)S(1)} %get-tuple-element.383.refs_1_), channel_id=1, source_target_pairs={{0,6},{1,7},{2,4},{3,5},{4,2},{5,3},{6,0},{7,1},{8,14},{9,15},{10,... | collective-permute-start | bytes 73736 | tf_op jit(solution)/shard_map/ppermute | solution.py:67
  211.3 1.3 collective-permute-start.49
  (7 other events, 8.2 us)

commit v6 on v5

--- a/solution.py
+++ b/solution.py
@@ -490,9 +490,8 @@
             return jnp.where(low, v[:length], v[length:])
 
         def attend(count, qkv_ref, probs, context):
-            @pl.loop(0, mine)
-            def _(p):
-                at = pl.ds(pl.multiple_of(p * length, length), length)
+            for p in range(mine):
+                at = slice(p * length, (p + 1) * length)
                 known = lax.broadcasted_iota(jnp.int32, (length, length), 1) < count[4 + p]
                 for u in range(twins):
                     lanes = slice(u * LANES, (u + 1) * LANES)
@@ -689,9 +688,8 @@
 
             sums[...] = jnp.zeros_like(sums)
 
-            @pl.loop(0, mine)
-            def _(p):
-                at = pl.ds(pl.multiple_of(p * length, length), length)
+            for p in range(mine):
+                at = slice(p * length, (p + 1) * length)
                 upstream, normal = work[at], normed[at]
                 grad = norm_back(upstream, normal, inverse[at], vec[3:4])
                 mid[at] = grad
@@ -728,9 +726,8 @@
         def values_back(probs_ref, back_ref, grad, sums):
             sums[...] = jnp.zeros_like(sums)
 
-            @pl.loop(0, mine)
-            def _(p):
-                at = pl.ds(pl.multiple_of(p * length, length), length)
+            for p in range(mine):
+                at = slice(p * length, (p + 1) * length)
                 for u in range(twins):
                     lanes = slice(u * LANES, (u + 1) * LANES)
                     value = join(lax.dot_general(
@@ -782,9 +779,8 @@
         def attend_back(probs_ref, back_ref, qkv_ref, grad_q, grad_k, sums):
             sums[...] = jnp.zeros_like(sums)
 
-            @pl.loop(0, mine)
-            def _(p):
-                at = pl.ds(pl.multiple_of(p * length, length), length)
+            for p in range(mine):
+                at = slice(p * length, (p + 1) * length)
                 for u in range(twins):
                     lanes = slice(u * LANES, (u + 1) * LANES)
                     prob = probs_ref[at, 2 * u * length : 2 * (u + 1) * length].astype(F32)

time: 215 us -> 215 us (level)
  waiting for transfers between devices: 71.3 us -> 73.9 us
    ppermute x50, waiting for transfers between devices: 71.3 us -> 73.9 us  [send(): return lax.ppermute(value, AXES, pairs)]
  transfers between devices with their start and end apart: 50 -> 50, of which waited for: 25 -> 25; matrix products, arithmetic and copies ran while one was open for 0% -> 0% of each run, Pallas kernels for 34% -> 33%
where the time goes in v6:
time: 215 us
  Pallas kernels  83.3 us (39%)
  waiting for transfers between devices  73.9 us (34%)
  starting transfers between devices  48.6 us (23%)
  local copies, waits for them, and re-layouts  6.63 us (3%)
    pallas_call x63, Pallas kernels, run(): pl.pallas_call(chain, out_shape=shapes, in_specs=[pl.BlockSpec(memory_spa...  83.3 us
    ppermute x50, waiting for transfers between devices, send(): return lax.ppermute(value, AXES, pairs)  73.9 us
    ppermute x50, starting transfers between devices, send(): return lax.ppermute(value, AXES, pairs)  48.6 us
    unnamed x42, local copies, waits for them, and re-layouts  6.47 us
  transfers between devices with their start and end apart: 50, of which 25 were waited for; matrix products, arithmetic and copies ran while one was open for 0% of the time, Pallas kernels for 33%

profile of v6, /device:TPU:0, one launch (start us, length us, event | category | flops | bytes accessed | tf_op | source)
XLA Modules:
  0.0 214.6 jit_solution(1836619677513612776)
XLA Ops:
  2.5 3.1 %collective-permute-start = (bf16[4,48,384]{2,1,0:T(8,128)(2,1)S(1)}, bf16[4,48,384]{2,1,0:T(8,128)(2,1)S(1)}, u32[]{:S(2)}, u32[]{:S(2)}) collective-permute-start(bf16[4,48,384]{2,1,0:T(8,128)(2,1)S(1)} %get-tuple-element.221.refs_2_), channel_id=1, source_target_pairs={{0,8},{1,9},{2,10},{3,11},{4,12},{5,13},{6,14},{7,15},{8,0},{9,1},... | collective-permute-start | bytes 442376 | tf_op jit(solution)/shard_map/ppermute | solution.py:67
  5.6 2.6 %collective-permute-start.1 = (bf16[4,48,384]{2,1,0:T(8,128)(2,1)S(1)}, bf16[4,48,384]{2,1,0:T(8,128)(2,1)S(1)}, u32[]{:S(2)}, u32[]{:S(2)}) collective-permute-start(bf16[4,48,384]{2,1,0:T(8,128)(2,1)S(1)} %get-tuple-element.221.refs_2_), channel_id=1, source_target_pairs={{0,16},{1,17},{2,18},{3,19},{4,20},{5,21},{6,22},{7,23},{8,24},{9,... | collective-permute-start | bytes 442376 | tf_op jit(solution)/shard_map/ppermute | solution.py:67
  10.0 1.4 copy-done
  11.4 1.4 copy-done.1
  14.6 5.0 %collective-permute-done.1.refs_4_ = bf16[4,48,384]{2,1,0:T(8,128)(2,1)S(1)} collective-permute-done((bf16[4,48,384]{2,1,0:T(8,128)(2,1)S(1)}, bf16[4,48,384]{2,1,0:T(8,128)(2,1)S(1)}, u32[]{:S(2)}, u32[]{:S(2)}) %collective-permute-start.1) | collective-permute-done | bytes 147488 | tf_op jit(solution)/shard_map/ppermute | solution.py:67
  20.2 1.6 collective-permute-start.4
  21.8 3.3 %collective-permute-start.3 = (bf16[1,48,1536]{2,1,0:T(8,128)(2,1)S(1)}, bf16[1,48,1536]{2,1,0:T(8,128)(2,1)S(1)}, u32[]{:S(2)}, u32[]{:S(2)}) collective-permute-start(bf16[1,48,1536]{2,1,0:T(8,128)(2,1)S(1)} %get-tuple-element.223.refs_2_), channel_id=1, source_target_pairs={{0,16},{1,17},{2,18},{3,19},{4,20},{5,21},{6,22},{7,23},{8,24},{9,... | collective-permute-start | bytes 442376 | tf_op jit(solution)/shard_map/ppermute | solution.py:67
  25.1 5.8 %collective-permute-done.3.refs_3_ = bf16[1,48,1536]{2,1,0:T(8,128)(2,1)S(1)} collective-permute-done((bf16[1,48,1536]{2,1,0:T(8,128)(2,1)S(1)}, bf16[1,48,1536]{2,1,0:T(8,128)(2,1)S(1)}, u32[]{:S(2)}, u32[]{:S(2)}) %collective-permute-start.3) | collective-permute-done | bytes 147488 | tf_op jit(solution)/shard_map/ppermute | solution.py:67
  32.7 2.0 collective-permute-start.6
  34.7 1.6 collective-permute-start.5
  36.3 5.3 %collective-permute-done.5.refs_3_ = bf16[1,96,768]{2,1,0:T(8,128)(2,1)S(1)} collective-permute-done((bf16[1,96,768]{2,1,0:T(8,128)(2,1)S(1)}, bf16[1,96,768]{2,1,0:T(8,128)(2,1)S(1)}, u32[]{:S(2)}, u32[]{:S(2)}) %collective-permute-start.5) | collective-permute-done | bytes 147488 | tf_op jit(solution)/shard_map/ppermute | solution.py:67
  42.8 1.6 collective-permute-start.9
  45.3 9.8 %collective-permute-done.7.refs_3_ = bf16[2,2,2,4,48,384]{5,4,3,2,1,0:T(8,128)(2,1)S(1)} collective-permute-done((bf16[2,2,2,4,48,384]{5,4,3,2,1,0:T(8,128)(2,1)S(1)}, bf16[2,2,2,4,48,384]{5,4,3,2,1,0:T(8,128)(2,1)S(1)}, u32[]{:S(2)}, u32[]{:S(2)}) %collective-permute-start.7) | collective-permute-done | bytes 1179680 | tf_op jit(solution)/shard_map/ppermute | solution.py:67
  58.4 1.7 collective-permute-start.13
  61.0 3.2 %project.1 = (bf16[3,512,768]{2,1,0:T(8,128)(2,1)S(1)}, f32[8,128]{1,0:T(8,128)S(1)}) custom-call(f32[8,128]{1,0:T(8,128)S(1)} %get-tuple-element.239.refs_0_, bf16[512,768]{1,0:T(8,128)(2,1)S(1)} %get-tuple-element.240.refs_1_.refs_2_, bf16[4,768,384]{2,1,0:T(8,128)(2,1)S(1)} %bitcast.61, bf16[4,768,384]{2,1,0:T(8,128)(2,1)S(1)} %bitcast.65, ...), custom_call_target="tpu_custom_call" | custom-call | flops 1811939328 | bytes 8388608 | tf_op jit(solution)/shard_map/project/pallas_call | solution.py:142
  64.1 3.3 %attend.1 = (bf16[512,1536]{1,0:T(8,128)(2,1)S(1)}, bf16[512,768]{1,0:T(8,128)(2,1)S(1)}, f32[8,128]{1,0:T(8,128)S(1)}) custom-call(s32[8]{0:T(128)S(1)} %concatenate.3.refs_0_, f32[8,128]{1,0:T(8,128)S(1)} %get-tuple-element.244.refs_1_, bf16[3,512,768]{2,1,0:T(8,128)(2,1)S(1)} %get-tuple-element.245.refs_2_.refs_3_), custom_call_target="tpu_custom_call" | custom-call | flops 805306368 | bytes 5242880 | tf_op jit(solution)/shard_map/attend/pallas_call | solution.py:142
  67.5 6.5 %collective-permute-done.12.refs_3_ = bf16[2,2,1,96,768]{4,3,2,1,0:T(8,128)(2,1)S(1)} collective-permute-done((bf16[2,2,1,96,768]{4,3,2,1,0:T(8,128)(2,1)S(1)}, bf16[2,2,1,96,768]{4,3,2,1,0:T(8,128)(2,1)S(1)}, u32[]{:S(2)}, u32[]{:S(2)}) %collective-permute-start.12) | collective-permute-done | bytes 589856 | tf_op jit(solution)/shard_map/ppermute | solution.py:67
  75.5 1.7 collective-permute-start.16
  77.2 1.1 collective-permute-done.15.refs_3_
  79.0 1.3 hide.1
  80.4 3.4 %_lambda_.2 = (bf16[512,1536]{1,0:T(8,128)(2,1)S(1)}, bf16[1536,512]{1,0:T(8,128)(2,1)S(1)}, bf16[512,1536]{1,0:T(8,128)(2,1)S(1)}, f32[8,128]{1,0:T(8,128)S(1)}) custom-call(f32[8,128]{1,0:T(8,128)S(1)} %get-tuple-element.254.refs_0_, bf16[512,768]{1,0:T(8,128)(2,1)S(1)} %get-tuple-element.255.refs_1_, bf16[768,1536]{1,0:T(8,128)(2,1)S(1)} %bitcast.74, ...), custom_call_target="tpu_custom_call" | custom-call | flops 1207959552 | bytes 8388608 | tf_op jit(solution)/shard_map/<lambda>/pallas_call | solution.py:142
  83.8 3.4 %_lambda_.3 = (bf16[512,1536]{1,0:T(8,128)(2,1)S(1)}, bf16[1536,512]{1,0:T(8,128)(2,1)S(1)}, bf16[512,1536]{1,0:T(8,128)(2,1)S(1)}, f32[8,128]{1,0:T(8,128)S(1)}) custom-call(f32[8,128]{1,0:T(8,128)S(1)} %get-tuple-element.258.refs_0_, bf16[512,768]{1,0:T(8,128)(2,1)S(1)} %get-tuple-element.255.refs_1_, bf16[768,1536]{1,0:T(8,128)(2,1)S(1)} %bitcast.76, ...), custom_call_target="tpu_custom_call" | custom-call | flops 1207959552 | bytes 8388608 | tf_op jit(solution)/shard_map/<lambda>/pallas_call | solution.py:142
  87.4 4.4 %collective-permute-done.16.refs_3_ = bf16[2,2,2,1,96,768]{5,4,3,2,1,0:T(8,128)(2,1)S(1)} collective-permute-done((bf16[2,2,2,1,96,768]{5,4,3,2,1,0:T(8,128)(2,1)S(1)}, bf16[2,2,2,1,96,768]{5,4,3,2,1,0:T(8,128)(2,1)S(1)}, u32[]{:S(2)}, u32[]{:S(2)}) %collective-permute-start.16) | collective-permute-done | bytes 1179680 | tf_op jit(solution)/shard_map/ppermute | solution.py:67
  92.6 1.7 lower_half.1
  94.4 1.1 collective-permute-done.18.refs_3_
  96.2 3.9 %lower.1 = (bf16[512,768]{1,0:T(8,128)(2,1)S(1)}, f32[512,768]{1,0:T(8,128)S(1)}, bf16[512,768]{1,0:T(8,128)(2,1)S(1)}, f32[8,768]{1,0:T(8,128)S(1)}, f32[8,128]{1,0:T(8,128)S(1)}) custom-call(s32[8]{0:T(128)S(1)} %concatenate.3.refs_0_, f32[8,128]{1,0:T(8,128)S(1)} %get-tuple-element.268.refs_1_, f32[512,768]{1,0:T(8,128)S(1)} %get-tuple-element.269.refs_2_, ...), custom_call_target="tpu_custom_call" | custom-call | flops 1207959552 | bytes 14680064 | tf_op jit(solution)/shard_map/lower/pallas_call | solution.py:142
  100.1 2.5 %sink.2 = (bf16[512,1536]{1,0:T(8,128)(2,1)S(1)}, f32[1,1536]{1,0:T(1,128)S(1)}, f32[8,128]{1,0:T(8,128)S(1)}) custom-call(f32[8,128]{1,0:T(8,128)S(1)} %get-tuple-element.274.refs_0_, bf16[512,768]{1,0:T(8,128)(2,1)S(1)} %get-tuple-element.275.refs_1_.refs_2_, bf16[1536,768]{1,0:T(8,128)(2,1)S(1)} %bitcast.70, bf16[512,1536]{1,0:T(8,128)(2,1)S(1)} %get-tuple-element.276.refs_3_), custom_call_target="tpu_custom_call" | custom-call | tf_op jit(solution)/shard_map/sink/pallas_call | solution.py:142
  102.6 2.2 %product.4 = (bf16[1536,768]{1,0:T(8,128)(2,1)S(1)}, f32[8,128]{1,0:T(8,128)S(1)}) custom-call(f32[8,128]{1,0:T(8,128)S(1)} %get-tuple-element.277.refs_0_, bf16[1536,512]{1,0:T(8,128)(2,1)S(1)} %get-tuple-element.278.refs_1_, bf16[512,768]{1,0:T(8,128)(2,1)S(1)} %get-tuple-element.275.refs_1_.refs_2_), custom_call_target="tpu_custom_call" | custom-call | flops 1207959552 | bytes 8388608 | tf_op jit(solution)/shard_map/product/pallas_call | solution.py:142
  105.0 2.2 %product.5 = (f32[1536,768]{1,0:T(8,128)S(1)}, f32[8,128]{1,0:T(8,128)S(1)}) custom-call(f32[8,128]{1,0:T(8,128)S(1)} %get-tuple-element.279.refs_0_, bf16[1536,512]{1,0:T(8,128)(2,1)S(1)} %get-tuple-element.280.refs_1_, bf16[512,768]{1,0:T(8,128)(2,1)S(1)} %get-tuple-element.275.refs_1_.refs_2_), custom_call_target="tpu_custom_call" | custom-call | flops 1207959552 | bytes 8388608 | tf_op jit(solution)/shard_map/product/pallas_call | solution.py:142
  107.3 1.7 product.6
  109.9 1.1 scatter_pair.3
  111.0 1.7 collective-permute-start.23
  112.7 2.5 %sink.3 = (bf16[512,1536]{1,0:T(8,128)(2,1)S(1)}, f32[1,1536]{1,0:T(1,128)S(1)}, f32[8,128]{1,0:T(8,128)S(1)}) custom-call(f32[8,128]{1,0:T(8,128)S(1)} %get-tuple-element.287.refs_0_, bf16[512,768]{1,0:T(8,128)(2,1)S(1)} %get-tuple-element.275.refs_1_.refs_2_, bf16[1536,768]{1,0:T(8,128)(2,1)S(1)} %bitcast.73, bf16[512,1536]{1,0:T(8,128)(2,1)S(1)} %get-tuple-element.288.refs_3_), custom_call_target="tpu_custom_call" | custom-call | tf_op jit(solution)/shard_map/sink/pallas_call | solution.py:142
  115.3 2.0 product.7
  118.2 4.9 %surface.1 = (f32[512,768]{1,0:T(8,128)S(1)}, bf16[768,512]{1,0:T(8,128)(2,1)S(1)}, bf16[512,768]{1,0:T(8,128)(2,1)S(1)}, f32[8,768]{1,0:T(8,128)S(1)}, f32[8,128]{1,0:T(8,128)S(1)}) custom-call(f32[8,128]{1,0:T(8,128)S(1)} %get-tuple-element.298.refs_0_, bf16[512,1536]{1,0:T(8,128)(2,1)S(1)} %get-tuple-element.290.refs_2_.refs_1_, ...), custom_call_target="tpu_custom_call" | custom-call | flops 3019898880 | bytes 14680064 | tf_op jit(solution)/shard_map/surface/pallas_call | solution.py:142
  125.5 1.8 collective-permute-done.23.refs_3_
  128.1 1.7 collective-permute-start.25
  129.8 6.6 %attend_back.1 = (bf16[512,768]{1,0:T(8,128)(2,1)S(1)}, bf16[512,768]{1,0:T(8,128)(2,1)S(1)}, f32[1,768]{1,0:T(1,128)S(1)}, f32[8,128]{1,0:T(8,128)S(1)}) custom-call(f32[8,128]{1,0:T(8,128)S(1)} %get-tuple-element.311.refs_0_, bf16[512,1536]{1,0:T(8,128)(2,1)S(1)} %get-tuple-element.302.refs_1_, bf16[512,768]{1,0:T(8,128)(2,1)S(1)} %get-tuple-element.303.refs_2_, ...), custom_call_target="tpu_custom_call" | custom-call | flops 805306368 | bytes 6291456 | tf_op jit(solution)/shard_map/attend_back/pallas_call | solution.py:142
  140.4 2.3 %collective-permute-done.25.refs_3_ = bf16[2,2,1,96,768]{4,3,2,1,0:T(8,128)(2,1)S(1)} collective-permute-done((bf16[2,2,1,96,768]{4,3,2,1,0:T(8,128)(2,1)S(1)}, bf16[2,2,1,96,768]{4,3,2,1,0:T(8,128)(2,1)S(1)}, u32[]{:S(2)}, u32[]{:S(2)}) %collective-permute-start.25) | collective-permute-done | bytes 589856 | tf_op jit(solution)/shard_map/ppermute | solution.py:67
  144.1 1.8 collective-permute-start.32
  147.6 1.3 collective-permute-start.34
  149.9 3.0 %states_back.1 = (bf16[512,768]{1,0:T(8,128)(2,1)S(1)}, f32[8,128]{1,0:T(8,128)S(1)}) custom-call(f32[8,128]{1,0:T(8,128)S(1)} %get-tuple-element.332.refs_0_, bf16[512,768]{1,0:T(8,128)(2,1)S(1)} %get-tuple-element.313.refs_3_.refs_1_, bf16[512,768]{1,0:T(8,128)(2,1)S(1)} %get-tuple-element.314.refs_4_.refs_2_, ...), custom_call_target="tpu_custom_call" | custom-call | flops 1811939328 | bytes 8388608 | tf_op jit(solution)/shard_map/states_back/pallas_call | solution.py:142
  153.5 1.2 collective-permute-done.30.refs_3_
  155.5 7.9 %collective-permute-done.31.refs_3_ = bf16[2,1,96,768]{3,2,1,0:T(8,128)(2,1)S(1)} collective-permute-done((bf16[2,1,96,768]{3,2,1,0:T(8,128)(2,1)S(1)}, bf16[2,1,96,768]{3,2,1,0:T(8,128)(2,1)S(1)}, u32[]{:S(2)}, u32[]{:S(2)}) %collective-permute-start.31) | collective-permute-done | bytes 294944 | tf_op jit(solution)/shard_map/ppermute | solution.py:67
  165.6 1.4 collective-permute-start.36
  166.9 3.3 %collective-permute-start.38 = (bf16[2,3,48,512]{3,2,1,0:T(8,128)(2,1)S(1)}, bf16[2,3,48,512]{3,2,1,0:T(8,128)(2,1)S(1)}, u32[]{:S(2)}, u32[]{:S(2)}) collective-permute-start(bf16[2,3,48,512]{3,2,1,0:T(8,128)(2,1)S(1)} %get-tuple-element.364), channel_id=1, source_target_pairs={{0,16},{1,17},{2,18},{3,19},{4,20},{5,21},{6,22},{7,23},{8,24},{9,... | collective-permute-start | bytes 884744 | tf_op jit(solution)/shard_map/ppermute | solution.py:67
  170.2 1.8 pair_up.2
  172.0 3.5 %collective-permute-done.36.refs_3_ = bf16[2,2,4,48,384]{4,3,2,1,0:T(8,128)(2,1)S(1)} collective-permute-done((bf16[2,2,4,48,384]{4,3,2,1,0:T(8,128)(2,1)S(1)}, bf16[2,2,4,48,384]{4,3,2,1,0:T(8,128)(2,1)S(1)}, u32[]{:S(2)}, u32[]{:S(2)}) %collective-permute-start.36) | collective-permute-done | bytes 589856 | tf_op jit(solution)/shard_map/ppermute | solution.py:67
  176.2 2.6 %collective-permute-start.39 = (bf16[2,4,48,384]{3,2,1,0:T(8,128)(2,1)S(1)}, bf16[2,4,48,384]{3,2,1,0:T(8,128)(2,1)S(1)}, u32[]{:S(2)}, u32[]{:S(2)}) collective-permute-start(bf16[2,4,48,384]{3,2,1,0:T(8,128)(2,1)S(1)} %get-tuple-element.367), channel_id=1, source_target_pairs={{0,8},{1,9},{2,10},{3,11},{4,12},{5,13},{6,14},{7,15},{8,0},{9,1},... | collective-permute-start | bytes 884744 | tf_op jit(solution)/shard_map/ppermute | solution.py:67
  179.4 4.6 %collective-permute-done.37.refs_2_ = bf16[1,96,768]{2,1,0:T(8,128)(2,1)S(1)} collective-permute-done((bf16[1,96,768]{2,1,0:T(8,128)(2,1)S(1)}, bf16[1,96,768]{2,1,0:T(8,128)(2,1)S(1)}, u32[]{:S(2)}, u32[]{:S(2)}) %collective-permute-start.37) | collective-permute-done | bytes 147488 | tf_op jit(solution)/shard_map/ppermute | solution.py:67
  184.0 1.2 step.2
  186.5 1.7 collective-permute-done.39.refs_3_
  188.8 2.2 %collective-permute-done.40.refs_2_ = bf16[3,48,512]{2,1,0:T(8,128)(2,1)S(1)} collective-permute-done((bf16[3,48,512]{2,1,0:T(8,128)(2,1)S(1)}, bf16[3,48,512]{2,1,0:T(8,128)(2,1)S(1)}, u32[]{:S(2)}, u32[]{:S(2)}) %collective-permute-start.40) | collective-permute-done | bytes 147488 | tf_op jit(solution)/shard_map/ppermute | solution.py:67
  191.1 1.2 step.3
  192.3 3.2 %collective-permute-done.41.refs_2_ = bf16[4,48,384]{2,1,0:T(8,128)(2,1)S(1)} collective-permute-done((bf16[4,48,384]{2,1,0:T(8,128)(2,1)S(1)}, bf16[4,48,384]{2,1,0:T(8,128)(2,1)S(1)}, u32[]{:S(2)}, u32[]{:S(2)}) %collective-permute-start.41) | collective-permute-done | bytes 147488 | tf_op jit(solution)/shard_map/ppermute | solution.py:67
  195.5 1.1 attend_step.1
  196.6 2.6 %collective-permute-start.44 = (f32[8,768]{1,0:T(8,128)S(1)}, f32[8,768]{1,0:T(8,128)S(1)}, u32[]{:S(2)}, u32[]{:S(2)}) collective-permute-start(f32[8,768]{1,0:T(8,128)S(1)} %get-tuple-element.381.refs_1_), channel_id=1, source_target_pairs={{0,16},{1,17},{2,18},{3,19},{4,20},{5,21},{6,22},{7,23},{8,24},{9,... | collective-permute-start | bytes 73736 | tf_op jit(solution)/shard_map/ppermute | solution.py:67
  199.2 1.8 collective-permute-start.45
  201.0 2.4 %pair_up.3 = (f32[2,512,768]{2,1,0:T(8,128)}, f32[8,128]{1,0:T(8,128)S(1)}) custom-call(s32[8]{0:T(128)S(1)} %concatenate.3.refs_0_, f32[8,128]{1,0:T(8,128)S(1)} %get-tuple-element.377.refs_1_, bf16[512,768]{1,0:T(8,128)(2,1)S(1)} %get-tuple-element.378.refs_2_, bf16[512,768]{1,0:T(8,128)(2,1)S(1)} %collective-permute-done.42.refs_3_), custom_call_target="tpu_custom_call" | custom-call | tf_op jit(solution)/shard_map/pair_up/pallas_call | solution.py:142
  203.4 1.4 collective-permute-done.45.refs_4_
  206.4 1.9 collective-permute-start.48
  209.6 1.6 collective-permute-done.48.refs_4_
  211.3 1.2 collective-permute-done.49.refs_3_
  212.5 2.0 update.1
  (144 shorter events, 41.1 us)
Async XLA Ops:
  2.5 12.1 %collective-permute-start = (bf16[4,48,384]{2,1,0:T(8,128)(2,1)S(1)}, bf16[4,48,384]{2,1,0:T(8,128)(2,1)S(1)}, u32[]{:S(2)}, u32[]{:S(2)}) collective-permute-start(bf16[4,48,384]{2,1,0:T(8,128)(2,1)S(1)} %get-tuple-element.221.refs_2_), channel_id=1, source_target_pairs={{0,8},{1,9},{2,10},{3,11},{4,12},{5,13},{6,14},{7,15},{8,0},{9,1},... | collective-permute-start | bytes 442376 | tf_op jit(solution)/shard_map/ppermute | solution.py:67
  5.6 14.0 %collective-permute-start.1 = (bf16[4,48,384]{2,1,0:T(8,128)(2,1)S(1)}, bf16[4,48,384]{2,1,0:T(8,128)(2,1)S(1)}, u32[]{:S(2)}, u32[]{:S(2)}) collective-permute-start(bf16[4,48,384]{2,1,0:T(8,128)(2,1)S(1)} %get-tuple-element.221.refs_2_), channel_id=1, source_target_pairs={{0,16},{1,17},{2,18},{3,19},{4,20},{5,21},{6,22},{7,23},{8,24},{9,... | collective-permute-start | bytes 442376 | tf_op jit(solution)/shard_map/ppermute | solution.py:67
  8.2 11.4 %collective-permute-start.2 = (bf16[4,48,384]{2,1,0:T(8,128)(2,1)S(1)}, bf16[4,48,384]{2,1,0:T(8,128)(2,1)S(1)}, u32[]{:S(2)}, u32[]{:S(2)}) collective-permute-start(bf16[4,48,384]{2,1,0:T(8,128)(2,1)S(1)} %get-tuple-element.221.refs_2_), channel_id=1, source_target_pairs={{0,24},{1,25},{2,26},{3,27},{4,28},{5,29},{6,30},{7,31},{8,16},{9,... | collective-permute-start | bytes 442376 | tf_op jit(solution)/shard_map/ppermute | solution.py:67
  14.6 20.1 %copy-start.4 = (f32[96,768]{1,0:T(8,128)S(1)}, f32[96,768]{1,0:T(8,128)}, u32[]{:S(2)}) copy-start(f32[96,768]{1,0:T(8,128)} %param.26) | copy-start | bytes 884740
  20.2 11.2 %collective-permute-start.4 = (bf16[2,2,4,48,384]{4,3,2,1,0:T(8,128)(2,1)S(1)}, bf16[2,2,4,48,384]{4,3,2,1,0:T(8,128)(2,1)S(1)}, u32[]{:S(2)}, u32[]{:S(2)}) collective-permute-start(bf16[2,2,4,48,384]{4,3,2,1,0:T(8,128)(2,1)S(1)} %get-tuple-element.225.refs_2_), channel_id=1, source_target_pairs={{0,2},{1,5},{2,0},{3,7},{4,6},{5,1},{6,4},{7,3},{8,10},{9,13},{10,... | collective-permute-start | bytes 1769480 | tf_op jit(solution)/shard_map/ppermute | solution.py:67
  21.8 9.1 %collective-permute-start.3 = (bf16[1,48,1536]{2,1,0:T(8,128)(2,1)S(1)}, bf16[1,48,1536]{2,1,0:T(8,128)(2,1)S(1)}, u32[]{:S(2)}, u32[]{:S(2)}) collective-permute-start(bf16[1,48,1536]{2,1,0:T(8,128)(2,1)S(1)} %get-tuple-element.223.refs_2_), channel_id=1, source_target_pairs={{0,16},{1,17},{2,18},{3,19},{4,20},{5,21},{6,22},{7,23},{8,24},{9,... | collective-permute-start | bytes 442376 | tf_op jit(solution)/shard_map/ppermute | solution.py:67
  32.1 23.1 %collective-permute-start.7 = (bf16[2,2,2,4,48,384]{5,4,3,2,1,0:T(8,128)(2,1)S(1)}, bf16[2,2,2,4,48,384]{5,4,3,2,1,0:T(8,128)(2,1)S(1)}, u32[]{:S(2)}, u32[]{:S(2)}) collective-permute-start(bf16[2,2,2,4,48,384]{5,4,3,2,1,0:T(8,128)(2,1)S(1)} %get-tuple-element.232.refs_2_), channel_id=1, source_target_pairs={{0,4},{1,3},{2,6},{3,1},{4,0},{5,7},{6,2},{7,5},{8,12},{9,11},{10,... | collective-permute-start | bytes 3538952 | tf_op jit(solution)/shard_map/ppermute | solution.py:67
  32.7 9.5 %collective-permute-start.6 = (bf16[2,1,48,1536]{3,2,1,0:T(8,128)(2,1)S(1)}, bf16[2,1,48,1536]{3,2,1,0:T(8,128)(2,1)S(1)}, u32[]{:S(2)}, u32[]{:S(2)}) collective-permute-start(bf16[2,1,48,1536]{3,2,1,0:T(8,128)(2,1)S(1)} %get-tuple-element.230.refs_2_), channel_id=1, source_target_pairs={{0,8},{1,9},{2,10},{3,11},{4,12},{5,13},{6,14},{7,15},{8,0},{9,1},... | collective-permute-start | bytes 884744 | tf_op jit(solution)/shard_map/ppermute | solution.py:67
  34.7 6.9 %collective-permute-start.5 = (bf16[1,96,768]{2,1,0:T(8,128)(2,1)S(1)}, bf16[1,96,768]{2,1,0:T(8,128)(2,1)S(1)}, u32[]{:S(2)}, u32[]{:S(2)}) collective-permute-start(bf16[1,96,768]{2,1,0:T(8,128)(2,1)S(1)} %get-tuple-element.228.refs_2_), channel_id=1, source_target_pairs={{0,2},{1,5},{2,0},{3,7},{4,6},{5,1},{6,4},{7,3},{8,10},{9,13},{10,... | collective-permute-start | bytes 442376 | tf_op jit(solution)/shard_map/ppermute | solution.py:67
  42.8 15.0 %collective-permute-start.9 = (bf16[2,2,1,48,1536]{4,3,2,1,0:T(8,128)(2,1)S(1)}, bf16[2,2,1,48,1536]{4,3,2,1,0:T(8,128)(2,1)S(1)}, u32[]{:S(2)}, u32[]{:S(2)}) collective-permute-start(bf16[2,2,1,48,1536]{4,3,2,1,0:T(8,128)(2,1)S(1)} %get-tuple-element.236.refs_2_), channel_id=1, source_target_pairs={{0,2},{1,5},{2,0},{3,7},{4,6},{5,1},{6,4},{7,3},{8,10},{9,13},{10,... | collective-permute-start | bytes 1769480 | tf_op jit(solution)/shard_map/ppermute | solution.py:67
  44.3 12.8 %collective-permute-start.8 = (bf16[2,1,96,768]{3,2,1,0:T(8,128)(2,1)S(1)}, bf16[2,1,96,768]{3,2,1,0:T(8,128)(2,1)S(1)}, u32[]{:S(2)}, u32[]{:S(2)}) collective-permute-start(bf16[2,1,96,768]{3,2,1,0:T(8,128)(2,1)S(1)} %get-tuple-element.234.refs_2_), channel_id=1, source_target_pairs={{0,16},{1,17},{2,18},{3,19},{4,20},{5,21},{6,22},{7,23},{8,24},{9,... | collective-permute-start | bytes 884744 | tf_op jit(solution)/shard_map/ppermute | solution.py:67
  45.3 14.9 %collective-permute-start.10 = (bf16[2,2,2,4,48,384]{5,4,3,2,1,0:T(8,128)(2,1)S(1)}, bf16[2,2,2,4,48,384]{5,4,3,2,1,0:T(8,128)(2,1)S(1)}, u32[]{:S(2)}, u32[]{:S(2)}) collective-permute-start(bf16[2,2,2,4,48,384]{5,4,3,2,1,0:T(8,128)(2,1)S(1)} %get-tuple-element.232.refs_2_), channel_id=1, source_target_pairs={{0,1},{1,0},{2,3},{3,2},{4,5},{5,4},{6,7},{7,6},{8,9},{9,8},{10,11... | collective-permute-start | bytes 3538952 | tf_op jit(solution)/shard_map/ppermute | solution.py:67
  56.0 4.2 %collective-permute-start.11 = (bf16[2,2,2,4,48,384]{5,4,3,2,1,0:T(8,128)(2,1)S(1)}, bf16[2,2,2,4,48,384]{5,4,3,2,1,0:T(8,128)(2,1)S(1)}, u32[]{:S(2)}, u32[]{:S(2)}) collective-permute-start(bf16[2,2,2,4,48,384]{5,4,3,2,1,0:T(8,128)(2,1)S(1)} %get-tuple-element.238), channel_id=1, source_target_pairs={{0,1},{1,0},{2,3},{3,2},{4,5},{5,4},{6,7},{7,6},{8,9},{9,8},{10,11... | collective-permute-start | bytes 3538952 | tf_op jit(solution)/shard_map/ppermute | solution.py:67
  58.4 16.3 %collective-permute-start.13 = (bf16[2,2,2,1,48,1536]{5,4,3,2,1,0:T(8,128)(2,1)S(1)}, bf16[2,2,2,1,48,1536]{5,4,3,2,1,0:T(8,128)(2,1)S(1)}, u32[]{:S(2)}, u32[]{:S(2)}) collective-permute-start(bf16[2,2,2,1,48,1536]{5,4,3,2,1,0:T(8,128)(2,1)S(1)} %get-tuple-element.249.refs_2_), channel_id=1, source_target_pairs={{0,4},{1,3},{2,6},{3,1},{4,0},{5,7},{6,2},{7,5},{8,12},{9,11},{10,... | collective-permute-start | bytes 3538952 | tf_op jit(solution)/shard_map/ppermute | solution.py:67
  60.1 13.8 %collective-permute-start.12 = (bf16[2,2,1,96,768]{4,3,2,1,0:T(8,128)(2,1)S(1)}, bf16[2,2,1,96,768]{4,3,2,1,0:T(8,128)(2,1)S(1)}, u32[]{:S(2)}, u32[]{:S(2)}) collective-permute-start(bf16[2,2,1,96,768]{4,3,2,1,0:T(8,128)(2,1)S(1)} %get-tuple-element.247.refs_2_), channel_id=1, source_target_pairs={{0,8},{1,9},{2,10},{3,11},{4,12},{5,13},{6,14},{7,15},{8,0},{9,1},... | collective-permute-start | bytes 1769480 | tf_op jit(solution)/shard_map/ppermute | solution.py:67
  60.2 17.0 %collective-permute-start.14 = (bf16[2,2,2,1,48,1536]{5,4,3,2,1,0:T(8,128)(2,1)S(1)}, bf16[2,2,2,1,48,1536]{5,4,3,2,1,0:T(8,128)(2,1)S(1)}, u32[]{:S(2)}, u32[]{:S(2)}) collective-permute-start(bf16[2,2,2,1,48,1536]{5,4,3,2,1,0:T(8,128)(2,1)S(1)} %get-tuple-element.249.refs_2_), channel_id=1, source_target_pairs={{0,1},{1,0},{2,3},{3,2},{4,5},{5,4},{6,7},{7,6},{8,9},{9,8},{10,11... | collective-permute-start | bytes 3538952 | tf_op jit(solution)/shard_map/ppermute | solution.py:67
  75.4 2.9 %collective-permute-start.15 = (bf16[2,2,2,1,48,1536]{5,4,3,2,1,0:T(8,128)(2,1)S(1)}, bf16[2,2,2,1,48,1536]{5,4,3,2,1,0:T(8,128)(2,1)S(1)}, u32[]{:S(2)}, u32[]{:S(2)}) collective-permute-start(bf16[2,2,2,1,48,1536]{5,4,3,2,1,0:T(8,128)(2,1)S(1)} %get-tuple-element.251), channel_id=1, source_target_pairs={{0,1},{1,0},{2,3},{3,2},{4,5},{5,4},{6,7},{7,6},{8,9},{9,8},{10,11... | collective-permute-start | bytes 3538952 | tf_op jit(solution)/shard_map/ppermute | solution.py:67
  75.5 16.3 %collective-permute-start.16 = (bf16[2,2,2,1,96,768]{5,4,3,2,1,0:T(8,128)(2,1)S(1)}, bf16[2,2,2,1,96,768]{5,4,3,2,1,0:T(8,128)(2,1)S(1)}, u32[]{:S(2)}, u32[]{:S(2)}) collective-permute-start(bf16[2,2,2,1,96,768]{5,4,3,2,1,0:T(8,128)(2,1)S(1)} %get-tuple-element.262.refs_2_), channel_id=1, source_target_pairs={{0,4},{1,3},{2,6},{3,1},{4,0},{5,7},{6,2},{7,5},{8,12},{9,11},{10,... | collective-permute-start | bytes 3538952 | tf_op jit(solution)/shard_map/ppermute | solution.py:67
  77.2 17.2 %collective-permute-start.17 = (bf16[2,2,2,1,96,768]{5,4,3,2,1,0:T(8,128)(2,1)S(1)}, bf16[2,2,2,1,96,768]{5,4,3,2,1,0:T(8,128)(2,1)S(1)}, u32[]{:S(2)}, u32[]{:S(2)}) collective-permute-start(bf16[2,2,2,1,96,768]{5,4,3,2,1,0:T(8,128)(2,1)S(1)} %get-tuple-element.262.refs_2_), channel_id=1, source_target_pairs={{0,1},{1,0},{2,3},{3,2},{4,5},{5,4},{6,7},{7,6},{8,9},{9,8},{10,11... | collective-permute-start | bytes 3538952 | tf_op jit(solution)/shard_map/ppermute | solution.py:67
  92.5 2.9 %collective-permute-start.18 = (bf16[2,2,2,1,96,768]{5,4,3,2,1,0:T(8,128)(2,1)S(1)}, bf16[2,2,2,1,96,768]{5,4,3,2,1,0:T(8,128)(2,1)S(1)}, u32[]{:S(2)}, u32[]{:S(2)}) collective-permute-start(bf16[2,2,2,1,96,768]{5,4,3,2,1,0:T(8,128)(2,1)S(1)} %get-tuple-element.267), channel_id=1, source_target_pairs={{0,1},{1,0},{2,3},{3,2},{4,5},{5,4},{6,7},{7,6},{8,9},{9,8},{10,11... | collective-permute-start | bytes 3538952 | tf_op jit(solution)/shard_map/ppermute | solution.py:67
  104.8 5.1 %collective-permute-start.19 = (bf16[1,16,96,768]{3,2,1,0:T(8,128)(2,1)S(1)}, bf16[1,16,96,768]{3,2,1,0:T(8,128)(2,1)S(1)}, u32[]{:S(2)}, u32[]{:S(2)}) collective-permute-start(bf16[1,16,96,768]{3,2,1,0:T(8,128)(2,1)S(1)} %bitcast.95), channel_id=1, source_target_pairs={{0,1},{1,0},{2,3},{3,2},{4,5},{5,4},{6,7},{7,6},{8,9},{9,8},{10,11... | collective-permute-start | bytes 7077896 | tf_op jit(solution)/shard_map/ppermute | solution.py:67
  109.0 8.2 %collective-permute-start.20 = (bf16[1,16,48,512]{3,2,1,0:T(8,128)(2,1)S(1)}, bf16[1,16,48,512]{3,2,1,0:T(8,128)(2,1)S(1)}, u32[]{:S(2)}, u32[]{:S(2)}) collective-permute-start(bf16[1,16,48,512]{3,2,1,0:T(8,128)(2,1)S(1)} %bitcast.98), channel_id=1, source_target_pairs={{0,1},{1,0},{2,3},{3,2},{4,5},{5,4},{6,7},{7,6},{8,9},{9,8},{10,11... | collective-permute-start | bytes 2359304 | tf_op jit(solution)/shard_map/ppermute | solution.py:67
  109.4 7.8 %collective-permute-start.21 = (bf16[1,16,48,512]{3,2,1,0:T(8,128)(2,1)S(1)}, bf16[1,16,48,512]{3,2,1,0:T(8,128)(2,1)S(1)}, u32[]{:S(2)}, u32[]{:S(2)}) collective-permute-start(bf16[1,16,48,512]{3,2,1,0:T(8,128)(2,1)S(1)} %bitcast.97), channel_id=1, source_target_pairs={{0,1},{1,0},{2,3},{3,2},{4,5},{5,4},{6,7},{7,6},{8,9},{9,8},{10,11... | collective-permute-start | bytes 2359304 | tf_op jit(solution)/shard_map/ppermute | solution.py:67
  109.6 7.7 %collective-permute-start.22 = (bf16[1,16,48,512]{3,2,1,0:T(8,128)(2,1)S(1)}, bf16[1,16,48,512]{3,2,1,0:T(8,128)(2,1)S(1)}, u32[]{:S(2)}, u32[]{:S(2)}) collective-permute-start(bf16[1,16,48,512]{3,2,1,0:T(8,128)(2,1)S(1)} %bitcast.96), channel_id=1, source_target_pairs={{0,1},{1,0},{2,3},{3,2},{4,5},{5,4},{6,7},{7,6},{8,9},{9,8},{10,11... | collective-permute-start | bytes 2359304 | tf_op jit(solution)/shard_map/ppermute | solution.py:67
  111.0 16.3 %collective-permute-start.23 = (bf16[2,2,2,1,96,768]{5,4,3,2,1,0:T(8,128)(2,1)S(1)}, bf16[2,2,2,1,96,768]{5,4,3,2,1,0:T(8,128)(2,1)S(1)}, u32[]{:S(2)}, u32[]{:S(2)}) collective-permute-start(bf16[2,2,2,1,96,768]{5,4,3,2,1,0:T(8,128)(2,1)S(1)} %get-tuple-element.310), channel_id=1, source_target_pairs={{0,4},{1,3},{2,6},{3,1},{4,0},{5,7},{6,2},{7,5},{8,12},{9,11},{10,... | collective-permute-start | bytes 3538952 | tf_op jit(solution)/shard_map/ppermute | solution.py:67
  124.7 14.3 %collective-permute-start.24 = (bf16[2,768,384]{2,1,0:T(8,128)(2,1)S(1)}, bf16[2,768,384]{2,1,0:T(8,128)(2,1)S(1)}, u32[]{:S(2)}, u32[]{:S(2)}) collective-permute-start(bf16[2,768,384]{2,1,0:T(8,128)(2,1)S(1)} %get-tuple-element.319), channel_id=1, source_target_pairs={{0,1},{1,0},{2,3},{3,2},{4,5},{5,4},{6,7},{7,6},{8,9},{9,8},{10,11... | collective-permute-start | bytes 3538952 | tf_op jit(solution)/shard_map/ppermute | solution.py:67
  124.8 18.5 %collective-permute-start.26 = (bf16[2,2,2,3,48,512]{5,4,3,2,1,0:T(8,128)(2,1)S(1)}, bf16[2,2,2,3,48,512]{5,4,3,2,1,0:T(8,128)(2,1)S(1)}, u32[]{:S(2)}, u32[]{:S(2)}) collective-permute-start(bf16[2,2,2,3,48,512]{5,4,3,2,1,0:T(8,128)(2,1)S(1)} %get-tuple-element.325), channel_id=1, source_target_pairs={{0,4},{1,3},{2,6},{3,1},{4,0},{5,7},{6,2},{7,5},{8,12},{9,11},{10,... | collective-permute-start | bytes 3538952 | tf_op jit(solution)/shard_map/ppermute | solution.py:67
  128.1 14.6 %collective-permute-start.25 = (bf16[2,2,1,96,768]{4,3,2,1,0:T(8,128)(2,1)S(1)}, bf16[2,2,1,96,768]{4,3,2,1,0:T(8,128)(2,1)S(1)}, u32[]{:S(2)}, u32[]{:S(2)}) collective-permute-start(bf16[2,2,1,96,768]{4,3,2,1,0:T(8,128)(2,1)S(1)} %get-tuple-element.322), channel_id=1, source_target_pairs={{0,8},{1,9},{2,10},{3,11},{4,12},{5,13},{6,14},{7,15},{8,0},{9,1},... | collective-permute-start | bytes 1769480 | tf_op jit(solution)/shard_map/ppermute | solution.py:67
  138.5 7.4 %collective-permute-start.27 = (bf16[2,16,48,128]{3,2,1,0:T(8,128)(2,1)S(1)}, bf16[2,16,48,128]{3,2,1,0:T(8,128)(2,1)S(1)}, u32[]{:S(2)}, u32[]{:S(2)}) collective-permute-start(bf16[2,16,48,128]{3,2,1,0:T(8,128)(2,1)S(1)} %bitcast.101), channel_id=1, source_target_pairs={{0,1},{1,0},{2,3},{3,2},{4,5},{5,4},{6,7},{7,6},{8,9},{9,8},{10,11... | collective-permute-start | bytes 1179656 | tf_op jit(solution)/shard_map/ppermute | solution.py:67
  138.6 7.3 %collective-permute-start.28 = (bf16[2,16,48,128]{3,2,1,0:T(8,128)(2,1)S(1)}, bf16[2,16,48,128]{3,2,1,0:T(8,128)(2,1)S(1)}, u32[]{:S(2)}, u32[]{:S(2)}) collective-permute-start(bf16[2,16,48,128]{3,2,1,0:T(8,128)(2,1)S(1)} %bitcast.100), channel_id=1, source_target_pairs={{0,1},{1,0},{2,3},{3,2},{4,5},{5,4},{6,7},{7,6},{8,9},{9,8},{10,11... | collective-permute-start | bytes 1179656 | tf_op jit(solution)/shard_map/ppermute | solution.py:67
  139.1 6.8 %collective-permute-start.29 = (bf16[2,16,48,128]{3,2,1,0:T(8,128)(2,1)S(1)}, bf16[2,16,48,128]{3,2,1,0:T(8,128)(2,1)S(1)}, u32[]{:S(2)}, u32[]{:S(2)}) collective-permute-start(bf16[2,16,48,128]{3,2,1,0:T(8,128)(2,1)S(1)} %bitcast.99), channel_id=1, source_target_pairs={{0,1},{1,0},{2,3},{3,2},{4,5},{5,4},{6,7},{7,6},{8,9},{9,8},{10,11... | collective-permute-start | bytes 1179656 | tf_op jit(solution)/shard_map/ppermute | solution.py:67
  144.1 20.0 %collective-permute-start.32 = (bf16[2,2,3,48,512]{4,3,2,1,0:T(8,128)(2,1)S(1)}, bf16[2,2,3,48,512]{4,3,2,1,0:T(8,128)(2,1)S(1)}, u32[]{:S(2)}, u32[]{:S(2)}) collective-permute-start(bf16[2,2,3,48,512]{4,3,2,1,0:T(8,128)(2,1)S(1)} %get-tuple-element.348), channel_id=1, source_target_pairs={{0,8},{1,9},{2,10},{3,11},{4,12},{5,13},{6,14},{7,15},{8,0},{9,1},... | collective-permute-start | bytes 1769480 | tf_op jit(solution)/shard_map/ppermute | solution.py:67
  146.8 17.9 %collective-permute-start.33 = (bf16[2,2,2,2,48,384]{5,4,3,2,1,0:T(8,128)(2,1)S(1)}, bf16[2,2,2,2,48,384]{5,4,3,2,1,0:T(8,128)(2,1)S(1)}, u32[]{:S(2)}, u32[]{:S(2)}) collective-permute-start(bf16[2,2,2,2,48,384]{5,4,3,2,1,0:T(8,128)(2,1)S(1)} %get-tuple-element.351), channel_id=1, source_target_pairs={{0,4},{1,3},{2,6},{3,1},{4,0},{5,7},{6,2},{7,5},{8,12},{9,11},{10,... | collective-permute-start | bytes 1769480 | tf_op jit(solution)/shard_map/ppermute | solution.py:67
  147.6 17.1 %collective-permute-start.34 = (bf16[2,2,2,2,48,384]{5,4,3,2,1,0:T(8,128)(2,1)S(1)}, bf16[2,2,2,2,48,384]{5,4,3,2,1,0:T(8,128)(2,1)S(1)}, u32[]{:S(2)}, u32[]{:S(2)}) collective-permute-start(bf16[2,2,2,2,48,384]{5,4,3,2,1,0:T(8,128)(2,1)S(1)} %get-tuple-element.352), channel_id=1, source_target_pairs={{0,4},{1,3},{2,6},{3,1},{4,0},{5,7},{6,2},{7,5},{8,12},{9,11},{10,... | collective-permute-start | bytes 1769480 | tf_op jit(solution)/shard_map/ppermute | solution.py:67
  148.9 14.4 %collective-permute-start.31 = (bf16[2,1,96,768]{3,2,1,0:T(8,128)(2,1)S(1)}, bf16[2,1,96,768]{3,2,1,0:T(8,128)(2,1)S(1)}, u32[]{:S(2)}, u32[]{:S(2)}) collective-permute-start(bf16[2,1,96,768]{3,2,1,0:T(8,128)(2,1)S(1)} %get-tuple-element.345), channel_id=1, source_target_pairs={{0,16},{1,17},{2,18},{3,19},{4,20},{5,21},{6,22},{7,23},{8,24},{9,... | collective-permute-start | bytes 884744 | tf_op jit(solution)/shard_map/ppermute | solution.py:67
  153.4 1.3 collective-permute-start.30
  154.7 15.5 %collective-permute-start.35 = (bf16[512,768]{1,0:T(8,128)(2,1)S(1)}, bf16[512,768]{1,0:T(8,128)(2,1)S(1)}, u32[]{:S(2)}, u32[]{:S(2)}) collective-permute-start(bf16[512,768]{1,0:T(8,128)(2,1)S(1)} %get-tuple-element.354.refs_2_), channel_id=1, source_target_pairs={{0,1},{1,0},{2,3},{3,2},{4,5},{5,4},{6,7},{7,6},{8,9},{9,8},{10,11... | collective-permute-start | bytes 2359304 | tf_op jit(solution)/shard_map/ppermute | solution.py:67
  165.6 9.9 %collective-permute-start.36 = (bf16[2,2,4,48,384]{4,3,2,1,0:T(8,128)(2,1)S(1)}, bf16[2,2,4,48,384]{4,3,2,1,0:T(8,128)(2,1)S(1)}, u32[]{:S(2)}, u32[]{:S(2)}) collective-permute-start(bf16[2,2,4,48,384]{4,3,2,1,0:T(8,128)(2,1)S(1)} %get-tuple-element.358), channel_id=1, source_target_pairs={{0,2},{1,5},{2,0},{3,7},{4,6},{5,1},{6,4},{7,3},{8,10},{9,13},{10,... | collective-permute-start | bytes 1769480 | tf_op jit(solution)/shard_map/ppermute | solution.py:67
  166.9 34.1 %collective-permute-start.42 = (bf16[512,768]{1,0:T(8,128)(2,1)S(1)}, bf16[512,768]{1,0:T(8,128)(2,1)S(1)}, u32[]{:S(2)}, u32[]{:S(2)}) collective-permute-start(bf16[512,768]{1,0:T(8,128)(2,1)S(1)} %get-tuple-element.378.refs_2_), channel_id=1, source_target_pairs={{0,1},{1,0},{2,3},{3,2},{4,5},{5,4},{6,7},{7,6},{8,9},{9,8},{10,11... | collective-permute-start | bytes 2359304 | tf_op jit(solution)/shard_map/ppermute | solution.py:67
  166.9 18.3 %collective-permute-start.38 = (bf16[2,3,48,512]{3,2,1,0:T(8,128)(2,1)S(1)}, bf16[2,3,48,512]{3,2,1,0:T(8,128)(2,1)S(1)}, u32[]{:S(2)}, u32[]{:S(2)}) collective-permute-start(bf16[2,3,48,512]{3,2,1,0:T(8,128)(2,1)S(1)} %get-tuple-element.364), channel_id=1, source_target_pairs={{0,16},{1,17},{2,18},{3,19},{4,20},{5,21},{6,22},{7,23},{8,24},{9,... | collective-permute-start | bytes 884744 | tf_op jit(solution)/shard_map/ppermute | solution.py:67
  170.2 13.8 %copy-start.11 = (f32[96,768]{1,0:T(8,128)S(1)}, f32[96,768]{1,0:T(8,128)}, u32[]{:S(2)}) copy-start(f32[96,768]{1,0:T(8,128)} %param.30) | copy-start | bytes 884740
  170.2 13.8 %copy-start.12 = (f32[96,768]{1,0:T(8,128)S(1)}, f32[96,768]{1,0:T(8,128)}, u32[]{:S(2)}) copy-start(f32[96,768]{1,0:T(8,128)} %param.34) | copy-start | bytes 884740
  176.2 14.9 %copy-start.6 = (f32[48,1536]{1,0:T(8,128)S(1)}, f32[48,1536]{1,0:T(8,128)}, u32[]{:S(2)}) copy-start(f32[48,1536]{1,0:T(8,128)} %param.25) | copy-start | bytes 884740
  176.2 14.9 %copy-start.13 = (f32[48,1536]{1,0:T(8,128)S(1)}, f32[48,1536]{1,0:T(8,128)}, u32[]{:S(2)}) copy-start(f32[48,1536]{1,0:T(8,128)} %param.29) | copy-start | bytes 884740
  176.2 14.9 %copy-start.14 = (f32[48,1536]{1,0:T(8,128)S(1)}, f32[48,1536]{1,0:T(8,128)}, u32[]{:S(2)}) copy-start(f32[48,1536]{1,0:T(8,128)} %param.33) | copy-start | bytes 884740
  176.2 12.0 %collective-permute-start.39 = (bf16[2,4,48,384]{3,2,1,0:T(8,128)(2,1)S(1)}, bf16[2,4,48,384]{3,2,1,0:T(8,128)(2,1)S(1)}, u32[]{:S(2)}, u32[]{:S(2)}) collective-permute-start(bf16[2,4,48,384]{3,2,1,0:T(8,128)(2,1)S(1)} %get-tuple-element.367), channel_id=1, source_target_pairs={{0,8},{1,9},{2,10},{3,11},{4,12},{5,13},{6,14},{7,15},{8,0},{9,1},... | collective-permute-start | bytes 884744 | tf_op jit(solution)/shard_map/ppermute | solution.py:67
  178.8 5.1 %collective-permute-start.37 = (bf16[1,96,768]{2,1,0:T(8,128)(2,1)S(1)}, bf16[1,96,768]{2,1,0:T(8,128)(2,1)S(1)}, u32[]{:S(2)}, u32[]{:S(2)}) collective-permute-start(bf16[1,96,768]{2,1,0:T(8,128)(2,1)S(1)} %get-tuple-element.361), channel_id=1, source_target_pairs={{0,2},{1,5},{2,0},{3,7},{4,6},{5,1},{6,4},{7,3},{8,10},{9,13},{10,... | collective-permute-start | bytes 442376 | tf_op jit(solution)/shard_map/ppermute | solution.py:67
  185.2 10.3 %copy-start.8 = (f32[3,48,384]{2,1,0:T(8,128)S(1)}, f32[3,48,384]{2,1,0:T(8,128)}, u32[]{:S(2)}) copy-start(f32[3,48,384]{2,1,0:T(8,128)} %refs_3_.3) | copy-start | bytes 663556
  185.2 10.3 %copy-start.10 = (f32[384,48]{0,1:T(8,128)S(1)}, f32[384,48]{0,1:T(8,128)}, u32[]{:S(2)}) copy-start(f32[384,48]{0,1:T(8,128)} %param.24) | copy-start | bytes 221188
  185.2 10.3 %copy-start.15 = (f32[3,48,384]{2,1,0:T(8,128)S(1)}, f32[3,48,384]{2,1,0:T(8,128)}, u32[]{:S(2)}) copy-start(f32[3,48,384]{2,1,0:T(8,128)} %refs_4_.4) | copy-start | bytes 663556
  185.2 10.3 %copy-start.16 = (f32[3,48,384]{2,1,0:T(8,128)S(1)}, f32[3,48,384]{2,1,0:T(8,128)}, u32[]{:S(2)}) copy-start(f32[3,48,384]{2,1,0:T(8,128)} %refs_5_.4) | copy-start | bytes 663556
  185.2 10.3 %copy-start.17 = (f32[384,48]{0,1:T(8,128)S(1)}, f32[384,48]{0,1:T(8,128)}, u32[]{:S(2)}) copy-start(f32[384,48]{0,1:T(8,128)} %param.28) | copy-start | bytes 221188
  185.2 10.3 %copy-start.18 = (f32[384,48]{0,1:T(8,128)S(1)}, f32[384,48]{0,1:T(8,128)}, u32[]{:S(2)}) copy-start(f32[384,48]{0,1:T(8,128)} %param.32) | copy-start | bytes 221188
  185.8 5.2 %collective-permute-start.40 = (bf16[3,48,512]{2,1,0:T(8,128)(2,1)S(1)}, bf16[3,48,512]{2,1,0:T(8,128)(2,1)S(1)}, u32[]{:S(2)}, u32[]{:S(2)}) collective-permute-start(bf16[3,48,512]{2,1,0:T(8,128)(2,1)S(1)} %get-tuple-element.370), channel_id=1, source_target_pairs={{0,2},{1,5},{2,0},{3,7},{4,6},{5,1},{6,4},{7,3},{8,10},{9,13},{10,... | collective-permute-start | bytes 442376 | tf_op jit(solution)/shard_map/ppermute | solution.py:67
  188.8 6.7 %collective-permute-start.41 = (bf16[4,48,384]{2,1,0:T(8,128)(2,1)S(1)}, bf16[4,48,384]{2,1,0:T(8,128)(2,1)S(1)}, u32[]{:S(2)}, u32[]{:S(2)}) collective-permute-start(bf16[4,48,384]{2,1,0:T(8,128)(2,1)S(1)} %get-tuple-element.373), channel_id=1, source_target_pairs={{0,16},{1,17},{2,18},{3,19},{4,20},{5,21},{6,22},{7,23},{8,24},{9,... | collective-permute-start | bytes 442376 | tf_op jit(solution)/shard_map/ppermute | solution.py:67
  195.5 17.0 %copy-start.19 = (f32[12,768]{1,0:T(8,128)S(1)}, f32[12,768]{1,0:T(8,128)}, u32[]{:S(2)}) copy-start(f32[12,768]{1,0:T(8,128)} %refs_5_.5) | copy-start | bytes 110596
  195.5 17.0 %copy-start.20 = (f32[12,768]{1,0:T(8,128)S(1)}, f32[12,768]{1,0:T(8,128)}, u32[]{:S(2)}) copy-start(f32[12,768]{1,0:T(8,128)} %refs_6_.1) | copy-start | bytes 110596
  196.6 6.8 %collective-permute-start.43 = (f32[8,768]{1,0:T(8,128)S(1)}, f32[8,768]{1,0:T(8,128)S(1)}, u32[]{:S(2)}, u32[]{:S(2)}) collective-permute-start(f32[8,768]{1,0:T(8,128)S(1)} %get-tuple-element.381.refs_1_), channel_id=1, source_target_pairs={{0,8},{1,9},{2,10},{3,11},{4,12},{5,13},{6,14},{7,15},{8,0},{9,1},... | collective-permute-start | bytes 73736 | tf_op jit(solution)/shard_map/ppermute | solution.py:67
  196.6 6.8 %collective-permute-start.44 = (f32[8,768]{1,0:T(8,128)S(1)}, f32[8,768]{1,0:T(8,128)S(1)}, u32[]{:S(2)}, u32[]{:S(2)}) collective-permute-start(f32[8,768]{1,0:T(8,128)S(1)} %get-tuple-element.381.refs_1_), channel_id=1, source_target_pairs={{0,16},{1,17},{2,18},{3,19},{4,20},{5,21},{6,22},{7,23},{8,24},{9,... | collective-permute-start | bytes 73736 | tf_op jit(solution)/shard_map/ppermute | solution.py:67
  199.2 5.6 %collective-permute-start.45 = (f32[8,768]{1,0:T(8,128)S(1)}, f32[8,768]{1,0:T(8,128)S(1)}, u32[]{:S(2)}, u32[]{:S(2)}) collective-permute-start(f32[8,768]{1,0:T(8,128)S(1)} %get-tuple-element.381.refs_1_), channel_id=1, source_target_pairs={{0,24},{1,25},{2,26},{3,27},{4,28},{5,29},{6,30},{7,31},{8,16},{9,... | collective-permute-start | bytes 73736 | tf_op jit(solution)/shard_map/ppermute | solution.py:67
  204.8 3.9 %collective-permute-start.46 = (f32[8,768]{1,0:T(8,128)S(1)}, f32[8,768]{1,0:T(8,128)S(1)}, u32[]{:S(2)}, u32[]{:S(2)}) collective-permute-start(f32[8,768]{1,0:T(8,128)S(1)} %get-tuple-element.383.refs_1_), channel_id=1, source_target_pairs={{0,4},{1,5},{2,6},{3,7},{4,0},{5,1},{6,2},{7,3},{8,12},{9,13},{10,... | collective-permute-start | bytes 73736 | tf_op jit(solution)/shard_map/ppermute | solution.py:67
  205.7 3.8 %collective-permute-start.47 = (f32[8,768]{1,0:T(8,128)S(1)}, f32[8,768]{1,0:T(8,128)S(1)}, u32[]{:S(2)}, u32[]{:S(2)}) collective-permute-start(f32[8,768]{1,0:T(8,128)S(1)} %get-tuple-element.383.refs_1_), channel_id=1, source_target_pairs={{0,2},{1,3},{2,0},{3,1},{4,6},{5,7},{6,4},{7,5},{8,10},{9,11},{10,... | collective-permute-start | bytes 73736 | tf_op jit(solution)/shard_map/ppermute | solution.py:67
  206.4 4.7 %collective-permute-start.48 = (f32[8,768]{1,0:T(8,128)S(1)}, f32[8,768]{1,0:T(8,128)S(1)}, u32[]{:S(2)}, u32[]{:S(2)}) collective-permute-start(f32[8,768]{1,0:T(8,128)S(1)} %get-tuple-element.383.refs_1_), channel_id=1, source_target_pairs={{0,6},{1,7},{2,4},{3,5},{4,2},{5,3},{6,0},{7,1},{8,14},{9,15},{10,... | collective-permute-start | bytes 73736 | tf_op jit(solution)/shard_map/ppermute | solution.py:67
  211.2 1.3 collective-permute-start.49
  (7 other events, 8.2 us)
